TPU v7x, 32 devices: a whole 2x2x4 slice. The times are simulated.
32 devices in a mesh: dom: 16 (over z, y, x), rep: 2 (over core).
Axes of the slice: x: 2, y: 2, z: 4, core: 2. Of those that a mesh axis runs over, the one named last changes fastest.
Arguments:
- embeds: bfloat16 [16384, 1024], P(('dom', 'rep')), may hold values from -6 to 6
- weight_in: bfloat16 [1024, 4096], replicated, may hold values from -0.1875 to 0.1875
- weight_out: bfloat16 [4096, 512], replicated, may hold values from -0.09375 to 0.09375
- prototypes: bfloat16 [1000, 512], replicated, may hold values from -4 to 4
- tile_column: int32 [128, 8], P(('dom', 'rep')), may hold values from 0 to 5, as said below
- tile_weight: bfloat16 [128, 8, 128, 128], P(('dom', 'rep')), may hold values from 0 to 1
- send_rows: int32 [32, 32, 8], P(('dom', 'rep')), may hold values from 0 to 511
- send_count: int32 [32, 32], P(('dom', 'rep')), may hold values from 1 to 8, as said below
- label_rows: int32 [2048], P(('dom', 'rep')), may hold values from 0 to 511, as said below
- label_class: int32 [2048], P(('dom', 'rep')), may hold values from 0 to 999
Outputs:
- embed_grad: bfloat16 [16384, 1024], P(('dom', 'rep'))
- grad_weight_out: float32 [4096, 512], P(('dom', 'rep'))
Inputs may be any that keep to these rules, and one draw needn't show every extreme that they name: `tile_column`: in each row block b the first tile names block b mod 4, tiles 1 to 3 name blocks below 4, the others name received blocks; every received block is named by some tile of its partition. `send_count`: every partition fills all 8 slots for at least one other partition. `label_rows`: distinct within a partition.
All inputs are finite; a program needn't handle non-finite values.
Results may differ from a plain program's by a relative error of at most 0.006.
The roundings to bfloat16 on the way count: a program that leaves them out, or rounds other values in their place, can miss the bound.
Values may be sent and summed in bfloat16 or wider, within the bound.
No kernel may reach another device: no remote copies, remote signals or barrier semaphores. Data moves between devices by JAX's collectives and lax.ppermute only.
A program may use at most 128 MiB of HBM per device.

v0:
```python
import math

import jax
import jax.numpy as jnp
from jax import lax
from jax.sharding import PartitionSpec as P

gelu_inner = 0.7978845608028654
gelu_cubic = 0.044715


def gelu_value(values):
    inner_arg = gelu_inner * (values + gelu_cubic * values * values * values)
    return 0.5 * values * (1.0 + jnp.tanh(inner_arg))


def gelu_slope(values):
    inner_arg = gelu_inner * (values + gelu_cubic * values * values * values)
    tangent = jnp.tanh(inner_arg)
    return 0.5 * (1.0 + tangent) + 0.5 * values * (1.0 - tangent * tangent) * gelu_inner * (
        1.0 + 3.0 * gelu_cubic * values * values
    )


def body(
    embeds,
    weight_in,
    weight_out,
    prototypes,
    tile_column,
    tile_weight,
    send_rows,
    send_count,
    label_rows,
    label_class,
):
    node_count = embeds.shape[0]
    block_count = tile_weight.shape[0]
    tile_count = tile_weight.shape[1]
    block_size = tile_weight.shape[2]
    width_out = weight_out.shape[1]
    dom_count = lax.axis_size("dom")
    rep_count = lax.axis_size("rep")
    peer_count = dom_count * rep_count
    slot_count = send_rows.shape[2]
    pre_act = jnp.dot(embeds, weight_in, preferred_element_type=jnp.float32)
    hidden = gelu_value(pre_act).astype(jnp.bfloat16)
    projected = jnp.dot(hidden, weight_out, preferred_element_type=jnp.float32)
    rowsum = jnp.sum(tile_weight, axis=(1, 3), dtype=jnp.float32).reshape(node_count)
    scaling = lax.rsqrt(1.0 + rowsum)
    unit_rows = (projected * scaling[:, None]).astype(jnp.bfloat16)
    slot_mask = (
        lax.broadcasted_iota(jnp.int32, (peer_count, slot_count), 1) < send_count[0][:, None]
    )
    flat_sends = send_rows[0].reshape(peer_count * slot_count)
    outgoing = jnp.take(unit_rows, flat_sends, axis=0).reshape(peer_count, slot_count, width_out)
    outgoing = jnp.where(slot_mask[:, :, None], outgoing, jnp.zeros_like(outgoing))
    incoming = lax.all_to_all(outgoing, ("dom", "rep"), split_axis=0, concat_axis=0, tiled=True)
    incoming = incoming.reshape(peer_count * slot_count, width_out)
    extended = jnp.concatenate([unit_rows, incoming], axis=0).reshape(-1, block_size, width_out)
    total_blocks = extended.shape[0]
    flat_columns = tile_column.reshape(block_count * tile_count)
    sources = jnp.take(extended, flat_columns, axis=0).reshape(
        block_count, tile_count, block_size, width_out
    )
    neighbour = jnp.einsum(
        "rtab,rtbd->rad", tile_weight, sources, preferred_element_type=jnp.float32
    )
    row_term = rowsum[:, None] * unit_rows.astype(jnp.float32) - neighbour.reshape(
        node_count, width_out
    )
    unit_blocks = unit_rows.reshape(block_count, block_size, width_out)
    column_sum = jnp.sum(tile_weight, axis=2, dtype=jnp.float32)
    column_term = column_sum[:, :, :, None] * sources.astype(jnp.float32) - jnp.einsum(
        "rtab,rad->rtbd", tile_weight, unit_blocks, preferred_element_type=jnp.float32
    )
    selector = (
        flat_columns[:, None]
        == lax.broadcasted_iota(jnp.int32, (block_count * tile_count, total_blocks), 1)
    ).astype(jnp.float32)
    gathered_terms = jnp.einsum(
        "tc,tf->cf",
        selector,
        column_term.reshape(block_count * tile_count, block_size * width_out),
        precision=lax.Precision.HIGHEST,
    )
    own_term = gathered_terms[:block_count].reshape(node_count, width_out)
    returned = (
        gathered_terms[block_count:].reshape(peer_count, slot_count, width_out).astype(jnp.bfloat16)
    )
    arrived = lax.all_to_all(returned, ("dom", "rep"), split_axis=0, concat_axis=0, tiled=True)
    back_rows = arrived.reshape(peer_count * slot_count, width_out)
    placement = (
        flat_sends[None, :]
        == lax.broadcasted_iota(jnp.int32, (node_count, peer_count * slot_count), 0)
    ) & slot_mask.reshape(peer_count * slot_count)[None, :]
    back_sum = jnp.dot(
        placement.astype(jnp.bfloat16), back_rows, preferred_element_type=jnp.float32
    )
    grad_proj = (row_term + own_term + back_sum) * scaling[:, None]
    class_table = (
        label_class[:, None]
        == lax.broadcasted_iota(jnp.int32, (label_class.shape[0], prototypes.shape[0]), 1)
    ).astype(jnp.bfloat16)
    targets = jnp.dot(class_table, prototypes, preferred_element_type=jnp.float32)
    grad_proj = grad_proj.at[label_rows].add(jnp.take(projected, label_rows, axis=0) - targets)
    grad_node = grad_proj.astype(jnp.bfloat16)
    grad_hidden = lax.dot_general(
        grad_node, weight_out, (((1,), (1,)), ((), ())), preferred_element_type=jnp.float32
    )
    grad_pre = (grad_hidden * gelu_slope(pre_act)).astype(jnp.bfloat16)
    embed_grad = lax.dot_general(
        grad_pre, weight_in, (((1,), (1,)), ((), ())), preferred_element_type=jnp.float32
    ).astype(jnp.bfloat16)
    factor = 1.0 / math.sqrt(node_count * peer_count)
    grad_weight = lax.psum_scatter(
        lax.dot_general(
            hidden, grad_node, (((0,), (0,)), ((), ())), preferred_element_type=jnp.float32
        ),
        ("dom", "rep"),
        scatter_dimension=0,
        tiled=True,
    )
    return (embed_grad, grad_weight * factor)


def solution(mesh):
    placed = (
        P(("dom", "rep"), None),
        P(),
        P(),
        P(),
        P(("dom", "rep"), None),
        P(("dom", "rep"), None, None, None),
        P(("dom", "rep"), None, None),
        P(("dom", "rep"), None),
        P(("dom", "rep")),
        P(("dom", "rep")),
    )
    return jax.shard_map(
        body,
        mesh=mesh,
        in_specs=placed,
        out_specs=(P(("dom", "rep"), None), P(("dom", "rep"), None)),
        check_vma=False,
    )
```

profile of v0, /device:TPU:0, one launch (start us, length us, event | category | flops | bytes accessed | tf_op | source)
XLA Modules:
  0.0 256.7 jit_solution(13872903154132555360)
XLA Ops:
  7.2 0.0 copy-start
  7.2 0.8 compare_and_fusion
  8.0 0.8 copy.17
  8.7 0.1 copy.16
  8.8 0.7 iota_compare_fusion.4
  9.5 0.1 reshape_squeeze.8
  9.7 1.5 convert_reduce_fusion.1
  11.2 0.0 copy-start.8
  11.2 7.0 %fusion.34 = f32[512,4096]{1,0:T(8,128)S(1)} fusion(bf16[512,1024]{1,0:T(8,128)(2,1)S(1)} %copy-done, bf16[1024,4096]{1,0:T(8,128)(2,1)} %param.11), kind=kOutput, calls=%fused_computation.67 | convolution fusion | flops 4294967296 | bytes 17825792 | tf_op jit(solution)/shard_map/dot_general | solution.py:46
  18.3 0.0 copy-start.9
  18.3 0.0 copy-start.5
  18.3 0.0 copy-start.7
  18.3 2.7 %multiply_convert_fusion.1 = (bf16[512,512]{1,0:T(8,128)(2,1)S(1)}, f32[512,512]{1,0:T(8,128)S(1)}) fusion(f32[512]{0:T(512)S(1)} %add_rsqrt_fusion, bf16[4096,512]{1,0:T(8,128)(2,1)S(1)} %copy-done.8, f32[512,4096]{1,0:T(8,128)S(1)} %fusion.34), kind=kOutput, calls=%fused_computation.27 | convolution fusion | flops 2166882304 | bytes 14157824 | tf_op jit(solution)/shard_map/dot_general | solution.py:48
  21.1 0.4 copy-done.10
  21.5 1.2 gather_fusion
  22.7 0.8 fusion.16
  23.5 7.3 %all-to-all-start = ((bf16[32,8,512]{2,1,0:T(8,128)(2,1)}), bf16[32,8,512]{2,1,0:T(8,128)(2,1)S(1)}, u32[]{:S(2)}, u32[]{:S(2)}) async-start(bf16[32,8,512]{2,1,0:T(8,128)(2,1)} %fusion.16), calls=%async_computation | async-start | bytes 524288 | tf_op jit(solution)/shard_map/all_to_all | solution.py:58
  30.9 0.1 reshape.165
  31.0 0.1 reshape.167
  31.1 0.1 lt.86
  31.1 0.1 reshape_squeeze.9
  31.2 0.7 gather_fusion.2
  31.9 0.3 convolution_subtract_fusion
  32.3 9.1 %all-to-all-done = bf16[32,8,512]{2,1,0:T(8,128)(2,1)S(1)} async-done(((bf16[32,8,512]{2,1,0:T(8,128)(2,1)}), bf16[32,8,512]{2,1,0:T(8,128)(2,1)S(1)}, u32[]{:S(2)}, u32[]{:S(2)}) %all-to-all-start) | async-done | bytes 262176 | tf_op jit(solution)/shard_map/all_to_all | solution.py:58
  41.4 0.1 pad_maximum_fusion
  41.5 0.0 copy-start.2
  41.5 2.8 %gather_fusion.1 = bf16[32,128,512]{2,1,0:T(8,128)(2,1)} fusion(bf16[6,128,512]{2,1,0:T(8,128)(2,1)S(1)} %bitcast.50, s32[1024]{0:T(1024)S(1)} %pad_clamp_fusion.1), kind=kCustom, calls=%fused_computation.1 | custom fusion | bytes 8388736 | tf_op jit(solution)/shard_map/jit(_take)/gather | solution.py:63
  44.3 6.5 %copy.18 = bf16[32,128,512]{1,2,0:T(8,128)(2,1)} copy(bf16[32,128,512]{2,1,0:T(8,128)(2,1)} %gather_fusion.1) | data formatting | bytes 8388608 | tf_op jit(solution)/shard_map/jit(_take)/gather | solution.py:63
  50.7 7.1 %bitcast_subtract_fusion = f32[4,8,128,512]{2,3,1,0:T(8,128)} fusion(f32[4,8,128]{2,1,0:T(8,128)S(1)} %get-tuple-element.3, bf16[4,8,128,512]{2,3,1,0:T(8,128)(2,1)} %bitcast.52, pred[4,8]{1,0:T(4,128)(4,1)S(1)} %compare_and_fusion.2, bf16[4,128,512,1]{2,1,3,0:T(8,128)(2,1)S(1)} %bitcast.51, bf16[4,8,128,128]{3,2,1,0:T(8,128)(2,1)S(1)} %copy-done.2), kind=kOutput, calls=%fused_computation.13 | convolution fusion | flops 545259520 | bytes 14172192 | tf_op jit(solution)/shard_map/rtab,rad->rtbd/dot_general | solution.py:74
  57.8 10.3 %copy.28 = f32[4,8,128,512]{3,1,2,0:T(8,128)} copy(f32[4,8,128,512]{2,3,1,0:T(8,128)} %bitcast_subtract_fusion) | data formatting | bytes 16777216
  68.1 5.3 %fusion.24 = f32[6,65536]{1,0:T(8,128)S(1)} fusion(f32[32,65536]{1,0:T(8,128)} %bitcast.49, s32[32]{0:T(128)S(1)} %reshape.167), kind=kOutput, calls=%fused_computation.45 | convolution fusion | flops 150995136 | bytes 9961600 | tf_op jit(solution)/shard_map/tc,tf->cf/dot_general | solution.py:81
  73.4 1.4 copy-done.3
  74.8 0.3 slice.18
  75.0 0.9 convert_element_type.37
  75.9 2.6 %all-to-all-start.1 = ((bf16[32,8,512]{2,1,0:T(8,128)(2,1)}), bf16[32,8,512]{2,1,0:T(8,128)(2,1)S(1)}, u32[]{:S(2)}, u32[]{:S(2)}) async-start(bf16[32,8,512]{2,1,0:T(8,128)(2,1)} %convert_element_type.37), calls=%async_computation.1 | async-start | bytes 524288 | tf_op jit(solution)/shard_map/all_to_all | solution.py:91
  78.5 0.2 reduce-scatter.2.cloned.1.call-start
  78.8 4.8 %fusion.7 = f32[4,512,128,1]{1,2,3,0:T(8,128)} fusion(bf16[4,8,128,128]{3,2,1,0:T(8,128)(2,1)S(1)} %copy-done.2, bf16[4,8,128,512]{2,3,1,0:T(8,128)(2,1)} %bitcast.53, pred[4,8]{1,0:T(4,128)(4,1)S(1)} %compare_and_fusion.2), kind=kOutput, calls=%fused_computation.16 | convolution fusion | flops 538968064 | bytes 6291488 | tf_op jit(solution)/shard_map/rtab,rtbd->rad/dot_general | solution.py:66
  83.6 0.2 slice.15
  83.8 0.7 reshape.170
  84.5 1.4 fusion.12
  86.0 3.2 %all-to-all-done.1 = bf16[32,8,512]{2,1,0:T(8,128)(2,1)S(1)} async-done(((bf16[32,8,512]{2,1,0:T(8,128)(2,1)}), bf16[32,8,512]{2,1,0:T(8,128)(2,1)S(1)}, u32[]{:S(2)}, u32[]{:S(2)}) %all-to-all-start.1) | async-done | bytes 262176 | tf_op jit(solution)/shard_map/all_to_all | solution.py:91
  89.1 0.3 fusion.11
  89.5 1.4 scatter_fusion
  90.8 10.3 %fusion.17 = f32[4096,512]{1,0:T(8,128)} fusion(f32[512,512]{1,0:T(8,128)S(1)} %scatter_fusion, f32[512,4096]{1,0:T(8,128)} %copy-done.10), kind=kOutput, calls=%fused_computation.35 | convolution fusion | flops 2166620160 | bytes 17825792 | tf_op jit(solution)/shard_map/dot_general | solution.py:117
  101.2 0.0 reduce-scatter.2.cloned.1.call-update
  101.2 17.5 %fusion.10 = bf16[512,1024]{1,0:T(8,128)(2,1)} fusion(bf16[1024,4096]{1,0:T(8,128)(2,1)} %param.11, f32[512,4096]{1,0:T(8,128)} %copy-done.10, bf16[4096,512]{1,0:T(8,128)(2,1)} %param.12, f32[512,512]{1,0:T(8,128)S(1)} %scatter_fusion), kind=kOutput, calls=%fused_computation.21 | convolution fusion | flops 6483083264 | bytes 23068672 | tf_op jit(solution)/shard_map/dot_general | solution.py:112
  118.7 129.4 %reduce-scatter.2.cloned.1.call-done = f32[128,512]{1,0:T(8,128)} async-done(((f32[4096,512]{1,0:T(8,128)}), f32[128,512]{1,0:T(8,128)}) %reduce-scatter.2.cloned.1.call-update) | async-done | bytes 262160 | tf_op jit(solution)/shard_map/reduce_scatter | solution.py:116
  248.2 1.7 broadcast_multiply_fusion
  (23 shorter events, 0.1 us)
Async XLA Ops:
  7.2 4.0 %copy-start = (bf16[512,1024]{1,0:T(8,128)(2,1)S(1)}, bf16[512,1024]{1,0:T(8,128)(2,1)}, u32[]{:S(2)}) copy-start(bf16[512,1024]{1,0:T(8,128)(2,1)} %param.10) | copy-start | bytes 3145732
  11.2 7.1 %copy-start.8 = (bf16[4096,512]{1,0:T(8,128)(2,1)S(1)}, bf16[4096,512]{1,0:T(8,128)(2,1)}, u32[]{:S(2)}) copy-start(bf16[4096,512]{1,0:T(8,128)(2,1)} %param.12) | copy-start | bytes 12582916
  18.3 3.2 %copy-start.10 = (f32[512,4096]{1,0:T(8,128)}, f32[512,4096]{1,0:T(8,128)S(1)}, u32[]{:S(2)}) copy-start(f32[512,4096]{1,0:T(8,128)S(1)} %fusion.34) | copy-start | bytes 25165828
  18.3 12.5 %copy-start.9 = (s32[64]{0:T(128)S(1)}, s32[64]{0:T(128)}, u32[]{:S(2)}) copy-start(s32[64]{0:T(128)} %param.18) | copy-start | bytes 772
  18.3 12.5 %copy-start.6 = (s32[4,8]{1,0:T(4,128)S(1)}, s32[4,8]{1,0:T(4,128)}, u32[]{:S(2)}) copy-start(s32[4,8]{1,0:T(4,128)} %param.14) | copy-start | bytes 388
  18.3 13.6 %copy-start.5 = (bf16[1000,512]{1,0:T(8,128)(2,1)S(1)}, bf16[1000,512]{1,0:T(8,128)(2,1)}, u32[]{:S(2)}) copy-start(bf16[1000,512]{1,0:T(8,128)(2,1)} %param.13) | copy-start | bytes 3072004
  18.3 13.6 %copy-start.7 = (s32[64]{0:T(128)S(1)}, s32[64]{0:T(128)}, u32[]{:S(2)}) copy-start(s32[64]{0:T(128)} %param.19) | copy-start | bytes 772
  23.5 17.9 %all-to-all-start = ((bf16[32,8,512]{2,1,0:T(8,128)(2,1)}), bf16[32,8,512]{2,1,0:T(8,128)(2,1)S(1)}, u32[]{:S(2)}, u32[]{:S(2)}) async-start(bf16[32,8,512]{2,1,0:T(8,128)(2,1)} %fusion.16), calls=%async_computation | async-start | bytes 524288 | tf_op jit(solution)/shard_map/all_to_all | solution.py:58
  41.5 9.2 %copy-start.2 = (bf16[4,8,128,128]{3,2,1,0:T(8,128)(2,1)S(1)}, bf16[4,8,128,128]{3,2,1,0:T(8,128)(2,1)}, u32[]{:S(2)}) copy-start(bf16[4,8,128,128]{3,2,1,0:T(8,128)(2,1)} %param.15) | copy-start | bytes 3145732
  73.4 1.4 copy-start.3
  75.9 13.2 %all-to-all-start.1 = ((bf16[32,8,512]{2,1,0:T(8,128)(2,1)}), bf16[32,8,512]{2,1,0:T(8,128)(2,1)S(1)}, u32[]{:S(2)}, u32[]{:S(2)}) async-start(bf16[32,8,512]{2,1,0:T(8,128)(2,1)} %convert_element_type.37), calls=%async_computation.1 | async-start | bytes 524288 | tf_op jit(solution)/shard_map/all_to_all | solution.py:91
  78.5 169.6 %reduce-scatter.2.cloned.1.call-start = ((), (), s32[]{:S(2)}) async-start(), calls=%async_computation.3 | async-start | bytes 8650752 | tf_op jit(solution)/shard_map/reduce_scatter | solution.py:116
  78.8 4.8 %copy-start.4 = (f32[6,65536]{1,0:T(8,128)S(1)}, f32[6,65536]{1,0:T(8,128)}, u32[]{:S(2)}) copy-start(f32[6,65536]{1,0:T(8,128)} %copy-done.3) | copy-start | bytes 4718596
  101.2 148.6 %copy-start.1 = (bf16[512,1024]{1,0:T(8,128)(2,1)S(1)}, bf16[512,1024]{1,0:T(8,128)(2,1)}, u32[]{:S(2)}) copy-start(bf16[512,1024]{1,0:T(8,128)(2,1)} %param.10) | copy-start | bytes 3145732
Sparse Core Ops, SparseCore 0:
  101.3 146.8 reduce-scatter.1
where the time goes:
time: 257 us
  waiting for transfers between devices  142 us (55%)
  matrix products  55.5 us (22%)
  local copies, waits for them, and re-layouts  26.6 us (10%)
  between operations  14.3 us (6%)
  starting transfers between devices  10.1 us (4%)
  other arithmetic  8.47 us (3%)
    reduce_scatter x1, waiting for transfers between devices, body(): lax.psum_scatter(lax.dot_general(hidden, grad_node, (((0,), (0,)), ((), (...  129 us
    dot_general x1, matrix products, body(): lax.dot_general(grad_pre, weight_in, (((1,), (1,)), ((), ())), preferred_...  17.5 us
    unnamed x24, local copies, waits for them, and re-layouts  12.9 us
    dot_general x1, matrix products, body(): lax.dot_general(hidden, grad_node, (((0,), (0,)), ((), ())), preferred_el...  10.3 us
    gather x2, local copies, waits for them, and re-layouts, body(): jnp.take(extended, flat_columns, axis=0)  9.23 us
    all_to_all x1, waiting for transfers between devices, body(): lax.all_to_all(outgoing, ('dom', 'rep'), split_axis=0, concat_axis=0, til...  9.14 us
    all_to_all x1, starting transfers between devices, body(): lax.all_to_all(outgoing, ('dom', 'rep'), split_axis=0, concat_axis=0, til...  7.3 us
    dot_general x1, matrix products, body(): jnp.einsum('rtab,rad->rtbd', tile_weight, unit_blocks, preferred_element_...  7.05 us
  transfers between devices with their start and end apart: 3, of which 3 were waited for; matrix products, arithmetic and copies ran while one was open for 10% of the time, Pallas kernels for 0%

commit v1 on v0

--- a/solution.py
+++ b/solution.py
@@ -20,6 +20,50 @@
     return 0.5 * (1.0 + tangent) + 0.5 * values * (1.0 - tangent * tangent) * gelu_inner * (
         1.0 + 3.0 * gelu_cubic * values * values
     )
+
+
+def bit_orders(count):
+    bits = list(range(count.bit_length() - 1))
+    first = len(bits) // 3
+    second = first + max(first, (len(bits) - first) // 3)
+    low, middle, high = bits[:first], bits[first:second], bits[second:]
+    return (low + middle + high, middle + low + high, high + low + middle)
+
+
+def halve_over(part, axis, spot, pairs, mine):
+    kept = lax.dynamic_index_in_dim(part, mine, spot, keepdims=False)
+    sent = lax.dynamic_index_in_dim(part, 1 - mine, spot, keepdims=False).astype(jnp.bfloat16)
+    return kept + lax.ppermute(sent, axis, pairs).astype(jnp.float32)
+
+
+def scatter_sum(total):
+    dom_count = lax.axis_size("dom")
+    rep_count = lax.axis_size("rep")
+    width = total.shape[1]
+    if rep_count != 2 or dom_count & (dom_count - 1) or dom_count < 8:
+        return lax.psum_scatter(total, ("dom", "rep"), scatter_dimension=0, tiled=True)
+    depth = total.shape[0] // (dom_count * rep_count)
+    place = lax.axis_index("dom")
+    blocks = total.reshape(dom_count, rep_count, depth, width)
+    chip_sum = halve_over(blocks, "rep", 1, [(0, 1), (1, 0)], lax.axis_index("rep"))
+    cut = depth * 3 // 8
+    edges = (0, cut, 2 * cut, depth)
+    streams = []
+    for order, low, high in zip(bit_orders(dom_count), edges[:-1], edges[1:]):
+        bit_count = len(order)
+        streams.append(
+            (chip_sum[:, low:high].reshape((2,) * bit_count + (high - low, width)), list(reversed(range(bit_count))), order)
+        )
+    for step in range(dom_count.bit_length() - 1):
+        later = []
+        for part, left, order in streams:
+            bit = order[step]
+            pairs = [(device, device ^ (1 << bit)) for device in range(dom_count)]
+            spot = left.index(bit)
+            part = halve_over(part, "dom", spot, pairs, (place >> bit) & 1)
+            later.append((part, [other for other in left if other != bit], order))
+        streams = later
+    return jnp.concatenate([part for part, _, _ in streams], axis=0)
 
 
 def body(
@@ -113,13 +157,10 @@
         grad_pre, weight_in, (((1,), (1,)), ((), ())), preferred_element_type=jnp.float32
     ).astype(jnp.bfloat16)
     factor = 1.0 / math.sqrt(node_count * peer_count)
-    grad_weight = lax.psum_scatter(
+    grad_weight = scatter_sum(
         lax.dot_general(
             hidden, grad_node, (((0,), (0,)), ((), ())), preferred_element_type=jnp.float32
-        ),
-        ("dom", "rep"),
-        scatter_dimension=0,
-        tiled=True,
+        )
     )
     return (embed_grad, grad_weight * factor)
 

time: 257 us -> 156 us (0.61)
  waiting for transfers between devices: 142 us -> 35.3 us
  starting transfers between devices: 10.1 us -> 24.8 us
  between operations: 14.3 us -> 1.14 us
  local copies, waits for them, and re-layouts: 26.6 us -> 31.3 us
  matrix products: 55.5 us -> 51.4 us
  other arithmetic: 8.47 us -> 11.6 us
    reduce_scatter x1 -> x0, waiting for transfers between devices: 129 us -> none  [body(): lax.psum_scatter(lax.dot_general(hidden, grad_node, (((0,), (0,)), ((), (...]
    ppermute x0 -> x13, waiting for transfers between devices: none -> 23.5 us  [halve_over(): return kept + lax.ppermute(sent, axis, pairs).astype(jnp.float32)]
    ppermute x0 -> x13, starting transfers between devices: none -> 14.7 us  [halve_over(): return kept + lax.ppermute(sent, axis, pairs).astype(jnp.float32)]
    dot_general x1, matrix products: 10.3 us -> 5.92 us  [body(): lax.dot_general(hidden, grad_node, (((0,), (0,)), ((), ())), preferred_el...]
    add x0 -> x13, other arithmetic: none -> 4.07 us  [halve_over(): return kept + lax.ppermute(sent, axis, pairs).astype(jnp.float32)]
    unnamed x24 -> x26, local copies, waits for them, and re-layouts: 12.9 us -> 16.1 us
  transfers between devices with their start and end apart: 3 -> 15, of which waited for: 3 -> 11; matrix products, arithmetic and copies ran while one was open for 10% -> 18% of each run, Pallas kernels for 0% -> 0%
where the time goes in v1:
time: 156 us
  matrix products  51.4 us (33%)
  waiting for transfers between devices  35.3 us (23%)
  local copies, waits for them, and re-layouts  31.3 us (20%)
  starting transfers between devices  24.8 us (16%)
  other arithmetic  11.6 us (7%)
    ppermute x13, waiting for transfers between devices, halve_over(): return kept + lax.ppermute(sent, axis, pairs).astype(jnp.float32)  23.5 us
    dot_general x1, matrix products, body(): lax.dot_general(grad_pre, weight_in, (((1,), (1,)), ((), ())), preferred_...  17.2 us
    unnamed x26, local copies, waits for them, and re-layouts  16.1 us
    ppermute x13, starting transfers between devices, halve_over(): return kept + lax.ppermute(sent, axis, pairs).astype(jnp.float32)  14.7 us
    gather x2, local copies, waits for them, and re-layouts, body(): jnp.take(extended, flat_columns, axis=0)  9.19 us
    all_to_all x1, waiting for transfers between devices, body(): lax.all_to_all(outgoing, ('dom', 'rep'), split_axis=0, concat_axis=0, til...  8.58 us
    all_to_all x1, starting transfers between devices, body(): lax.all_to_all(outgoing, ('dom', 'rep'), split_axis=0, concat_axis=0, til...  7.3 us
    dot_general x1, matrix products, body(): pre_act = jnp.dot(embeds, weight_in, preferred_element_type=jnp.float32)  7.05 us
  transfers between devices with their start and end apart: 15, of which 11 were waited for; matrix products, arithmetic and copies ran while one was open for 18% of the time, Pallas kernels for 0%

profile of v1, /device:TPU:0, one launch (start us, length us, event | category | flops | bytes accessed | tf_op | source)
XLA Modules:
  0.0 155.5 jit_solution(13890147920259605834)
XLA Ops:
  0.6 0.8 compare_and_fusion
  1.4 0.8 copy.17
  2.3 0.7 iota_compare_fusion.4
  3.1 1.5 convert_reduce_fusion.1
  4.7 7.0 %fusion.48 = f32[512,4096]{1,0:T(8,128)S(1)} fusion(bf16[512,1024]{1,0:T(8,128)(2,1)S(1)} %copy-done, bf16[1024,4096]{1,0:T(8,128)(2,1)} %param.11), kind=kOutput, calls=%fused_computation.111 | convolution fusion | flops 4294967296 | bytes 17825792 | tf_op jit(solution)/shard_map/dot_general | solution.py:90
  11.8 2.7 %multiply_convert_fusion.1 = (bf16[512,512]{1,0:T(8,128)(2,1)S(1)}, f32[512,512]{1,0:T(8,128)S(1)}) fusion(f32[512]{0:T(512)S(1)} %add_rsqrt_fusion, bf16[4096,512]{1,0:T(8,128)(2,1)S(1)} %copy-done.9, f32[512,4096]{1,0:T(8,128)S(1)} %fusion.48), kind=kOutput, calls=%fused_computation.30 | convolution fusion | flops 2166882304 | bytes 14157824 | tf_op jit(solution)/shard_map/dot_general | solution.py:92
  15.0 1.2 gather_fusion
  16.2 0.8 fusion.20
  17.0 7.3 %all-to-all-start = ((bf16[32,8,512]{2,1,0:T(8,128)(2,1)}), bf16[32,8,512]{2,1,0:T(8,128)(2,1)S(1)}, u32[]{:S(2)}, u32[]{:S(2)}) async-start(bf16[32,8,512]{2,1,0:T(8,128)(2,1)} %fusion.20), calls=%async_computation | async-start | bytes 524288 | tf_op jit(solution)/shard_map/all_to_all | solution.py:102
  24.6 0.6 lt.142
  25.3 0.7 gather_fusion.2
  26.3 8.6 %all-to-all-done = bf16[32,8,512]{2,1,0:T(8,128)(2,1)S(1)} async-done(((bf16[32,8,512]{2,1,0:T(8,128)(2,1)}), bf16[32,8,512]{2,1,0:T(8,128)(2,1)S(1)}, u32[]{:S(2)}, u32[]{:S(2)}) %all-to-all-start) | async-done | bytes 262176 | tf_op jit(solution)/shard_map/all_to_all | solution.py:102
  35.0 2.8 %gather_fusion.1 = bf16[32,128,512]{2,1,0:T(8,128)(2,1)} fusion(bf16[6,128,512]{2,1,0:T(8,128)(2,1)S(1)} %bitcast.110, s32[1024]{0:T(1024)S(1)} %pad_clamp_fusion.1), kind=kCustom, calls=%fused_computation.1 | custom fusion | bytes 8388736 | tf_op jit(solution)/shard_map/jit(_take)/gather | solution.py:107
  37.8 6.4 %copy.18 = bf16[32,128,512]{1,2,0:T(8,128)(2,1)} copy(bf16[32,128,512]{2,1,0:T(8,128)(2,1)} %gather_fusion.1) | data formatting | bytes 8388608 | tf_op jit(solution)/shard_map/jit(_take)/gather | solution.py:107
  44.2 7.0 %bitcast_subtract_fusion = f32[4,8,128,512]{2,3,1,0:T(8,128)} fusion(f32[4,8,128]{2,1,0:T(8,128)S(1)} %get-tuple-element.3, bf16[4,8,128,512]{2,3,1,0:T(8,128)(2,1)} %bitcast.112, pred[4,8]{1,0:T(4,128)(4,1)S(1)} %compare_and_fusion.2, bf16[4,128,512,1]{2,1,3,0:T(8,128)(2,1)S(1)} %bitcast.111, bf16[4,8,128,128]{3,2,1,0:T(8,128)(2,1)S(1)} %copy-done.2), kind=kOutput, calls=%fused_computation.13 | convolution fusion | flops 545259520 | bytes 14172192 | tf_op jit(solution)/shard_map/rtab,rad->rtbd/dot_general | solution.py:118
  51.2 10.3 %copy.36 = f32[4,8,128,512]{3,1,2,0:T(8,128)} copy(f32[4,8,128,512]{2,3,1,0:T(8,128)} %bitcast_subtract_fusion) | data formatting | bytes 16777216
  61.5 5.3 %fusion.37 = f32[6,65536]{1,0:T(8,128)S(1)} fusion(f32[32,65536]{1,0:T(8,128)} %bitcast.109, s32[32]{0:T(128)S(1)} %reshape.192), kind=kOutput, calls=%fused_computation.84 | convolution fusion | flops 150995136 | bytes 9961600 | tf_op jit(solution)/shard_map/tc,tf->cf/dot_general | solution.py:125
  66.8 1.4 copy-done.3
  68.5 0.9 convert_element_type.154
  69.4 2.8 %all-to-all-start.1 = ((bf16[32,8,512]{2,1,0:T(8,128)(2,1)}), bf16[32,8,512]{2,1,0:T(8,128)(2,1)S(1)}, u32[]{:S(2)}, u32[]{:S(2)}) async-start(bf16[32,8,512]{2,1,0:T(8,128)(2,1)} %convert_element_type.154), calls=%async_computation.1 | async-start | bytes 524288 | tf_op jit(solution)/shard_map/all_to_all | solution.py:135
  72.2 4.8 %fusion.7 = f32[4,512,128,1]{1,2,3,0:T(8,128)} fusion(bf16[4,8,128,128]{3,2,1,0:T(8,128)(2,1)S(1)} %copy-done.2, bf16[4,8,128,512]{2,3,1,0:T(8,128)(2,1)} %bitcast.113, pred[4,8]{1,0:T(4,128)(4,1)S(1)} %compare_and_fusion.2), kind=kOutput, calls=%fused_computation.18 | convolution fusion | flops 538968064 | bytes 6291488 | tf_op jit(solution)/shard_map/rtab,rtbd->rad/dot_general | solution.py:110
  77.2 0.7 reshape.195
  77.9 1.4 fusion.13
  79.4 3.2 %all-to-all-done.1 = bf16[32,8,512]{2,1,0:T(8,128)(2,1)S(1)} async-done(((bf16[32,8,512]{2,1,0:T(8,128)(2,1)}), bf16[32,8,512]{2,1,0:T(8,128)(2,1)S(1)}, u32[]{:S(2)}, u32[]{:S(2)}) %all-to-all-start.1) | async-done | bytes 262176 | tf_op jit(solution)/shard_map/all_to_all | solution.py:135
  82.6 0.9 fusion.12
  83.5 1.4 scatter_fusion
  84.9 5.9 %fusion.21 = f32[4096,512]{1,0:T(8,128)S(1)} fusion(f32[512,512]{1,0:T(8,128)S(1)} %scatter_fusion, f32[512,4096]{1,0:T(8,128)} %copy-done.11), kind=kOutput, calls=%fused_computation.54 | convolution fusion | flops 2166620160 | bytes 17825792 | tf_op jit(solution)/shard_map/dot_general | solution.py:161
  90.8 3.2 %copy-done.5 = f32[4096,512]{1,0:T(8,128)} copy-done((f32[4096,512]{1,0:T(8,128)}, f32[4096,512]{1,0:T(8,128)S(1)}, u32[]{:S(2)}) %copy-start.5) | copy-done | bytes 8388632
  94.4 17.2 %fusion.11 = bf16[512,1024]{1,0:T(8,128)(2,1)} fusion(bf16[1024,4096]{1,0:T(8,128)(2,1)} %param.11, f32[512,4096]{1,0:T(8,128)} %copy-done.11, bf16[4096,512]{1,0:T(8,128)(2,1)} %param.12, f32[512,512]{1,0:T(8,128)S(1)} %scatter_fusion), kind=kOutput, calls=%fused_computation.24 | convolution fusion | flops 6483083264 | bytes 23068672 | tf_op jit(solution)/shard_map/dot_general | solution.py:156
  111.7 3.5 %bitcast_add_fusion = f32[16,128,512]{2,1,0:T(8,128)S(1)} fusion(bf16[16,128,512]{2,1,0:T(8,128)(2,1)} %collective-permute-done, f32[16,2,128,512]{3,2,1,0:T(8,128)} %bitcast.119, s32[]{:T(128)S(6)} %select_n.123), kind=kLoop, calls=%fused_computation.16 | loop fusion | flops 2097152 | bytes 10485764 | tf_op jit(solution)/shard_map/add | solution.py:36
  115.4 1.0 collective-permute-start.9
  116.7 7.5 %collective-permute-done.9 = bf16[2,2,2,32,512]{4,3,1,2,0:T(8,128)(2,1)S(1)} collective-permute-done((bf16[2,2,2,32,512]{4,3,1,2,0:T(8,128)(2,1)S(1)}, bf16[2,2,2,32,512]{4,3,1,2,0:T(8,128)(2,1)S(1)}, u32[]{:S(2)}, u32[]{:S(2)}) %collective-permute-start.9) | collective-permute-done | bytes 262176 | tf_op jit(solution)/shard_map/ppermute | solution.py:36
  124.7 1.0 collective-permute-start.1
  125.7 1.1 collective-permute-start.5
  126.8 6.3 %collective-permute-done.10 = bf16[2,2,32,512]{3,2,0,1:T(8,128)(2,1)S(1)} collective-permute-done((bf16[2,2,32,512]{3,2,0,1:T(8,128)(2,1)S(1)}, bf16[2,2,32,512]{3,2,0,1:T(8,128)(2,1)S(1)}, u32[]{:S(2)}, u32[]{:S(2)}) %collective-permute-start.10) | collective-permute-done | bytes 131104 | tf_op jit(solution)/shard_map/ppermute | solution.py:36
  133.3 1.9 %collective-permute-done.1 = bf16[2,2,2,48,512]{4,3,2,1,0:T(8,128)(2,1)S(1)} collective-permute-done((bf16[2,2,2,48,512]{4,3,2,1,0:T(8,128)(2,1)S(1)}, bf16[2,2,2,48,512]{4,3,2,1,0:T(8,128)(2,1)S(1)}, u32[]{:S(2)}, u32[]{:S(2)}) %collective-permute-start.1) | collective-permute-done | bytes 393248 | tf_op jit(solution)/shard_map/ppermute | solution.py:36
  135.3 0.9 collective-permute-start.2
  136.4 1.1 collective-permute-done.11
  137.6 0.9 collective-permute-start.12
  138.5 0.7 collective-permute-start.6
  139.3 2.3 %collective-permute-done.12 = bf16[32,512]{1,0:T(8,128)(2,1)S(1)} collective-permute-done((bf16[32,512]{1,0:T(8,128)(2,1)S(1)}, bf16[32,512]{1,0:T(8,128)(2,1)S(1)}, u32[]{:S(2)}, u32[]{:S(2)}) %collective-permute-start.12) | collective-permute-done | bytes 32800 | tf_op jit(solution)/shard_map/ppermute | solution.py:36
  141.7 2.1 %collective-permute-start.3 = (bf16[2,48,512]{2,1,0:T(8,128)(2,1)S(1)}, bf16[2,48,512]{2,1,0:T(8,128)(2,1)S(1)}, u32[]{:S(2)}, u32[]{:S(2)}) collective-permute-start(bf16[2,48,512]{2,1,0:T(8,128)(2,1)S(1)} %fusion.31), channel_id=1, source_target_pairs={{0,8},{2,10},{4,12},{6,14},{8,0},{10,2},{12,4},{14,6},{16,24},{18,... | collective-permute-start | bytes 294920 | tf_op jit(solution)/shard_map/ppermute | solution.py:36
  144.4 1.4 collective-permute-start.7
  145.8 0.8 collective-permute-done.3
  146.6 3.0 %collective-permute-start.4 = (bf16[48,512]{1,0:T(8,128)(2,1)S(1)}, bf16[48,512]{1,0:T(8,128)(2,1)S(1)}, u32[]{:S(2)}, u32[]{:S(2)}) collective-permute-start(bf16[48,512]{1,0:T(8,128)(2,1)S(1)} %fusion.34), channel_id=1, source_target_pairs={{0,16},{2,18},{4,20},{6,22},{8,24},{10,26},{12,28},{14,30},{16,0},... | collective-permute-start | bytes 147464 | tf_op jit(solution)/shard_map/ppermute | solution.py:36
  149.7 1.9 %collective-permute-start.8 = (bf16[48,512]{1,0:T(8,128)(2,1)S(1)}, bf16[48,512]{1,0:T(8,128)(2,1)S(1)}, u32[]{:S(2)}, u32[]{:S(2)}) collective-permute-start(bf16[48,512]{1,0:T(8,128)(2,1)S(1)} %fusion.35), channel_id=1, source_target_pairs={{0,16},{2,18},{4,20},{6,22},{8,24},{10,26},{12,28},{14,30},{16,0},... | collective-permute-start | bytes 147464 | tf_op jit(solution)/shard_map/ppermute | solution.py:36
  151.8 3.0 %collective-permute-done.8 = bf16[48,512]{1,0:T(8,128)(2,1)S(1)} collective-permute-done((bf16[48,512]{1,0:T(8,128)(2,1)S(1)}, bf16[48,512]{1,0:T(8,128)(2,1)S(1)}, u32[]{:S(2)}, u32[]{:S(2)}) %collective-permute-start.8) | collective-permute-done | bytes 49184 | tf_op jit(solution)/shard_map/ppermute | solution.py:36
  154.8 0.7 maximum_multiply_fusion
  (76 shorter events, 4.5 us)
Async XLA Ops:
  0.6 4.0 %copy-start = (bf16[512,1024]{1,0:T(8,128)(2,1)S(1)}, bf16[512,1024]{1,0:T(8,128)(2,1)}, u32[]{:S(2)}) copy-start(bf16[512,1024]{1,0:T(8,128)(2,1)} %param.10) | copy-start | bytes 3145732
  4.7 7.1 %copy-start.9 = (bf16[4096,512]{1,0:T(8,128)(2,1)S(1)}, bf16[4096,512]{1,0:T(8,128)(2,1)}, u32[]{:S(2)}) copy-start(bf16[4096,512]{1,0:T(8,128)(2,1)} %param.12) | copy-start | bytes 12582916
  11.7 3.3 %copy-start.11 = (f32[512,4096]{1,0:T(8,128)}, f32[512,4096]{1,0:T(8,128)S(1)}, u32[]{:S(2)}) copy-start(f32[512,4096]{1,0:T(8,128)S(1)} %fusion.48) | copy-start | bytes 25165828
  11.8 12.5 %copy-start.10 = (s32[64]{0:T(128)S(1)}, s32[64]{0:T(128)}, u32[]{:S(2)}) copy-start(s32[64]{0:T(128)} %param.18) | copy-start | bytes 772
  11.8 12.6 %copy-start.7 = (s32[4,8]{1,0:T(4,128)S(1)}, s32[4,8]{1,0:T(4,128)}, u32[]{:S(2)}) copy-start(s32[4,8]{1,0:T(4,128)} %param.14) | copy-start | bytes 388
  11.8 14.2 %copy-start.6 = (bf16[1000,512]{1,0:T(8,128)(2,1)S(1)}, bf16[1000,512]{1,0:T(8,128)(2,1)}, u32[]{:S(2)}) copy-start(bf16[1000,512]{1,0:T(8,128)(2,1)} %param.13) | copy-start | bytes 3072004
  11.8 14.2 %copy-start.8 = (s32[64]{0:T(128)S(1)}, s32[64]{0:T(128)}, u32[]{:S(2)}) copy-start(s32[64]{0:T(128)} %param.19) | copy-start | bytes 772
  17.0 17.9 %all-to-all-start = ((bf16[32,8,512]{2,1,0:T(8,128)(2,1)}), bf16[32,8,512]{2,1,0:T(8,128)(2,1)S(1)}, u32[]{:S(2)}, u32[]{:S(2)}) async-start(bf16[32,8,512]{2,1,0:T(8,128)(2,1)} %fusion.20), calls=%async_computation | async-start | bytes 524288 | tf_op jit(solution)/shard_map/all_to_all | solution.py:102
  35.0 9.2 %copy-start.2 = (bf16[4,8,128,128]{3,2,1,0:T(8,128)(2,1)S(1)}, bf16[4,8,128,128]{3,2,1,0:T(8,128)(2,1)}, u32[]{:S(2)}) copy-start(bf16[4,8,128,128]{3,2,1,0:T(8,128)(2,1)} %param.15) | copy-start | bytes 3145732
  66.8 1.4 copy-start.3
  69.4 13.2 %all-to-all-start.1 = ((bf16[32,8,512]{2,1,0:T(8,128)(2,1)}), bf16[32,8,512]{2,1,0:T(8,128)(2,1)S(1)}, u32[]{:S(2)}, u32[]{:S(2)}) async-start(bf16[32,8,512]{2,1,0:T(8,128)(2,1)} %convert_element_type.154), calls=%async_computation.1 | async-start | bytes 524288 | tf_op jit(solution)/shard_map/all_to_all | solution.py:135
  72.2 4.9 %copy-start.4 = (f32[6,65536]{1,0:T(8,128)S(1)}, f32[6,65536]{1,0:T(8,128)}, u32[]{:S(2)}) copy-start(f32[6,65536]{1,0:T(8,128)} %copy-done.3) | copy-start | bytes 4718596
  90.8 3.2 %copy-start.5 = (f32[4096,512]{1,0:T(8,128)}, f32[4096,512]{1,0:T(8,128)S(1)}, u32[]{:S(2)}) copy-start(f32[4096,512]{1,0:T(8,128)S(1)} %fusion.21) | copy-start | bytes 25165828
  94.3 17.3 %collective-permute-start = (bf16[16,128,512]{2,1,0:T(8,128)(2,1)S(1)}, bf16[16,128,512]{2,1,0:T(8,128)(2,1)}, u32[]{:S(2)}, u32[]{:S(2)}) collective-permute-start(bf16[16,128,512]{2,1,0:T(8,128)(2,1)S(1)} %fusion.9), channel_id=1, source_target_pairs={{0,1},{1,0},{2,3},{3,2},{4,5},{5,4},{6,7},{7,6},{8,9},{9,8},{10,11... | collective-permute-start | bytes 6291464 | tf_op jit(solution)/shard_map/ppermute | solution.py:36
  115.4 8.8 %collective-permute-start.9 = (bf16[2,2,2,32,512]{4,3,1,2,0:T(8,128)(2,1)S(1)}, bf16[2,2,2,32,512]{4,3,1,2,0:T(8,128)(2,1)S(1)}, u32[]{:S(2)}, u32[]{:S(2)}) collective-permute-start(bf16[2,2,2,32,512]{4,3,1,2,0:T(8,128)(2,1)S(1)} %fusion.18), channel_id=1, source_target_pairs={{0,8},{2,10},{4,12},{6,14},{8,0},{10,2},{12,4},{14,6},{16,24},{18,... | collective-permute-start | bytes 786440 | tf_op jit(solution)/shard_map/ppermute | solution.py:36
  116.3 39.2 %copy-start.1 = (bf16[512,1024]{1,0:T(8,128)(2,1)S(1)}, bf16[512,1024]{1,0:T(8,128)(2,1)}, u32[]{:S(2)}) copy-start(bf16[512,1024]{1,0:T(8,128)(2,1)} %param.10) | copy-start | bytes 3145732
  124.2 8.9 %collective-permute-start.10 = (bf16[2,2,32,512]{3,2,0,1:T(8,128)(2,1)S(1)}, bf16[2,2,32,512]{3,2,0,1:T(8,128)(2,1)S(1)}, u32[]{:S(2)}, u32[]{:S(2)}) collective-permute-start(bf16[2,2,32,512]{3,2,0,1:T(8,128)(2,1)S(1)} %fusion.29), channel_id=1, source_target_pairs={{0,16},{2,18},{4,20},{6,22},{8,24},{10,26},{12,28},{14,30},{16,0},... | collective-permute-start | bytes 393224 | tf_op jit(solution)/shard_map/ppermute | solution.py:36
  124.7 10.5 %collective-permute-start.1 = (bf16[2,2,2,48,512]{4,3,2,1,0:T(8,128)(2,1)S(1)}, bf16[2,2,2,48,512]{4,3,2,1,0:T(8,128)(2,1)S(1)}, u32[]{:S(2)}, u32[]{:S(2)}) collective-permute-start(bf16[2,2,2,48,512]{4,3,2,1,0:T(8,128)(2,1)S(1)} %fusion.16), channel_id=1, source_target_pairs={{0,2},{2,0},{4,6},{6,4},{8,10},{10,8},{12,14},{14,12},{16,18},{18,... | collective-permute-start | bytes 1179656 | tf_op jit(solution)/shard_map/ppermute | solution.py:36
  125.7 10.6 %collective-permute-start.5 = (bf16[2,2,2,48,512]{4,3,0,1,2:T(8,128)(2,1)S(1)}, bf16[2,2,2,48,512]{4,3,0,1,2:T(8,128)(2,1)S(1)}, u32[]{:S(2)}, u32[]{:S(2)}) collective-permute-start(bf16[2,2,2,48,512]{4,3,0,1,2:T(8,128)(2,1)S(1)} %fusion.17), channel_id=1, source_target_pairs={{0,4},{2,6},{4,0},{6,2},{8,12},{10,14},{12,8},{14,10},{16,20},{18,... | collective-permute-start | bytes 1179656 | tf_op jit(solution)/shard_map/ppermute | solution.py:36
  133.2 4.3 %collective-permute-start.11 = (bf16[2,32,512]{2,1,0:T(8,128)(2,1)S(1)}, bf16[2,32,512]{2,1,0:T(8,128)(2,1)S(1)}, u32[]{:S(2)}, u32[]{:S(2)}) collective-permute-start(bf16[2,32,512]{2,1,0:T(8,128)(2,1)S(1)} %fusion.33), channel_id=1, source_target_pairs={{0,2},{2,0},{4,6},{6,4},{8,10},{10,8},{12,14},{14,12},{16,18},{18,... | collective-permute-start | bytes 196616 | tf_op jit(solution)/shard_map/ppermute | solution.py:36
  135.3 6.3 %collective-permute-start.2 = (bf16[2,2,48,512]{3,2,1,0:T(8,128)(2,1)S(1)}, bf16[2,2,48,512]{3,2,1,0:T(8,128)(2,1)S(1)}, u32[]{:S(2)}, u32[]{:S(2)}) collective-permute-start(bf16[2,2,48,512]{3,2,1,0:T(8,128)(2,1)S(1)} %fusion.27), channel_id=1, source_target_pairs={{0,4},{2,6},{4,0},{6,2},{8,12},{10,14},{12,8},{14,10},{16,20},{18,... | collective-permute-start | bytes 589832 | tf_op jit(solution)/shard_map/ppermute | solution.py:36
  137.6 4.0 %collective-permute-start.12 = (bf16[32,512]{1,0:T(8,128)(2,1)S(1)}, bf16[32,512]{1,0:T(8,128)(2,1)S(1)}, u32[]{:S(2)}, u32[]{:S(2)}) collective-permute-start(bf16[32,512]{1,0:T(8,128)(2,1)S(1)} %fusion.36), channel_id=1, source_target_pairs={{0,4},{2,6},{4,0},{6,2},{8,12},{10,14},{12,8},{14,10},{16,20},{18,... | collective-permute-start | bytes 98312 | tf_op jit(solution)/shard_map/ppermute | solution.py:36
  138.5 5.7 %collective-permute-start.6 = (bf16[2,2,48,512]{3,2,0,1:T(8,128)(2,1)S(1)}, bf16[2,2,48,512]{3,2,0,1:T(8,128)(2,1)S(1)}, u32[]{:S(2)}, u32[]{:S(2)}) collective-permute-start(bf16[2,2,48,512]{3,2,0,1:T(8,128)(2,1)S(1)} %fusion.28), channel_id=1, source_target_pairs={{0,2},{2,0},{4,6},{6,4},{8,10},{10,8},{12,14},{14,12},{16,18},{18,... | collective-permute-start | bytes 589832 | tf_op jit(solution)/shard_map/ppermute | solution.py:36
  141.7 4.9 %collective-permute-start.3 = (bf16[2,48,512]{2,1,0:T(8,128)(2,1)S(1)}, bf16[2,48,512]{2,1,0:T(8,128)(2,1)S(1)}, u32[]{:S(2)}, u32[]{:S(2)}) collective-permute-start(bf16[2,48,512]{2,1,0:T(8,128)(2,1)S(1)} %fusion.31), channel_id=1, source_target_pairs={{0,8},{2,10},{4,12},{6,14},{8,0},{10,2},{12,4},{14,6},{16,24},{18,... | collective-permute-start | bytes 294920 | tf_op jit(solution)/shard_map/ppermute | solution.py:36
  144.4 5.3 %collective-permute-start.7 = (bf16[2,48,512]{2,1,0:T(8,128)(2,1)S(1)}, bf16[2,48,512]{2,1,0:T(8,128)(2,1)S(1)}, u32[]{:S(2)}, u32[]{:S(2)}) collective-permute-start(bf16[2,48,512]{2,1,0:T(8,128)(2,1)S(1)} %fusion.32), channel_id=1, source_target_pairs={{0,8},{2,10},{4,12},{6,14},{8,0},{10,2},{12,4},{14,6},{16,24},{18,... | collective-permute-start | bytes 294920 | tf_op jit(solution)/shard_map/ppermute | solution.py:36
  146.6 5.1 %collective-permute-start.4 = (bf16[48,512]{1,0:T(8,128)(2,1)S(1)}, bf16[48,512]{1,0:T(8,128)(2,1)S(1)}, u32[]{:S(2)}, u32[]{:S(2)}) collective-permute-start(bf16[48,512]{1,0:T(8,128)(2,1)S(1)} %fusion.34), channel_id=1, source_target_pairs={{0,16},{2,18},{4,20},{6,22},{8,24},{10,26},{12,28},{14,30},{16,0},... | collective-permute-start | bytes 147464 | tf_op jit(solution)/shard_map/ppermute | solution.py:36
  149.7 5.1 %collective-permute-start.8 = (bf16[48,512]{1,0:T(8,128)(2,1)S(1)}, bf16[48,512]{1,0:T(8,128)(2,1)S(1)}, u32[]{:S(2)}, u32[]{:S(2)}) collective-permute-start(bf16[48,512]{1,0:T(8,128)(2,1)S(1)} %fusion.35), channel_id=1, source_target_pairs={{0,16},{2,18},{4,20},{6,22},{8,24},{10,26},{12,28},{14,30},{16,0},... | collective-permute-start | bytes 147464 | tf_op jit(solution)/shard_map/ppermute | solution.py:36

commit v2 on v1

v2 whole, which is shorter than its diff:
```python
import math

import jax
import jax.numpy as jnp
from jax import lax
from jax.experimental import pallas as pl
from jax.experimental.pallas import tpu as pltpu
from jax.sharding import PartitionSpec as P

gelu_inner = 0.7978845608028654
gelu_cubic = 0.044715
LANES = 128
VMEM_BYTES = 48 * 1024 * 1024
both = ("dom", "rep")


def gelu_value(values):
    inner_arg = gelu_inner * (values + gelu_cubic * values * values * values)
    return 0.5 * values * (1.0 + jnp.tanh(inner_arg))


def gelu_slope(values):
    inner_arg = gelu_inner * (values + gelu_cubic * values * values * values)
    tangent = jnp.tanh(inner_arg)
    return 0.5 * (1.0 + tangent) + 0.5 * values * (1.0 - tangent * tangent) * gelu_inner * (
        1.0 + 3.0 * gelu_cubic * values * values
    )


def dot(left, right, left_dim=1, right_dim=0):
    return lax.dot_general(
        left, right, (((left_dim,), (right_dim,)), ((), ())), preferred_element_type=jnp.float32
    )


def params():
    return pltpu.CompilerParams(vmem_limit_bytes=VMEM_BYTES)


def whole(shape):
    return pl.BlockSpec(shape, lambda *_: (0,) * len(shape))


def bits_of(values):
    high = values.astype(jnp.bfloat16).astype(jnp.float32)
    middle = (values - high).astype(jnp.bfloat16).astype(jnp.float32)
    return high, middle, values - high - middle


def prepare_kernel(rows_ref, count_ref, tiles_ref, embeds_ref, out_ref, pick_ref, side_ref):
    slots, peers = rows_ref.shape
    nodes, width = embeds_ref.shape
    sent = slots * peers
    blocks, tiles = tiles_ref.shape[:2]
    spread = jnp.concatenate([rows_ref[...].astype(jnp.float32)] * peers, axis=0)
    row = lax.broadcasted_iota(jnp.int32, (sent, peers), 0)
    chosen = lax.div(row, slots) == lax.broadcasted_iota(jnp.int32, (sent, peers), 1)
    index = jnp.sum(jnp.where(chosen, spread, 0.0), axis=1, keepdims=True).astype(jnp.int32)
    counts = jnp.broadcast_to(count_ref[...].astype(jnp.float32), (sent, peers))
    count = jnp.sum(jnp.where(chosen, counts, 0.0), axis=1, keepdims=True).astype(jnp.int32)
    slot = lax.rem(lax.broadcasted_iota(jnp.int32, (sent, nodes), 0), slots)
    node = lax.broadcasted_iota(jnp.int32, (sent, nodes), 1)
    pick = jnp.where((node == index) & (slot < count), 1.0, 0.0).astype(jnp.bfloat16)
    pick_ref[...] = pick
    out_ref[:, :width] = dot(pick, embeds_ref[...]).astype(jnp.bfloat16)
    size = tiles_ref.shape[2]
    lane = lax.broadcasted_iota(jnp.int32, (size, LANES), 1)
    parts = []
    for block in range(blocks):
        total = tiles_ref[block, 0].astype(jnp.float32)
        for tile in range(1, tiles):
            total = total + tiles_ref[block, tile].astype(jnp.float32)
        rowsum = jnp.sum(total, axis=1, keepdims=True)
        scaling = lax.rsqrt(1.0 + rowsum)
        side_ref[block * size : (block + 1) * size, :] = jnp.where(lane == 0, rowsum, scaling)
        high, middle, low = bits_of(scaling)
        part = jnp.where(lane == 0, high, jnp.where(lane == 1, middle, jnp.where(lane == 2, low, 0.0)))
        parts.append(part.astype(jnp.bfloat16))
    out_ref[:, width:] = dot(pick, jnp.concatenate(parts, axis=0)).astype(jnp.bfloat16)


def prepare(rows, count, tile_weight, embeds):
    sent = rows.shape[0] * rows.shape[1]
    nodes, width = embeds.shape
    return pl.pallas_call(
        prepare_kernel,
        out_shape=(
            jax.ShapeDtypeStruct((sent, width + LANES), jnp.bfloat16),
            jax.ShapeDtypeStruct((sent, nodes), jnp.bfloat16),
            jax.ShapeDtypeStruct((nodes, LANES), jnp.float32),
        ),
        compiler_params=params(),
        name="prepare",
    )(rows, count, tile_weight, embeds)


def forward_kernel(x_ref, win_ref, wout_ref, pre_ref, hid_ref, proj_ref):
    step = pl.program_id(0)
    pre = dot(x_ref[...], win_ref[...])
    pre_ref[...] = pre
    hidden = gelu_value(pre).astype(jnp.bfloat16)
    for pair in range(hidden.shape[1] // (2 * LANES)):
        for rep in range(2):
            low = (2 * pair + rep) * LANES
            hid_ref[rep, :, pair * LANES : (pair + 1) * LANES] = hidden[:, low : low + LANES]
    part = dot(hidden, wout_ref[...])

    @pl.when(step == 0)
    def _():
        proj_ref[...] = part

    @pl.when(step > 0)
    def _():
        proj_ref[...] += part


def forward(embeds, weight_in, weight_out, chunk=512):
    nodes, depth = embeds.shape
    hidden = weight_in.shape[1]
    width = weight_out.shape[1]
    return pl.pallas_call(
        forward_kernel,
        grid=(hidden // chunk,),
        in_specs=[
            whole((nodes, depth)),
            pl.BlockSpec((depth, chunk), lambda i: (0, i)),
            pl.BlockSpec((chunk, width), lambda i: (i, 0)),
        ],
        out_specs=(
            pl.BlockSpec((nodes, chunk), lambda i: (0, i)),
            pl.BlockSpec((2, nodes, chunk // 2), lambda i: (0, 0, i)),
            whole((nodes, width)),
        ),
        out_shape=(
            jax.ShapeDtypeStruct((nodes, hidden), jnp.float32),
            jax.ShapeDtypeStruct((2, nodes, hidden // 2), jnp.bfloat16),
            jax.ShapeDtypeStruct((nodes, width), jnp.float32),
        ),
        compiler_params=params(),
        name="forward",
    )(embeds, weight_in, weight_out)


def local_kernel(
    column_ref,
    tiles_ref,
    side_ref,
    proj_ref,
    rows_ref,
    class_ref,
    proto_ref,
    grad_ref,
    weight_ref,
    back_ref,
    dense_ref,
):
    blocks, tiles, size, _ = tiles_ref.shape
    nodes, width = proj_ref.shape
    extent = dense_ref.shape[0]
    dense_ref[...] = jnp.zeros_like(dense_ref)
    for block in range(blocks):
        for tile in range(tiles):
            column = column_ref[block, tile]
            place = slice(block * size, (block + 1) * size)
            dense_ref[column, place, :] += tiles_ref[block, tile].astype(jnp.float32)
    dense = jnp.concatenate([dense_ref[column] for column in range(extent)], axis=1)
    high = dense.astype(jnp.bfloat16)
    low = (dense - high.astype(jnp.float32)).astype(jnp.bfloat16)
    weight_ref[0] = high[:, nodes:]
    weight_ref[1] = low[:, nodes:]
    rowsum = side_ref[:, 0:1]
    scaling = side_ref[:, 1:2]
    projected = proj_ref[...]
    unit = (projected * scaling).astype(jnp.bfloat16)
    unit_float = unit.astype(jnp.float32)
    beside = jnp.concatenate([unit, jnp.ones((nodes, LANES), jnp.bfloat16)], axis=1)
    turned = dot(high, beside, 0, 0) + dot(low, beside, 0, 0)
    back_ref[...] = turned[nodes:]
    neighbour = dot(high[:, :nodes], unit) + dot(low[:, :nodes], unit)
    own = turned[:nodes, width : width + 1] * unit_float - turned[:nodes, :width]
    marked = rows_ref.shape[1]
    node = lax.broadcasted_iota(jnp.int32, (nodes, marked), 0)
    label = jnp.where(node == rows_ref[...], 1.0, 0.0)
    name = lax.broadcasted_iota(jnp.int32, (proto_ref.shape[0], marked), 0)
    named = jnp.where(name == class_ref[...], 1.0, 0.0).astype(jnp.bfloat16)
    target = dot(named, proto_ref[...], 0, 0).astype(jnp.bfloat16)
    pull = jnp.sum(label, axis=1, keepdims=True) * projected - dot(label.astype(jnp.bfloat16), target)
    grad_ref[...] = (rowsum * unit_float - neighbour + own) * scaling + pull


def local_part(tile_column, tile_weight, side, projected, label_rows, label_class, prototypes, received):
    nodes, width = projected.shape
    size = tile_weight.shape[2]
    vmem = pl.BlockSpec(memory_space=pltpu.VMEM)
    return pl.pallas_call(
        local_kernel,
        in_specs=[pl.BlockSpec(memory_space=pltpu.SMEM)] + [vmem] * 6,
        out_shape=(
            jax.ShapeDtypeStruct((nodes, width), jnp.float32),
            jax.ShapeDtypeStruct((2, nodes, received), jnp.bfloat16),
            jax.ShapeDtypeStruct((received, width + LANES), jnp.float32),
        ),
        scratch_shapes=[pltpu.VMEM(((nodes + received) // size, nodes, size), jnp.float32)],
        compiler_params=params(),
        name="local_part",
    )(tile_column, tile_weight, side, projected, label_rows, label_class, prototypes)


def received_kernel(
    x_ref,
    win_ref,
    wout_ref,
    side_ref,
    grad_ref,
    weight_ref,
    back_ref,
    hid_ref,
    full_ref,
    turned_ref,
    return_ref,
    proj_ref,
):
    step = pl.program_id(0)
    depth = win_ref.shape[0]
    pre = dot(x_ref[:, :depth], win_ref[...])
    hidden = gelu_value(pre).astype(jnp.bfloat16)
    for pair in range(hidden.shape[1] // (2 * LANES)):
        for rep in range(2):
            low = (2 * pair + rep) * LANES
            hid_ref[rep, :, pair * LANES : (pair + 1) * LANES] = hidden[:, low : low + LANES]
    part = dot(hidden, wout_ref[...])

    @pl.when(step == 0)
    def _():
        proj_ref[...] = part

    @pl.when(step > 0)
    def _():
        proj_ref[...] += part

    @pl.when(step == pl.num_programs(0) - 1)
    def _():
        nodes, width = grad_ref.shape
        scaling = jnp.sum(x_ref[:, depth:].astype(jnp.float32), axis=1, keepdims=True)
        unit = (proj_ref[...] * scaling).astype(jnp.bfloat16)
        neighbour = dot(weight_ref[0], unit) + dot(weight_ref[1], unit)
        full = grad_ref[...] - neighbour * side_ref[:, 1:2]
        full_ref[...] = full
        back = (back_ref[:, width : width + 1] * unit.astype(jnp.float32) - back_ref[:, :width]).astype(jnp.bfloat16)
        return_ref[...] = back
        turned_ref[:, :nodes] = full.T.astype(jnp.bfloat16)
        turned_ref[:, nodes:] = (back.astype(jnp.float32) * scaling).T.astype(jnp.bfloat16)


def received_part(arrived, weight_in, weight_out, side, grad, weight, back, chunk=512):
    rows = arrived.shape[0]
    depth, hidden = weight_in.shape
    nodes, width = grad.shape
    return pl.pallas_call(
        received_kernel,
        grid=(hidden // chunk,),
        in_specs=[
            whole(arrived.shape),
            pl.BlockSpec((depth, chunk), lambda i: (0, i)),
            pl.BlockSpec((chunk, width), lambda i: (i, 0)),
            whole(side.shape),
            whole(grad.shape),
            whole(weight.shape),
            whole(back.shape),
        ],
        out_specs=(
            pl.BlockSpec((2, rows, chunk // 2), lambda i: (0, 0, i)),
            whole((nodes, width)),
            whole((width, nodes + rows)),
            whole((rows, width)),
        ),
        out_shape=(
            jax.ShapeDtypeStruct((2, rows, hidden // 2), jnp.bfloat16),
            jax.ShapeDtypeStruct((nodes, width), jnp.float32),
            jax.ShapeDtypeStruct((width, nodes + rows), jnp.bfloat16),
            jax.ShapeDtypeStruct((rows, width), jnp.bfloat16),
        ),
        scratch_shapes=[pltpu.VMEM((rows, width), jnp.float32)],
        compiler_params=params(),
        name="received_part",
    )(arrived, weight_in, weight_out, side, grad, weight, back)


def product_kernel(rep_ref, turned_ref, other_ref, own_ref, came_ref, other_own_ref, other_came_ref, out_ref):
    nodes = own_ref.shape[1]
    total = dot(turned_ref[:, :nodes], own_ref[0]) + dot(turned_ref[:, nodes:], came_ref[0])
    total += dot(other_ref[:, :nodes], other_own_ref[...]) + dot(other_ref[:, nodes:], other_came_ref[...])
    for place in range(out_ref.shape[0]):
        out_ref[place] = total[:, place * LANES : (place + 1) * LANES]


def product(rep, turned, other, own, came, other_own, other_came, chunk=512):
    width = turned.shape[0]
    nodes, hidden = other_own.shape
    rows = other_came.shape[0]
    return pl.pallas_call(
        product_kernel,
        grid_spec=pltpu.PrefetchScalarGridSpec(
            num_scalar_prefetch=1,
            grid=(hidden // chunk,),
            in_specs=[
                whole(turned.shape),
                whole(other.shape),
                pl.BlockSpec((1, nodes, chunk), lambda i, rep: (rep[0], 0, i)),
                pl.BlockSpec((1, rows, chunk), lambda i, rep: (rep[0], 0, i)),
                pl.BlockSpec((nodes, chunk), lambda i, rep: (0, i)),
                pl.BlockSpec((rows, chunk), lambda i, rep: (0, i)),
            ],
            out_specs=pl.BlockSpec((chunk // LANES, width, LANES), lambda i, rep: (i, 0, 0)),
        ),
        out_shape=jax.ShapeDtypeStruct((hidden // LANES, width, LANES), jnp.float32),
        compiler_params=params(),
        name="product",
    )(rep, turned, other, own, came, other_own, other_came)


def backward_kernel(full_ref, pick_ref, back_ref, side_ref, pre_ref, wout_ref, win_ref, out_ref, node_ref, total_ref):
    step = pl.program_id(0)

    @pl.when(step == 0)
    def _():
        back = dot(pick_ref[...], back_ref[...], 0, 0)
        node_ref[...] = (full_ref[...] + back * side_ref[:, 1:2]).astype(jnp.bfloat16)

    grad_hidden = dot(node_ref[...], wout_ref[...], 1, 1)
    grad_pre = (grad_hidden * gelu_slope(pre_ref[...])).astype(jnp.bfloat16)
    part = dot(grad_pre, win_ref[...], 1, 1)

    @pl.when(step == 0)
    def _():
        total_ref[...] = part

    @pl.when(step > 0)
    def _():
        total_ref[...] += part

    @pl.when(step == pl.num_programs(0) - 1)
    def _():
        out_ref[...] = total_ref[...].astype(jnp.bfloat16)


def backward(full, pick, back, side, pre, weight_out, weight_in, chunk=512):
    nodes, hidden = pre.shape
    depth = weight_in.shape[0]
    width = weight_out.shape[1]
    return pl.pallas_call(
        backward_kernel,
        grid=(hidden // chunk,),
        in_specs=[
            whole(full.shape),
            whole(pick.shape),
            whole(back.shape),
            whole(side.shape),
            pl.BlockSpec((nodes, chunk), lambda i: (0, i)),
            pl.BlockSpec((chunk, width), lambda i: (i, 0)),
            pl.BlockSpec((depth, chunk), lambda i: (0, i)),
        ],
        out_specs=whole((nodes, depth)),
        out_shape=jax.ShapeDtypeStruct((nodes, depth), jnp.bfloat16),
        scratch_shapes=[pltpu.VMEM((nodes, width), jnp.bfloat16), pltpu.VMEM((nodes, depth), jnp.float32)],
        compiler_params=params(),
        name="backward",
    )(full, pick, back, side, pre, weight_out, weight_in)


def bit_orders(count):
    bits = list(range(count.bit_length() - 1))
    first = len(bits) // 3
    second = first + max(first, (len(bits) - first) // 3)
    low, middle, high = bits[:first], bits[first:second], bits[second:]
    return (low + middle + high, middle + low + high, high + low + middle)


def halve_over(part, axis, spot, pairs, mine):
    kept = lax.dynamic_index_in_dim(part, mine, spot, keepdims=False)
    sent = lax.dynamic_index_in_dim(part, 1 - mine, spot, keepdims=False).astype(jnp.bfloat16)
    return kept + lax.ppermute(sent, axis, pairs).astype(jnp.float32)


def scatter_sum(chip_sum):
    dom_count, width, depth = chip_sum.shape
    place = lax.axis_index("dom")
    cut = width * 3 // 8
    edges = (0, cut, 2 * cut, width)
    streams = []
    for order, low, high in zip(bit_orders(dom_count), edges[:-1], edges[1:]):
        bit_count = len(order)
        part = chip_sum[:, low:high].reshape((2,) * bit_count + (high - low, depth))
        streams.append((part, list(reversed(range(bit_count))), order))
    for step in range(dom_count.bit_length() - 1):
        later = []
        for part, left, order in streams:
            bit = order[step]
            pairs = [(device, device ^ (1 << bit)) for device in range(dom_count)]
            spot = left.index(bit)
            part = halve_over(part, "dom", spot, pairs, (place >> bit) & 1)
            later.append((part, [other for other in left if other != bit], order))
        streams = later
    return jnp.concatenate([part for part, _, _ in streams], axis=0)


def body(
    embeds,
    weight_in,
    weight_out,
    prototypes,
    tile_column,
    tile_weight,
    send_rows,
    send_count,
    label_rows,
    label_class,
):
    nodes = embeds.shape[0]
    dom_count = lax.axis_size("dom")
    rep_count = lax.axis_size("rep")
    peers = dom_count * rep_count
    slots = send_rows.shape[2]
    hidden_width, width = weight_out.shape
    depth = hidden_width // peers
    rep = lax.axis_index("rep")
    swap = [(0, 1), (1, 0)]
    fold = LANES // depth
    if fold > 1:
        order = (dom_count // fold, fold, rep_count, depth)
        weight_in = weight_in.reshape((-1,) + order).swapaxes(2, 3).reshape(-1, hidden_width)
        weight_out = weight_out.reshape(order + (-1,)).swapaxes(1, 2).reshape(hidden_width, -1)

    outgoing, pick, side = prepare(send_rows[0].T, send_count, tile_weight, embeds)
    arrived = lax.all_to_all(
        outgoing.reshape(peers, slots, -1), both, split_axis=0, concat_axis=0, tiled=True
    ).reshape(peers * slots, -1)
    pre_act, own_hidden, projected = forward(embeds, weight_in, weight_out)
    other_own = lax.ppermute(lax.dynamic_index_in_dim(own_hidden, 1 - rep, 0, keepdims=False), "rep", swap)
    grad, weight, back = local_part(
        tile_column,
        tile_weight,
        side,
        projected,
        label_rows[None, :],
        label_class[None, :],
        prototypes,
        peers * slots,
    )
    came_hidden, full, turned, returned = received_part(arrived, weight_in, weight_out, side, grad, weight, back)
    other_turned = lax.ppermute(turned, "rep", swap)
    other_came = lax.ppermute(lax.dynamic_index_in_dim(came_hidden, 1 - rep, 0, keepdims=False), "rep", swap)
    given = lax.all_to_all(
        returned.reshape(peers, slots, width), both, split_axis=0, concat_axis=0, tiled=True
    ).reshape(peers * slots, width)
    chip_sum = product(rep[None], turned, other_turned, own_hidden, came_hidden, other_own, other_came)
    if fold > 1:
        chip_sum = chip_sum.reshape(-1, width, fold, depth).swapaxes(1, 2).reshape(dom_count, width, depth)
    summed = scatter_sum(chip_sum)
    embed_grad = backward(full, pick, given, side, pre_act, weight_out, weight_in)
    return (embed_grad, summed.T * (1.0 / math.sqrt(nodes * peers)))


def solution(mesh):
    placed = (
        P(both, None),
        P(),
        P(),
        P(),
        P(both, None),
        P(both, None, None, None),
        P(both, None, None),
        P(both, None),
        P(both),
        P(both),
    )
    return jax.shard_map(
        body,
        mesh=mesh,
        in_specs=placed,
        out_specs=(P(both, None), P(both, None)),
        check_vma=False,
    )
```

time: 156 us -> 156 us (level)
  Pallas kernels: 0 us -> 55.1 us
  matrix products: 51.4 us -> 0 us
  other arithmetic: 11.6 us -> 4.4 us
  local copies, waits for them, and re-layouts: 31.3 us -> 33.2 us
  starting transfers between devices: 24.8 us -> 26.4 us
    pallas_call x0 -> x6, Pallas kernels: none -> 55.1 us  [the longest x1 16.5 us: backward(): pl.pallas_call(backward_kernel, grid=(hidden // chunk,), in_specs=[whole(...]
    dot_general x9 -> x0, matrix products: 51.4 us -> none  [the longest x1 17.2 us: body(): lax.dot_general(grad_pre, weight_in, (((1,), (1,)), ((), ())), preferred_...]
    gather x4 -> x0, local copies, waits for them, and re-layouts: 11 us -> none  [the longest x2 9.19 us: body(): jnp.take(extended, flat_columns, axis=0)]
    dynamic_slice x0 -> x9, local copies, waits for them, and re-layouts: none -> 8.57 us  [the longest x6 7.64 us: halve_over(): kept = lax.dynamic_index_in_dim(part, mine, spot, keepdims=False)]
    squeeze x0 -> x2, local copies, waits for them, and re-layouts: none -> 5.59 us  [the longest x1 3.28 us: body(): lax.dynamic_index_in_dim(own_hidden, 1 - rep, 0, keepdims=False)]
    all_to_all x2, starting transfers between devices: 10.1 us -> 13.2 us  [the longest x1 7.3 us: body(): lax.all_to_all(outgoing.reshape(peers, slots, -1), both, split_axis=0, co...]
    slice x4 -> x2, local copies, waits for them, and re-layouts: 0.86 us -> 3.78 us  [scatter_sum(): part = chip_sum[:, low:high].reshape((2,) * bit_count + (high - low, depth))]
    ppermute x13 -> x12, starting transfers between devices: 14.7 us -> 12.4 us  [halve_over(): return kept + lax.ppermute(sent, axis, pairs).astype(jnp.float32)]
  transfers between devices with their start and end apart: 15 -> 17, of which waited for: 11 -> 12; matrix products, arithmetic and copies ran while one was open for 18% -> 13% of each run, Pallas kernels for 0% -> 30%
where the time goes in v2:
time: 156 us; the launch traced here: 155 us
  Pallas kernels  55.1 us (35%)
  waiting for transfers between devices  34.5 us (22%)
  local copies, waits for them, and re-layouts  33.2 us (21%)
  starting transfers between devices  26.4 us (17%)
  other arithmetic  4.4 us (3%)
    ppermute x12, waiting for transfers between devices, halve_over(): return kept + lax.ppermute(sent, axis, pairs).astype(jnp.float32)  24.1 us
    pallas_call x1, Pallas kernels, backward(): pl.pallas_call(backward_kernel, grid=(hidden // chunk,), in_specs=[whole(...  16.5 us
    unnamed x47, local copies, waits for them, and re-layouts  15 us
    pallas_call x1, Pallas kernels, forward(): pl.pallas_call(forward_kernel, grid=(hidden // chunk,), in_specs=[whole((...  14.7 us
    ppermute x12, starting transfers between devices, halve_over(): return kept + lax.ppermute(sent, axis, pairs).astype(jnp.float32)  12.4 us
    pallas_call x1, Pallas kernels, received_part(): pl.pallas_call(received_kernel, grid=(hidden // chunk,), in_specs=[whole(...  11.7 us
    all_to_all x1, waiting for transfers between devices, body(): lax.all_to_all(returned.reshape(peers, slots, width), both, split_axis=0,...  10.4 us
    dynamic_slice x6, local copies, waits for them, and re-layouts, halve_over(): kept = lax.dynamic_index_in_dim(part, mine, spot, keepdims=False)  7.64 us
  transfers between devices with their start and end apart: 17, of which 12 were waited for; matrix products, arithmetic and copies ran while one was open for 13% of the time, Pallas kernels for 30%

profile of v2, /device:TPU:0, one launch (start us, length us, event | category | flops | bytes accessed | tf_op | source)
XLA Modules:
  0.0 154.6 jit_solution(14530835477016111291)
XLA Ops:
  0.6 1.2 copy-done.2
  1.9 1.2 copy-done.4
  4.4 1.6 %prepare.1 = (bf16[256,1152]{1,0:T(8,128)(2,1)}, bf16[256,512]{1,0:T(8,128)(2,1)S(1)}, f32[512,128]{1,0:T(8,128)S(1)}) custom-call(s32[8,32]{1,0:T(8,128)S(1)} %bitcast.73, s32[1,32]{1,0:T(1,128)S(1)} %copy-done.16, bf16[4,8,128,128]{3,2,1,0:T(8,128)(2,1)S(1)} %copy-done.2, bf16[512,1024]{1,0:T(8,128)(2,1)S(1)} %copy-done.4), custom_call_target="tpu_custom_call" | custom-call | tf_op jit(solution)/shard_map/prepare/pallas_call | solution.py:85
  6.7 7.3 %all-to-all-start = ((bf16[32,8,1152]{2,1,0:T(8,128)(2,1)}), bf16[32,8,1152]{2,1,0:T(8,128)(2,1)S(1)}, u32[]{:S(2)}, u32[]{:S(2)}) async-start(bf16[32,8,1152]{2,1,0:T(8,128)(2,1)} %bitcast.2), calls=%async_computation | async-start | bytes 1179648 | tf_op jit(solution)/shard_map/all_to_all | solution.py:435
  14.0 14.7 %forward.1 = (f32[512,4096]{1,0:T(8,128)}, bf16[2,512,2048]{2,1,0:T(8,128)(2,1)}, f32[512,512]{1,0:T(8,128)S(1)}) custom-call(bf16[512,1024]{1,0:T(8,128)(2,1)S(1)} %copy-done.5, bf16[1024,4096]{1,0:T(8,128)(2,1)} %win_ref.5, bf16[4096,512]{1,0:T(8,128)(2,1)} %wout_ref.5), custom_call_target="tpu_custom_call" | custom-call | tf_op jit(solution)/shard_map/forward/pallas_call | solution.py:121
  28.8 3.3 %dynamic-slice_bitcast_fusion = bf16[512,2048]{1,0:T(8,128)(2,1)} fusion(bf16[2,512,2048]{2,1,0:T(8,128)(2,1)} %get-tuple-element.26.own_ref, s32[]{:T(128)S(6)} %select_n.55), kind=kLoop, calls=%fused_computation | loop fusion | bytes 4194308 | tf_op jit(solution)/shard_map/jit(dynamic_index_in_dim)/squeeze | solution.py:439
  32.3 3.4 %local_part.1 = (f32[512,512]{1,0:T(8,128)S(1)}, bf16[2,512,256]{2,1,0:T(8,128)(2,1)S(1)}, f32[256,640]{1,0:T(8,128)S(1)}) custom-call(s32[4,8]{1,0:T(4,128)S(1)} %copy-done.15, bf16[4,8,128,128]{3,2,1,0:T(8,128)(2,1)S(1)} %copy-done.3, f32[512,128]{1,0:T(8,128)S(1)} %get-tuple-element.16.side_ref, f32[512,512]{1,0:T(8,128)S(1)} %get-tuple-element.17.proj_ref, ...), custom_call_target="tpu_custom_call" | custom-call | tf_op jit(solution)/shard_map/local_part/pallas_call | solution.py:195
  35.8 0.8 copy-done.7
  37.4 1.1 copy-done.8
  38.5 1.0 copy-done.10
  39.6 11.7 %received_part.1 = (bf16[2,256,2048]{2,1,0:T(8,128)(2,1)}, f32[512,512]{1,0:T(8,128)S(1)}, bf16[512,768]{1,0:T(8,128)(2,1)}, bf16[256,512]{1,0:T(8,128)(2,1)S(1)}) custom-call(bf16[256,1152]{1,0:T(8,128)(2,1)S(1)} %bitcast.70, bf16[1024,4096]{1,0:T(8,128)(2,1)} %win_ref.5, bf16[4096,512]{1,0:T(8,128)(2,1)} %wout_ref.5, ...), custom_call_target="tpu_custom_call" | custom-call | tf_op jit(solution)/shard_map/received_part/pallas_call | solution.py:259
  52.0 2.3 %dynamic-slice_bitcast_fusion.1 = bf16[256,2048]{1,0:T(8,128)(2,1)} fusion(bf16[2,256,2048]{2,1,0:T(8,128)(2,1)} %get-tuple-element.27.came_ref, s32[]{:T(128)S(6)} %select_n.55), kind=kLoop, calls=%fused_computation.3 | loop fusion | bytes 2097156 | tf_op jit(solution)/shard_map/jit(dynamic_index_in_dim)/squeeze | solution.py:452
  54.8 5.9 %all-to-all-start.1 = ((bf16[32,8,512]{2,1,0:T(8,128)(2,1)}), bf16[32,8,512]{2,1,0:T(8,128)(2,1)S(1)}, u32[]{:S(2)}, u32[]{:S(2)}) async-start(bf16[32,8,512]{2,1,0:T(8,128)(2,1)} %bitcast.72), calls=%async_computation.1 | async-start | bytes 524288 | tf_op jit(solution)/shard_map/all_to_all | solution.py:453
  60.7 10.4 %all-to-all-done.1 = bf16[32,8,512]{2,1,0:T(8,128)(2,1)S(1)} async-done(((bf16[32,8,512]{2,1,0:T(8,128)(2,1)}), bf16[32,8,512]{2,1,0:T(8,128)(2,1)S(1)}, u32[]{:S(2)}, u32[]{:S(2)}) %all-to-all-start.1) | async-done | bytes 262176 | tf_op jit(solution)/shard_map/all_to_all | solution.py:453
  71.1 2.2 %copy-done = bf16[4096,512]{1,0:T(8,128)(2,1)S(1)} copy-done((bf16[4096,512]{1,0:T(8,128)(2,1)S(1)}, bf16[4096,512]{1,0:T(8,128)(2,1)}, u32[]{:S(2)}) %copy-start) | copy-done | bytes 4194328
  73.3 0.9 copy-done.12
  74.3 16.5 %backward.1 = bf16[512,1024]{1,0:T(8,128)(2,1)} custom-call(f32[512,512]{1,0:T(8,128)S(1)} %get-tuple-element.21.full_ref, bf16[256,512]{1,0:T(8,128)(2,1)S(1)} %copy-done.12, bf16[256,512]{1,0:T(8,128)(2,1)S(1)} %bitcast.71, f32[512,128]{1,0:T(8,128)S(1)} %get-tuple-element.16.side_ref, f32[512,4096]{1,0:T(8,128)} %get-tuple-element.24.pre_ref, ...), custom_call_target="tpu_custom_call" | custom-call | tf_op jit(solution)/shard_map/backward/pallas_call | solution.py:351
  90.8 7.2 %product.1 = f32[16,512,128]{2,1,0:T(8,128)} custom-call(s32[1]{0:T(128)} %bitcast.8.rep_ref, bf16[512,768]{1,0:T(8,128)(2,1)} %get-tuple-element.25.turned_ref, bf16[512,768]{1,0:T(8,128)(2,1)S(1)} %collective-permute-done.other_ref, bf16[2,512,2048]{2,1,0:T(8,128)(2,1)} %get-tuple-element.26.own_ref, bf16[2,256,2048]{2,1,0:T(8,128)(2,1)S(1)} %copy-done.1, ...), custom_call_target="tpu_custom_call" | custom-call | tf_op jit(solution)/shard_map/product/pallas_call | solution.py:301
  98.0 1.3 slice.14
  99.3 2.5 %fusion.10 = (f32[16,192,128]{2,1,0:T(8,128)S(1)}, f32[16,192,128]{2,1,0:T(8,128)S(1)}) fusion(f32[16,512,128]{2,1,0:T(8,128)} %product.1), kind=kLoop, calls=%fused_computation.43 | loop fusion | bytes 6291456 | tf_op jit(solution)/shard_map/slice | solution.py:393
  101.9 0.9 copy.20
  102.7 0.9 collective-permute-start.11
  103.7 1.9 %constant_dynamic-slice_fusion.1 = f32[2,1,2,2,128,128]{5,4,3,2,1,0:T(8,128)} fusion(f32[2,2,2,2,128,128]{5,4,3,2,1,0:T(8,128)} %bitcast.81, s32[]{:T(128)S(6)} %select_n.60), kind=kLoop, calls=%fused_computation.38 | loop fusion | bytes 1048580 | tf_op jit(solution)/shard_map/jit(dynamic_index_in_dim)/dynamic_slice | solution.py:380
  105.5 2.0 %copy.16 = f32[2,1,2,2,128,128]{4,5,2,3,0,1:T(8,128)} copy(f32[2,1,2,2,128,128]{5,4,3,2,1,0:T(8,128)} %constant_dynamic-slice_fusion.1) | data formatting | bytes 1048576 | tf_op jit(solution)/shard_map/jit(dynamic_index_in_dim)/dynamic_slice | solution.py:380
  107.6 1.0 copy.19
  109.3 0.9 constant_dynamic-slice_fusion.3
  110.2 0.9 collective-permute-done.11
  111.2 1.2 bitcast_add_fusion.2
  112.4 1.0 collective-permute-start.12
  113.4 0.9 constant_dynamic-slice_fusion.5
  115.5 1.5 copy.12
  117.0 1.0 copy.18
  118.4 1.9 %collective-permute-done.12 = bf16[2,2,128,128]{2,3,0,1:T(8,128)(2,1)} collective-permute-done((bf16[2,2,128,128]{2,3,0,1:T(8,128)(2,1)S(1)}, bf16[2,2,128,128]{2,3,0,1:T(8,128)(2,1)}, u32[]{:S(2)}, u32[]{:S(2)}) %collective-permute-start.12) | collective-permute-done | bytes 131104 | tf_op jit(solution)/shard_map/ppermute | solution.py:382
  120.3 0.9 bitcast_add_fusion.5
  121.3 2.1 %collective-permute-start.13 = (bf16[2,128,128]{1,2,0:T(8,128)(2,1)S(1)}, bf16[2,128,128]{1,2,0:T(8,128)(2,1)S(1)}, u32[]{:S(2)}, u32[]{:S(2)}) collective-permute-start(bf16[2,128,128]{1,2,0:T(8,128)(2,1)S(1)} %fusion.8), channel_id=1, source_target_pairs={{0,2},{2,0},{4,6},{6,4},{8,10},{10,8},{12,14},{14,12},{16,18},{18,... | collective-permute-start | bytes 196616 | tf_op jit(solution)/shard_map/ppermute | solution.py:382
  123.4 1.2 bitcast_add_fusion
  124.7 8.4 %collective-permute-done.3 = bf16[2,2,2,192,128]{3,4,0,1,2:T(8,128)(2,1)S(1)} collective-permute-done((bf16[2,2,2,192,128]{3,4,0,1,2:T(8,128)(2,1)}, bf16[2,2,2,192,128]{3,4,0,1,2:T(8,128)(2,1)S(1)}, u32[]{:S(2)}, u32[]{:S(2)}) %collective-permute-start.3) | collective-permute-done | bytes 393248 | tf_op jit(solution)/shard_map/ppermute | solution.py:382
  133.2 1.3 collective-permute-done.13
  135.2 1.5 collective-permute-start.4
  136.7 1.8 %collective-permute-done.14 = bf16[128,128]{0,1:T(8,128)(2,1)S(1)} collective-permute-done((bf16[128,128]{0,1:T(8,128)(2,1)S(1)}, bf16[128,128]{0,1:T(8,128)(2,1)S(1)}, u32[]{:S(2)}, u32[]{:S(2)}) %collective-permute-start.14) | collective-permute-done | bytes 32800 | tf_op jit(solution)/shard_map/ppermute | solution.py:382
  139.5 2.2 %collective-permute-done.4 = bf16[2,2,192,128]{2,3,0,1:T(8,128)(2,1)S(1)} collective-permute-done((bf16[2,2,192,128]{2,3,0,1:T(8,128)(2,1)S(1)}, bf16[2,2,192,128]{2,3,0,1:T(8,128)(2,1)S(1)}, u32[]{:S(2)}, u32[]{:S(2)}) %collective-permute-start.4) | collective-permute-done | bytes 196640 | tf_op jit(solution)/shard_map/ppermute | solution.py:382
  141.7 1.0 collective-permute-start.5
  142.8 1.4 collective-permute-done.9
  144.2 1.8 %collective-permute-start.10 = (bf16[192,128]{0,1:T(8,128)(2,1)S(1)}, bf16[192,128]{0,1:T(8,128)(2,1)S(1)}, u32[]{:S(2)}, u32[]{:S(2)}) collective-permute-start(bf16[192,128]{0,1:T(8,128)(2,1)S(1)} %fusion.7), channel_id=1, source_target_pairs={{0,16},{2,18},{4,20},{6,22},{8,24},{10,26},{12,28},{14,30},{16,0},... | collective-permute-start | bytes 147464 | tf_op jit(solution)/shard_map/ppermute | solution.py:382
  146.0 1.8 %collective-permute-done.5 = bf16[2,192,128]{1,2,0:T(8,128)(2,1)S(1)} collective-permute-done((bf16[2,192,128]{1,2,0:T(8,128)(2,1)S(1)}, bf16[2,192,128]{1,2,0:T(8,128)(2,1)S(1)}, u32[]{:S(2)}, u32[]{:S(2)}) %collective-permute-start.5) | collective-permute-done | bytes 98336 | tf_op jit(solution)/shard_map/ppermute | solution.py:382
  147.8 1.6 %collective-permute-start.6 = (bf16[192,128]{0,1:T(8,128)(2,1)S(1)}, bf16[192,128]{0,1:T(8,128)(2,1)S(1)}, u32[]{:S(2)}, u32[]{:S(2)}) collective-permute-start(bf16[192,128]{0,1:T(8,128)(2,1)S(1)} %fusion.6), channel_id=1, source_target_pairs={{0,16},{2,18},{4,20},{6,22},{8,24},{10,26},{12,28},{14,30},{16,0},... | collective-permute-start | bytes 147464 | tf_op jit(solution)/shard_map/ppermute | solution.py:382
  150.2 3.6 %collective-permute-done.6 = bf16[192,128]{0,1:T(8,128)(2,1)S(1)} collective-permute-done((bf16[192,128]{0,1:T(8,128)(2,1)S(1)}, bf16[192,128]{0,1:T(8,128)(2,1)S(1)}, u32[]{:S(2)}, u32[]{:S(2)}) %collective-permute-start.6) | collective-permute-done | bytes 49184 | tf_op jit(solution)/shard_map/ppermute | solution.py:382
  153.8 0.8 fusion.2
  (74 shorter events, 9.4 us)
Async XLA Ops:
  0.6 1.2 copy-start.2
  1.9 1.2 copy-start.4
  3.1 0.7 copy-start.14
  3.8 0.7 copy-start.16
  4.4 9.6 %copy-start.5 = (bf16[512,1024]{1,0:T(8,128)(2,1)S(1)}, bf16[512,1024]{1,0:T(8,128)(2,1)}, u32[]{:S(2)}) copy-start(bf16[512,1024]{1,0:T(8,128)(2,1)} %x_ref.1) | copy-start | bytes 3145732
  6.0 0.7 copy-start.11
  6.7 30.7 %all-to-all-start = ((bf16[32,8,1152]{2,1,0:T(8,128)(2,1)}), bf16[32,8,1152]{2,1,0:T(8,128)(2,1)S(1)}, u32[]{:S(2)}, u32[]{:S(2)}) async-start(bf16[32,8,1152]{2,1,0:T(8,128)(2,1)} %bitcast.2), calls=%async_computation | async-start | bytes 1179648 | tf_op jit(solution)/shard_map/all_to_all | solution.py:435
  28.7 3.6 %copy-start.3 = (bf16[4,8,128,128]{3,2,1,0:T(8,128)(2,1)S(1)}, bf16[4,8,128,128]{3,2,1,0:T(8,128)(2,1)}, u32[]{:S(2)}) copy-start(bf16[4,8,128,128]{3,2,1,0:T(8,128)(2,1)} %tiles_ref.3) | copy-start | bytes 3145732
  28.7 3.6 %copy-start.6 = (bf16[1000,512]{1,0:T(8,128)(2,1)S(1)}, bf16[1000,512]{1,0:T(8,128)(2,1)}, u32[]{:S(2)}) copy-start(bf16[1000,512]{1,0:T(8,128)(2,1)} %proto_ref.1) | copy-start | bytes 3072004
  28.7 3.6 %copy-start.15 = (s32[4,8]{1,0:T(4,128)S(1)}, s32[4,8]{1,0:T(4,128)}, u32[]{:S(2)}) copy-start(s32[4,8]{1,0:T(4,128)} %column_ref.1) | copy-start | bytes 388
  28.7 3.6 %copy-start.17 = (s32[64]{0:T(128)S(1)}, s32[64]{0:T(128)}, u32[]{:S(2)}) copy-start(s32[64]{0:T(128)} %param.18) | copy-start | bytes 772
  28.8 3.6 %copy-start.18 = (s32[64]{0:T(128)S(1)}, s32[64]{0:T(128)}, u32[]{:S(2)}) copy-start(s32[64]{0:T(128)} %param.19) | copy-start | bytes 772
  32.0 58.8 %collective-permute-start.1 = (bf16[512,2048]{1,0:T(8,128)(2,1)}, bf16[512,2048]{1,0:T(8,128)(2,1)}, u32[]{:S(2)}, u32[]{:S(2)}) collective-permute-start(bf16[512,2048]{1,0:T(8,128)(2,1)} %dynamic-slice_bitcast_fusion), channel_id=1, source_target_pairs={{0,1},{1,0},{2,3},{3,2},{4,5},{5,4},{6,7},{7,6},{8,9},{9,8},{10,11... | collective-permute-start | bytes 6291464 | tf_op jit(solution)/shard_map/ppermute | solution.py:439
  35.8 0.8 copy-start.7
  36.6 0.8 copy-start.9
  37.4 1.1 copy-start.8
  38.5 1.0 copy-start.10
  51.3 0.7 copy-start.13
  54.3 36.5 %collective-permute-start.2 = (bf16[256,2048]{1,0:T(8,128)(2,1)}, bf16[256,2048]{1,0:T(8,128)(2,1)S(1)}, u32[]{:S(2)}, u32[]{:S(2)}) collective-permute-start(bf16[256,2048]{1,0:T(8,128)(2,1)} %dynamic-slice_bitcast_fusion.1), channel_id=1, source_target_pairs={{0,1},{1,0},{2,3},{3,2},{4,5},{5,4},{6,7},{7,6},{8,9},{9,8},{10,11... | collective-permute-start | bytes 3145736 | tf_op jit(solution)/shard_map/ppermute | solution.py:452
  54.5 36.3 %collective-permute-start = (bf16[512,768]{1,0:T(8,128)(2,1)}, bf16[512,768]{1,0:T(8,128)(2,1)S(1)}, u32[]{:S(2)}, u32[]{:S(2)}) collective-permute-start(bf16[512,768]{1,0:T(8,128)(2,1)} %get-tuple-element.25.turned_ref), channel_id=1, source_target_pairs={{0,1},{1,0},{2,3},{3,2},{4,5},{5,4},{6,7},{7,6},{8,9},{9,8},{10,11... | collective-permute-start | bytes 2359304 | tf_op jit(solution)/shard_map/ppermute | solution.py:451
  54.8 16.3 %all-to-all-start.1 = ((bf16[32,8,512]{2,1,0:T(8,128)(2,1)}), bf16[32,8,512]{2,1,0:T(8,128)(2,1)S(1)}, u32[]{:S(2)}, u32[]{:S(2)}) async-start(bf16[32,8,512]{2,1,0:T(8,128)(2,1)} %bitcast.72), calls=%async_computation.1 | async-start | bytes 524288 | tf_op jit(solution)/shard_map/all_to_all | solution.py:453
  71.1 2.2 %copy-start = (bf16[4096,512]{1,0:T(8,128)(2,1)S(1)}, bf16[4096,512]{1,0:T(8,128)(2,1)}, u32[]{:S(2)}) copy-start(bf16[4096,512]{1,0:T(8,128)(2,1)} %wout_ref.5) | copy-start | bytes 12582916
  73.3 0.9 copy-start.12
  74.3 16.6 %copy-start.1 = (bf16[2,256,2048]{2,1,0:T(8,128)(2,1)S(1)}, bf16[2,256,2048]{2,1,0:T(8,128)(2,1)}, u32[]{:S(2)}) copy-start(bf16[2,256,2048]{2,1,0:T(8,128)(2,1)} %get-tuple-element.27.came_ref) | copy-start | bytes 6291460
  99.3 2.5 %copy-start.19 = (f32[16,128,128]{2,1,0:T(8,128)}, f32[16,128,128]{2,1,0:T(8,128)S(1)}, u32[]{:S(2)}) copy-start(f32[16,128,128]{2,1,0:T(8,128)S(1)} %slice.14) | copy-start | bytes 3145732
  102.7 8.4 %collective-permute-start.11 = (bf16[2,2,2,128,128]{3,4,1,2,0:T(8,128)(2,1)}, bf16[2,2,2,128,128]{3,4,1,2,0:T(8,128)(2,1)}, u32[]{:S(2)}, u32[]{:S(2)}) collective-permute-start(bf16[2,2,2,128,128]{3,4,1,2,0:T(8,128)(2,1)} %bitcast.84), channel_id=1, source_target_pairs={{0,8},{2,10},{4,12},{6,14},{8,0},{10,2},{12,4},{14,6},{16,24},{18,... | collective-permute-start | bytes 786440 | tf_op jit(solution)/shard_map/ppermute | solution.py:382
  108.7 14.7 %collective-permute-start.7 = (bf16[2,2,2,192,128]{3,4,0,1,2:T(8,128)(2,1)}, bf16[2,2,2,192,128]{3,4,0,1,2:T(8,128)(2,1)}, u32[]{:S(2)}, u32[]{:S(2)}) collective-permute-start(bf16[2,2,2,192,128]{3,4,0,1,2:T(8,128)(2,1)} %bitcast.82), channel_id=1, source_target_pairs={{0,4},{2,6},{4,0},{6,2},{8,12},{10,14},{12,8},{14,10},{16,20},{18,... | collective-permute-start | bytes 1179656 | tf_op jit(solution)/shard_map/ppermute | solution.py:382
  110.2 4.9 %copy-start.20 = (f32[2,2,1,2,192,128]{5,4,3,2,1,0:T(8,128)S(1)}, f32[2,2,1,2,192,128]{5,4,3,2,1,0:T(8,128)}, u32[]{:S(2)}) copy-start(f32[2,2,1,2,192,128]{5,4,3,2,1,0:T(8,128)} %constant_dynamic-slice_fusion.3) | copy-start | bytes 2359300
  112.4 8.0 %collective-permute-start.12 = (bf16[2,2,128,128]{2,3,0,1:T(8,128)(2,1)S(1)}, bf16[2,2,128,128]{2,3,0,1:T(8,128)(2,1)}, u32[]{:S(2)}, u32[]{:S(2)}) collective-permute-start(bf16[2,2,128,128]{2,3,0,1:T(8,128)(2,1)S(1)} %fusion.5), channel_id=1, source_target_pairs={{0,16},{2,18},{4,20},{6,22},{8,24},{10,26},{12,28},{14,30},{16,0},... | collective-permute-start | bytes 393224 | tf_op jit(solution)/shard_map/ppermute | solution.py:382
  115.5 1.5 copy-start.21
  118.0 15.1 %collective-permute-start.3 = (bf16[2,2,2,192,128]{3,4,0,1,2:T(8,128)(2,1)}, bf16[2,2,2,192,128]{3,4,0,1,2:T(8,128)(2,1)S(1)}, u32[]{:S(2)}, u32[]{:S(2)}) collective-permute-start(bf16[2,2,2,192,128]{3,4,0,1,2:T(8,128)(2,1)} %bitcast.83), channel_id=1, source_target_pairs={{0,2},{2,0},{4,6},{6,4},{8,10},{10,8},{12,14},{14,12},{16,18},{18,... | collective-permute-start | bytes 1179656 | tf_op jit(solution)/shard_map/ppermute | solution.py:382
  121.3 13.2 %collective-permute-start.13 = (bf16[2,128,128]{1,2,0:T(8,128)(2,1)S(1)}, bf16[2,128,128]{1,2,0:T(8,128)(2,1)S(1)}, u32[]{:S(2)}, u32[]{:S(2)}) collective-permute-start(bf16[2,128,128]{1,2,0:T(8,128)(2,1)S(1)} %fusion.8), channel_id=1, source_target_pairs={{0,2},{2,0},{4,6},{6,4},{8,10},{10,8},{12,14},{14,12},{16,18},{18,... | collective-permute-start | bytes 196616 | tf_op jit(solution)/shard_map/ppermute | solution.py:382
  124.6 14.0 %collective-permute-start.8 = (bf16[2,2,192,128]{2,3,0,1:T(8,128)(2,1)S(1)}, bf16[2,2,192,128]{2,3,0,1:T(8,128)(2,1)S(1)}, u32[]{:S(2)}, u32[]{:S(2)}) collective-permute-start(bf16[2,2,192,128]{2,3,0,1:T(8,128)(2,1)S(1)} %fusion.1), channel_id=1, source_target_pairs={{0,2},{2,0},{4,6},{6,4},{8,10},{10,8},{12,14},{14,12},{16,18},{18,... | collective-permute-start | bytes 589832 | tf_op jit(solution)/shard_map/ppermute | solution.py:382
  134.6 4.0 %collective-permute-start.14 = (bf16[128,128]{0,1:T(8,128)(2,1)S(1)}, bf16[128,128]{0,1:T(8,128)(2,1)S(1)}, u32[]{:S(2)}, u32[]{:S(2)}) collective-permute-start(bf16[128,128]{0,1:T(8,128)(2,1)S(1)} %fusion.9), channel_id=1, source_target_pairs={{0,4},{2,6},{4,0},{6,2},{8,12},{10,14},{12,8},{14,10},{16,20},{18,... | collective-permute-start | bytes 98312 | tf_op jit(solution)/shard_map/ppermute | solution.py:382
  135.2 6.4 %collective-permute-start.4 = (bf16[2,2,192,128]{2,3,0,1:T(8,128)(2,1)S(1)}, bf16[2,2,192,128]{2,3,0,1:T(8,128)(2,1)S(1)}, u32[]{:S(2)}, u32[]{:S(2)}) collective-permute-start(bf16[2,2,192,128]{2,3,0,1:T(8,128)(2,1)S(1)} %fusion), channel_id=1, source_target_pairs={{0,4},{2,6},{4,0},{6,2},{8,12},{10,14},{12,8},{14,10},{16,20},{18,... | collective-permute-start | bytes 589832 | tf_op jit(solution)/shard_map/ppermute | solution.py:382
  138.7 5.5 %collective-permute-start.9 = (bf16[2,192,128]{1,2,0:T(8,128)(2,1)S(1)}, bf16[2,192,128]{1,2,0:T(8,128)(2,1)S(1)}, u32[]{:S(2)}, u32[]{:S(2)}) collective-permute-start(bf16[2,192,128]{1,2,0:T(8,128)(2,1)S(1)} %fusion.4), channel_id=1, source_target_pairs={{0,8},{2,10},{4,12},{6,14},{8,0},{10,2},{12,4},{14,6},{16,24},{18,... | collective-permute-start | bytes 294920 | tf_op jit(solution)/shard_map/ppermute | solution.py:382
  141.7 6.1 %collective-permute-start.5 = (bf16[2,192,128]{1,2,0:T(8,128)(2,1)S(1)}, bf16[2,192,128]{1,2,0:T(8,128)(2,1)S(1)}, u32[]{:S(2)}, u32[]{:S(2)}) collective-permute-start(bf16[2,192,128]{1,2,0:T(8,128)(2,1)S(1)} %fusion.3), channel_id=1, source_target_pairs={{0,8},{2,10},{4,12},{6,14},{8,0},{10,2},{12,4},{14,6},{16,24},{18,... | collective-permute-start | bytes 294920 | tf_op jit(solution)/shard_map/ppermute | solution.py:382
  144.2 5.9 %collective-permute-start.10 = (bf16[192,128]{0,1:T(8,128)(2,1)S(1)}, bf16[192,128]{0,1:T(8,128)(2,1)S(1)}, u32[]{:S(2)}, u32[]{:S(2)}) collective-permute-start(bf16[192,128]{0,1:T(8,128)(2,1)S(1)} %fusion.7), channel_id=1, source_target_pairs={{0,16},{2,18},{4,20},{6,22},{8,24},{10,26},{12,28},{14,30},{16,0},... | collective-permute-start | bytes 147464 | tf_op jit(solution)/shard_map/ppermute | solution.py:382
  147.8 5.9 %collective-permute-start.6 = (bf16[192,128]{0,1:T(8,128)(2,1)S(1)}, bf16[192,128]{0,1:T(8,128)(2,1)S(1)}, u32[]{:S(2)}, u32[]{:S(2)}) collective-permute-start(bf16[192,128]{0,1:T(8,128)(2,1)S(1)} %fusion.6), channel_id=1, source_target_pairs={{0,16},{2,18},{4,20},{6,22},{8,24},{10,26},{12,28},{14,30},{16,0},... | collective-permute-start | bytes 147464 | tf_op jit(solution)/shard_map/ppermute | solution.py:382

commit v3 on v2

v3 whole, which is shorter than its diff:
```python
import functools
import math

import jax
import jax.numpy as jnp
from jax import lax
from jax.experimental import pallas as pl
from jax.experimental.pallas import tpu as pltpu
from jax.sharding import PartitionSpec as P

gelu_inner = 0.7978845608028654
gelu_cubic = 0.044715
LANES = 128
MIB = 1024 * 1024
both = ("dom", "rep")


def gelu_pair(values):
    square = values * values
    half = 0.5 + 0.5 * jnp.tanh(values * (gelu_inner + gelu_inner * gelu_cubic * square))
    value = values * half
    slope = half + value * (2.0 - 2.0 * half) * (gelu_inner + 3.0 * gelu_inner * gelu_cubic * square)
    return value, slope


def dot(left, right, left_dim=1, right_dim=0):
    return lax.dot_general(
        left, right, (((left_dim,), (right_dim,)), ((), ())), preferred_element_type=jnp.float32
    )


def params(mib=64):
    return pltpu.CompilerParams(vmem_limit_bytes=mib * MIB)


VMEM = pl.BlockSpec(memory_space=pltpu.VMEM)
SMEM = pl.BlockSpec(memory_space=pltpu.SMEM)
HBM = pl.BlockSpec(memory_space=pltpu.HBM)


class Copies:
    def __init__(self, semaphores):
        self.semaphores = semaphores
        self.started = {}

    def start(self, name, source, target):
        copy = pltpu.make_async_copy(source, target, self.semaphores.at[len(self.started)])
        copy.start()
        self.started[name] = copy

    def wait(self, name):
        self.started[name].wait()


def bits_of(values):
    high = values.astype(jnp.bfloat16).astype(jnp.float32)
    middle = (values - high).astype(jnp.bfloat16).astype(jnp.float32)
    return high, middle, values - high - middle


def prepare_kernel(
    rows_any,
    count_any,
    tiles_any,
    embeds_any,
    out_ref,
    pick_ref,
    side_ref,
    rows_ref,
    count_ref,
    tiles_ref,
    embeds_ref,
    semaphores,
):
    copies = Copies(semaphores)
    copies.start("rows", rows_any, rows_ref)
    copies.start("count", count_any, count_ref)
    copies.start("tiles", tiles_any, tiles_ref)
    copies.start("embeds", embeds_any, embeds_ref)
    copies.wait("rows")
    copies.wait("count")
    slots, peers = rows_ref.shape
    nodes, width = embeds_ref.shape
    sent = slots * peers
    blocks, tiles = tiles_ref.shape[:2]
    spread = jnp.concatenate([rows_ref[...].astype(jnp.float32)] * peers, axis=0)
    row = lax.broadcasted_iota(jnp.int32, (sent, peers), 0)
    chosen = lax.div(row, slots) == lax.broadcasted_iota(jnp.int32, (sent, peers), 1)
    index = jnp.sum(jnp.where(chosen, spread, 0.0), axis=1, keepdims=True).astype(jnp.int32)
    counts = jnp.broadcast_to(count_ref[...].astype(jnp.float32), (sent, peers))
    count = jnp.sum(jnp.where(chosen, counts, 0.0), axis=1, keepdims=True).astype(jnp.int32)
    slot = lax.rem(lax.broadcasted_iota(jnp.int32, (sent, nodes), 0), slots)
    node = lax.broadcasted_iota(jnp.int32, (sent, nodes), 1)
    pick = jnp.where((node == index) & (slot < count), 1.0, 0.0).astype(jnp.bfloat16)
    pick_ref[...] = pick
    copies.wait("tiles")
    size = tiles_ref.shape[2]
    lane = lax.broadcasted_iota(jnp.int32, (size, LANES), 1)
    parts = []
    for block in range(blocks):
        total = tiles_ref[block, 0].astype(jnp.float32)
        for tile in range(1, tiles):
            total = total + tiles_ref[block, tile].astype(jnp.float32)
        rowsum = jnp.sum(total, axis=1, keepdims=True)
        scaling = lax.rsqrt(1.0 + rowsum)
        side_ref[block * size : (block + 1) * size, :] = jnp.where(lane == 0, rowsum, scaling)
        high, middle, low = bits_of(scaling)
        part = jnp.where(lane == 0, high, jnp.where(lane == 1, middle, jnp.where(lane == 2, low, 0.0)))
        parts.append(part.astype(jnp.bfloat16))
    out_ref[:, width:] = dot(pick, jnp.concatenate(parts, axis=0)).astype(jnp.bfloat16)
    copies.wait("embeds")
    out_ref[:, :width] = dot(pick, embeds_ref[...]).astype(jnp.bfloat16)


def prepare(rows, count, tile_weight, embeds):
    sent = rows.shape[0] * rows.shape[1]
    nodes, width = embeds.shape
    return pl.pallas_call(
        prepare_kernel,
        in_specs=[HBM] * 4,
        out_shape=(
            jax.ShapeDtypeStruct((sent, width + LANES), jnp.bfloat16),
            jax.ShapeDtypeStruct((sent, nodes), jnp.bfloat16),
            jax.ShapeDtypeStruct((nodes, LANES), jnp.float32),
        ),
        scratch_shapes=[
            pltpu.VMEM(rows.shape, jnp.int32),
            pltpu.VMEM(count.shape, jnp.int32),
            pltpu.VMEM(tile_weight.shape, jnp.bfloat16),
            pltpu.VMEM(embeds.shape, jnp.bfloat16),
            pltpu.SemaphoreType.DMA((4,)),
        ],
        compiler_params=params(),
        name="prepare",
    )(rows, count, tile_weight, embeds)


def split_hidden(hidden, rep, mine_ref, other_ref, start):
    for pair in range(hidden.shape[1] // (2 * LANES)):
        low = hidden[:, 2 * pair * LANES : (2 * pair + 1) * LANES]
        high = hidden[:, (2 * pair + 1) * LANES : (2 * pair + 2) * LANES]
        place = slice(start // 2 + pair * LANES, start // 2 + (pair + 1) * LANES)
        mine_ref[:, place] = jnp.where(rep == 0, low, high)
        other_ref[:, place] = jnp.where(rep == 0, high, low)


def hidden_chunks(x, win_ref, wout_ref, waiting, arrive, take):
    chunk = waiting[0].shape[1]
    count = win_ref.shape[1] // chunk
    projected = None
    for step in range(count + 1):
        arrive(step)
        if step < count:
            waiting[step % 2][...] = dot(x, win_ref[:, step * chunk : (step + 1) * chunk])
        if step > 0:
            start = (step - 1) * chunk
            value, slope = gelu_pair(waiting[(step - 1) % 2][...])
            hidden = value.astype(jnp.bfloat16)
            take(start, hidden, slope)
            part = dot(hidden, wout_ref[start : start + chunk])
            projected = part if projected is None else projected + part
    return projected


class Weights:
    def __init__(self, copies, win_any, wout_any, win_ref, wout_ref, chunk):
        self.copies = copies
        self.count = win_ref.shape[1] // chunk
        for step in range(self.count):
            place = pl.ds(step * chunk, chunk)
            copies.start(("in", step), win_any.at[:, place], win_ref.at[:, place])
            copies.start(("out", step), wout_any.at[place], wout_ref.at[place])

    def wait(self, step):
        if step < self.count:
            self.copies.wait(("in", step))
        if step > 0:
            self.copies.wait(("out", step - 1))


def forward_kernel(
    rep_ref,
    column_ref,
    x_any,
    win_any,
    wout_any,
    tiles_any,
    side_any,
    rows_any,
    class_any,
    proto_any,
    slope_any,
    mine_any,
    other_any,
    grad_ref,
    weight_ref,
    back_ref,
    x_ref,
    win_ref,
    wout_ref,
    tiles_ref,
    side_ref,
    rows_ref,
    class_ref,
    proto_ref,
    slope_ref,
    mine_ref,
    other_ref,
    even_ref,
    odd_ref,
    dense_ref,
    semaphores,
):
    copies = Copies(semaphores)
    chunk = even_ref.shape[1]
    copies.start("x", x_any, x_ref)
    weights = Weights(copies, win_any, wout_any, win_ref, wout_ref, chunk)
    later = {
        "tiles": (tiles_any, tiles_ref),
        "side": (side_any, side_ref),
        "rows": (rows_any, rows_ref),
        "class": (class_any, class_ref),
        "proto": (proto_any, proto_ref),
    }
    for name, (source, target) in later.items():
        copies.start(name, source, target)
    copies.wait("x")

    def give(step):
        whole_place = pl.ds(step * chunk, chunk)
        half_place = pl.ds(step * chunk // 2, chunk // 2)
        copies.start(("slope", step), slope_ref.at[:, whole_place], slope_any.at[:, whole_place])
        copies.start(("mine", step), mine_ref.at[:, half_place], mine_any.at[:, half_place])
        copies.start(("other", step), other_ref.at[:, half_place], other_any.at[:, half_place])

    def arrive(step):
        weights.wait(step)
        if step > 1:
            give(step - 2)

    def take(start, hidden, slope):
        slope_ref[:, start : start + hidden.shape[1]] = slope.astype(jnp.bfloat16)
        split_hidden(hidden, rep_ref[0], mine_ref, other_ref, start)

    projected = hidden_chunks(x_ref[...], win_ref, wout_ref, (even_ref, odd_ref), arrive, take)
    give(weights.count - 1)
    for name in later:
        copies.wait(name)
    local_part(
        column_ref,
        tiles_ref,
        side_ref,
        projected,
        rows_ref,
        class_ref,
        proto_ref,
        grad_ref,
        weight_ref,
        back_ref,
        dense_ref,
    )
    for step in range(weights.count):
        for name in ("slope", "mine", "other"):
            copies.wait((name, step))


def local_part(
    column_ref,
    tiles_ref,
    side_ref,
    projected,
    rows_ref,
    class_ref,
    proto_ref,
    grad_ref,
    weight_ref,
    back_ref,
    dense_ref,
):
    blocks, tiles, size, _ = tiles_ref.shape
    nodes, width = projected.shape
    extent = dense_ref.shape[0]
    dense_ref[...] = jnp.zeros_like(dense_ref)
    for block in range(blocks):
        for tile in range(tiles):
            column = column_ref[block, tile]
            place = slice(block * size, (block + 1) * size)
            dense_ref[column, place, :] += tiles_ref[block, tile].astype(jnp.float32)
    dense = jnp.concatenate([dense_ref[column] for column in range(extent)], axis=1)
    high = dense.astype(jnp.bfloat16)
    low = (dense - high.astype(jnp.float32)).astype(jnp.bfloat16)
    weight_ref[0] = high[:, nodes:]
    weight_ref[1] = low[:, nodes:]
    rowsum = side_ref[:, 0:1]
    scaling = side_ref[:, 1:2]
    unit = (projected * scaling).astype(jnp.bfloat16)
    unit_float = unit.astype(jnp.float32)
    beside = jnp.concatenate([unit, jnp.ones((nodes, LANES), jnp.bfloat16)], axis=1)
    turned = dot(high, beside, 0, 0) + dot(low, beside, 0, 0)
    back_ref[...] = turned[nodes:]
    neighbour = dot(high[:, :nodes], unit) + dot(low[:, :nodes], unit)
    own = turned[:nodes, width : width + 1] * unit_float - turned[:nodes, :width]
    marked = rows_ref.shape[1]
    node = lax.broadcasted_iota(jnp.int32, (nodes, marked), 0)
    label = jnp.where(node == rows_ref[...], 1.0, 0.0)
    name = lax.broadcasted_iota(jnp.int32, (proto_ref.shape[0], marked), 0)
    named = jnp.where(name == class_ref[...], 1.0, 0.0).astype(jnp.bfloat16)
    target = dot(named, proto_ref[...], 0, 0).astype(jnp.bfloat16)
    pull = jnp.sum(label, axis=1, keepdims=True) * projected - dot(label.astype(jnp.bfloat16), target)
    grad_ref[...] = (rowsum * unit_float - neighbour + own) * scaling + pull


def forward(
    rep,
    tile_column,
    embeds,
    weight_in,
    weight_out,
    tile_weight,
    side,
    label_rows,
    label_class,
    prototypes,
    received,
    chunk=1024,
):
    nodes, depth = embeds.shape
    hidden = weight_in.shape[1]
    width = weight_out.shape[1]
    size = tile_weight.shape[2]
    low = jnp.bfloat16
    arrays = (embeds, weight_in, weight_out, tile_weight, side, label_rows, label_class, prototypes)
    return pl.pallas_call(
        forward_kernel,
        in_specs=[SMEM] * 2 + [HBM] * 8,
        out_specs=(HBM, HBM, HBM, VMEM, VMEM, VMEM),
        out_shape=(
            jax.ShapeDtypeStruct((nodes, hidden), low),
            jax.ShapeDtypeStruct((nodes, hidden // 2), low),
            jax.ShapeDtypeStruct((nodes, hidden // 2), low),
            jax.ShapeDtypeStruct((nodes, width), jnp.float32),
            jax.ShapeDtypeStruct((2, nodes, received), low),
            jax.ShapeDtypeStruct((received, width + LANES), jnp.float32),
        ),
        scratch_shapes=[pltpu.VMEM(array.shape, array.dtype) for array in arrays]
        + [
            pltpu.VMEM((nodes, hidden), low),
            pltpu.VMEM((nodes, hidden // 2), low),
            pltpu.VMEM((nodes, hidden // 2), low),
            pltpu.VMEM((nodes, chunk), jnp.float32),
            pltpu.VMEM((nodes, chunk), jnp.float32),
            pltpu.VMEM(((nodes + received) // size, nodes, size), jnp.float32),
            pltpu.SemaphoreType.DMA((6 + 5 * (hidden // chunk),)),
        ],
        compiler_params=params(),
        name="forward",
    )(rep, tile_column, *arrays)


def received_kernel(
    rep_ref,
    x_any,
    win_any,
    wout_any,
    side_any,
    grad_any,
    weight_any,
    back_any,
    mine_any,
    other_any,
    full_ref,
    turned_ref,
    return_ref,
    x_ref,
    win_ref,
    wout_ref,
    side_ref,
    grad_ref,
    weight_ref,
    back_ref,
    mine_ref,
    other_ref,
    even_ref,
    odd_ref,
    semaphores,
):
    depth = win_ref.shape[0]
    nodes, width = grad_ref.shape
    chunk = even_ref.shape[1]
    copies = Copies(semaphores)
    copies.start("x", x_any, x_ref)
    weights = Weights(copies, win_any, wout_any, win_ref, wout_ref, chunk)
    later = {
        "side": (side_any, side_ref),
        "grad": (grad_any, grad_ref),
        "weight": (weight_any, weight_ref),
        "back": (back_any, back_ref),
    }
    for name, (source, target) in later.items():
        copies.start(name, source, target)
    copies.wait("x")

    def give(step):
        place = pl.ds(step * chunk // 2, chunk // 2)
        copies.start(("mine", step), mine_ref.at[:, place], mine_any.at[:, place])
        copies.start(("other", step), other_ref.at[:, place], other_any.at[:, place])

    def arrive(step):
        weights.wait(step)
        if step > 1:
            give(step - 2)

    def take(start, hidden, slope):
        split_hidden(hidden, rep_ref[0], mine_ref, other_ref, start)

    projected = hidden_chunks(x_ref[:, :depth], win_ref, wout_ref, (even_ref, odd_ref), arrive, take)
    give(weights.count - 1)
    for name in later:
        copies.wait(name)
    scaling = jnp.sum(x_ref[:, depth:].astype(jnp.float32), axis=1, keepdims=True)
    unit = (projected * scaling).astype(jnp.bfloat16)
    neighbour = dot(weight_ref[0], unit) + dot(weight_ref[1], unit)
    full = grad_ref[...] - neighbour * side_ref[:, 1:2]
    full_ref[...] = full
    back = (back_ref[:, width : width + 1] * unit.astype(jnp.float32) - back_ref[:, :width]).astype(jnp.bfloat16)
    return_ref[...] = back
    turned_ref[:, :nodes] = full.T.astype(jnp.bfloat16)
    turned_ref[:, nodes:] = (back.astype(jnp.float32) * scaling).T.astype(jnp.bfloat16)
    for step in range(weights.count):
        copies.wait(("mine", step))
        copies.wait(("other", step))


def received_part(rep, arrived, weight_in, weight_out, side, grad, weight, back, chunk=1024):
    rows = arrived.shape[0]
    hidden = weight_in.shape[1]
    nodes, width = grad.shape
    low = jnp.bfloat16
    arrays = (arrived, weight_in, weight_out, side, grad, weight, back)
    return pl.pallas_call(
        received_kernel,
        in_specs=[SMEM] + [HBM] * 7,
        out_specs=(HBM, HBM, VMEM, VMEM, VMEM),
        out_shape=(
            jax.ShapeDtypeStruct((rows, hidden // 2), low),
            jax.ShapeDtypeStruct((rows, hidden // 2), low),
            jax.ShapeDtypeStruct((nodes, width), jnp.float32),
            jax.ShapeDtypeStruct((width, nodes + rows), low),
            jax.ShapeDtypeStruct((rows, width), low),
        ),
        scratch_shapes=[pltpu.VMEM(array.shape, array.dtype) for array in arrays]
        + [
            pltpu.VMEM((rows, hidden // 2), low),
            pltpu.VMEM((rows, hidden // 2), low),
            pltpu.VMEM((rows, chunk), jnp.float32),
            pltpu.VMEM((rows, chunk), jnp.float32),
            pltpu.SemaphoreType.DMA((5 + 4 * (hidden // chunk),)),
        ],
        compiler_params=params(),
        name="received_part",
    )(rep, *arrays)


def chip_total(arrays, turned_ref, other_ref, own_ref, came_ref, other_own_ref, other_came_ref, semaphores, total_ref, chunk):
    nodes, hidden = own_ref.shape
    copies = Copies(semaphores)
    steps = range(0, hidden, chunk)
    whole = (turned_ref, other_ref, came_ref, other_came_ref)
    copies.start(0, arrays[0], turned_ref)
    copies.start(1, arrays[1], other_ref)
    for start in steps:
        place = pl.ds(start, chunk)
        for index, target in ((2, own_ref), (3, came_ref), (4, other_own_ref), (5, other_came_ref)):
            copies.start((index, start), arrays[index].at[:, place], target.at[:, place])
    copies.wait(0)
    copies.wait(1)
    for start in steps:
        for index in range(2, 6):
            copies.wait((index, start))
        place = slice(start, start + chunk)
        total = dot(turned_ref[:, :nodes], own_ref[:, place]) + dot(turned_ref[:, nodes:], came_ref[:, place])
        total += dot(other_ref[:, :nodes], other_own_ref[:, place])
        total += dot(other_ref[:, nodes:], other_came_ref[:, place])
        for step in range(chunk // LANES):
            total_ref[start // LANES + step] = total[:, step * LANES : (step + 1) * LANES]


def total_kernel(chunk, *refs):
    chip_total(refs[:6], *refs[7:13], refs[13], refs[6], chunk)


def product_kernel(streams, chunk, place_ref, *refs):
    outputs = refs[6 : 6 + 2 * len(streams)]
    scratch = refs[6 + 2 * len(streams) :]
    total_ref = scratch[-1]
    chip_total(refs[:6], *scratch[:7], total_ref, chunk)
    for stream, (order, low, high) in enumerate(streams):
        sent_ref, kept_ref = outputs[2 * stream : 2 * stream + 2]
        for spot in range(sent_ref.shape[0]):
            sent, kept = places(spot, order[0], place_ref[0])
            sent_ref[spot] = total_ref[sent, low:high].astype(jnp.bfloat16)
            kept_ref[spot] = total_ref[kept, low:high]


def places(spot, weight, place, bit=None):
    mine = lax.rem(lax.div(place, 1 << (weight if bit is None else bit)), 2)
    base = ((spot >> weight) << (weight + 1)) | (spot & ((1 << weight) - 1))
    return base + (1 - mine) * (1 << weight), base + mine * (1 << weight)


def fold_kernel(weight, bit, place_ref, kept_ref, came_ref, sent_ref, next_ref):
    for spot in range(sent_ref.shape[0]):
        sent, kept = places(spot, weight, place_ref[0], bit)
        sent_ref[spot] = (kept_ref[sent] + came_ref[sent].astype(jnp.float32)).astype(jnp.bfloat16)
    for spot in range(sent_ref.shape[0]):
        sent, kept = places(spot, weight, place_ref[0], bit)
        next_ref[spot] = kept_ref[kept] + came_ref[kept].astype(jnp.float32)


def fold_halves(place, weight, bit, kept, came):
    half = (kept.shape[0] // 2,) + kept.shape[1:]
    return pl.pallas_call(
        functools.partial(fold_kernel, weight, bit),
        in_specs=[SMEM, VMEM, VMEM],
        out_shape=(jax.ShapeDtypeStruct(half, jnp.bfloat16), jax.ShapeDtypeStruct(half, jnp.float32)),
        compiler_params=params(12),
        name="fold_halves",
    )(place, kept, came)


def product(place, streams, operands, chunk=512):
    width = operands[0].shape[0]
    hidden = operands[2].shape[1]
    blocks = hidden // LANES
    total = (blocks, width, LANES)
    scratch = [pltpu.VMEM(array.shape, array.dtype) for array in operands]
    scratch.append(pltpu.SemaphoreType.DMA((2 + 4 * (hidden // chunk),)))
    if not streams:
        return pl.pallas_call(
            functools.partial(total_kernel, chunk),
            in_specs=[HBM] * 6,
            out_shape=jax.ShapeDtypeStruct(total, jnp.float32),
            scratch_shapes=scratch,
            compiler_params=params(),
            name="chip_total",
        )(*operands)
    shapes = []
    for _, low, high in streams:
        shapes.append(jax.ShapeDtypeStruct((blocks // 2, high - low, LANES), jnp.bfloat16))
        shapes.append(jax.ShapeDtypeStruct((blocks // 2, high - low, LANES), jnp.float32))
    return pl.pallas_call(
        functools.partial(product_kernel, streams, chunk),
        in_specs=[SMEM] + [HBM] * 6,
        out_shape=tuple(shapes),
        scratch_shapes=scratch + [pltpu.VMEM(total, jnp.float32)],
        compiler_params=params(),
        name="product",
    )(place, *operands)


def backward_kernel(
    full_any,
    pick_any,
    back_any,
    side_any,
    slope_any,
    wout_any,
    win_any,
    out_ref,
    full_ref,
    pick_ref,
    back_ref,
    side_ref,
    slope_ref,
    wout_ref,
    win_ref,
    grad_ref,
    semaphores,
):
    hidden = slope_ref.shape[1]
    depth = win_ref.shape[0]
    count = 4
    chunk, rows = hidden // count, depth // count
    copies = Copies(semaphores)
    first = ((full_any, full_ref), (pick_any, pick_ref), (back_any, back_ref), (side_any, side_ref))
    for index, (source, target) in enumerate(first):
        copies.start(index, source, target)
    for step in range(count):
        place = pl.ds(step * chunk, chunk)
        copies.start(("out", step), wout_any.at[place], wout_ref.at[place])
        copies.start(("slope", step), slope_any.at[:, place], slope_ref.at[:, place])
    for step in range(count):
        place = pl.ds(step * rows, rows)
        copies.start(("in", step), win_any.at[place], win_ref.at[place])
    for index in range(len(first)):
        copies.wait(index)
    back = dot(pick_ref[...], back_ref[...], 0, 0)
    node = (full_ref[...] + back * side_ref[:, 1:2]).astype(jnp.bfloat16)
    for step in range(count):
        place = slice(step * chunk, (step + 1) * chunk)
        copies.wait(("out", step))
        copies.wait(("slope", step))
        grad_hidden = dot(node, wout_ref[place], 1, 1)
        grad_ref[:, place] = (grad_hidden * slope_ref[:, place].astype(jnp.float32)).astype(jnp.bfloat16)
    for step in range(count):
        place = slice(step * rows, (step + 1) * rows)
        copies.wait(("in", step))
        out_ref[:, place] = dot(grad_ref[...], win_ref[place], 1, 1).astype(jnp.bfloat16)


def backward(full, pick, back, side, slope, weight_out, weight_in):
    low = jnp.bfloat16
    arrays = (full, pick, back, side, slope, weight_out, weight_in)
    return pl.pallas_call(
        backward_kernel,
        in_specs=[HBM] * 7,
        out_shape=jax.ShapeDtypeStruct((full.shape[0], weight_in.shape[0]), low),
        scratch_shapes=[pltpu.VMEM(array.shape, array.dtype) for array in arrays]
        + [pltpu.VMEM(slope.shape, low), pltpu.SemaphoreType.DMA((16,))],
        compiler_params=params(61),
        name="backward",
    )(*arrays)


def bit_orders(count):
    bits = list(range(count.bit_length() - 1))
    first = len(bits) // 3
    second = first + max(first, (len(bits) - first) // 3)
    low, middle, high = bits[:first], bits[first:second], bits[second:]
    return (low + middle + high, middle + low + high, high + low + middle)


def streams_of(dom_count, width):
    cut = width * 3 // 8
    edges = (0, cut, 2 * cut, width)
    return tuple(zip(bit_orders(dom_count), edges[:-1], edges[1:]))


def halves(part, spot, mine):
    sent = lax.dynamic_index_in_dim(part, 1 - mine, spot, keepdims=False).astype(jnp.bfloat16)
    return sent, lax.dynamic_index_in_dim(part, mine, spot, keepdims=False)


def exchange(sent, bit):
    dom_count = lax.axis_size("dom")
    return lax.ppermute(sent, "dom", [(device, device ^ (1 << bit)) for device in range(dom_count)])


def body(
    embeds,
    weight_in,
    weight_out,
    prototypes,
    tile_column,
    tile_weight,
    send_rows,
    send_count,
    label_rows,
    label_class,
):
    nodes = embeds.shape[0]
    dom_count = lax.axis_size("dom")
    rep_count = lax.axis_size("rep")
    peers = dom_count * rep_count
    slots = send_rows.shape[2]
    hidden_width, width = weight_out.shape
    depth = hidden_width // peers
    place = lax.axis_index("dom")
    rep = lax.axis_index("rep")
    swap = [(0, 1), (1, 0)]
    fold = LANES // depth
    if fold > 1:
        order = (dom_count // fold, fold, rep_count, depth)
        weight_in = weight_in.reshape((-1,) + order).swapaxes(2, 3).reshape(-1, hidden_width)
        weight_out = weight_out.reshape(order + (-1,)).swapaxes(1, 2).reshape(hidden_width, -1)

    outgoing, pick, side = prepare(send_rows[0].T, send_count, tile_weight, embeds)
    arrived = lax.all_to_all(
        outgoing.reshape(peers, slots, -1), both, split_axis=0, concat_axis=0, tiled=True
    ).reshape(peers * slots, -1)
    slope, own, sent_own, grad, weight, back = forward(
        rep[None],
        tile_column,
        embeds,
        weight_in,
        weight_out,
        tile_weight,
        side,
        label_rows[None, :],
        label_class[None, :],
        prototypes,
        peers * slots,
    )
    other_own = lax.ppermute(sent_own, "rep", swap)
    came, sent_came, full, turned, returned = received_part(
        rep[None], arrived, weight_in, weight_out, side, grad, weight, back
    )
    other_turned = lax.ppermute(turned, "rep", swap)
    other_came = lax.ppermute(sent_came, "rep", swap)
    operands = (turned, other_turned, own, came, other_own, other_came)

    streams = streams_of(dom_count, width)
    bit_count = dom_count.bit_length() - 1
    parts = []
    if fold > 1:
        total = product(place[None], (), operands)
        total = total.reshape(-1, width, fold, depth).swapaxes(1, 2).reshape((2,) * bit_count + (width, depth))
        for order, low, high in streams:
            spot = bit_count - 1 - order[0]
            pair = halves(total[..., low:high, :], spot, (place >> order[0]) & 1)
            parts.append(tuple(array.reshape(-1, high - low, depth) for array in pair))
    else:
        flat = product(place[None], streams, operands)
        parts = [tuple(flat[2 * stream : 2 * stream + 2]) for stream in range(len(streams))]
    parts, returned = lax.optimization_barrier((parts, returned))
    given = lax.all_to_all(
        returned.reshape(peers, slots, width), both, split_axis=0, concat_axis=0, tiled=True
    ).reshape(peers * slots, width)
    left = [[bit for bit in range(bit_count) if bit != order[0]] for order, _, _ in streams]
    for step in range(bit_count - 1):
        if step == 1:
            parts, full = lax.optimization_barrier((parts, full))
        later = []
        for (sent, kept), bits, (order, _, _) in zip(parts, left, streams):
            bit = order[step + 1]
            later.append(fold_halves(place[None], bits.index(bit), bit, kept, exchange(sent, order[step])))
            bits.remove(bit)
        parts = later
    sums = [
        kept[0] + exchange(sent, order[-1])[0].astype(jnp.float32)
        for (sent, kept), (order, _, _) in zip(parts, streams)
    ]
    summed = jnp.concatenate(sums, axis=0)
    embed_grad = backward(full, pick, given, side, slope, weight_out, weight_in)
    return (embed_grad, summed.T * (1.0 / math.sqrt(nodes * peers)))


def solution(mesh):
    placed = (
        P(both, None),
        P(),
        P(),
        P(),
        P(both, None),
        P(both, None, None, None),
        P(both, None, None),
        P(both, None),
        P(both),
        P(both),
    )
    return jax.shard_map(
        body,
        mesh=mesh,
        in_specs=placed,
        out_specs=(P(both, None), P(both, None)),
        check_vma=False,
    )
```

time: 156 us -> 112 us (0.72)
  local copies, waits for them, and re-layouts: 33.2 us -> 4.83 us
  waiting for transfers between devices: 34.5 us -> 19.3 us
  starting transfers between devices: 26.4 us -> 31.3 us
  other arithmetic: 4.4 us -> 0.05 us
    all_to_all x1, waiting for transfers between devices: 10.4 us -> 0.01 us  [body(): lax.all_to_all(returned.reshape(peers, slots, width), both, split_axis=0,...]
    unnamed x47 -> x9, local copies, waits for them, and re-layouts: 15 us -> 4.83 us
    dynamic_slice x9 -> x0, local copies, waits for them, and re-layouts: 8.57 us -> none  [the longest x6 7.64 us: halve_over(): kept = lax.dynamic_index_in_dim(part, mine, spot, keepdims=False)]
    ppermute x14, waiting for transfers between devices: 24.1 us -> 15.7 us  [the longest x12 15.7 us: exchange(): lax.ppermute(sent, 'dom', [(device, device ^ 1 << bit) for device in rang...]
    ppermute x14, starting transfers between devices: 13 us -> 20.6 us  [the longest x12 20 us: exchange(): lax.ppermute(sent, 'dom', [(device, device ^ 1 << bit) for device in rang...]
    squeeze x2 -> x0, local copies, waits for them, and re-layouts: 5.59 us -> none  [the longest x1 3.28 us: body(): lax.dynamic_index_in_dim(own_hidden, 1 - rep, 0, keepdims=False)]
    slice x2 -> x0, local copies, waits for them, and re-layouts: 3.78 us -> none  [scatter_sum(): part = chip_sum[:, low:high].reshape((2,) * bit_count + (high - low, depth))]
    ppermute x1, waiting for transfers between devices: 0.01 us -> 3.62 us  [body(): other_turned = lax.ppermute(turned, 'rep', swap)]
  transfers between devices with their start and end apart: 17 -> 17, of which waited for: 12 -> 6; matrix products, arithmetic and copies ran while one was open for 13% -> 0% of each run, Pallas kernels for 30% -> 40%
where the time goes in v3:
time: 112 us
  Pallas kernels  55.6 us (50%)
  starting transfers between devices  31.3 us (28%)
  waiting for transfers between devices  19.3 us (17%)
  local copies, waits for them, and re-layouts  4.83 us (4%)
    ppermute x12, starting transfers between devices, exchange(): lax.ppermute(sent, 'dom', [(device, device ^ 1 << bit) for device in rang...  20 us
    pallas_call x1, Pallas kernels, forward(): pl.pallas_call(forward_kernel, in_specs=[SMEM] * 2 + [HBM] * 8, out_specs...  19.6 us
    ppermute x12, waiting for transfers between devices, exchange(): lax.ppermute(sent, 'dom', [(device, device ^ 1 << bit) for device in rang...  15.7 us
    pallas_call x1, Pallas kernels, backward(): pl.pallas_call(backward_kernel, in_specs=[HBM] * 7, out_shape=jax.ShapeDt...  15.5 us
    pallas_call x1, Pallas kernels, received_part(): pl.pallas_call(received_kernel, in_specs=[SMEM] + [HBM] * 7, out_specs=(H...  9.21 us
    pallas_call x1, Pallas kernels, product(): pl.pallas_call(functools.partial(product_kernel, streams, chunk), in_spec...  7.84 us
    all_to_all x1, starting transfers between devices, body(): lax.all_to_all(outgoing.reshape(peers, slots, -1), both, split_axis=0, co...  7.42 us
    unnamed x9, local copies, waits for them, and re-layouts  4.83 us
  transfers between devices with their start and end apart: 17, of which 6 were waited for; matrix products, arithmetic and copies ran while one was open for 0% of the time, Pallas kernels for 40%

profile of v3, /device:TPU:0, one launch (start us, length us, event | category | flops | bytes accessed | tf_op | source)
XLA Modules:
  0.0 111.8 jit_solution(15291479574499216224)
XLA Ops:
  0.6 3.0 %prepare.1 = (bf16[256,1152]{1,0:T(8,128)(2,1)}, bf16[256,512]{1,0:T(8,128)(2,1)}, f32[512,128]{1,0:T(8,128)}) custom-call(s32[8,32]{1,0:T(8,128)} %bitcast.22, s32[1,32]{1,0:T(1,128)} %count_any.1, bf16[4,8,128,128]{3,2,1,0:T(8,128)(2,1)} %tiles_any.3, bf16[512,1024]{1,0:T(8,128)(2,1)} %x_any.1), custom_call_target="tpu_custom_call" | custom-call | tf_op jit(solution)/shard_map/prepare/pallas_call | solution.py:118
  3.6 7.4 %all-to-all-start = ((bf16[32,8,1152]{2,1,0:T(8,128)(2,1)}), bf16[32,8,1152]{2,1,0:T(8,128)(2,1)}, u32[]{:S(2)}, u32[]{:S(2)}) async-start(bf16[32,8,1152]{2,1,0:T(8,128)(2,1)} %bitcast.20), calls=%async_computation | async-start | bytes 1179648 | tf_op jit(solution)/shard_map/all_to_all | solution.py:678
  11.1 19.6 %forward.1 = (bf16[512,4096]{1,0:T(8,128)(2,1)}, bf16[512,2048]{1,0:T(8,128)(2,1)}, bf16[512,2048]{1,0:T(8,128)(2,1)}, f32[512,512]{1,0:T(8,128)}, bf16[2,512,256]{2,1,0:T(8,128)(2,1)}, /*index=5*/f32[256,640]{1,0:T(8,128)}) custom-call(s32[1]{0:T(128)} %bitcast.1.rep_ref, s32[4,8]{1,0:T(4,128)} %column_ref.1, bf16[512,1024]{1,0:T(8,128)(2,1)} %x_any.1, ...), custom_call_target="tpu_custom_call" | custom-call | tf_op jit(solution)/shard_map/forward/pallas_call | solution.py:333
  30.7 0.3 collective-permute-start.1
  31.0 0.0 all-to-all-done
  31.0 9.2 %received_part.1 = (bf16[256,2048]{1,0:T(8,128)(2,1)}, bf16[256,2048]{1,0:T(8,128)(2,1)}, f32[512,512]{1,0:T(8,128)}, bf16[512,768]{1,0:T(8,128)(2,1)}, bf16[256,512]{1,0:T(8,128)(2,1)}) custom-call(s32[1]{0:T(128)} %bitcast.1.rep_ref, bf16[256,1152]{1,0:T(8,128)(2,1)} %bitcast.5.x_any, bf16[1024,4096]{1,0:T(8,128)(2,1)} %win_any.5, ...), custom_call_target="tpu_custom_call" | custom-call | tf_op jit(solution)/shard_map/received_part/pallas_call | solution.py:440
  40.2 0.4 collective-permute-start.2
  40.6 0.2 collective-permute-start
  40.8 3.6 %collective-permute-done.refs_1_ = bf16[512,768]{1,0:T(8,128)(2,1)} collective-permute-done((bf16[512,768]{1,0:T(8,128)(2,1)}, bf16[512,768]{1,0:T(8,128)(2,1)}, u32[]{:S(2)}, u32[]{:S(2)}) %collective-permute-start) | collective-permute-done | bytes 786464 | tf_op jit(solution)/shard_map/ppermute | solution.py:698
  44.4 0.0 collective-permute-done.1.refs_4_
  44.4 0.0 collective-permute-done.2.refs_5_
  44.4 7.8 %product.1 = (bf16[8,192,128]{2,1,0:T(8,128)(2,1)}, f32[8,192,128]{2,1,0:T(8,128)}, bf16[8,192,128]{2,1,0:T(8,128)(2,1)}, f32[8,192,128]{2,1,0:T(8,128)}, bf16[8...) custom-call(s32[1]{0:T(128)} %bitcast.place_ref, bf16[512,768]{1,0:T(8,128)(2,1)} %get-tuple-element.59.refs_0_, ...), custom_call_target="tpu_custom_call" | custom-call | tf_op jit(solution)/shard_map/product/pallas_call | solution.py:551
  52.2 1.7 %collective-permute-start.3 = (bf16[8,192,128]{2,1,0:T(8,128)(2,1)}, bf16[8,192,128]{2,1,0:T(8,128)(2,1)S(1)}, u32[]{:S(2)}, u32[]{:S(2)}) collective-permute-start(bf16[8,192,128]{2,1,0:T(8,128)(2,1)} %get-tuple-element.72), channel_id=1, source_target_pairs={{0,2},{2,0},{4,6},{6,4},{8,10},{10,8},{12,14},{14,12},{16,18},{18,... | collective-permute-start | bytes 1179656 | tf_op jit(solution)/shard_map/ppermute | solution.py:646
  54.0 1.5 %collective-permute-start.4 = (bf16[8,192,128]{2,1,0:T(8,128)(2,1)}, bf16[8,192,128]{2,1,0:T(8,128)(2,1)S(1)}, u32[]{:S(2)}, u32[]{:S(2)}) collective-permute-start(bf16[8,192,128]{2,1,0:T(8,128)(2,1)} %get-tuple-element.76), channel_id=1, source_target_pairs={{0,4},{2,6},{4,0},{6,2},{8,12},{10,14},{12,8},{14,10},{16,20},{18,... | collective-permute-start | bytes 1179656 | tf_op jit(solution)/shard_map/ppermute | solution.py:646
  55.4 1.5 %collective-permute-start.5 = (bf16[8,128,128]{2,1,0:T(8,128)(2,1)}, bf16[8,128,128]{2,1,0:T(8,128)(2,1)S(1)}, u32[]{:S(2)}, u32[]{:S(2)}) collective-permute-start(bf16[8,128,128]{2,1,0:T(8,128)(2,1)} %get-tuple-element.80), channel_id=1, source_target_pairs={{0,8},{2,10},{4,12},{6,14},{8,0},{10,2},{12,4},{14,6},{16,24},{18,... | collective-permute-start | bytes 786440 | tf_op jit(solution)/shard_map/ppermute | solution.py:646
  56.9 3.1 %all-to-all-start.1 = ((bf16[32,8,512]{2,1,0:T(8,128)(2,1)}), bf16[32,8,512]{2,1,0:T(8,128)(2,1)S(1)}, u32[]{:S(2)}, u32[]{:S(2)}) async-start(bf16[32,8,512]{2,1,0:T(8,128)(2,1)} %bitcast.21), calls=%async_computation.1 | async-start | bytes 524288 | tf_op jit(solution)/shard_map/all_to_all | solution.py:716
  59.9 5.2 %collective-permute-done.5.came_ref = bf16[8,128,128]{2,1,0:T(8,128)(2,1)S(1)} collective-permute-done((bf16[8,128,128]{2,1,0:T(8,128)(2,1)}, bf16[8,128,128]{2,1,0:T(8,128)(2,1)S(1)}, u32[]{:S(2)}, u32[]{:S(2)}) %collective-permute-start.5) | collective-permute-done | bytes 262176 | tf_op jit(solution)/shard_map/ppermute | solution.py:646
  65.1 1.0 copy-done.2
  66.2 0.0 collective-permute-done.3.came_ref
  66.2 0.0 copy-start.1
  66.2 1.1 %copy-done.1 = f32[8,192,128]{2,1,0:T(8,128)S(1)} copy-done((f32[8,192,128]{2,1,0:T(8,128)S(1)}, f32[8,192,128]{2,1,0:T(8,128)}, u32[]{:S(2)}) %copy-start.1) | copy-done | bytes 786456
  67.4 0.1 fold_halves.9
  67.4 0.0 collective-permute-done.4.came_ref
  67.4 0.0 copy-start
  67.4 1.1 %copy-done = f32[8,192,128]{2,1,0:T(8,128)S(1)} copy-done((f32[8,192,128]{2,1,0:T(8,128)S(1)}, f32[8,192,128]{2,1,0:T(8,128)}, u32[]{:S(2)}) %copy-start) | copy-done | bytes 786456
  68.6 0.1 fold_halves.10
  68.6 1.6 %collective-permute-start.6 = (bf16[4,192,128]{2,1,0:T(8,128)(2,1)S(1)}, bf16[4,192,128]{2,1,0:T(8,128)(2,1)S(1)}, u32[]{:S(2)}, u32[]{:S(2)}) collective-permute-start(bf16[4,192,128]{2,1,0:T(8,128)(2,1)S(1)} %get-tuple-element.89), channel_id=1, source_target_pairs={{0,4},{2,6},{4,0},{6,2},{8,12},{10,14},{12,8},{14,10},{16,20},{18,... | collective-permute-start | bytes 589832 | tf_op jit(solution)/shard_map/ppermute | solution.py:646
  70.2 2.8 %collective-permute-start.12 = (bf16[4,128,128]{2,1,0:T(8,128)(2,1)S(1)}, bf16[4,128,128]{2,1,0:T(8,128)(2,1)S(1)}, u32[]{:S(2)}, u32[]{:S(2)}) collective-permute-start(bf16[4,128,128]{2,1,0:T(8,128)(2,1)S(1)} %get-tuple-element.101), channel_id=1, source_target_pairs={{0,16},{2,18},{4,20},{6,22},{8,24},{10,26},{12,28},{14,30},{16,0},... | collective-permute-start | bytes 393224 | tf_op jit(solution)/shard_map/ppermute | solution.py:646
  73.0 1.1 %collective-permute-start.9 = (bf16[4,192,128]{2,1,0:T(8,128)(2,1)S(1)}, bf16[4,192,128]{2,1,0:T(8,128)(2,1)S(1)}, u32[]{:S(2)}, u32[]{:S(2)}) collective-permute-start(bf16[4,192,128]{2,1,0:T(8,128)(2,1)S(1)} %get-tuple-element.95), channel_id=1, source_target_pairs={{0,2},{2,0},{4,6},{6,4},{8,10},{10,8},{12,14},{14,12},{16,18},{18,... | collective-permute-start | bytes 589832 | tf_op jit(solution)/shard_map/ppermute | solution.py:646
  74.2 3.4 %collective-permute-done.12.came_ref = bf16[4,128,128]{2,1,0:T(8,128)(2,1)S(1)} collective-permute-done((bf16[4,128,128]{2,1,0:T(8,128)(2,1)S(1)}, bf16[4,128,128]{2,1,0:T(8,128)(2,1)S(1)}, u32[]{:S(2)}, u32[]{:S(2)}) %collective-permute-start.12) | collective-permute-done | bytes 131104 | tf_op jit(solution)/shard_map/ppermute | solution.py:646
  77.6 0.0 collective-permute-done.6.came_ref
  77.7 0.9 collective-permute-start.7
  78.5 1.1 %collective-permute-start.13 = (bf16[2,128,128]{2,1,0:T(8,128)(2,1)S(1)}, bf16[2,128,128]{2,1,0:T(8,128)(2,1)S(1)}, u32[]{:S(2)}, u32[]{:S(2)}) collective-permute-start(bf16[2,128,128]{2,1,0:T(8,128)(2,1)S(1)} %get-tuple-element.103), channel_id=1, source_target_pairs={{0,2},{2,0},{4,6},{6,4},{8,10},{10,8},{12,14},{14,12},{16,18},{18,... | collective-permute-start | bytes 196616 | tf_op jit(solution)/shard_map/ppermute | solution.py:646
  79.7 3.1 %collective-permute-done.13.came_ref = bf16[2,128,128]{2,1,0:T(8,128)(2,1)S(1)} collective-permute-done((bf16[2,128,128]{2,1,0:T(8,128)(2,1)S(1)}, bf16[2,128,128]{2,1,0:T(8,128)(2,1)S(1)}, u32[]{:S(2)}, u32[]{:S(2)}) %collective-permute-start.13) | collective-permute-done | bytes 65568 | tf_op jit(solution)/shard_map/ppermute | solution.py:646
  82.8 1.1 collective-permute-start.14
  83.9 0.0 all-to-all-done.1
  83.9 0.7 copy-done.3
  84.6 15.5 %backward.1 = bf16[512,1024]{1,0:T(8,128)(2,1)} custom-call(f32[512,512]{1,0:T(8,128)} %get-tuple-element.84.full_any, bf16[256,512]{1,0:T(8,128)(2,1)} %get-tuple-element.85.pick_any, bf16[256,512]{1,0:T(8,128)(2,1)} %bitcast.19, f32[512,128]{1,0:T(8,128)} %get-tuple-element.55.side_any, bf16[512,4096]{1,0:T(8,128)(2,1)} %get-tuple-element.87.slope_any, ...), custom_call_target="tpu_custom_call" | custom-call | tf_op jit(solution)/shard_map/backward/pallas_call | solution.py:614
  100.2 0.0 collective-permute-done.9.came_ref
  100.2 0.3 collective-permute-start.10
  100.5 0.0 collective-permute-done.7.came_ref
  100.6 3.4 %collective-permute-start.8 = (bf16[1,192,128]{2,1,0:T(8,128)(2,1)S(1)}, bf16[1,192,128]{2,1,0:T(8,128)(2,1)S(1)}, u32[]{:S(2)}, u32[]{:S(2)}) collective-permute-start(bf16[1,192,128]{2,1,0:T(8,128)(2,1)S(1)} %get-tuple-element.93), channel_id=1, source_target_pairs={{0,16},{2,18},{4,20},{6,22},{8,24},{10,26},{12,28},{14,30},{16,0},... | collective-permute-start | bytes 147464 | tf_op jit(solution)/shard_map/ppermute | solution.py:646
  103.9 0.0 collective-permute-done.14
  103.9 1.5 %collective-permute-done.10.came_ref = bf16[2,192,128]{2,1,0:T(8,128)(2,1)S(1)} collective-permute-done((bf16[2,192,128]{2,1,0:T(8,128)(2,1)S(1)}, bf16[2,192,128]{2,1,0:T(8,128)(2,1)S(1)}, u32[]{:S(2)}, u32[]{:S(2)}) %collective-permute-start.10) | collective-permute-done | bytes 98336 | tf_op jit(solution)/shard_map/ppermute | solution.py:646
  105.5 3.0 %collective-permute-start.11 = (bf16[1,192,128]{2,1,0:T(8,128)(2,1)S(1)}, bf16[1,192,128]{2,1,0:T(8,128)(2,1)S(1)}, u32[]{:S(2)}, u32[]{:S(2)}) collective-permute-start(bf16[1,192,128]{2,1,0:T(8,128)(2,1)S(1)} %get-tuple-element.99), channel_id=1, source_target_pairs={{0,16},{2,18},{4,20},{6,22},{8,24},{10,26},{12,28},{14,30},{16,0},... | collective-permute-start | bytes 147464 | tf_op jit(solution)/shard_map/ppermute | solution.py:646
  108.5 0.0 collective-permute-done.8
  108.5 2.5 %collective-permute-done.11 = bf16[1,192,128]{2,1,0:T(8,128)(2,1)S(1)} collective-permute-done((bf16[1,192,128]{2,1,0:T(8,128)(2,1)S(1)}, bf16[1,192,128]{2,1,0:T(8,128)(2,1)S(1)}, u32[]{:S(2)}, u32[]{:S(2)}) %collective-permute-start.11) | collective-permute-done | bytes 49184 | tf_op jit(solution)/shard_map/ppermute | solution.py:646
  111.0 0.8 copy.12
  (13 shorter events, 0.3 us)
Async XLA Ops:
  3.6 27.3 %all-to-all-start = ((bf16[32,8,1152]{2,1,0:T(8,128)(2,1)}), bf16[32,8,1152]{2,1,0:T(8,128)(2,1)}, u32[]{:S(2)}, u32[]{:S(2)}) async-start(bf16[32,8,1152]{2,1,0:T(8,128)(2,1)} %bitcast.20), calls=%async_computation | async-start | bytes 1179648 | tf_op jit(solution)/shard_map/all_to_all | solution.py:678
  30.7 13.7 %collective-permute-start.1 = (bf16[512,2048]{1,0:T(8,128)(2,1)}, bf16[512,2048]{1,0:T(8,128)(2,1)}, u32[]{:S(2)}, u32[]{:S(2)}) collective-permute-start(bf16[512,2048]{1,0:T(8,128)(2,1)} %get-tuple-element.62), channel_id=1, source_target_pairs={{0,1},{1,0},{2,3},{3,2},{4,5},{5,4},{6,7},{7,6},{8,9},{9,8},{10,11... | collective-permute-start | bytes 6291464 | tf_op jit(solution)/shard_map/ppermute | solution.py:694
  40.2 4.2 %collective-permute-start.2 = (bf16[256,2048]{1,0:T(8,128)(2,1)}, bf16[256,2048]{1,0:T(8,128)(2,1)}, u32[]{:S(2)}, u32[]{:S(2)}) collective-permute-start(bf16[256,2048]{1,0:T(8,128)(2,1)} %get-tuple-element.63), channel_id=1, source_target_pairs={{0,1},{1,0},{2,3},{3,2},{4,5},{5,4},{6,7},{7,6},{8,9},{9,8},{10,11... | collective-permute-start | bytes 3145736 | tf_op jit(solution)/shard_map/ppermute | solution.py:699
  40.6 3.8 %collective-permute-start = (bf16[512,768]{1,0:T(8,128)(2,1)}, bf16[512,768]{1,0:T(8,128)(2,1)}, u32[]{:S(2)}, u32[]{:S(2)}) collective-permute-start(bf16[512,768]{1,0:T(8,128)(2,1)} %get-tuple-element.59.refs_0_), channel_id=1, source_target_pairs={{0,1},{1,0},{2,3},{3,2},{4,5},{5,4},{6,7},{7,6},{8,9},{9,8},{10,11... | collective-permute-start | bytes 2359304 | tf_op jit(solution)/shard_map/ppermute | solution.py:698
  52.2 14.0 %collective-permute-start.3 = (bf16[8,192,128]{2,1,0:T(8,128)(2,1)}, bf16[8,192,128]{2,1,0:T(8,128)(2,1)S(1)}, u32[]{:S(2)}, u32[]{:S(2)}) collective-permute-start(bf16[8,192,128]{2,1,0:T(8,128)(2,1)} %get-tuple-element.72), channel_id=1, source_target_pairs={{0,2},{2,0},{4,6},{6,4},{8,10},{10,8},{12,14},{14,12},{16,18},{18,... | collective-permute-start | bytes 1179656 | tf_op jit(solution)/shard_map/ppermute | solution.py:646
  54.0 13.4 %collective-permute-start.4 = (bf16[8,192,128]{2,1,0:T(8,128)(2,1)}, bf16[8,192,128]{2,1,0:T(8,128)(2,1)S(1)}, u32[]{:S(2)}, u32[]{:S(2)}) collective-permute-start(bf16[8,192,128]{2,1,0:T(8,128)(2,1)} %get-tuple-element.76), channel_id=1, source_target_pairs={{0,4},{2,6},{4,0},{6,2},{8,12},{10,14},{12,8},{14,10},{16,20},{18,... | collective-permute-start | bytes 1179656 | tf_op jit(solution)/shard_map/ppermute | solution.py:646
  55.4 9.7 %collective-permute-start.5 = (bf16[8,128,128]{2,1,0:T(8,128)(2,1)}, bf16[8,128,128]{2,1,0:T(8,128)(2,1)S(1)}, u32[]{:S(2)}, u32[]{:S(2)}) collective-permute-start(bf16[8,128,128]{2,1,0:T(8,128)(2,1)} %get-tuple-element.80), channel_id=1, source_target_pairs={{0,8},{2,10},{4,12},{6,14},{8,0},{10,2},{12,4},{14,6},{16,24},{18,... | collective-permute-start | bytes 786440 | tf_op jit(solution)/shard_map/ppermute | solution.py:646
  56.9 27.0 %all-to-all-start.1 = ((bf16[32,8,512]{2,1,0:T(8,128)(2,1)}), bf16[32,8,512]{2,1,0:T(8,128)(2,1)S(1)}, u32[]{:S(2)}, u32[]{:S(2)}) async-start(bf16[32,8,512]{2,1,0:T(8,128)(2,1)} %bitcast.21), calls=%async_computation.1 | async-start | bytes 524288 | tf_op jit(solution)/shard_map/all_to_all | solution.py:716
  65.1 1.0 copy-start.2
  66.2 1.1 %copy-start.1 = (f32[8,192,128]{2,1,0:T(8,128)S(1)}, f32[8,192,128]{2,1,0:T(8,128)}, u32[]{:S(2)}) copy-start(f32[8,192,128]{2,1,0:T(8,128)} %get-tuple-element.71.kept_ref) | copy-start | bytes 2359300
  67.4 1.1 %copy-start = (f32[8,192,128]{2,1,0:T(8,128)S(1)}, f32[8,192,128]{2,1,0:T(8,128)}, u32[]{:S(2)}) copy-start(f32[8,192,128]{2,1,0:T(8,128)} %get-tuple-element.75.kept_ref) | copy-start | bytes 2359300
  68.6 9.0 %collective-permute-start.6 = (bf16[4,192,128]{2,1,0:T(8,128)(2,1)S(1)}, bf16[4,192,128]{2,1,0:T(8,128)(2,1)S(1)}, u32[]{:S(2)}, u32[]{:S(2)}) collective-permute-start(bf16[4,192,128]{2,1,0:T(8,128)(2,1)S(1)} %get-tuple-element.89), channel_id=1, source_target_pairs={{0,4},{2,6},{4,0},{6,2},{8,12},{10,14},{12,8},{14,10},{16,20},{18,... | collective-permute-start | bytes 589832 | tf_op jit(solution)/shard_map/ppermute | solution.py:646
  70.2 7.4 %collective-permute-start.12 = (bf16[4,128,128]{2,1,0:T(8,128)(2,1)S(1)}, bf16[4,128,128]{2,1,0:T(8,128)(2,1)S(1)}, u32[]{:S(2)}, u32[]{:S(2)}) collective-permute-start(bf16[4,128,128]{2,1,0:T(8,128)(2,1)S(1)} %get-tuple-element.101), channel_id=1, source_target_pairs={{0,16},{2,18},{4,20},{6,22},{8,24},{10,26},{12,28},{14,30},{16,0},... | collective-permute-start | bytes 393224 | tf_op jit(solution)/shard_map/ppermute | solution.py:646
  73.0 27.1 %collective-permute-start.9 = (bf16[4,192,128]{2,1,0:T(8,128)(2,1)S(1)}, bf16[4,192,128]{2,1,0:T(8,128)(2,1)S(1)}, u32[]{:S(2)}, u32[]{:S(2)}) collective-permute-start(bf16[4,192,128]{2,1,0:T(8,128)(2,1)S(1)} %get-tuple-element.95), channel_id=1, source_target_pairs={{0,2},{2,0},{4,6},{6,4},{8,10},{10,8},{12,14},{14,12},{16,18},{18,... | collective-permute-start | bytes 589832 | tf_op jit(solution)/shard_map/ppermute | solution.py:646
  77.7 22.9 %collective-permute-start.7 = (bf16[2,192,128]{2,1,0:T(8,128)(2,1)S(1)}, bf16[2,192,128]{2,1,0:T(8,128)(2,1)S(1)}, u32[]{:S(2)}, u32[]{:S(2)}) collective-permute-start(bf16[2,192,128]{2,1,0:T(8,128)(2,1)S(1)} %get-tuple-element.91), channel_id=1, source_target_pairs={{0,8},{2,10},{4,12},{6,14},{8,0},{10,2},{12,4},{14,6},{16,24},{18,... | collective-permute-start | bytes 294920 | tf_op jit(solution)/shard_map/ppermute | solution.py:646
  78.5 4.3 %collective-permute-start.13 = (bf16[2,128,128]{2,1,0:T(8,128)(2,1)S(1)}, bf16[2,128,128]{2,1,0:T(8,128)(2,1)S(1)}, u32[]{:S(2)}, u32[]{:S(2)}) collective-permute-start(bf16[2,128,128]{2,1,0:T(8,128)(2,1)S(1)} %get-tuple-element.103), channel_id=1, source_target_pairs={{0,2},{2,0},{4,6},{6,4},{8,10},{10,8},{12,14},{14,12},{16,18},{18,... | collective-permute-start | bytes 196616 | tf_op jit(solution)/shard_map/ppermute | solution.py:646
  82.8 21.1 %collective-permute-start.14 = (bf16[1,128,128]{2,1,0:T(8,128)(2,1)S(1)}, bf16[1,128,128]{2,1,0:T(8,128)(2,1)S(1)}, u32[]{:S(2)}, u32[]{:S(2)}) collective-permute-start(bf16[1,128,128]{2,1,0:T(8,128)(2,1)S(1)} %get-tuple-element.105), channel_id=1, source_target_pairs={{0,4},{2,6},{4,0},{6,2},{8,12},{10,14},{12,8},{14,10},{16,20},{18,... | collective-permute-start | bytes 98312 | tf_op jit(solution)/shard_map/ppermute | solution.py:646
  83.9 0.7 copy-start.3
  100.2 5.2 %collective-permute-start.10 = (bf16[2,192,128]{2,1,0:T(8,128)(2,1)S(1)}, bf16[2,192,128]{2,1,0:T(8,128)(2,1)S(1)}, u32[]{:S(2)}, u32[]{:S(2)}) collective-permute-start(bf16[2,192,128]{2,1,0:T(8,128)(2,1)S(1)} %get-tuple-element.97), channel_id=1, source_target_pairs={{0,8},{2,10},{4,12},{6,14},{8,0},{10,2},{12,4},{14,6},{16,24},{18,... | collective-permute-start | bytes 294920 | tf_op jit(solution)/shard_map/ppermute | solution.py:646
  100.6 7.9 %collective-permute-start.8 = (bf16[1,192,128]{2,1,0:T(8,128)(2,1)S(1)}, bf16[1,192,128]{2,1,0:T(8,128)(2,1)S(1)}, u32[]{:S(2)}, u32[]{:S(2)}) collective-permute-start(bf16[1,192,128]{2,1,0:T(8,128)(2,1)S(1)} %get-tuple-element.93), channel_id=1, source_target_pairs={{0,16},{2,18},{4,20},{6,22},{8,24},{10,26},{12,28},{14,30},{16,0},... | collective-permute-start | bytes 147464 | tf_op jit(solution)/shard_map/ppermute | solution.py:646
  105.5 5.5 %collective-permute-start.11 = (bf16[1,192,128]{2,1,0:T(8,128)(2,1)S(1)}, bf16[1,192,128]{2,1,0:T(8,128)(2,1)S(1)}, u32[]{:S(2)}, u32[]{:S(2)}) collective-permute-start(bf16[1,192,128]{2,1,0:T(8,128)(2,1)S(1)} %get-tuple-element.99), channel_id=1, source_target_pairs={{0,16},{2,18},{4,20},{6,22},{8,24},{10,26},{12,28},{14,30},{16,0},... | collective-permute-start | bytes 147464 | tf_op jit(solution)/shard_map/ppermute | solution.py:646

commit v4 on v3

--- a/solution.py
+++ b/solution.py
@@ -192,9 +192,9 @@
     slope_any,
     mine_any,
     other_any,
-    grad_ref,
-    weight_ref,
-    back_ref,
+    grad_any,
+    weight_any,
+    back_any,
     x_ref,
     win_ref,
     wout_ref,
@@ -209,14 +209,18 @@
     even_ref,
     odd_ref,
     dense_ref,
+    high_ref,
+    low_ref,
+    grad_ref,
+    back_ref,
     semaphores,
 ):
     copies = Copies(semaphores)
     chunk = even_ref.shape[1]
     copies.start("x", x_any, x_ref)
+    copies.start("tiles", tiles_any, tiles_ref)
     weights = Weights(copies, win_any, wout_any, win_ref, wout_ref, chunk)
     later = {
-        "tiles": (tiles_any, tiles_ref),
         "side": (side_any, side_ref),
         "rows": (rows_any, rows_ref),
         "class": (class_any, class_ref),
@@ -224,6 +228,7 @@
     }
     for name, (source, target) in later.items():
         copies.start(name, source, target)
+    nodes = x_ref.shape[0]
     copies.wait("x")
 
     def give(step):
@@ -237,6 +242,13 @@
         weights.wait(step)
         if step > 1:
             give(step - 2)
+        if step == 0:
+            copies.wait("tiles")
+            dense_graph(column_ref, tiles_ref, dense_ref, high_ref, low_ref)
+        if step == 1:
+            extra = pl.ds(nodes, high_ref.shape[1] - nodes)
+            copies.start("high", high_ref.at[:, extra], weight_any.at[0])
+            copies.start("low", low_ref.at[:, extra], weight_any.at[1])
 
     def take(start, hidden, slope):
         slope_ref[:, start : start + hidden.shape[1]] = slope.astype(jnp.bfloat16)
@@ -246,58 +258,16 @@
     give(weights.count - 1)
     for name in later:
         copies.wait(name)
-    local_part(
-        column_ref,
-        tiles_ref,
-        side_ref,
-        projected,
-        rows_ref,
-        class_ref,
-        proto_ref,
-        grad_ref,
-        weight_ref,
-        back_ref,
-        dense_ref,
-    )
-    for step in range(weights.count):
-        for name in ("slope", "mine", "other"):
-            copies.wait((name, step))
-
-
-def local_part(
-    column_ref,
-    tiles_ref,
-    side_ref,
-    projected,
-    rows_ref,
-    class_ref,
-    proto_ref,
-    grad_ref,
-    weight_ref,
-    back_ref,
-    dense_ref,
-):
-    blocks, tiles, size, _ = tiles_ref.shape
-    nodes, width = projected.shape
-    extent = dense_ref.shape[0]
-    dense_ref[...] = jnp.zeros_like(dense_ref)
-    for block in range(blocks):
-        for tile in range(tiles):
-            column = column_ref[block, tile]
-            place = slice(block * size, (block + 1) * size)
-            dense_ref[column, place, :] += tiles_ref[block, tile].astype(jnp.float32)
-    dense = jnp.concatenate([dense_ref[column] for column in range(extent)], axis=1)
-    high = dense.astype(jnp.bfloat16)
-    low = (dense - high.astype(jnp.float32)).astype(jnp.bfloat16)
-    weight_ref[0] = high[:, nodes:]
-    weight_ref[1] = low[:, nodes:]
+    width = projected.shape[1]
     rowsum = side_ref[:, 0:1]
     scaling = side_ref[:, 1:2]
     unit = (projected * scaling).astype(jnp.bfloat16)
     unit_float = unit.astype(jnp.float32)
     beside = jnp.concatenate([unit, jnp.ones((nodes, LANES), jnp.bfloat16)], axis=1)
+    high, low = high_ref[...], low_ref[...]
     turned = dot(high, beside, 0, 0) + dot(low, beside, 0, 0)
     back_ref[...] = turned[nodes:]
+    copies.start("back", back_ref, back_any)
     neighbour = dot(high[:, :nodes], unit) + dot(low[:, :nodes], unit)
     own = turned[:nodes, width : width + 1] * unit_float - turned[:nodes, :width]
     marked = rows_ref.shape[1]
@@ -308,6 +278,28 @@
     target = dot(named, proto_ref[...], 0, 0).astype(jnp.bfloat16)
     pull = jnp.sum(label, axis=1, keepdims=True) * projected - dot(label.astype(jnp.bfloat16), target)
     grad_ref[...] = (rowsum * unit_float - neighbour + own) * scaling + pull
+    copies.start("grad", grad_ref, grad_any)
+    for step in range(weights.count):
+        for name in ("slope", "mine", "other"):
+            copies.wait((name, step))
+    for name in ("high", "low", "back", "grad"):
+        copies.wait(name)
+
+
+def dense_graph(column_ref, tiles_ref, dense_ref, high_ref, low_ref):
+    blocks, tiles, size, _ = tiles_ref.shape
+    dense_ref[...] = jnp.zeros_like(dense_ref)
+    for block in range(blocks):
+        for tile in range(tiles):
+            column = column_ref[block, tile]
+            place = slice(block * size, (block + 1) * size)
+            dense_ref[column, place, :] += tiles_ref[block, tile].astype(jnp.float32)
+    for column in range(dense_ref.shape[0]):
+        dense = dense_ref[column]
+        high = dense.astype(jnp.bfloat16)
+        place = slice(column * size, (column + 1) * size)
+        high_ref[:, place] = high
+        low_ref[:, place] = (dense - high.astype(jnp.float32)).astype(jnp.bfloat16)
 
 
 def forward(
@@ -333,7 +325,7 @@
     return pl.pallas_call(
         forward_kernel,
         in_specs=[SMEM] * 2 + [HBM] * 8,
-        out_specs=(HBM, HBM, HBM, VMEM, VMEM, VMEM),
+        out_specs=(HBM,) * 6,
         out_shape=(
             jax.ShapeDtypeStruct((nodes, hidden), low),
             jax.ShapeDtypeStruct((nodes, hidden // 2), low),
@@ -350,7 +342,11 @@
             pltpu.VMEM((nodes, chunk), jnp.float32),
             pltpu.VMEM((nodes, chunk), jnp.float32),
             pltpu.VMEM(((nodes + received) // size, nodes, size), jnp.float32),
-            pltpu.SemaphoreType.DMA((6 + 5 * (hidden // chunk),)),
+            pltpu.VMEM((nodes, nodes + received), low),
+            pltpu.VMEM((nodes, nodes + received), low),
+            pltpu.VMEM((nodes, width), jnp.float32),
+            pltpu.VMEM((received, width + LANES), jnp.float32),
+            pltpu.SemaphoreType.DMA((10 + 5 * (hidden // chunk),)),
         ],
         compiler_params=params(),
         name="forward",
@@ -461,39 +457,39 @@
     )(rep, *arrays)
 
 
-def chip_total(arrays, turned_ref, other_ref, own_ref, came_ref, other_own_ref, other_came_ref, semaphores, total_ref, chunk):
-    nodes, hidden = own_ref.shape
+def chip_total(chunk, arrays, turned_ref, hidden_ref, semaphores, total_ref):
     copies = Copies(semaphores)
-    steps = range(0, hidden, chunk)
-    whole = (turned_ref, other_ref, came_ref, other_came_ref)
-    copies.start(0, arrays[0], turned_ref)
-    copies.start(1, arrays[1], other_ref)
+    steps = range(0, hidden_ref.shape[1], chunk)
+    base = 0
+    for index in range(2):
+        length = arrays[index].shape[1]
+        copies.start(index, arrays[index], turned_ref.at[:, pl.ds(base, length)])
+        base += length
     for start in steps:
         place = pl.ds(start, chunk)
-        for index, target in ((2, own_ref), (3, came_ref), (4, other_own_ref), (5, other_came_ref)):
-            copies.start((index, start), arrays[index].at[:, place], target.at[:, place])
+        base = 0
+        for index in range(2, 6):
+            length = arrays[index].shape[0]
+            copies.start((index, start), arrays[index].at[:, place], hidden_ref.at[pl.ds(base, length), place])
+            base += length
     copies.wait(0)
     copies.wait(1)
     for start in steps:
         for index in range(2, 6):
             copies.wait((index, start))
-        place = slice(start, start + chunk)
-        total = dot(turned_ref[:, :nodes], own_ref[:, place]) + dot(turned_ref[:, nodes:], came_ref[:, place])
-        total += dot(other_ref[:, :nodes], other_own_ref[:, place])
-        total += dot(other_ref[:, nodes:], other_came_ref[:, place])
+        total = dot(turned_ref[...], hidden_ref[:, start : start + chunk])
         for step in range(chunk // LANES):
             total_ref[start // LANES + step] = total[:, step * LANES : (step + 1) * LANES]
 
 
 def total_kernel(chunk, *refs):
-    chip_total(refs[:6], *refs[7:13], refs[13], refs[6], chunk)
+    chip_total(chunk, refs[:6], *refs[7:10], refs[6])
 
 
 def product_kernel(streams, chunk, place_ref, *refs):
     outputs = refs[6 : 6 + 2 * len(streams)]
-    scratch = refs[6 + 2 * len(streams) :]
-    total_ref = scratch[-1]
-    chip_total(refs[:6], *scratch[:7], total_ref, chunk)
+    turned_ref, hidden_ref, semaphores, total_ref = refs[6 + 2 * len(streams) :]
+    chip_total(chunk, refs[:6], turned_ref, hidden_ref, semaphores, total_ref)
     for stream, (order, low, high) in enumerate(streams):
         sent_ref, kept_ref = outputs[2 * stream : 2 * stream + 2]
         for spot in range(sent_ref.shape[0]):
@@ -508,24 +504,62 @@
     return base + (1 - mine) * (1 << weight), base + mine * (1 << weight)
 
 
-def fold_kernel(weight, bit, place_ref, kept_ref, came_ref, sent_ref, next_ref):
-    for spot in range(sent_ref.shape[0]):
-        sent, kept = places(spot, weight, place_ref[0], bit)
-        sent_ref[spot] = (kept_ref[sent] + came_ref[sent].astype(jnp.float32)).astype(jnp.bfloat16)
-    for spot in range(sent_ref.shape[0]):
-        sent, kept = places(spot, weight, place_ref[0], bit)
-        next_ref[spot] = kept_ref[kept] + came_ref[kept].astype(jnp.float32)
-
-
-def fold_halves(place, weight, bit, kept, came):
-    half = (kept.shape[0] // 2,) + kept.shape[1:]
+def fold_kernel(digits, merge, place_ref, *refs):
+    count = len(digits)
+    outputs = refs[2 * count :]
+    base = 0
+    for stream, (weight, bit) in enumerate(digits):
+        kept_ref, came_ref = refs[2 * stream : 2 * stream + 2]
+        target = max(stream - 1, 0) if merge else stream
+        if not (merge and stream == 1):
+            base = 0
+        sent_ref, next_ref = outputs[2 * target : 2 * target + 2]
+        rows = slice(base, base + kept_ref.shape[1])
+        base = rows.stop
+        for spot in range(sent_ref.shape[0]):
+            sent, kept = places(spot, weight, place_ref[0], bit)
+            sent_ref[spot, rows] = (kept_ref[sent] + came_ref[sent].astype(jnp.float32)).astype(jnp.bfloat16)
+            next_ref[spot, rows] = kept_ref[kept] + came_ref[kept].astype(jnp.float32)
+
+
+def fold_halves(place, digits, merge, kept, came):
+    heights = [array.shape[1] for array in kept]
+    if merge:
+        heights = [heights[0] + heights[1]] + heights[2:]
+    blocks, _, depth = kept[0].shape
+    shapes = []
+    for height in heights:
+        shapes.append(jax.ShapeDtypeStruct((blocks // 2, height, depth), jnp.bfloat16))
+        shapes.append(jax.ShapeDtypeStruct((blocks // 2, height, depth), jnp.float32))
+    operands = [array for pair in zip(kept, came) for array in pair]
+    flat = pl.pallas_call(
+        functools.partial(fold_kernel, digits, merge),
+        in_specs=[SMEM] + [VMEM] * len(operands),
+        out_shape=tuple(shapes),
+        compiler_params=params(16),
+        name="fold_halves",
+    )(place, *operands)
+    return [tuple(flat[2 * stream : 2 * stream + 2]) for stream in range(len(heights))]
+
+
+def finish_kernel(factor, *refs):
+    base = 0
+    for stream in range(len(refs) // 2):
+        kept_ref, came_ref = refs[2 * stream : 2 * stream + 2]
+        rows = kept_ref.shape[1]
+        total = kept_ref[0] + came_ref[0].astype(jnp.float32)
+        refs[-1][:, base : base + rows] = total.T * factor
+        base += rows
+
+
+def finish(factor, kept, came):
+    width = sum(array.shape[1] for array in kept)
     return pl.pallas_call(
-        functools.partial(fold_kernel, weight, bit),
-        in_specs=[SMEM, VMEM, VMEM],
-        out_shape=(jax.ShapeDtypeStruct(half, jnp.bfloat16), jax.ShapeDtypeStruct(half, jnp.float32)),
-        compiler_params=params(12),
-        name="fold_halves",
-    )(place, kept, came)
+        functools.partial(finish_kernel, factor),
+        out_shape=jax.ShapeDtypeStruct((kept[0].shape[2], width), jnp.float32),
+        compiler_params=params(16),
+        name="finish",
+    )(*[array for pair in zip(kept, came) for array in pair])
 
 
 def product(place, streams, operands, chunk=512):
@@ -533,8 +567,12 @@
     hidden = operands[2].shape[1]
     blocks = hidden // LANES
     total = (blocks, width, LANES)
-    scratch = [pltpu.VMEM(array.shape, array.dtype) for array in operands]
-    scratch.append(pltpu.SemaphoreType.DMA((2 + 4 * (hidden // chunk),)))
+    rows = 2 * operands[0].shape[1]
+    scratch = [
+        pltpu.VMEM((width, rows), jnp.bfloat16),
+        pltpu.VMEM((rows, hidden), jnp.bfloat16),
+        pltpu.SemaphoreType.DMA((2 + 4 * (hidden // chunk),)),
+    ]
     if not streams:
         return pl.pallas_call(
             functools.partial(total_kernel, chunk),
@@ -553,73 +591,93 @@
         in_specs=[SMEM] + [HBM] * 6,
         out_shape=tuple(shapes),
         scratch_shapes=scratch + [pltpu.VMEM(total, jnp.float32)],
-        compiler_params=params(),
+        compiler_params=params(60),
         name="product",
     )(place, *operands)
 
 
-def backward_kernel(
-    full_any,
-    pick_any,
-    back_any,
-    side_any,
-    slope_any,
-    wout_any,
-    win_any,
-    out_ref,
-    full_ref,
-    pick_ref,
-    back_ref,
-    side_ref,
-    slope_ref,
-    wout_ref,
-    win_ref,
-    grad_ref,
-    semaphores,
-):
-    hidden = slope_ref.shape[1]
-    depth = win_ref.shape[0]
-    count = 4
-    chunk, rows = hidden // count, depth // count
+def slope_kernel(chunk, *refs):
+    full_any, pick_any, back_any, side_any, slope_any, wout_any, out_any = refs[:7]
+    full_ref, pick_ref, back_ref, side_ref, slope_ref, wout_ref, grad_ref, semaphores = refs[7:]
     copies = Copies(semaphores)
     first = ((full_any, full_ref), (pick_any, pick_ref), (back_any, back_ref), (side_any, side_ref))
+    steps = range(0, slope_ref.shape[1], chunk)
     for index, (source, target) in enumerate(first):
         copies.start(index, source, target)
-    for step in range(count):
-        place = pl.ds(step * chunk, chunk)
-        copies.start(("out", step), wout_any.at[place], wout_ref.at[place])
-        copies.start(("slope", step), slope_any.at[:, place], slope_ref.at[:, place])
-    for step in range(count):
-        place = pl.ds(step * rows, rows)
-        copies.start(("in", step), win_any.at[place], win_ref.at[place])
+    for start in steps:
+        place = pl.ds(start, chunk)
+        copies.start(("out", start), wout_any.at[place], wout_ref.at[place])
+        copies.start(("slope", start), slope_any.at[:, place], slope_ref.at[:, place])
     for index in range(len(first)):
         copies.wait(index)
     back = dot(pick_ref[...], back_ref[...], 0, 0)
     node = (full_ref[...] + back * side_ref[:, 1:2]).astype(jnp.bfloat16)
-    for step in range(count):
-        place = slice(step * chunk, (step + 1) * chunk)
-        copies.wait(("out", step))
-        copies.wait(("slope", step))
+    for start in steps:
+        copies.wait(("out", start))
+        copies.wait(("slope", start))
+        place = slice(start, start + chunk)
         grad_hidden = dot(node, wout_ref[place], 1, 1)
         grad_ref[:, place] = (grad_hidden * slope_ref[:, place].astype(jnp.float32)).astype(jnp.bfloat16)
-    for step in range(count):
-        place = slice(step * rows, (step + 1) * rows)
-        copies.wait(("in", step))
-        out_ref[:, place] = dot(grad_ref[...], win_ref[place], 1, 1).astype(jnp.bfloat16)
-
-
-def backward(full, pick, back, side, slope, weight_out, weight_in):
-    low = jnp.bfloat16
-    arrays = (full, pick, back, side, slope, weight_out, weight_in)
+        copies.start(("grad", start), grad_ref.at[:, pl.ds(start, chunk)], out_any.at[:, pl.ds(start, chunk)])
+    for start in steps:
+        copies.wait(("grad", start))
+
+
+def slope_part(full, pick, back, side, slope, weight_out, chunk=1024):
+    arrays = (full, pick, back, side, slope, weight_out)
     return pl.pallas_call(
-        backward_kernel,
-        in_specs=[HBM] * 7,
-        out_shape=jax.ShapeDtypeStruct((full.shape[0], weight_in.shape[0]), low),
+        functools.partial(slope_kernel, chunk),
+        in_specs=[HBM] * 6,
+        out_specs=HBM,
+        out_shape=jax.ShapeDtypeStruct(slope.shape, jnp.bfloat16),
         scratch_shapes=[pltpu.VMEM(array.shape, array.dtype) for array in arrays]
-        + [pltpu.VMEM(slope.shape, low), pltpu.SemaphoreType.DMA((16,))],
-        compiler_params=params(61),
-        name="backward",
+        + [
+            pltpu.VMEM(slope.shape, jnp.bfloat16),
+            pltpu.SemaphoreType.DMA((4 + 3 * (slope.shape[1] // chunk),)),
+        ],
+        cost_estimate=pl.CostEstimate(flops=2 * slope.size * full.shape[1], bytes_accessed=16 * MIB, transcendentals=0),
+        compiler_params=params(60),
+        name="slope_part",
     )(*arrays)
+
+
+def embed_kernel(chunk, grad_any, win_any, out_ref, grad_ref, win_ref, total_ref, semaphores):
+    copies = Copies(semaphores)
+    steps = range(0, grad_ref.shape[1], chunk)
+    for start in steps:
+        place = pl.ds(start, chunk)
+        copies.start(("grad", start), grad_any.at[:, place], grad_ref.at[:, place])
+        copies.start(("in", start), win_any.at[:, place], win_ref.at[:, place])
+    for start in steps:
+        copies.wait(("grad", start))
+        copies.wait(("in", start))
+        place = slice(start, start + chunk)
+        part = dot(grad_ref[:, place], win_ref[:, place], 1, 1)
+        if start == 0:
+            total_ref[...] = part
+        elif start + chunk < grad_ref.shape[1]:
+            total_ref[...] += part
+        else:
+            out_ref[...] = (total_ref[...] + part).astype(jnp.bfloat16)
+
+
+def embed_part(grad, weight_in, chunk=1024):
+    nodes, hidden = grad.shape
+    depth = weight_in.shape[0]
+    return pl.pallas_call(
+        functools.partial(embed_kernel, chunk),
+        in_specs=[HBM] * 2,
+        out_shape=jax.ShapeDtypeStruct((nodes, depth), jnp.bfloat16),
+        scratch_shapes=[
+            pltpu.VMEM(grad.shape, jnp.bfloat16),
+            pltpu.VMEM(weight_in.shape, jnp.bfloat16),
+            pltpu.VMEM((nodes, depth), jnp.float32),
+            pltpu.SemaphoreType.DMA((2 * (hidden // chunk),)),
+        ],
+        cost_estimate=pl.CostEstimate(flops=2 * grad.size * depth, bytes_accessed=13 * MIB, transcendentals=0),
+        compiler_params=params(60),
+        name="embed_part",
+    )(grad, weight_in)
 
 
 def bit_orders(count):
@@ -697,6 +755,9 @@
     )
     other_turned = lax.ppermute(turned, "rep", swap)
     other_came = lax.ppermute(sent_came, "rep", swap)
+    given = lax.all_to_all(
+        returned.reshape(peers, slots, width), both, split_axis=0, concat_axis=0, tiled=True
+    ).reshape(peers * slots, width)
     operands = (turned, other_turned, own, came, other_own, other_came)
 
     streams = streams_of(dom_count, width)
@@ -712,27 +773,36 @@
     else:
         flat = product(place[None], streams, operands)
         parts = [tuple(flat[2 * stream : 2 * stream + 2]) for stream in range(len(streams))]
-    parts, returned = lax.optimization_barrier((parts, returned))
-    given = lax.all_to_all(
-        returned.reshape(peers, slots, width), both, split_axis=0, concat_axis=0, tiled=True
-    ).reshape(peers * slots, width)
+    parts, full = lax.optimization_barrier((parts, full))
+    grad_pre = slope_part(full, pick, given, side, slope, weight_out)
     left = [[bit for bit in range(bit_count) if bit != order[0]] for order, _, _ in streams]
-    for step in range(bit_count - 1):
-        if step == 1:
-            parts, full = lax.optimization_barrier((parts, full))
-        later = []
-        for (sent, kept), bits, (order, _, _) in zip(parts, left, streams):
-            bit = order[step + 1]
-            later.append(fold_halves(place[None], bits.index(bit), bit, kept, exchange(sent, order[step])))
-            bits.remove(bit)
-        parts = later
-    sums = [
-        kept[0] + exchange(sent, order[-1])[0].astype(jnp.float32)
-        for (sent, kept), (order, _, _) in zip(parts, streams)
-    ]
-    summed = jnp.concatenate(sums, axis=0)
-    embed_grad = backward(full, pick, given, side, slope, weight_out, weight_in)
-    return (embed_grad, summed.T * (1.0 / math.sqrt(nodes * peers)))
+    orders = [order for order, _, _ in streams]
+    shared = next(step for step in range(bit_count) if orders[0][step:] == orders[1][step:])
+    embed_grad = None
+    for step in range(bit_count):
+        came = [exchange(sent, order[step]) for (sent, _), order in zip(parts, orders)]
+        if step == 0:
+            came, grad_pre = lax.optimization_barrier((came, grad_pre))
+        elif step == 1:
+            came, embed_grad = lax.optimization_barrier((came, embed_grad))
+        else:
+            came = lax.optimization_barrier(came)
+        kept = [array for _, array in parts]
+        if step + 1 == bit_count:
+            break
+        digits = [(bits.index(order[step + 1]), order[step + 1]) for bits, order in zip(left, orders)]
+        for bits, order in zip(left, orders):
+            bits.remove(order[step + 1])
+        parts = fold_halves(place[None], digits, step + 1 == shared, kept, came)
+        if step + 1 == shared:
+            left, orders = left[1:], orders[1:]
+        if step == 0:
+            parts, grad_pre = lax.optimization_barrier((parts, grad_pre))
+            embed_grad = embed_part(grad_pre, weight_in)
+        else:
+            parts = lax.optimization_barrier(parts)
+    summed = finish(1.0 / math.sqrt(nodes * peers), kept, came)
+    return (embed_grad, summed)
 
 
 def solution(mesh):

time: 112 us -> 95.4 us (0.85)
  waiting for transfers between devices: 19.3 us -> 7.56 us
  starting transfers between devices: 31.3 us -> 27.3 us
  local copies, waits for them, and re-layouts: 4.83 us -> 3.55 us
    ppermute x12 -> x10, waiting for transfers between devices: 15.7 us -> 7.54 us  [exchange(): lax.ppermute(sent, 'dom', [(device, device ^ 1 << bit) for device in rang...]
    ppermute x12 -> x10, starting transfers between devices: 20 us -> 13.4 us  [exchange(): lax.ppermute(sent, 'dom', [(device, device ^ 1 << bit) for device in rang...]
    ppermute x1, waiting for transfers between devices: 3.62 us -> 0.01 us  [body(): other_turned = lax.ppermute(turned, 'rep', swap)]
    all_to_all x1, starting transfers between devices: 3.05 us -> 5.73 us  [body(): lax.all_to_all(returned.reshape(peers, slots, width), both, split_axis=0,...]
    unnamed x9 -> x16, local copies, waits for them, and re-layouts: 4.83 us -> 3.55 us
    pallas_call x10 -> x6, Pallas kernels: 15.9 us -> 16 us  [the longest x1 7.74 us: embed_part(): pl.pallas_call(functools.partial(embed_kernel, chunk), in_specs=[HBM] * 2...]
  transfers between devices with their start and end apart: 17 -> 15, of which waited for: 6 -> 4; matrix products, arithmetic and copies ran while one was open for 0% -> 0% of each run, Pallas kernels for 40% -> 54%
where the time goes in v4:
time: 95.4 us; the launch traced here: 95.1 us
  Pallas kernels  55.9 us (59%)
  starting transfers between devices  27.3 us (29%)
  waiting for transfers between devices  7.56 us (8%)
  local copies, waits for them, and re-layouts  3.55 us (4%)
    pallas_call x1, Pallas kernels, forward(): pl.pallas_call(forward_kernel, in_specs=[SMEM] * 2 + [HBM] * 8, out_specs...  19.8 us
    ppermute x10, starting transfers between devices, exchange(): lax.ppermute(sent, 'dom', [(device, device ^ 1 << bit) for device in rang...  13.4 us
    pallas_call x1, Pallas kernels, received_part(): pl.pallas_call(received_kernel, in_specs=[SMEM] + [HBM] * 7, out_specs=(H...  9.21 us
    pallas_call x1, Pallas kernels, product(): pl.pallas_call(functools.partial(product_kernel, streams, chunk), in_spec...  7.84 us
    pallas_call x1, Pallas kernels, embed_part(): pl.pallas_call(functools.partial(embed_kernel, chunk), in_specs=[HBM] * 2...  7.74 us
    ppermute x10, waiting for transfers between devices, exchange(): lax.ppermute(sent, 'dom', [(device, device ^ 1 << bit) for device in rang...  7.54 us
    all_to_all x1, starting transfers between devices, body(): lax.all_to_all(outgoing.reshape(peers, slots, -1), both, split_axis=0, co...  7.42 us
    pallas_call x1, Pallas kernels, slope_part(): pl.pallas_call(functools.partial(slope_kernel, chunk), in_specs=[HBM] * 6...  6.46 us
  transfers between devices with their start and end apart: 15, of which 4 were waited for; matrix products, arithmetic and copies ran while one was open for 0% of the time, Pallas kernels for 54%

profile of v4, /device:TPU:0, one launch (start us, length us, event | category | flops | bytes accessed | tf_op | source)
XLA Modules:
  0.0 95.1 jit_solution(8580936520085866985)
XLA Ops:
  0.6 3.0 %prepare.1 = (bf16[256,1152]{1,0:T(8,128)(2,1)}, bf16[256,512]{1,0:T(8,128)(2,1)}, f32[512,128]{1,0:T(8,128)}) custom-call(s32[8,32]{1,0:T(8,128)} %bitcast.14, s32[1,32]{1,0:T(1,128)} %count_any.1, bf16[4,8,128,128]{3,2,1,0:T(8,128)(2,1)} %tiles_any.3, bf16[512,1024]{1,0:T(8,128)(2,1)} %x_any.1), custom_call_target="tpu_custom_call" | custom-call | tf_op jit(solution)/shard_map/prepare/pallas_call | solution.py:118
  3.6 7.4 %all-to-all-start = ((bf16[32,8,1152]{2,1,0:T(8,128)(2,1)}), bf16[32,8,1152]{2,1,0:T(8,128)(2,1)}, u32[]{:S(2)}, u32[]{:S(2)}) async-start(bf16[32,8,1152]{2,1,0:T(8,128)(2,1)} %bitcast.12), calls=%async_computation | async-start | bytes 1179648 | tf_op jit(solution)/shard_map/all_to_all | solution.py:736
  11.1 19.8 %forward.1 = (bf16[512,4096]{1,0:T(8,128)(2,1)}, bf16[512,2048]{1,0:T(8,128)(2,1)}, bf16[512,2048]{1,0:T(8,128)(2,1)}, f32[512,512]{1,0:T(8,128)}, bf16[2,512,256]{2,1,0:T(8,128)(2,1)}, /*index=5*/f32[256,640]{1,0:T(8,128)}) custom-call(s32[1]{0:T(128)} %bitcast.1.rep_ref, s32[4,8]{1,0:T(4,128)} %column_ref.1, bf16[512,1024]{1,0:T(8,128)(2,1)} %x_any.1, ...), custom_call_target="tpu_custom_call" | custom-call | tf_op jit(solution)/shard_map/forward/pallas_call | solution.py:325
  30.9 0.2 collective-permute-start.1
  31.1 0.0 all-to-all-done
  31.1 9.2 %received_part.1 = (bf16[256,2048]{1,0:T(8,128)(2,1)}, bf16[256,2048]{1,0:T(8,128)(2,1)}, f32[512,512]{1,0:T(8,128)}, bf16[512,768]{1,0:T(8,128)(2,1)}, bf16[256,512]{1,0:T(8,128)(2,1)}) custom-call(s32[1]{0:T(128)} %bitcast.1.rep_ref, bf16[256,1152]{1,0:T(8,128)(2,1)} %bitcast.5.x_any, bf16[1024,4096]{1,0:T(8,128)(2,1)} %win_any.5, ...), custom_call_target="tpu_custom_call" | custom-call | tf_op jit(solution)/shard_map/received_part/pallas_call | solution.py:436
  40.3 0.4 collective-permute-start.2
  40.7 0.2 collective-permute-start
  40.9 5.7 %all-to-all-start.1 = ((bf16[32,8,512]{2,1,0:T(8,128)(2,1)}), bf16[32,8,512]{2,1,0:T(8,128)(2,1)S(1)}, u32[]{:S(2)}, u32[]{:S(2)}) async-start(bf16[32,8,512]{2,1,0:T(8,128)(2,1)} %bitcast.13), calls=%async_computation.1 | async-start | bytes 524288 | tf_op jit(solution)/shard_map/all_to_all | solution.py:758
  46.6 0.0 collective-permute-done.refs_1_
  46.7 0.0 copy-start.7
  46.7 0.0 collective-permute-done.1.refs_4_
  46.7 0.0 collective-permute-done.2.refs_5_
  46.7 0.0 copy-start.6
  46.7 0.9 copy-done.7
  47.6 0.3 copy-done.6
  47.9 7.8 %product.1 = (bf16[8,192,128]{2,1,0:T(8,128)(2,1)}, f32[8,192,128]{2,1,0:T(8,128)}, bf16[8,192,128]{2,1,0:T(8,128)(2,1)}, f32[8,192,128]{2,1,0:T(8,128)}, bf16[8...) custom-call(s32[1]{0:T(128)} %bitcast.place_ref, bf16[512,768]{1,0:T(8,128)(2,1)} %get-tuple-element.67.refs_0_, ...), custom_call_target="tpu_custom_call" | custom-call | tf_op jit(solution)/shard_map/product/pallas_call | solution.py:589
  55.7 1.8 %collective-permute-start.3 = (bf16[8,192,128]{2,1,0:T(8,128)(2,1)}, bf16[8,192,128]{2,1,0:T(8,128)(2,1)S(1)}, u32[]{:S(2)}, u32[]{:S(2)}) collective-permute-start(bf16[8,192,128]{2,1,0:T(8,128)(2,1)} %get-tuple-element.80), channel_id=1, source_target_pairs={{0,2},{2,0},{4,6},{6,4},{8,10},{10,8},{12,14},{14,12},{16,18},{18,... | collective-permute-start | bytes 1179656 | tf_op jit(solution)/shard_map/ppermute | solution.py:704
  57.6 1.5 %collective-permute-start.4 = (bf16[8,192,128]{2,1,0:T(8,128)(2,1)}, bf16[8,192,128]{2,1,0:T(8,128)(2,1)S(1)}, u32[]{:S(2)}, u32[]{:S(2)}) collective-permute-start(bf16[8,192,128]{2,1,0:T(8,128)(2,1)} %get-tuple-element.81), channel_id=1, source_target_pairs={{0,4},{2,6},{4,0},{6,2},{8,12},{10,14},{12,8},{14,10},{16,20},{18,... | collective-permute-start | bytes 1179656 | tf_op jit(solution)/shard_map/ppermute | solution.py:704
  59.0 1.5 %collective-permute-start.5 = (bf16[8,128,128]{2,1,0:T(8,128)(2,1)}, bf16[8,128,128]{2,1,0:T(8,128)(2,1)S(1)}, u32[]{:S(2)}, u32[]{:S(2)}) collective-permute-start(bf16[8,128,128]{2,1,0:T(8,128)(2,1)} %get-tuple-element.82), channel_id=1, source_target_pairs={{0,8},{2,10},{4,12},{6,14},{8,0},{10,2},{12,4},{14,6},{16,24},{18,... | collective-permute-start | bytes 786440 | tf_op jit(solution)/shard_map/ppermute | solution.py:704
  60.5 0.0 all-to-all-done.1
  60.5 0.7 copy-done.5
  61.2 6.5 %slope_part.1.grad_any = bf16[512,4096]{1,0:T(8,128)(2,1)} custom-call(f32[512,512]{1,0:T(8,128)} %get-tuple-element.83.refs_0_, bf16[256,512]{1,0:T(8,128)(2,1)} %get-tuple-element.84.refs_1_, bf16[256,512]{1,0:T(8,128)(2,1)} %bitcast.11, f32[512,128]{1,0:T(8,128)} %get-tuple-element.63.side_any.refs_3_, bf16[512,4096]{1,0:T(8,128)(2,1)} %get-tuple-element.86.refs_4_, ...), custom_call_target="tpu_custom_call" | custom-call | flops 2147483648 | bytes 16777216 | tf_op jit(solution)/shard_map/slope_part/pallas_call | solution.py:628
  67.7 0.0 collective-permute-done.5.refs_5_
  67.7 0.0 copy-start.3
  67.7 0.7 copy-done.3
  68.4 0.0 collective-permute-done.3.refs_1_
  68.4 0.3 collective-permute-done.4.refs_3_
  68.7 0.0 copy-start.4
  68.7 0.9 copy-done.4
  69.6 0.9 fold_halves.3
  70.5 2.4 %collective-permute-start.8 = (bf16[4,128,128]{2,1,0:T(8,128)(2,1)}, bf16[4,128,128]{2,1,0:T(8,128)(2,1)S(1)}, u32[]{:S(2)}, u32[]{:S(2)}) collective-permute-start(bf16[4,128,128]{2,1,0:T(8,128)(2,1)} %get-tuple-element.101), channel_id=1, source_target_pairs={{0,16},{2,18},{4,20},{6,22},{8,24},{10,26},{12,28},{14,30},{16,0},... | collective-permute-start | bytes 393224 | tf_op jit(solution)/shard_map/ppermute | solution.py:704
  72.8 1.5 %collective-permute-start.6 = (bf16[4,192,128]{2,1,0:T(8,128)(2,1)}, bf16[4,192,128]{2,1,0:T(8,128)(2,1)S(1)}, u32[]{:S(2)}, u32[]{:S(2)}) collective-permute-start(bf16[4,192,128]{2,1,0:T(8,128)(2,1)} %get-tuple-element.99), channel_id=1, source_target_pairs={{0,4},{2,6},{4,0},{6,2},{8,12},{10,14},{12,8},{14,10},{16,20},{18,... | collective-permute-start | bytes 589832 | tf_op jit(solution)/shard_map/ppermute | solution.py:704
  74.3 0.6 collective-permute-start.7
  74.9 7.7 %embed_part.1 = bf16[512,1024]{1,0:T(8,128)(2,1)} custom-call(bf16[512,4096]{1,0:T(8,128)(2,1)} %slope_part.1.grad_any, bf16[1024,4096]{1,0:T(8,128)(2,1)} %win_any.5), custom_call_target="tpu_custom_call" | custom-call | flops 4294967296 | bytes 13631488 | tf_op jit(solution)/shard_map/embed_part/pallas_call | solution.py:667
  82.6 0.0 collective-permute-done.8.refs_5_
  82.7 0.0 collective-permute-done.6.refs_1_
  82.7 0.0 collective-permute-done.7.refs_3_
  82.7 0.1 fold_halves.4
  82.8 1.6 %collective-permute-start.9 = (bf16[2,384,128]{2,1,0:T(8,128)(2,1)S(1)}, bf16[2,384,128]{2,1,0:T(8,128)(2,1)S(1)}, u32[]{:S(2)}, u32[]{:S(2)}) collective-permute-start(bf16[2,384,128]{2,1,0:T(8,128)(2,1)S(1)} %get-tuple-element.111), channel_id=1, source_target_pairs={{0,8},{2,10},{4,12},{6,14},{8,0},{10,2},{12,4},{14,6},{16,24},{18,... | collective-permute-start | bytes 589832 | tf_op jit(solution)/shard_map/ppermute | solution.py:704
  84.4 1.5 %collective-permute-start.10 = (bf16[2,128,128]{2,1,0:T(8,128)(2,1)S(1)}, bf16[2,128,128]{2,1,0:T(8,128)(2,1)S(1)}, u32[]{:S(2)}, u32[]{:S(2)}) collective-permute-start(bf16[2,128,128]{2,1,0:T(8,128)(2,1)S(1)} %get-tuple-element.112), channel_id=1, source_target_pairs={{0,2},{2,0},{4,6},{6,4},{8,10},{10,8},{12,14},{14,12},{16,18},{18,... | collective-permute-start | bytes 196616 | tf_op jit(solution)/shard_map/ppermute | solution.py:704
  85.8 2.8 %collective-permute-done.10.refs_3_ = bf16[2,128,128]{2,1,0:T(8,128)(2,1)S(1)} collective-permute-done((bf16[2,128,128]{2,1,0:T(8,128)(2,1)S(1)}, bf16[2,128,128]{2,1,0:T(8,128)(2,1)S(1)}, u32[]{:S(2)}, u32[]{:S(2)}) %collective-permute-start.10) | collective-permute-done | bytes 65568 | tf_op jit(solution)/shard_map/ppermute | solution.py:704
  88.6 0.0 collective-permute-done.9.refs_1_
  88.7 0.5 collective-permute-start.11
  89.2 0.6 collective-permute-start.12
  89.8 3.4 %collective-permute-done.12.refs_3_ = bf16[1,128,128]{2,1,0:T(8,128)(2,1)S(1)} collective-permute-done((bf16[1,128,128]{2,1,0:T(8,128)(2,1)S(1)}, bf16[1,128,128]{2,1,0:T(8,128)(2,1)S(1)}, u32[]{:S(2)}, u32[]{:S(2)}) %collective-permute-start.12) | collective-permute-done | bytes 32800 | tf_op jit(solution)/shard_map/ppermute | solution.py:704
  93.2 1.1 %collective-permute-done.11.refs_1_ = bf16[1,384,128]{2,1,0:T(8,128)(2,1)S(1)} collective-permute-done((bf16[1,384,128]{2,1,0:T(8,128)(2,1)S(1)}, bf16[1,384,128]{2,1,0:T(8,128)(2,1)S(1)}, u32[]{:S(2)}, u32[]{:S(2)}) %collective-permute-start.11) | collective-permute-done | bytes 98336 | tf_op jit(solution)/shard_map/ppermute | solution.py:704
  94.3 0.8 finish.1
  (8 shorter events, 0.1 us)
Async XLA Ops:
  3.6 27.5 %all-to-all-start = ((bf16[32,8,1152]{2,1,0:T(8,128)(2,1)}), bf16[32,8,1152]{2,1,0:T(8,128)(2,1)}, u32[]{:S(2)}, u32[]{:S(2)}) async-start(bf16[32,8,1152]{2,1,0:T(8,128)(2,1)} %bitcast.12), calls=%async_computation | async-start | bytes 1179648 | tf_op jit(solution)/shard_map/all_to_all | solution.py:736
  30.9 15.8 %collective-permute-start.1 = (bf16[512,2048]{1,0:T(8,128)(2,1)}, bf16[512,2048]{1,0:T(8,128)(2,1)}, u32[]{:S(2)}, u32[]{:S(2)}) collective-permute-start(bf16[512,2048]{1,0:T(8,128)(2,1)} %get-tuple-element.70), channel_id=1, source_target_pairs={{0,1},{1,0},{2,3},{3,2},{4,5},{5,4},{6,7},{7,6},{8,9},{9,8},{10,11... | collective-permute-start | bytes 6291464 | tf_op jit(solution)/shard_map/ppermute | solution.py:752
  40.3 6.4 %collective-permute-start.2 = (bf16[256,2048]{1,0:T(8,128)(2,1)}, bf16[256,2048]{1,0:T(8,128)(2,1)S(1)}, u32[]{:S(2)}, u32[]{:S(2)}) collective-permute-start(bf16[256,2048]{1,0:T(8,128)(2,1)} %get-tuple-element.71), channel_id=1, source_target_pairs={{0,1},{1,0},{2,3},{3,2},{4,5},{5,4},{6,7},{7,6},{8,9},{9,8},{10,11... | collective-permute-start | bytes 3145736 | tf_op jit(solution)/shard_map/ppermute | solution.py:757
  40.7 5.9 %collective-permute-start = (bf16[512,768]{1,0:T(8,128)(2,1)}, bf16[512,768]{1,0:T(8,128)(2,1)S(1)}, u32[]{:S(2)}, u32[]{:S(2)}) collective-permute-start(bf16[512,768]{1,0:T(8,128)(2,1)} %get-tuple-element.67.refs_0_), channel_id=1, source_target_pairs={{0,1},{1,0},{2,3},{3,2},{4,5},{5,4},{6,7},{7,6},{8,9},{9,8},{10,11... | collective-permute-start | bytes 2359304 | tf_op jit(solution)/shard_map/ppermute | solution.py:756
  40.9 19.6 %all-to-all-start.1 = ((bf16[32,8,512]{2,1,0:T(8,128)(2,1)}), bf16[32,8,512]{2,1,0:T(8,128)(2,1)S(1)}, u32[]{:S(2)}, u32[]{:S(2)}) async-start(bf16[32,8,512]{2,1,0:T(8,128)(2,1)} %bitcast.13), calls=%async_computation.1 | async-start | bytes 524288 | tf_op jit(solution)/shard_map/all_to_all | solution.py:758
  46.7 0.9 copy-start.7
  46.7 1.2 %copy-start.6 = (bf16[256,2048]{1,0:T(8,128)(2,1)}, bf16[256,2048]{1,0:T(8,128)(2,1)S(1)}, u32[]{:S(2)}) copy-start(bf16[256,2048]{1,0:T(8,128)(2,1)S(1)} %collective-permute-done.2.refs_5_) | copy-start | bytes 3145732
  55.7 12.7 %collective-permute-start.3 = (bf16[8,192,128]{2,1,0:T(8,128)(2,1)}, bf16[8,192,128]{2,1,0:T(8,128)(2,1)S(1)}, u32[]{:S(2)}, u32[]{:S(2)}) collective-permute-start(bf16[8,192,128]{2,1,0:T(8,128)(2,1)} %get-tuple-element.80), channel_id=1, source_target_pairs={{0,2},{2,0},{4,6},{6,4},{8,10},{10,8},{12,14},{14,12},{16,18},{18,... | collective-permute-start | bytes 1179656 | tf_op jit(solution)/shard_map/ppermute | solution.py:704
  57.6 11.1 %collective-permute-start.4 = (bf16[8,192,128]{2,1,0:T(8,128)(2,1)}, bf16[8,192,128]{2,1,0:T(8,128)(2,1)S(1)}, u32[]{:S(2)}, u32[]{:S(2)}) collective-permute-start(bf16[8,192,128]{2,1,0:T(8,128)(2,1)} %get-tuple-element.81), channel_id=1, source_target_pairs={{0,4},{2,6},{4,0},{6,2},{8,12},{10,14},{12,8},{14,10},{16,20},{18,... | collective-permute-start | bytes 1179656 | tf_op jit(solution)/shard_map/ppermute | solution.py:704
  59.0 8.7 %collective-permute-start.5 = (bf16[8,128,128]{2,1,0:T(8,128)(2,1)}, bf16[8,128,128]{2,1,0:T(8,128)(2,1)S(1)}, u32[]{:S(2)}, u32[]{:S(2)}) collective-permute-start(bf16[8,128,128]{2,1,0:T(8,128)(2,1)} %get-tuple-element.82), channel_id=1, source_target_pairs={{0,8},{2,10},{4,12},{6,14},{8,0},{10,2},{12,4},{14,6},{16,24},{18,... | collective-permute-start | bytes 786440 | tf_op jit(solution)/shard_map/ppermute | solution.py:704
  60.5 0.7 copy-start.5
  61.2 7.5 %copy-start = (f32[8,192,128]{2,1,0:T(8,128)S(1)}, f32[8,192,128]{2,1,0:T(8,128)}, u32[]{:S(2)}) copy-start(f32[8,192,128]{2,1,0:T(8,128)} %get-tuple-element.79.refs_0_) | copy-start | bytes 2359300
  61.2 7.5 %copy-start.1 = (f32[8,192,128]{2,1,0:T(8,128)S(1)}, f32[8,192,128]{2,1,0:T(8,128)}, u32[]{:S(2)}) copy-start(f32[8,192,128]{2,1,0:T(8,128)} %get-tuple-element.88.refs_2_) | copy-start | bytes 2359300
  61.2 7.5 %copy-start.2 = (f32[8,128,128]{2,1,0:T(8,128)S(1)}, f32[8,128,128]{2,1,0:T(8,128)}, u32[]{:S(2)}) copy-start(f32[8,128,128]{2,1,0:T(8,128)} %get-tuple-element.90.refs_4_) | copy-start | bytes 1572868
  67.7 0.7 copy-start.3
  68.7 1.0 %copy-start.4 = (bf16[8,128,128]{2,1,0:T(8,128)(2,1)S(1)}, bf16[8,128,128]{2,1,0:T(8,128)(2,1)}, u32[]{:S(2)}) copy-start(bf16[8,128,128]{2,1,0:T(8,128)(2,1)} %copy-done.3) | copy-start | bytes 786436
  70.5 12.2 %collective-permute-start.8 = (bf16[4,128,128]{2,1,0:T(8,128)(2,1)}, bf16[4,128,128]{2,1,0:T(8,128)(2,1)S(1)}, u32[]{:S(2)}, u32[]{:S(2)}) collective-permute-start(bf16[4,128,128]{2,1,0:T(8,128)(2,1)} %get-tuple-element.101), channel_id=1, source_target_pairs={{0,16},{2,18},{4,20},{6,22},{8,24},{10,26},{12,28},{14,30},{16,0},... | collective-permute-start | bytes 393224 | tf_op jit(solution)/shard_map/ppermute | solution.py:704
  72.8 9.8 %collective-permute-start.6 = (bf16[4,192,128]{2,1,0:T(8,128)(2,1)}, bf16[4,192,128]{2,1,0:T(8,128)(2,1)S(1)}, u32[]{:S(2)}, u32[]{:S(2)}) collective-permute-start(bf16[4,192,128]{2,1,0:T(8,128)(2,1)} %get-tuple-element.99), channel_id=1, source_target_pairs={{0,4},{2,6},{4,0},{6,2},{8,12},{10,14},{12,8},{14,10},{16,20},{18,... | collective-permute-start | bytes 589832 | tf_op jit(solution)/shard_map/ppermute | solution.py:704
  74.3 8.3 %collective-permute-start.7 = (bf16[4,192,128]{2,1,0:T(8,128)(2,1)S(1)}, bf16[4,192,128]{2,1,0:T(8,128)(2,1)S(1)}, u32[]{:S(2)}, u32[]{:S(2)}) collective-permute-start(bf16[4,192,128]{2,1,0:T(8,128)(2,1)S(1)} %get-tuple-element.100), channel_id=1, source_target_pairs={{0,2},{2,0},{4,6},{6,4},{8,10},{10,8},{12,14},{14,12},{16,18},{18,... | collective-permute-start | bytes 589832 | tf_op jit(solution)/shard_map/ppermute | solution.py:704
  82.8 5.9 %collective-permute-start.9 = (bf16[2,384,128]{2,1,0:T(8,128)(2,1)S(1)}, bf16[2,384,128]{2,1,0:T(8,128)(2,1)S(1)}, u32[]{:S(2)}, u32[]{:S(2)}) collective-permute-start(bf16[2,384,128]{2,1,0:T(8,128)(2,1)S(1)} %get-tuple-element.111), channel_id=1, source_target_pairs={{0,8},{2,10},{4,12},{6,14},{8,0},{10,2},{12,4},{14,6},{16,24},{18,... | collective-permute-start | bytes 589832 | tf_op jit(solution)/shard_map/ppermute | solution.py:704
  84.4 4.3 %collective-permute-start.10 = (bf16[2,128,128]{2,1,0:T(8,128)(2,1)S(1)}, bf16[2,128,128]{2,1,0:T(8,128)(2,1)S(1)}, u32[]{:S(2)}, u32[]{:S(2)}) collective-permute-start(bf16[2,128,128]{2,1,0:T(8,128)(2,1)S(1)} %get-tuple-element.112), channel_id=1, source_target_pairs={{0,2},{2,0},{4,6},{6,4},{8,10},{10,8},{12,14},{14,12},{16,18},{18,... | collective-permute-start | bytes 196616 | tf_op jit(solution)/shard_map/ppermute | solution.py:704
  88.7 5.6 %collective-permute-start.11 = (bf16[1,384,128]{2,1,0:T(8,128)(2,1)S(1)}, bf16[1,384,128]{2,1,0:T(8,128)(2,1)S(1)}, u32[]{:S(2)}, u32[]{:S(2)}) collective-permute-start(bf16[1,384,128]{2,1,0:T(8,128)(2,1)S(1)} %get-tuple-element.117), channel_id=1, source_target_pairs={{0,16},{2,18},{4,20},{6,22},{8,24},{10,26},{12,28},{14,30},{16,0},... | collective-permute-start | bytes 294920 | tf_op jit(solution)/shard_map/ppermute | solution.py:704
  89.2 3.9 %collective-permute-start.12 = (bf16[1,128,128]{2,1,0:T(8,128)(2,1)S(1)}, bf16[1,128,128]{2,1,0:T(8,128)(2,1)S(1)}, u32[]{:S(2)}, u32[]{:S(2)}) collective-permute-start(bf16[1,128,128]{2,1,0:T(8,128)(2,1)S(1)} %get-tuple-element.118), channel_id=1, source_target_pairs={{0,4},{2,6},{4,0},{6,2},{8,12},{10,14},{12,8},{14,10},{16,20},{18,... | collective-permute-start | bytes 98312 | tf_op jit(solution)/shard_map/ppermute | solution.py:704

commit v5 on v4

--- a/solution.py
+++ b/solution.py
@@ -144,21 +144,24 @@
         other_ref[:, place] = jnp.where(rep == 0, high, low)
 
 
-def hidden_chunks(x, win_ref, wout_ref, waiting, arrive, take):
+def hidden_chunks(x, win_ref, wout_ref, waiting, arrive, take, piece=256):
     chunk = waiting[0].shape[1]
     count = win_ref.shape[1] // chunk
     projected = None
     for step in range(count + 1):
         arrive(step)
-        if step < count:
-            waiting[step % 2][...] = dot(x, win_ref[:, step * chunk : (step + 1) * chunk])
-        if step > 0:
-            start = (step - 1) * chunk
-            value, slope = gelu_pair(waiting[(step - 1) % 2][...])
-            hidden = value.astype(jnp.bfloat16)
-            take(start, hidden, slope)
-            part = dot(hidden, wout_ref[start : start + chunk])
-            projected = part if projected is None else projected + part
+        for low in range(0, chunk, piece):
+            place = slice(low, low + piece)
+            if step < count:
+                ahead = step * chunk + low
+                waiting[step % 2][:, place] = dot(x, win_ref[:, ahead : ahead + piece])
+            if step > 0:
+                start = (step - 1) * chunk + low
+                value, slope = gelu_pair(waiting[(step - 1) % 2][:, place])
+                hidden = value.astype(jnp.bfloat16)
+                take(start, hidden, slope)
+                part = dot(hidden, wout_ref[start : start + piece])
+                projected = part if projected is None else projected + part
     return projected
 
 
@@ -427,7 +430,7 @@
         copies.wait(("other", step))
 
 
-def received_part(rep, arrived, weight_in, weight_out, side, grad, weight, back, chunk=1024):
+def received_part(rep, arrived, weight_in, weight_out, side, grad, weight, back, chunk=512):
     rows = arrived.shape[0]
     hidden = weight_in.shape[1]
     nodes, width = grad.shape
@@ -457,8 +460,7 @@
     )(rep, *arrays)
 
 
-def chip_total(chunk, arrays, turned_ref, hidden_ref, semaphores, total_ref):
-    copies = Copies(semaphores)
+def chip_total(chunk, copies, arrays, turned_ref, hidden_ref, total_ref, arrive):
     steps = range(0, hidden_ref.shape[1], chunk)
     base = 0
     for index in range(2):
@@ -477,25 +479,50 @@
     for start in steps:
         for index in range(2, 6):
             copies.wait((index, start))
+        arrive(start // LANES)
         total = dot(turned_ref[...], hidden_ref[:, start : start + chunk])
         for step in range(chunk // LANES):
             total_ref[start // LANES + step] = total[:, step * LANES : (step + 1) * LANES]
 
 
 def total_kernel(chunk, *refs):
-    chip_total(chunk, refs[:6], *refs[7:10], refs[6])
+    turned_ref, hidden_ref, semaphores = refs[7:]
+    chip_total(chunk, Copies(semaphores), refs[:6], turned_ref, hidden_ref, refs[6], lambda ready: None)
 
 
 def product_kernel(streams, chunk, place_ref, *refs):
-    outputs = refs[6 : 6 + 2 * len(streams)]
-    turned_ref, hidden_ref, semaphores, total_ref = refs[6 + 2 * len(streams) :]
-    chip_total(chunk, refs[:6], turned_ref, hidden_ref, semaphores, total_ref)
-    for stream, (order, low, high) in enumerate(streams):
-        sent_ref, kept_ref = outputs[2 * stream : 2 * stream + 2]
-        for spot in range(sent_ref.shape[0]):
-            sent, kept = places(spot, order[0], place_ref[0])
-            sent_ref[spot] = total_ref[sent, low:high].astype(jnp.bfloat16)
-            kept_ref[spot] = total_ref[kept, low:high]
+    count = 2 * len(streams)
+    outputs, scratch = refs[6 : 6 + count], refs[6 + count : 6 + 2 * count]
+    turned_ref, hidden_ref, semaphores, total_ref = refs[6 + 2 * count :]
+    copies = Copies(semaphores)
+    done = [0] * len(streams)
+
+    def arrive(ready):
+        given = []
+        for stream, (order, low, high) in enumerate(streams):
+            bit = order[0]
+            first = done[stream]
+            spot = first
+            while spot < scratch[2 * stream].shape[0]:
+                base = ((spot >> bit) << (bit + 1)) | (spot & ((1 << bit) - 1))
+                if base + (1 << bit) >= ready:
+                    break
+                sent, kept = places(spot, bit, place_ref[0])
+                scratch[2 * stream][spot] = total_ref[sent, low:high].astype(jnp.bfloat16)
+                scratch[2 * stream + 1][spot] = total_ref[kept, low:high]
+                spot += 1
+            done[stream] = spot
+            if spot > first:
+                given += [(2 * stream, first, spot), (2 * stream + 1, first, spot)]
+        for index, first, last in given:
+            place = pl.ds(first, last - first)
+            copies.start(("give", index, first), scratch[index].at[place], outputs[index].at[place])
+
+    chip_total(chunk, copies, refs[:6], turned_ref, hidden_ref, total_ref, arrive)
+    arrive(total_ref.shape[0])
+    for name in list(copies.started):
+        if isinstance(name, tuple) and name[0] == "give":
+            copies.wait(name)
 
 
 def places(spot, weight, place, bit=None):
@@ -571,7 +598,7 @@
     scratch = [
         pltpu.VMEM((width, rows), jnp.bfloat16),
         pltpu.VMEM((rows, hidden), jnp.bfloat16),
-        pltpu.SemaphoreType.DMA((2 + 4 * (hidden // chunk),)),
+        pltpu.SemaphoreType.DMA((2 + 10 * (hidden // chunk),)),
     ]
     if not streams:
         return pl.pallas_call(
@@ -589,9 +616,12 @@
     return pl.pallas_call(
         functools.partial(product_kernel, streams, chunk),
         in_specs=[SMEM] + [HBM] * 6,
+        out_specs=(HBM,) * len(shapes),
         out_shape=tuple(shapes),
-        scratch_shapes=scratch + [pltpu.VMEM(total, jnp.float32)],
-        compiler_params=params(60),
+        scratch_shapes=[pltpu.VMEM(shape.shape, shape.dtype) for shape in shapes]
+        + scratch
+        + [pltpu.VMEM(total, jnp.float32)],
+        compiler_params=params(),
         name="product",
     )(place, *operands)
 
@@ -636,7 +666,7 @@
             pltpu.SemaphoreType.DMA((4 + 3 * (slope.shape[1] // chunk),)),
         ],
         cost_estimate=pl.CostEstimate(flops=2 * slope.size * full.shape[1], bytes_accessed=16 * MIB, transcendentals=0),
-        compiler_params=params(60),
+        compiler_params=params(58),
         name="slope_part",
     )(*arrays)
 
@@ -689,7 +719,7 @@
 
 
 def streams_of(dom_count, width):
-    cut = width * 3 // 8
+    cut = width * 11 // 32
     edges = (0, cut, 2 * cut, width)
     return tuple(zip(bit_orders(dom_count), edges[:-1], edges[1:]))
 

time: 95.4 us -> 89.6 us (0.939)
  Pallas kernels: 55.9 us -> 51.7 us
  local copies, waits for them, and re-layouts: 3.55 us -> 0.01 us
  waiting for transfers between devices: 7.56 us -> 9.36 us
    unnamed x16 -> x6, local copies, waits for them, and re-layouts: 3.55 us -> 0.01 us
    pallas_call x1, Pallas kernels: 19.8 us -> 17.5 us  [forward(): pl.pallas_call(forward_kernel, in_specs=[SMEM] * 2 + [HBM] * 8, out_specs...]
    ppermute x10, waiting for transfers between devices: 7.54 us -> 9.35 us  [exchange(): lax.ppermute(sent, 'dom', [(device, device ^ 1 << bit) for device in rang...]
  transfers between devices with their start and end apart: 15 -> 15, of which waited for: 4 -> 4; matrix products, arithmetic and copies ran while one was open for 0% -> 0% of each run, Pallas kernels for 54% -> 53%
where the time goes in v5:
time: 89.6 us; the launch traced here: 89.3 us
  Pallas kernels  51.7 us (58%)
  starting transfers between devices  27.4 us (31%)
  waiting for transfers between devices  9.36 us (10%)
    pallas_call x1, Pallas kernels, forward(): pl.pallas_call(forward_kernel, in_specs=[SMEM] * 2 + [HBM] * 8, out_specs...  17.5 us
    ppermute x10, starting transfers between devices, exchange(): lax.ppermute(sent, 'dom', [(device, device ^ 1 << bit) for device in rang...  13.3 us
    ppermute x10, waiting for transfers between devices, exchange(): lax.ppermute(sent, 'dom', [(device, device ^ 1 << bit) for device in rang...  9.35 us
    pallas_call x1, Pallas kernels, received_part(): pl.pallas_call(received_kernel, in_specs=[SMEM] + [HBM] * 7, out_specs=(H...  8.43 us
    pallas_call x1, Pallas kernels, embed_part(): pl.pallas_call(functools.partial(embed_kernel, chunk), in_specs=[HBM] * 2...  7.74 us
    all_to_all x1, starting transfers between devices, body(): lax.all_to_all(outgoing.reshape(peers, slots, -1), both, split_axis=0, co...  7.42 us
    pallas_call x1, Pallas kernels, product(): pl.pallas_call(functools.partial(product_kernel, streams, chunk), in_spec...  7.27 us
    pallas_call x1, Pallas kernels, slope_part(): pl.pallas_call(functools.partial(slope_kernel, chunk), in_specs=[HBM] * 6...  6.43 us
  transfers between devices with their start and end apart: 15, of which 4 were waited for; matrix products, arithmetic and copies ran while one was open for 0% of the time, Pallas kernels for 53%

profile of v5, /device:TPU:0, one launch (start us, length us, event | category | flops | bytes accessed | tf_op | source)
XLA Modules:
  0.0 89.3 jit_solution(7974877020286678212)
XLA Ops:
  0.6 3.0 %prepare.1 = (bf16[256,1152]{1,0:T(8,128)(2,1)}, bf16[256,512]{1,0:T(8,128)(2,1)}, f32[512,128]{1,0:T(8,128)}) custom-call(s32[8,32]{1,0:T(8,128)} %bitcast.13, s32[1,32]{1,0:T(1,128)} %count_any.1, bf16[4,8,128,128]{3,2,1,0:T(8,128)(2,1)} %tiles_any.3, bf16[512,1024]{1,0:T(8,128)(2,1)} %x_any.1), custom_call_target="tpu_custom_call" | custom-call | tf_op jit(solution)/shard_map/prepare/pallas_call | solution.py:118
  3.7 7.4 %all-to-all-start = ((bf16[32,8,1152]{2,1,0:T(8,128)(2,1)}), bf16[32,8,1152]{2,1,0:T(8,128)(2,1)}, u32[]{:S(2)}, u32[]{:S(2)}) async-start(bf16[32,8,1152]{2,1,0:T(8,128)(2,1)} %bitcast.11), calls=%async_computation | async-start | bytes 1179648 | tf_op jit(solution)/shard_map/all_to_all | solution.py:766
  11.1 17.5 %forward.1 = (bf16[512,4096]{1,0:T(8,128)(2,1)}, bf16[512,2048]{1,0:T(8,128)(2,1)}, bf16[512,2048]{1,0:T(8,128)(2,1)}, f32[512,512]{1,0:T(8,128)}, bf16[2,512,256]{2,1,0:T(8,128)(2,1)}, /*index=5*/f32[256,640]{1,0:T(8,128)}) custom-call(s32[1]{0:T(128)} %bitcast.1.rep_ref, s32[4,8]{1,0:T(4,128)} %column_ref.1, bf16[512,1024]{1,0:T(8,128)(2,1)} %x_any.1, ...), custom_call_target="tpu_custom_call" | custom-call | tf_op jit(solution)/shard_map/forward/pallas_call | solution.py:328
  28.6 0.2 collective-permute-start.1
  28.9 0.0 all-to-all-done
  28.9 8.4 %received_part.1 = (bf16[256,2048]{1,0:T(8,128)(2,1)}, bf16[256,2048]{1,0:T(8,128)(2,1)}, f32[512,512]{1,0:T(8,128)}, bf16[512,768]{1,0:T(8,128)(2,1)}, bf16[256,512]{1,0:T(8,128)(2,1)}) custom-call(s32[1]{0:T(128)} %bitcast.1.rep_ref, bf16[256,1152]{1,0:T(8,128)(2,1)} %bitcast.5.x_any, bf16[1024,4096]{1,0:T(8,128)(2,1)} %win_any.5, ...), custom_call_target="tpu_custom_call" | custom-call | tf_op jit(solution)/shard_map/received_part/pallas_call | solution.py:439
  37.3 0.4 collective-permute-start.2
  37.7 0.2 collective-permute-start
  37.9 5.9 %all-to-all-start.1 = ((bf16[32,8,512]{2,1,0:T(8,128)(2,1)}), bf16[32,8,512]{2,1,0:T(8,128)(2,1)}, u32[]{:S(2)}, u32[]{:S(2)}) async-start(bf16[32,8,512]{2,1,0:T(8,128)(2,1)} %bitcast.12), calls=%async_computation.1 | async-start | bytes 524288 | tf_op jit(solution)/shard_map/all_to_all | solution.py:788
  43.8 0.0 collective-permute-done.refs_1_
  43.8 0.0 collective-permute-done.1.refs_4_
  43.8 0.0 collective-permute-done.2.refs_5_
  43.8 7.3 %product.1 = (bf16[8,176,128]{2,1,0:T(8,128)(2,1)}, f32[8,176,128]{2,1,0:T(8,128)}, bf16[8,176,128]{2,1,0:T(8,128)(2,1)}, f32[8,176,128]{2,1,0:T(8,128)}, bf16[8...) custom-call(s32[1]{0:T(128)} %bitcast.place_ref, bf16[512,768]{1,0:T(8,128)(2,1)} %get-tuple-element.67.refs_0_, ...), custom_call_target="tpu_custom_call" | custom-call | tf_op jit(solution)/shard_map/product/pallas_call | solution.py:616
  51.1 1.8 %collective-permute-start.3 = (bf16[8,176,128]{2,1,0:T(8,128)(2,1)}, bf16[8,176,128]{2,1,0:T(8,128)(2,1)S(1)}, u32[]{:S(2)}, u32[]{:S(2)}) collective-permute-start(bf16[8,176,128]{2,1,0:T(8,128)(2,1)} %get-tuple-element.80), channel_id=1, source_target_pairs={{0,2},{2,0},{4,6},{6,4},{8,10},{10,8},{12,14},{14,12},{16,18},{18,... | collective-permute-start | bytes 1081352 | tf_op jit(solution)/shard_map/ppermute | solution.py:734
  52.8 1.5 %collective-permute-start.4 = (bf16[8,176,128]{2,1,0:T(8,128)(2,1)}, bf16[8,176,128]{2,1,0:T(8,128)(2,1)S(1)}, u32[]{:S(2)}, u32[]{:S(2)}) collective-permute-start(bf16[8,176,128]{2,1,0:T(8,128)(2,1)} %get-tuple-element.81), channel_id=1, source_target_pairs={{0,4},{2,6},{4,0},{6,2},{8,12},{10,14},{12,8},{14,10},{16,20},{18,... | collective-permute-start | bytes 1081352 | tf_op jit(solution)/shard_map/ppermute | solution.py:734
  54.3 1.5 %collective-permute-start.5 = (bf16[8,160,128]{2,1,0:T(8,128)(2,1)}, bf16[8,160,128]{2,1,0:T(8,128)(2,1)S(1)}, u32[]{:S(2)}, u32[]{:S(2)}) collective-permute-start(bf16[8,160,128]{2,1,0:T(8,128)(2,1)} %get-tuple-element.82), channel_id=1, source_target_pairs={{0,8},{2,10},{4,12},{6,14},{8,0},{10,2},{12,4},{14,6},{16,24},{18,... | collective-permute-start | bytes 983048 | tf_op jit(solution)/shard_map/ppermute | solution.py:734
  55.8 0.0 all-to-all-done.1
  55.8 0.0 copy-start
  55.8 0.0 copy-start.1
  55.8 0.0 copy-start.2
  55.8 6.4 %slope_part.1.grad_any = bf16[512,4096]{1,0:T(8,128)(2,1)} custom-call(f32[512,512]{1,0:T(8,128)} %get-tuple-element.83.refs_0_, bf16[256,512]{1,0:T(8,128)(2,1)} %get-tuple-element.84.refs_1_, bf16[256,512]{1,0:T(8,128)(2,1)} %bitcast.9.refs_2_, f32[512,128]{1,0:T(8,128)} %get-tuple-element.63.side_any.refs_3_, ...), custom_call_target="tpu_custom_call" | custom-call | flops 2147483648 | bytes 16777216 | tf_op jit(solution)/shard_map/slope_part/pallas_call | solution.py:658
  62.2 1.5 %collective-permute-done.5.refs_5_ = bf16[8,160,128]{2,1,0:T(8,128)(2,1)S(1)} collective-permute-done((bf16[8,160,128]{2,1,0:T(8,128)(2,1)}, bf16[8,160,128]{2,1,0:T(8,128)(2,1)S(1)}, u32[]{:S(2)}, u32[]{:S(2)}) %collective-permute-start.5) | collective-permute-done | bytes 327712 | tf_op jit(solution)/shard_map/ppermute | solution.py:734
  63.7 0.0 collective-permute-done.3.refs_1_
  63.7 0.0 collective-permute-done.4.refs_3_
  63.7 0.0 copy-done
  63.7 0.0 copy-done.1
  63.7 0.0 copy-done.2
  63.7 0.2 fold_halves.3
  63.9 2.5 %collective-permute-start.8 = (bf16[4,160,128]{2,1,0:T(8,128)(2,1)S(1)}, bf16[4,160,128]{2,1,0:T(8,128)(2,1)S(1)}, u32[]{:S(2)}, u32[]{:S(2)}) collective-permute-start(bf16[4,160,128]{2,1,0:T(8,128)(2,1)S(1)} %get-tuple-element.101), channel_id=1, source_target_pairs={{0,16},{2,18},{4,20},{6,22},{8,24},{10,26},{12,28},{14,30},{16,0},... | collective-permute-start | bytes 491528 | tf_op jit(solution)/shard_map/ppermute | solution.py:734
  66.4 1.0 %collective-permute-start.6 = (bf16[4,176,128]{2,1,0:T(8,128)(2,1)S(1)}, bf16[4,176,128]{2,1,0:T(8,128)(2,1)S(1)}, u32[]{:S(2)}, u32[]{:S(2)}) collective-permute-start(bf16[4,176,128]{2,1,0:T(8,128)(2,1)S(1)} %get-tuple-element.99), channel_id=1, source_target_pairs={{0,4},{2,6},{4,0},{6,2},{8,12},{10,14},{12,8},{14,10},{16,20},{18,... | collective-permute-start | bytes 540680 | tf_op jit(solution)/shard_map/ppermute | solution.py:734
  67.4 0.6 collective-permute-start.7
  67.9 7.7 %embed_part.1 = bf16[512,1024]{1,0:T(8,128)(2,1)} custom-call(bf16[512,4096]{1,0:T(8,128)(2,1)} %slope_part.1.grad_any, bf16[1024,4096]{1,0:T(8,128)(2,1)} %win_any.5), custom_call_target="tpu_custom_call" | custom-call | flops 4294967296 | bytes 13631488 | tf_op jit(solution)/shard_map/embed_part/pallas_call | solution.py:697
  75.7 0.0 collective-permute-done.8.refs_5_
  75.7 0.0 collective-permute-done.6.refs_1_
  75.7 0.0 collective-permute-done.7.refs_3_
  75.7 0.1 fold_halves.4
  75.8 1.6 %collective-permute-start.9 = (bf16[2,352,128]{2,1,0:T(8,128)(2,1)S(1)}, bf16[2,352,128]{2,1,0:T(8,128)(2,1)S(1)}, u32[]{:S(2)}, u32[]{:S(2)}) collective-permute-start(bf16[2,352,128]{2,1,0:T(8,128)(2,1)S(1)} %get-tuple-element.111), channel_id=1, source_target_pairs={{0,8},{2,10},{4,12},{6,14},{8,0},{10,2},{12,4},{14,6},{16,24},{18,... | collective-permute-start | bytes 540680 | tf_op jit(solution)/shard_map/ppermute | solution.py:734
  77.4 1.5 %collective-permute-start.10 = (bf16[2,160,128]{2,1,0:T(8,128)(2,1)S(1)}, bf16[2,160,128]{2,1,0:T(8,128)(2,1)S(1)}, u32[]{:S(2)}, u32[]{:S(2)}) collective-permute-start(bf16[2,160,128]{2,1,0:T(8,128)(2,1)S(1)} %get-tuple-element.112), channel_id=1, source_target_pairs={{0,2},{2,0},{4,6},{6,4},{8,10},{10,8},{12,14},{14,12},{16,18},{18,... | collective-permute-start | bytes 245768 | tf_op jit(solution)/shard_map/ppermute | solution.py:734
  78.9 3.0 %collective-permute-done.10.refs_3_ = bf16[2,160,128]{2,1,0:T(8,128)(2,1)S(1)} collective-permute-done((bf16[2,160,128]{2,1,0:T(8,128)(2,1)S(1)}, bf16[2,160,128]{2,1,0:T(8,128)(2,1)S(1)}, u32[]{:S(2)}, u32[]{:S(2)}) %collective-permute-start.10) | collective-permute-done | bytes 81952 | tf_op jit(solution)/shard_map/ppermute | solution.py:734
  81.9 0.0 collective-permute-done.9.refs_1_
  81.9 0.1 fold_halves.5
  81.9 0.5 collective-permute-start.11
  82.5 1.1 %collective-permute-start.12 = (bf16[1,160,128]{2,1,0:T(8,128)(2,1)S(1)}, bf16[1,160,128]{2,1,0:T(8,128)(2,1)S(1)}, u32[]{:S(2)}, u32[]{:S(2)}) collective-permute-start(bf16[1,160,128]{2,1,0:T(8,128)(2,1)S(1)} %get-tuple-element.118), channel_id=1, source_target_pairs={{0,4},{2,6},{4,0},{6,2},{8,12},{10,14},{12,8},{14,10},{16,20},{18,... | collective-permute-start | bytes 122888 | tf_op jit(solution)/shard_map/ppermute | solution.py:734
  83.5 2.9 %collective-permute-done.12.refs_3_ = bf16[1,160,128]{2,1,0:T(8,128)(2,1)S(1)} collective-permute-done((bf16[1,160,128]{2,1,0:T(8,128)(2,1)S(1)}, bf16[1,160,128]{2,1,0:T(8,128)(2,1)S(1)}, u32[]{:S(2)}, u32[]{:S(2)}) %collective-permute-start.12) | collective-permute-done | bytes 40992 | tf_op jit(solution)/shard_map/ppermute | solution.py:734
  86.5 1.9 %collective-permute-done.11.refs_1_ = bf16[1,352,128]{2,1,0:T(8,128)(2,1)S(1)} collective-permute-done((bf16[1,352,128]{2,1,0:T(8,128)(2,1)S(1)}, bf16[1,352,128]{2,1,0:T(8,128)(2,1)S(1)}, u32[]{:S(2)}, u32[]{:S(2)}) %collective-permute-start.11) | collective-permute-done | bytes 90144 | tf_op jit(solution)/shard_map/ppermute | solution.py:734
  88.4 1.0 %finish.1 = f32[128,512]{1,0:T(8,128)} custom-call(f32[1,352,128]{2,1,0:T(8,128)S(1)} %get-tuple-element.116.refs_0_, bf16[1,352,128]{2,1,0:T(8,128)(2,1)S(1)} %collective-permute-done.11.refs_1_, f32[1,160,128]{2,1,0:T(8,128)S(1)} %get-tuple-element.120.refs_2_, bf16[1,160,128]{2,1,0:T(8,128)(2,1)S(1)} %collective-permute-done.12.refs_3_), custom_call_target="tpu_custom_call" | custom-call | tf_op jit(solution)/shard_map/finish/pallas_call | solution.py:584
Async XLA Ops:
  3.7 25.2 %all-to-all-start = ((bf16[32,8,1152]{2,1,0:T(8,128)(2,1)}), bf16[32,8,1152]{2,1,0:T(8,128)(2,1)}, u32[]{:S(2)}, u32[]{:S(2)}) async-start(bf16[32,8,1152]{2,1,0:T(8,128)(2,1)} %bitcast.11), calls=%async_computation | async-start | bytes 1179648 | tf_op jit(solution)/shard_map/all_to_all | solution.py:766
  28.6 15.1 %collective-permute-start.1 = (bf16[512,2048]{1,0:T(8,128)(2,1)}, bf16[512,2048]{1,0:T(8,128)(2,1)}, u32[]{:S(2)}, u32[]{:S(2)}) collective-permute-start(bf16[512,2048]{1,0:T(8,128)(2,1)} %get-tuple-element.70), channel_id=1, source_target_pairs={{0,1},{1,0},{2,3},{3,2},{4,5},{5,4},{6,7},{7,6},{8,9},{9,8},{10,11... | collective-permute-start | bytes 6291464 | tf_op jit(solution)/shard_map/ppermute | solution.py:782
  37.3 6.5 %collective-permute-start.2 = (bf16[256,2048]{1,0:T(8,128)(2,1)}, bf16[256,2048]{1,0:T(8,128)(2,1)}, u32[]{:S(2)}, u32[]{:S(2)}) collective-permute-start(bf16[256,2048]{1,0:T(8,128)(2,1)} %get-tuple-element.71), channel_id=1, source_target_pairs={{0,1},{1,0},{2,3},{3,2},{4,5},{5,4},{6,7},{7,6},{8,9},{9,8},{10,11... | collective-permute-start | bytes 3145736 | tf_op jit(solution)/shard_map/ppermute | solution.py:787
  37.7 6.1 %collective-permute-start = (bf16[512,768]{1,0:T(8,128)(2,1)}, bf16[512,768]{1,0:T(8,128)(2,1)}, u32[]{:S(2)}, u32[]{:S(2)}) collective-permute-start(bf16[512,768]{1,0:T(8,128)(2,1)} %get-tuple-element.67.refs_0_), channel_id=1, source_target_pairs={{0,1},{1,0},{2,3},{3,2},{4,5},{5,4},{6,7},{7,6},{8,9},{9,8},{10,11... | collective-permute-start | bytes 2359304 | tf_op jit(solution)/shard_map/ppermute | solution.py:786
  37.9 17.9 %all-to-all-start.1 = ((bf16[32,8,512]{2,1,0:T(8,128)(2,1)}), bf16[32,8,512]{2,1,0:T(8,128)(2,1)}, u32[]{:S(2)}, u32[]{:S(2)}) async-start(bf16[32,8,512]{2,1,0:T(8,128)(2,1)} %bitcast.12), calls=%async_computation.1 | async-start | bytes 524288 | tf_op jit(solution)/shard_map/all_to_all | solution.py:788
  51.1 12.6 %collective-permute-start.3 = (bf16[8,176,128]{2,1,0:T(8,128)(2,1)}, bf16[8,176,128]{2,1,0:T(8,128)(2,1)S(1)}, u32[]{:S(2)}, u32[]{:S(2)}) collective-permute-start(bf16[8,176,128]{2,1,0:T(8,128)(2,1)} %get-tuple-element.80), channel_id=1, source_target_pairs={{0,2},{2,0},{4,6},{6,4},{8,10},{10,8},{12,14},{14,12},{16,18},{18,... | collective-permute-start | bytes 1081352 | tf_op jit(solution)/shard_map/ppermute | solution.py:734
  52.8 10.9 %collective-permute-start.4 = (bf16[8,176,128]{2,1,0:T(8,128)(2,1)}, bf16[8,176,128]{2,1,0:T(8,128)(2,1)S(1)}, u32[]{:S(2)}, u32[]{:S(2)}) collective-permute-start(bf16[8,176,128]{2,1,0:T(8,128)(2,1)} %get-tuple-element.81), channel_id=1, source_target_pairs={{0,4},{2,6},{4,0},{6,2},{8,12},{10,14},{12,8},{14,10},{16,20},{18,... | collective-permute-start | bytes 1081352 | tf_op jit(solution)/shard_map/ppermute | solution.py:734
  54.3 9.4 %collective-permute-start.5 = (bf16[8,160,128]{2,1,0:T(8,128)(2,1)}, bf16[8,160,128]{2,1,0:T(8,128)(2,1)S(1)}, u32[]{:S(2)}, u32[]{:S(2)}) collective-permute-start(bf16[8,160,128]{2,1,0:T(8,128)(2,1)} %get-tuple-element.82), channel_id=1, source_target_pairs={{0,8},{2,10},{4,12},{6,14},{8,0},{10,2},{12,4},{14,6},{16,24},{18,... | collective-permute-start | bytes 983048 | tf_op jit(solution)/shard_map/ppermute | solution.py:734
  55.8 8.0 %copy-start = (f32[8,176,128]{2,1,0:T(8,128)S(1)}, f32[8,176,128]{2,1,0:T(8,128)}, u32[]{:S(2)}) copy-start(f32[8,176,128]{2,1,0:T(8,128)} %get-tuple-element.79.refs_0_) | copy-start | bytes 2162692
  55.8 8.0 %copy-start.1 = (f32[8,176,128]{2,1,0:T(8,128)S(1)}, f32[8,176,128]{2,1,0:T(8,128)}, u32[]{:S(2)}) copy-start(f32[8,176,128]{2,1,0:T(8,128)} %get-tuple-element.88.refs_2_) | copy-start | bytes 2162692
  55.8 8.0 %copy-start.2 = (f32[8,160,128]{2,1,0:T(8,128)S(1)}, f32[8,160,128]{2,1,0:T(8,128)}, u32[]{:S(2)}) copy-start(f32[8,160,128]{2,1,0:T(8,128)} %get-tuple-element.90.refs_4_) | copy-start | bytes 1966084
  63.9 11.7 %collective-permute-start.8 = (bf16[4,160,128]{2,1,0:T(8,128)(2,1)S(1)}, bf16[4,160,128]{2,1,0:T(8,128)(2,1)S(1)}, u32[]{:S(2)}, u32[]{:S(2)}) collective-permute-start(bf16[4,160,128]{2,1,0:T(8,128)(2,1)S(1)} %get-tuple-element.101), channel_id=1, source_target_pairs={{0,16},{2,18},{4,20},{6,22},{8,24},{10,26},{12,28},{14,30},{16,0},... | collective-permute-start | bytes 491528 | tf_op jit(solution)/shard_map/ppermute | solution.py:734
  66.4 9.3 %collective-permute-start.6 = (bf16[4,176,128]{2,1,0:T(8,128)(2,1)S(1)}, bf16[4,176,128]{2,1,0:T(8,128)(2,1)S(1)}, u32[]{:S(2)}, u32[]{:S(2)}) collective-permute-start(bf16[4,176,128]{2,1,0:T(8,128)(2,1)S(1)} %get-tuple-element.99), channel_id=1, source_target_pairs={{0,4},{2,6},{4,0},{6,2},{8,12},{10,14},{12,8},{14,10},{16,20},{18,... | collective-permute-start | bytes 540680 | tf_op jit(solution)/shard_map/ppermute | solution.py:734
  67.4 8.3 %collective-permute-start.7 = (bf16[4,176,128]{2,1,0:T(8,128)(2,1)S(1)}, bf16[4,176,128]{2,1,0:T(8,128)(2,1)S(1)}, u32[]{:S(2)}, u32[]{:S(2)}) collective-permute-start(bf16[4,176,128]{2,1,0:T(8,128)(2,1)S(1)} %get-tuple-element.100), channel_id=1, source_target_pairs={{0,2},{2,0},{4,6},{6,4},{8,10},{10,8},{12,14},{14,12},{16,18},{18,... | collective-permute-start | bytes 540680 | tf_op jit(solution)/shard_map/ppermute | solution.py:734
  75.8 6.0 %collective-permute-start.9 = (bf16[2,352,128]{2,1,0:T(8,128)(2,1)S(1)}, bf16[2,352,128]{2,1,0:T(8,128)(2,1)S(1)}, u32[]{:S(2)}, u32[]{:S(2)}) collective-permute-start(bf16[2,352,128]{2,1,0:T(8,128)(2,1)S(1)} %get-tuple-element.111), channel_id=1, source_target_pairs={{0,8},{2,10},{4,12},{6,14},{8,0},{10,2},{12,4},{14,6},{16,24},{18,... | collective-permute-start | bytes 540680 | tf_op jit(solution)/shard_map/ppermute | solution.py:734
  77.4 4.4 %collective-permute-start.10 = (bf16[2,160,128]{2,1,0:T(8,128)(2,1)S(1)}, bf16[2,160,128]{2,1,0:T(8,128)(2,1)S(1)}, u32[]{:S(2)}, u32[]{:S(2)}) collective-permute-start(bf16[2,160,128]{2,1,0:T(8,128)(2,1)S(1)} %get-tuple-element.112), channel_id=1, source_target_pairs={{0,2},{2,0},{4,6},{6,4},{8,10},{10,8},{12,14},{14,12},{16,18},{18,... | collective-permute-start | bytes 245768 | tf_op jit(solution)/shard_map/ppermute | solution.py:734
  81.9 6.5 %collective-permute-start.11 = (bf16[1,352,128]{2,1,0:T(8,128)(2,1)S(1)}, bf16[1,352,128]{2,1,0:T(8,128)(2,1)S(1)}, u32[]{:S(2)}, u32[]{:S(2)}) collective-permute-start(bf16[1,352,128]{2,1,0:T(8,128)(2,1)S(1)} %get-tuple-element.117), channel_id=1, source_target_pairs={{0,16},{2,18},{4,20},{6,22},{8,24},{10,26},{12,28},{14,30},{16,0},... | collective-permute-start | bytes 270344 | tf_op jit(solution)/shard_map/ppermute | solution.py:734
  82.5 4.0 %collective-permute-start.12 = (bf16[1,160,128]{2,1,0:T(8,128)(2,1)S(1)}, bf16[1,160,128]{2,1,0:T(8,128)(2,1)S(1)}, u32[]{:S(2)}, u32[]{:S(2)}) collective-permute-start(bf16[1,160,128]{2,1,0:T(8,128)(2,1)S(1)} %get-tuple-element.118), channel_id=1, source_target_pairs={{0,4},{2,6},{4,0},{6,2},{8,12},{10,14},{12,8},{14,10},{16,20},{18,... | collective-permute-start | bytes 122888 | tf_op jit(solution)/shard_map/ppermute | solution.py:734

commit v6 on v5

--- a/solution.py
+++ b/solution.py
@@ -11,16 +11,18 @@
 gelu_inner = 0.7978845608028654
 gelu_cubic = 0.044715
 LANES = 128
+SLOPED = 2048
 MIB = 1024 * 1024
 both = ("dom", "rep")
 
 
-def gelu_pair(values):
+def gelu_half(values):
     square = values * values
-    half = 0.5 + 0.5 * jnp.tanh(values * (gelu_inner + gelu_inner * gelu_cubic * square))
-    value = values * half
-    slope = half + value * (2.0 - 2.0 * half) * (gelu_inner + 3.0 * gelu_inner * gelu_cubic * square)
-    return value, slope
+    return 0.5 + 0.5 * jnp.tanh(values * (gelu_inner + gelu_inner * gelu_cubic * square)), square
+
+
+def gelu_slope(values, half, square):
+    return half + values * half * (2.0 - 2.0 * half) * (gelu_inner + 3.0 * gelu_inner * gelu_cubic * square)
 
 
 def dot(left, right, left_dim=1, right_dim=0):
@@ -63,20 +65,23 @@
     count_any,
     tiles_any,
     embeds_any,
-    out_ref,
-    pick_ref,
-    side_ref,
+    out_any,
+    pick_any,
+    side_any,
     rows_ref,
     count_ref,
     tiles_ref,
     embeds_ref,
+    out_ref,
+    pick_ref,
+    side_ref,
     semaphores,
 ):
     copies = Copies(semaphores)
     copies.start("rows", rows_any, rows_ref)
     copies.start("count", count_any, count_ref)
+    copies.start("embeds", embeds_any, embeds_ref)
     copies.start("tiles", tiles_any, tiles_ref)
-    copies.start("embeds", embeds_any, embeds_ref)
     copies.wait("rows")
     copies.wait("count")
     slots, peers = rows_ref.shape
@@ -93,7 +98,11 @@
     node = lax.broadcasted_iota(jnp.int32, (sent, nodes), 1)
     pick = jnp.where((node == index) & (slot < count), 1.0, 0.0).astype(jnp.bfloat16)
     pick_ref[...] = pick
+    copies.wait("embeds")
+    copies.start("pick", pick_ref, pick_any)
+    out_ref[:, :width] = dot(pick, embeds_ref[...]).astype(jnp.bfloat16)
     copies.wait("tiles")
+    copies.start("wide", out_ref.at[:, pl.ds(0, width)], out_any.at[:, pl.ds(0, width)])
     size = tiles_ref.shape[2]
     lane = lax.broadcasted_iota(jnp.int32, (size, LANES), 1)
     parts = []
@@ -108,28 +117,33 @@
         part = jnp.where(lane == 0, high, jnp.where(lane == 1, middle, jnp.where(lane == 2, low, 0.0)))
         parts.append(part.astype(jnp.bfloat16))
     out_ref[:, width:] = dot(pick, jnp.concatenate(parts, axis=0)).astype(jnp.bfloat16)
-    copies.wait("embeds")
-    out_ref[:, :width] = dot(pick, embeds_ref[...]).astype(jnp.bfloat16)
+    copies.start("side", side_ref, side_any)
+    copies.start("narrow", out_ref.at[:, pl.ds(width, LANES)], out_any.at[:, pl.ds(width, LANES)])
+    for name in ("pick", "wide", "side", "narrow"):
+        copies.wait(name)
 
 
 def prepare(rows, count, tile_weight, embeds):
     sent = rows.shape[0] * rows.shape[1]
     nodes, width = embeds.shape
+    shapes = (
+        jax.ShapeDtypeStruct((sent, width + LANES), jnp.bfloat16),
+        jax.ShapeDtypeStruct((sent, nodes), jnp.bfloat16),
+        jax.ShapeDtypeStruct((nodes, LANES), jnp.float32),
+    )
     return pl.pallas_call(
         prepare_kernel,
         in_specs=[HBM] * 4,
-        out_shape=(
-            jax.ShapeDtypeStruct((sent, width + LANES), jnp.bfloat16),
-            jax.ShapeDtypeStruct((sent, nodes), jnp.bfloat16),
-            jax.ShapeDtypeStruct((nodes, LANES), jnp.float32),
-        ),
+        out_specs=(HBM,) * 3,
+        out_shape=shapes,
         scratch_shapes=[
             pltpu.VMEM(rows.shape, jnp.int32),
             pltpu.VMEM(count.shape, jnp.int32),
             pltpu.VMEM(tile_weight.shape, jnp.bfloat16),
             pltpu.VMEM(embeds.shape, jnp.bfloat16),
-            pltpu.SemaphoreType.DMA((4,)),
-        ],
+        ]
+        + [pltpu.VMEM(shape.shape, shape.dtype) for shape in shapes]
+        + [pltpu.SemaphoreType.DMA((8,))],
         compiler_params=params(),
         name="prepare",
     )(rows, count, tile_weight, embeds)
@@ -157,9 +171,10 @@
                 waiting[step % 2][:, place] = dot(x, win_ref[:, ahead : ahead + piece])
             if step > 0:
                 start = (step - 1) * chunk + low
-                value, slope = gelu_pair(waiting[(step - 1) % 2][:, place])
-                hidden = value.astype(jnp.bfloat16)
-                take(start, hidden, slope)
+                values = waiting[(step - 1) % 2][:, place]
+                half, square = gelu_half(values)
+                hidden = (values * half).astype(jnp.bfloat16)
+                take(start, hidden, values, half, square)
                 part = dot(hidden, wout_ref[start : start + piece])
                 projected = part if projected is None else projected + part
     return projected
@@ -192,7 +207,7 @@
     rows_any,
     class_any,
     proto_any,
-    slope_any,
+    pre_any,
     mine_any,
     other_any,
     grad_any,
@@ -206,7 +221,7 @@
     rows_ref,
     class_ref,
     proto_ref,
-    slope_ref,
+    pre_ref,
     mine_ref,
     other_ref,
     even_ref,
@@ -237,7 +252,7 @@
     def give(step):
         whole_place = pl.ds(step * chunk, chunk)
         half_place = pl.ds(step * chunk // 2, chunk // 2)
-        copies.start(("slope", step), slope_ref.at[:, whole_place], slope_any.at[:, whole_place])
+        copies.start(("pre", step), pre_ref.at[:, whole_place], pre_any.at[:, whole_place])
         copies.start(("mine", step), mine_ref.at[:, half_place], mine_any.at[:, half_place])
         copies.start(("other", step), other_ref.at[:, half_place], other_any.at[:, half_place])
 
@@ -253,8 +268,9 @@
             copies.start("high", high_ref.at[:, extra], weight_any.at[0])
             copies.start("low", low_ref.at[:, extra], weight_any.at[1])
 
-    def take(start, hidden, slope):
-        slope_ref[:, start : start + hidden.shape[1]] = slope.astype(jnp.bfloat16)
+    def take(start, hidden, values, half, square):
+        kept = gelu_slope(values, half, square) if start < SLOPED else values
+        pre_ref[:, start : start + hidden.shape[1]] = kept.astype(jnp.bfloat16)
         split_hidden(hidden, rep_ref[0], mine_ref, other_ref, start)
 
     projected = hidden_chunks(x_ref[...], win_ref, wout_ref, (even_ref, odd_ref), arrive, take)
@@ -283,7 +299,7 @@
     grad_ref[...] = (rowsum * unit_float - neighbour + own) * scaling + pull
     copies.start("grad", grad_ref, grad_any)
     for step in range(weights.count):
-        for name in ("slope", "mine", "other"):
+        for name in ("pre", "mine", "other"):
             copies.wait((name, step))
     for name in ("high", "low", "back", "grad"):
         copies.wait(name)
@@ -367,9 +383,9 @@
     back_any,
     mine_any,
     other_any,
-    full_ref,
-    turned_ref,
-    return_ref,
+    full_any,
+    turned_any,
+    return_any,
     x_ref,
     win_ref,
     wout_ref,
@@ -379,6 +395,9 @@
     back_ref,
     mine_ref,
     other_ref,
+    full_ref,
+    turned_ref,
+    return_ref,
     even_ref,
     odd_ref,
     semaphores,
@@ -409,7 +428,7 @@
         if step > 1:
             give(step - 2)
 
-    def take(start, hidden, slope):
+    def take(start, hidden, values, half, square):
         split_hidden(hidden, rep_ref[0], mine_ref, other_ref, start)
 
     projected = hidden_chunks(x_ref[:, :depth], win_ref, wout_ref, (even_ref, odd_ref), arrive, take)
@@ -423,11 +442,16 @@
     full_ref[...] = full
     back = (back_ref[:, width : width + 1] * unit.astype(jnp.float32) - back_ref[:, :width]).astype(jnp.bfloat16)
     return_ref[...] = back
+    copies.start("full", full_ref, full_any)
+    copies.start("return", return_ref, return_any)
     turned_ref[:, :nodes] = full.T.astype(jnp.bfloat16)
     turned_ref[:, nodes:] = (back.astype(jnp.float32) * scaling).T.astype(jnp.bfloat16)
+    copies.start("turned", turned_ref, turned_any)
     for step in range(weights.count):
         copies.wait(("mine", step))
         copies.wait(("other", step))
+    for name in ("full", "return", "turned"):
+        copies.wait(name)
 
 
 def received_part(rep, arrived, weight_in, weight_out, side, grad, weight, back, chunk=512):
@@ -439,7 +463,7 @@
     return pl.pallas_call(
         received_kernel,
         in_specs=[SMEM] + [HBM] * 7,
-        out_specs=(HBM, HBM, VMEM, VMEM, VMEM),
+        out_specs=(HBM,) * 5,
         out_shape=(
             jax.ShapeDtypeStruct((rows, hidden // 2), low),
             jax.ShapeDtypeStruct((rows, hidden // 2), low),
@@ -451,9 +475,12 @@
         + [
             pltpu.VMEM((rows, hidden // 2), low),
             pltpu.VMEM((rows, hidden // 2), low),
+            pltpu.VMEM((nodes, width), jnp.float32),
+            pltpu.VMEM((width, nodes + rows), low),
+            pltpu.VMEM((rows, width), low),
             pltpu.VMEM((rows, chunk), jnp.float32),
             pltpu.VMEM((rows, chunk), jnp.float32),
-            pltpu.SemaphoreType.DMA((5 + 4 * (hidden // chunk),)),
+            pltpu.SemaphoreType.DMA((8 + 4 * (hidden // chunk),)),
         ],
         compiler_params=params(),
         name="received_part",
@@ -627,57 +654,68 @@
 
 
 def slope_kernel(chunk, *refs):
-    full_any, pick_any, back_any, side_any, slope_any, wout_any, out_any = refs[:7]
-    full_ref, pick_ref, back_ref, side_ref, slope_ref, wout_ref, grad_ref, semaphores = refs[7:]
+    full_any, pick_any, back_any, side_any, pre_any, wout_any, out_any = refs[:7]
+    full_ref, pick_ref, back_ref, side_ref, pre_ref, wout_ref, grad_ref, semaphores = refs[7:]
     copies = Copies(semaphores)
     first = ((full_any, full_ref), (pick_any, pick_ref), (back_any, back_ref), (side_any, side_ref))
-    steps = range(0, slope_ref.shape[1], chunk)
+    steps = range(0, pre_ref.shape[1], chunk)
     for index, (source, target) in enumerate(first):
         copies.start(index, source, target)
     for start in steps:
         place = pl.ds(start, chunk)
         copies.start(("out", start), wout_any.at[place], wout_ref.at[place])
-        copies.start(("slope", start), slope_any.at[:, place], slope_ref.at[:, place])
+        copies.start(("pre", start), pre_any.at[:, place], pre_ref.at[:, place])
     for index in range(len(first)):
         copies.wait(index)
     back = dot(pick_ref[...], back_ref[...], 0, 0)
     node = (full_ref[...] + back * side_ref[:, 1:2]).astype(jnp.bfloat16)
+    piece = chunk // 2
     for start in steps:
         copies.wait(("out", start))
-        copies.wait(("slope", start))
-        place = slice(start, start + chunk)
-        grad_hidden = dot(node, wout_ref[place], 1, 1)
-        grad_ref[:, place] = (grad_hidden * slope_ref[:, place].astype(jnp.float32)).astype(jnp.bfloat16)
-        copies.start(("grad", start), grad_ref.at[:, pl.ds(start, chunk)], out_any.at[:, pl.ds(start, chunk)])
+        copies.wait(("pre", start))
+        if start > 0:
+            place = pl.ds(start - chunk, chunk)
+            copies.start(("grad", start - chunk), grad_ref.at[:, place], out_any.at[:, place])
+        for low in range(start, start + chunk, piece):
+            place = slice(low, low + piece)
+            grad_hidden = dot(node, wout_ref[place], 1, 1)
+            slope = pre_ref[:, place].astype(jnp.float32)
+            if low >= SLOPED:
+                slope = gelu_slope(slope, *gelu_half(slope))
+            grad_ref[:, place] = (grad_hidden * slope).astype(jnp.bfloat16)
+    place = pl.ds(steps[-1], chunk)
+    copies.start(("grad", steps[-1]), grad_ref.at[:, place], out_any.at[:, place])
     for start in steps:
         copies.wait(("grad", start))
 
 
-def slope_part(full, pick, back, side, slope, weight_out, chunk=1024):
-    arrays = (full, pick, back, side, slope, weight_out)
+def slope_part(full, pick, back, side, pre, weight_out, chunk=1024):
+    arrays = (full, pick, back, side, pre, weight_out)
     return pl.pallas_call(
         functools.partial(slope_kernel, chunk),
         in_specs=[HBM] * 6,
         out_specs=HBM,
-        out_shape=jax.ShapeDtypeStruct(slope.shape, jnp.bfloat16),
+        out_shape=jax.ShapeDtypeStruct(pre.shape, jnp.bfloat16),
         scratch_shapes=[pltpu.VMEM(array.shape, array.dtype) for array in arrays]
         + [
-            pltpu.VMEM(slope.shape, jnp.bfloat16),
-            pltpu.SemaphoreType.DMA((4 + 3 * (slope.shape[1] // chunk),)),
+            pltpu.VMEM(pre.shape, jnp.bfloat16),
+            pltpu.SemaphoreType.DMA((4 + 3 * (pre.shape[1] // chunk),)),
         ],
-        cost_estimate=pl.CostEstimate(flops=2 * slope.size * full.shape[1], bytes_accessed=16 * MIB, transcendentals=0),
+        cost_estimate=pl.CostEstimate(flops=2 * pre.size * full.shape[1], bytes_accessed=16 * MIB, transcendentals=0),
         compiler_params=params(58),
         name="slope_part",
     )(*arrays)
 
 
-def embed_kernel(chunk, grad_any, win_any, out_ref, grad_ref, win_ref, total_ref, semaphores):
+def embed_kernel(chunk, first, grad_any, win_any, *refs):
+    out_any, grad_ref, win_ref, out_ref, total_ref, semaphores = refs[-6:]
     copies = Copies(semaphores)
     steps = range(0, grad_ref.shape[1], chunk)
+    columns = pl.ds(first, win_ref.shape[0])
     for start in steps:
         place = pl.ds(start, chunk)
         copies.start(("grad", start), grad_any.at[:, place], grad_ref.at[:, place])
-        copies.start(("in", start), win_any.at[:, place], win_ref.at[:, place])
+        copies.start(("in", start), win_any.at[columns, place], win_ref.at[:, place])
     for start in steps:
         copies.wait(("grad", start))
         copies.wait(("in", start))
@@ -689,25 +727,31 @@
             total_ref[...] += part
         else:
             out_ref[...] = (total_ref[...] + part).astype(jnp.bfloat16)
-
-
-def embed_part(grad, weight_in, chunk=1024):
+    copies.start("give", out_ref, out_any.at[:, columns])
+    copies.wait("give")
+
+
+def embed_part(first, length, grad, weight_in, other=None, chunk=1024):
     nodes, hidden = grad.shape
     depth = weight_in.shape[0]
+    operands = (grad, weight_in) if other is None else (grad, weight_in, other)
     return pl.pallas_call(
-        functools.partial(embed_kernel, chunk),
-        in_specs=[HBM] * 2,
+        functools.partial(embed_kernel, chunk, first),
+        in_specs=[HBM] * len(operands),
+        out_specs=HBM,
         out_shape=jax.ShapeDtypeStruct((nodes, depth), jnp.bfloat16),
+        input_output_aliases={} if other is None else {2: 0},
         scratch_shapes=[
             pltpu.VMEM(grad.shape, jnp.bfloat16),
-            pltpu.VMEM(weight_in.shape, jnp.bfloat16),
-            pltpu.VMEM((nodes, depth), jnp.float32),
-            pltpu.SemaphoreType.DMA((2 * (hidden // chunk),)),
+            pltpu.VMEM((length, hidden), jnp.bfloat16),
+            pltpu.VMEM((nodes, length), jnp.bfloat16),
+            pltpu.VMEM((nodes, length), jnp.float32),
+            pltpu.SemaphoreType.DMA((1 + 2 * (hidden // chunk),)),
         ],
-        cost_estimate=pl.CostEstimate(flops=2 * grad.size * depth, bytes_accessed=13 * MIB, transcendentals=0),
+        cost_estimate=pl.CostEstimate(flops=2 * grad.size * length, bytes_accessed=9 * MIB, transcendentals=0),
         compiler_params=params(60),
         name="embed_part",
-    )(grad, weight_in)
+    )(*operands)
 
 
 def bit_orders(count):
@@ -746,7 +790,7 @@
     label_rows,
     label_class,
 ):
-    nodes = embeds.shape[0]
+    nodes, embed_width = embeds.shape
     dom_count = lax.axis_size("dom")
     rep_count = lax.axis_size("rep")
     peers = dom_count * rep_count
@@ -766,7 +810,7 @@
     arrived = lax.all_to_all(
         outgoing.reshape(peers, slots, -1), both, split_axis=0, concat_axis=0, tiled=True
     ).reshape(peers * slots, -1)
-    slope, own, sent_own, grad, weight, back = forward(
+    pre_act, own, sent_own, grad, weight, back = forward(
         rep[None],
         tile_column,
         embeds,
@@ -804,16 +848,17 @@
         flat = product(place[None], streams, operands)
         parts = [tuple(flat[2 * stream : 2 * stream + 2]) for stream in range(len(streams))]
     parts, full = lax.optimization_barrier((parts, full))
-    grad_pre = slope_part(full, pick, given, side, slope, weight_out)
+    grad_pre = slope_part(full, pick, given, side, pre_act, weight_out)
     left = [[bit for bit in range(bit_count) if bit != order[0]] for order, _, _ in streams]
     orders = [order for order, _, _ in streams]
     shared = next(step for step in range(bit_count) if orders[0][step:] == orders[1][step:])
+    cuts = (0, embed_width // 2, embed_width)
     embed_grad = None
     for step in range(bit_count):
         came = [exchange(sent, order[step]) for (sent, _), order in zip(parts, orders)]
         if step == 0:
             came, grad_pre = lax.optimization_barrier((came, grad_pre))
-        elif step == 1:
+        elif step < len(cuts):
             came, embed_grad = lax.optimization_barrier((came, embed_grad))
         else:
             came = lax.optimization_barrier(came)
@@ -826,9 +871,9 @@
         parts = fold_halves(place[None], digits, step + 1 == shared, kept, came)
         if step + 1 == shared:
             left, orders = left[1:], orders[1:]
-        if step == 0:
+        if step + 1 < len(cuts):
             parts, grad_pre = lax.optimization_barrier((parts, grad_pre))
-            embed_grad = embed_part(grad_pre, weight_in)
+            embed_grad = embed_part(cuts[step], cuts[step + 1] - cuts[step], grad_pre, weight_in, embed_grad)
         else:
             parts = lax.optimization_barrier(parts)
     summed = finish(1.0 / math.sqrt(nodes * peers), kept, came)

time: 89.6 us -> 87.8 us (0.980)
  waiting for transfers between devices: 9.36 us -> 4.27 us
  Pallas kernels: 51.7 us -> 54.3 us
    ppermute x10, waiting for transfers between devices: 9.35 us -> 4.26 us  [exchange(): lax.ppermute(sent, 'dom', [(device, device ^ 1 << bit) for device in rang...]
    pallas_call x2 -> x3, Pallas kernels: 10.8 us -> 12.9 us  [the longest x2 10.1 us: embed_part(): pl.pallas_call(functools.partial(embed_kernel, chunk, first), in_specs=[H...]
    pallas_call x1, Pallas kernels: 6.43 us -> 7.88 us  [slope_part(): pl.pallas_call(functools.partial(slope_kernel, chunk), in_specs=[HBM] * 6...]
    pallas_call x1, Pallas kernels: 17.5 us -> 16.5 us  [forward(): pl.pallas_call(forward_kernel, in_specs=[SMEM] * 2 + [HBM] * 8, out_specs...]
  transfers between devices with their start and end apart: 15 -> 15, of which waited for: 4 -> 3; matrix products, arithmetic and copies ran while one was open for 0% -> 0% of each run, Pallas kernels for 53% -> 57%
where the time goes in v6:
time: 87.8 us; the launch traced here: 87.5 us
  Pallas kernels  54.3 us (62%)
  starting transfers between devices  28.1 us (32%)
  waiting for transfers between devices  4.27 us (5%)
    pallas_call x1, Pallas kernels, forward(): pl.pallas_call(forward_kernel, in_specs=[SMEM] * 2 + [HBM] * 8, out_specs...  16.5 us
    ppermute x10, starting transfers between devices, exchange(): lax.ppermute(sent, 'dom', [(device, device ^ 1 << bit) for device in rang...  14 us
    pallas_call x2, Pallas kernels, embed_part(): pl.pallas_call(functools.partial(embed_kernel, chunk, first), in_specs=[H...  10.1 us
    pallas_call x1, Pallas kernels, received_part(): pl.pallas_call(received_kernel, in_specs=[SMEM] + [HBM] * 7, out_specs=(H...  8.4 us
    pallas_call x1, Pallas kernels, slope_part(): pl.pallas_call(functools.partial(slope_kernel, chunk), in_specs=[HBM] * 6...  7.88 us
    all_to_all x1, starting transfers between devices, body(): lax.all_to_all(outgoing.reshape(peers, slots, -1), both, split_axis=0, co...  7.42 us
    pallas_call x1, Pallas kernels, product(): pl.pallas_call(functools.partial(product_kernel, streams, chunk), in_spec...  7.26 us
    all_to_all x1, starting transfers between devices, body(): lax.all_to_all(returned.reshape(peers, slots, width), both, split_axis=0,...  5.86 us
  transfers between devices with their start and end apart: 15, of which 3 were waited for; matrix products, arithmetic and copies ran while one was open for 0% of the time, Pallas kernels for 57%

profile of v6, /device:TPU:0, one launch (start us, length us, event | category | flops | bytes accessed | tf_op | source)
XLA Modules:
  0.0 87.5 jit_solution(17323863924835972112)
XLA Ops:
  0.6 2.8 %prepare.1 = (bf16[256,1152]{1,0:T(8,128)(2,1)}, bf16[256,512]{1,0:T(8,128)(2,1)}, f32[512,128]{1,0:T(8,128)}) custom-call(s32[8,32]{1,0:T(8,128)} %bitcast.13, s32[1,32]{1,0:T(1,128)} %count_any.1, bf16[4,8,128,128]{3,2,1,0:T(8,128)(2,1)} %tiles_any.3, bf16[512,1024]{1,0:T(8,128)(2,1)} %x_any.1), custom_call_target="tpu_custom_call" | custom-call | tf_op jit(solution)/shard_map/prepare/pallas_call | solution.py:134
  3.4 7.4 %all-to-all-start = ((bf16[32,8,1152]{2,1,0:T(8,128)(2,1)}), bf16[32,8,1152]{2,1,0:T(8,128)(2,1)}, u32[]{:S(2)}, u32[]{:S(2)}) async-start(bf16[32,8,1152]{2,1,0:T(8,128)(2,1)} %bitcast.11), calls=%async_computation | async-start | bytes 1179648 | tf_op jit(solution)/shard_map/all_to_all | solution.py:810
  10.9 16.5 %forward.1 = (bf16[512,4096]{1,0:T(8,128)(2,1)}, bf16[512,2048]{1,0:T(8,128)(2,1)}, bf16[512,2048]{1,0:T(8,128)(2,1)}, f32[512,512]{1,0:T(8,128)}, bf16[2,512,256]{2,1,0:T(8,128)(2,1)}, /*index=5*/f32[256,640]{1,0:T(8,128)}) custom-call(s32[1]{0:T(128)} %bitcast.1.rep_ref, s32[4,8]{1,0:T(4,128)} %column_ref.1, bf16[512,1024]{1,0:T(8,128)(2,1)} %x_any.1, ...), custom_call_target="tpu_custom_call" | custom-call | tf_op jit(solution)/shard_map/forward/pallas_call | solution.py:344
  27.4 0.3 collective-permute-start.1
  27.7 0.0 all-to-all-done
  27.7 8.4 %received_part.1 = (bf16[256,2048]{1,0:T(8,128)(2,1)}, bf16[256,2048]{1,0:T(8,128)(2,1)}, f32[512,512]{1,0:T(8,128)}, bf16[512,768]{1,0:T(8,128)(2,1)}, bf16[256,512]{1,0:T(8,128)(2,1)}) custom-call(s32[1]{0:T(128)} %bitcast.1.rep_ref, bf16[256,1152]{1,0:T(8,128)(2,1)} %bitcast.5.x_any, bf16[1024,4096]{1,0:T(8,128)(2,1)} %win_any.7, ...), custom_call_target="tpu_custom_call" | custom-call | tf_op jit(solution)/shard_map/received_part/pallas_call | solution.py:463
  36.1 0.4 collective-permute-start.2
  36.5 0.2 collective-permute-start
  36.7 5.9 %all-to-all-start.1 = ((bf16[32,8,512]{2,1,0:T(8,128)(2,1)}), bf16[32,8,512]{2,1,0:T(8,128)(2,1)}, u32[]{:S(2)}, u32[]{:S(2)}) async-start(bf16[32,8,512]{2,1,0:T(8,128)(2,1)} %bitcast.12), calls=%async_computation.1 | async-start | bytes 524288 | tf_op jit(solution)/shard_map/all_to_all | solution.py:832
  42.5 0.0 collective-permute-done.refs_1_
  42.6 0.0 collective-permute-done.1.refs_4_
  42.6 0.0 collective-permute-done.2.refs_5_
  42.6 7.3 %product.1 = (bf16[8,176,128]{2,1,0:T(8,128)(2,1)}, f32[8,176,128]{2,1,0:T(8,128)}, bf16[8,176,128]{2,1,0:T(8,128)(2,1)}, f32[8,176,128]{2,1,0:T(8,128)}, bf16[8...) custom-call(s32[1]{0:T(128)} %bitcast.place_ref, bf16[512,768]{1,0:T(8,128)(2,1)} %get-tuple-element.73.refs_0_, ...), custom_call_target="tpu_custom_call" | custom-call | tf_op jit(solution)/shard_map/product/pallas_call | solution.py:643
  49.8 1.8 %collective-permute-start.3 = (bf16[8,176,128]{2,1,0:T(8,128)(2,1)}, bf16[8,176,128]{2,1,0:T(8,128)(2,1)S(1)}, u32[]{:S(2)}, u32[]{:S(2)}) collective-permute-start(bf16[8,176,128]{2,1,0:T(8,128)(2,1)} %get-tuple-element.86), channel_id=1, source_target_pairs={{0,2},{2,0},{4,6},{6,4},{8,10},{10,8},{12,14},{14,12},{16,18},{18,... | collective-permute-start | bytes 1081352 | tf_op jit(solution)/shard_map/ppermute | solution.py:778
  51.6 1.5 %collective-permute-start.4 = (bf16[8,176,128]{2,1,0:T(8,128)(2,1)}, bf16[8,176,128]{2,1,0:T(8,128)(2,1)S(1)}, u32[]{:S(2)}, u32[]{:S(2)}) collective-permute-start(bf16[8,176,128]{2,1,0:T(8,128)(2,1)} %get-tuple-element.87), channel_id=1, source_target_pairs={{0,4},{2,6},{4,0},{6,2},{8,12},{10,14},{12,8},{14,10},{16,20},{18,... | collective-permute-start | bytes 1081352 | tf_op jit(solution)/shard_map/ppermute | solution.py:778
  53.1 1.5 %collective-permute-start.5 = (bf16[8,160,128]{2,1,0:T(8,128)(2,1)}, bf16[8,160,128]{2,1,0:T(8,128)(2,1)S(1)}, u32[]{:S(2)}, u32[]{:S(2)}) collective-permute-start(bf16[8,160,128]{2,1,0:T(8,128)(2,1)} %get-tuple-element.88), channel_id=1, source_target_pairs={{0,8},{2,10},{4,12},{6,14},{8,0},{10,2},{12,4},{14,6},{16,24},{18,... | collective-permute-start | bytes 983048 | tf_op jit(solution)/shard_map/ppermute | solution.py:778
  54.5 0.0 all-to-all-done.1
  54.5 0.0 copy-start
  54.5 0.0 copy-start.1
  54.5 0.0 copy-start.2
  54.5 7.9 %slope_part.1.grad_any = bf16[512,4096]{1,0:T(8,128)(2,1)} custom-call(f32[512,512]{1,0:T(8,128)} %get-tuple-element.89.refs_0_, bf16[256,512]{1,0:T(8,128)(2,1)} %get-tuple-element.90.refs_1_, bf16[256,512]{1,0:T(8,128)(2,1)} %bitcast.9.refs_2_, f32[512,128]{1,0:T(8,128)} %get-tuple-element.69.side_any.refs_3_, ...), custom_call_target="tpu_custom_call" | custom-call | flops 2147483648 | bytes 16777216 | tf_op jit(solution)/shard_map/slope_part/pallas_call | solution.py:694
  62.4 0.0 collective-permute-done.5.refs_5_
  62.5 0.0 collective-permute-done.3.refs_1_
  62.5 0.0 collective-permute-done.4.refs_3_
  62.5 0.0 copy-done
  62.5 0.0 copy-done.1
  62.5 0.0 copy-done.2
  62.5 0.2 fold_halves.3
  62.7 2.5 %collective-permute-start.8 = (bf16[4,160,128]{2,1,0:T(8,128)(2,1)S(1)}, bf16[4,160,128]{2,1,0:T(8,128)(2,1)S(1)}, u32[]{:S(2)}, u32[]{:S(2)}) collective-permute-start(bf16[4,160,128]{2,1,0:T(8,128)(2,1)S(1)} %get-tuple-element.108), channel_id=1, source_target_pairs={{0,16},{2,18},{4,20},{6,22},{8,24},{10,26},{12,28},{14,30},{16,0},... | collective-permute-start | bytes 491528 | tf_op jit(solution)/shard_map/ppermute | solution.py:778
  65.2 0.9 %collective-permute-start.6 = (bf16[4,176,128]{2,1,0:T(8,128)(2,1)S(1)}, bf16[4,176,128]{2,1,0:T(8,128)(2,1)S(1)}, u32[]{:S(2)}, u32[]{:S(2)}) collective-permute-start(bf16[4,176,128]{2,1,0:T(8,128)(2,1)S(1)} %get-tuple-element.106), channel_id=1, source_target_pairs={{0,4},{2,6},{4,0},{6,2},{8,12},{10,14},{12,8},{14,10},{16,20},{18,... | collective-permute-start | bytes 540680 | tf_op jit(solution)/shard_map/ppermute | solution.py:778
  66.1 0.6 collective-permute-start.7
  66.7 5.1 %embed_part.2.refs_0_ = bf16[512,1024]{1,0:T(8,128)(2,1)} custom-call(bf16[512,4096]{1,0:T(8,128)(2,1)} %slope_part.1.grad_any, bf16[1024,4096]{1,0:T(8,128)(2,1)} %win_any.7), custom_call_target="tpu_custom_call" | custom-call | flops 2147483648 | bytes 9437184 | tf_op jit(solution)/shard_map/embed_part/pallas_call | solution.py:738
  71.8 0.8 collective-permute-done.8.refs_5_
  72.6 0.0 collective-permute-done.6.refs_1_
  72.6 0.0 collective-permute-done.7.refs_3_
  72.6 0.1 fold_halves.4
  72.7 0.8 collective-permute-start.10
  73.4 1.5 %collective-permute-start.9 = (bf16[2,352,128]{2,1,0:T(8,128)(2,1)S(1)}, bf16[2,352,128]{2,1,0:T(8,128)(2,1)S(1)}, u32[]{:S(2)}, u32[]{:S(2)}) collective-permute-start(bf16[2,352,128]{2,1,0:T(8,128)(2,1)S(1)} %get-tuple-element.119), channel_id=1, source_target_pairs={{0,8},{2,10},{4,12},{6,14},{8,0},{10,2},{12,4},{14,6},{16,24},{18,... | collective-permute-start | bytes 540680 | tf_op jit(solution)/shard_map/ppermute | solution.py:778
  75.0 5.1 %embed_part.3 = bf16[512,1024]{1,0:T(8,128)(2,1)} custom-call(bf16[512,4096]{1,0:T(8,128)(2,1)} %slope_part.1.grad_any, bf16[1024,4096]{1,0:T(8,128)(2,1)} %win_any.7, bf16[512,1024]{1,0:T(8,128)(2,1)} %embed_part.2.refs_0_), custom_call_target="tpu_custom_call", output_to_operand_aliasing={{}: (2, {})} | custom-call | flops 2147483648 | bytes 9437184 | tf_op jit(solution)/shard_map/embed_part/pallas_call | solution.py:738
  80.1 0.0 collective-permute-done.10.refs_3_
  80.1 0.0 collective-permute-done.9.refs_1_
  80.1 0.1 fold_halves.5
  80.1 1.7 %collective-permute-start.11 = (bf16[1,352,128]{2,1,0:T(8,128)(2,1)S(1)}, bf16[1,352,128]{2,1,0:T(8,128)(2,1)S(1)}, u32[]{:S(2)}, u32[]{:S(2)}) collective-permute-start(bf16[1,352,128]{2,1,0:T(8,128)(2,1)S(1)} %get-tuple-element.129), channel_id=1, source_target_pairs={{0,16},{2,18},{4,20},{6,22},{8,24},{10,26},{12,28},{14,30},{16,0},... | collective-permute-start | bytes 270344 | tf_op jit(solution)/shard_map/ppermute | solution.py:778
  81.9 1.3 %collective-permute-start.12 = (bf16[1,160,128]{2,1,0:T(8,128)(2,1)S(1)}, bf16[1,160,128]{2,1,0:T(8,128)(2,1)S(1)}, u32[]{:S(2)}, u32[]{:S(2)}) collective-permute-start(bf16[1,160,128]{2,1,0:T(8,128)(2,1)S(1)} %get-tuple-element.130), channel_id=1, source_target_pairs={{0,4},{2,6},{4,0},{6,2},{8,12},{10,14},{12,8},{14,10},{16,20},{18,... | collective-permute-start | bytes 122888 | tf_op jit(solution)/shard_map/ppermute | solution.py:778
  83.1 2.7 %collective-permute-done.12.refs_3_ = bf16[1,160,128]{2,1,0:T(8,128)(2,1)S(1)} collective-permute-done((bf16[1,160,128]{2,1,0:T(8,128)(2,1)S(1)}, bf16[1,160,128]{2,1,0:T(8,128)(2,1)S(1)}, u32[]{:S(2)}, u32[]{:S(2)}) %collective-permute-start.12) | collective-permute-done | bytes 40992 | tf_op jit(solution)/shard_map/ppermute | solution.py:778
  85.9 0.7 collective-permute-done.11.refs_1_
  86.5 1.0 %finish.1 = f32[128,512]{1,0:T(8,128)} custom-call(f32[1,352,128]{2,1,0:T(8,128)S(1)} %get-tuple-element.128.refs_0_, bf16[1,352,128]{2,1,0:T(8,128)(2,1)S(1)} %collective-permute-done.11.refs_1_, f32[1,160,128]{2,1,0:T(8,128)S(1)} %get-tuple-element.132.refs_2_, bf16[1,160,128]{2,1,0:T(8,128)(2,1)S(1)} %collective-permute-done.12.refs_3_), custom_call_target="tpu_custom_call" | custom-call | tf_op jit(solution)/shard_map/finish/pallas_call | solution.py:611
Async XLA Ops:
  3.4 24.2 %all-to-all-start = ((bf16[32,8,1152]{2,1,0:T(8,128)(2,1)}), bf16[32,8,1152]{2,1,0:T(8,128)(2,1)}, u32[]{:S(2)}, u32[]{:S(2)}) async-start(bf16[32,8,1152]{2,1,0:T(8,128)(2,1)} %bitcast.11), calls=%async_computation | async-start | bytes 1179648 | tf_op jit(solution)/shard_map/all_to_all | solution.py:810
  27.4 15.1 %collective-permute-start.1 = (bf16[512,2048]{1,0:T(8,128)(2,1)}, bf16[512,2048]{1,0:T(8,128)(2,1)}, u32[]{:S(2)}, u32[]{:S(2)}) collective-permute-start(bf16[512,2048]{1,0:T(8,128)(2,1)} %get-tuple-element.76), channel_id=1, source_target_pairs={{0,1},{1,0},{2,3},{3,2},{4,5},{5,4},{6,7},{7,6},{8,9},{9,8},{10,11... | collective-permute-start | bytes 6291464 | tf_op jit(solution)/shard_map/ppermute | solution.py:826
  36.1 6.5 %collective-permute-start.2 = (bf16[256,2048]{1,0:T(8,128)(2,1)}, bf16[256,2048]{1,0:T(8,128)(2,1)}, u32[]{:S(2)}, u32[]{:S(2)}) collective-permute-start(bf16[256,2048]{1,0:T(8,128)(2,1)} %get-tuple-element.77), channel_id=1, source_target_pairs={{0,1},{1,0},{2,3},{3,2},{4,5},{5,4},{6,7},{7,6},{8,9},{9,8},{10,11... | collective-permute-start | bytes 3145736 | tf_op jit(solution)/shard_map/ppermute | solution.py:831
  36.5 6.1 %collective-permute-start = (bf16[512,768]{1,0:T(8,128)(2,1)}, bf16[512,768]{1,0:T(8,128)(2,1)}, u32[]{:S(2)}, u32[]{:S(2)}) collective-permute-start(bf16[512,768]{1,0:T(8,128)(2,1)} %get-tuple-element.73.refs_0_), channel_id=1, source_target_pairs={{0,1},{1,0},{2,3},{3,2},{4,5},{5,4},{6,7},{7,6},{8,9},{9,8},{10,11... | collective-permute-start | bytes 2359304 | tf_op jit(solution)/shard_map/ppermute | solution.py:830
  36.7 17.9 %all-to-all-start.1 = ((bf16[32,8,512]{2,1,0:T(8,128)(2,1)}), bf16[32,8,512]{2,1,0:T(8,128)(2,1)}, u32[]{:S(2)}, u32[]{:S(2)}) async-start(bf16[32,8,512]{2,1,0:T(8,128)(2,1)} %bitcast.12), calls=%async_computation.1 | async-start | bytes 524288 | tf_op jit(solution)/shard_map/all_to_all | solution.py:832
  49.8 12.6 %collective-permute-start.3 = (bf16[8,176,128]{2,1,0:T(8,128)(2,1)}, bf16[8,176,128]{2,1,0:T(8,128)(2,1)S(1)}, u32[]{:S(2)}, u32[]{:S(2)}) collective-permute-start(bf16[8,176,128]{2,1,0:T(8,128)(2,1)} %get-tuple-element.86), channel_id=1, source_target_pairs={{0,2},{2,0},{4,6},{6,4},{8,10},{10,8},{12,14},{14,12},{16,18},{18,... | collective-permute-start | bytes 1081352 | tf_op jit(solution)/shard_map/ppermute | solution.py:778
  51.6 10.9 %collective-permute-start.4 = (bf16[8,176,128]{2,1,0:T(8,128)(2,1)}, bf16[8,176,128]{2,1,0:T(8,128)(2,1)S(1)}, u32[]{:S(2)}, u32[]{:S(2)}) collective-permute-start(bf16[8,176,128]{2,1,0:T(8,128)(2,1)} %get-tuple-element.87), channel_id=1, source_target_pairs={{0,4},{2,6},{4,0},{6,2},{8,12},{10,14},{12,8},{14,10},{16,20},{18,... | collective-permute-start | bytes 1081352 | tf_op jit(solution)/shard_map/ppermute | solution.py:778
  53.1 9.4 %collective-permute-start.5 = (bf16[8,160,128]{2,1,0:T(8,128)(2,1)}, bf16[8,160,128]{2,1,0:T(8,128)(2,1)S(1)}, u32[]{:S(2)}, u32[]{:S(2)}) collective-permute-start(bf16[8,160,128]{2,1,0:T(8,128)(2,1)} %get-tuple-element.88), channel_id=1, source_target_pairs={{0,8},{2,10},{4,12},{6,14},{8,0},{10,2},{12,4},{14,6},{16,24},{18,... | collective-permute-start | bytes 983048 | tf_op jit(solution)/shard_map/ppermute | solution.py:778
  54.5 8.0 %copy-start = (f32[8,176,128]{2,1,0:T(8,128)S(1)}, f32[8,176,128]{2,1,0:T(8,128)}, u32[]{:S(2)}) copy-start(f32[8,176,128]{2,1,0:T(8,128)} %get-tuple-element.85.refs_0_) | copy-start | bytes 2162692
  54.5 8.0 %copy-start.1 = (f32[8,176,128]{2,1,0:T(8,128)S(1)}, f32[8,176,128]{2,1,0:T(8,128)}, u32[]{:S(2)}) copy-start(f32[8,176,128]{2,1,0:T(8,128)} %get-tuple-element.94.refs_2_) | copy-start | bytes 2162692
  54.5 8.0 %copy-start.2 = (f32[8,160,128]{2,1,0:T(8,128)S(1)}, f32[8,160,128]{2,1,0:T(8,128)}, u32[]{:S(2)}) copy-start(f32[8,160,128]{2,1,0:T(8,128)} %get-tuple-element.96.refs_4_) | copy-start | bytes 1966084
  62.7 9.9 %collective-permute-start.8 = (bf16[4,160,128]{2,1,0:T(8,128)(2,1)S(1)}, bf16[4,160,128]{2,1,0:T(8,128)(2,1)S(1)}, u32[]{:S(2)}, u32[]{:S(2)}) collective-permute-start(bf16[4,160,128]{2,1,0:T(8,128)(2,1)S(1)} %get-tuple-element.108), channel_id=1, source_target_pairs={{0,16},{2,18},{4,20},{6,22},{8,24},{10,26},{12,28},{14,30},{16,0},... | collective-permute-start | bytes 491528 | tf_op jit(solution)/shard_map/ppermute | solution.py:778
  65.2 7.4 %collective-permute-start.6 = (bf16[4,176,128]{2,1,0:T(8,128)(2,1)S(1)}, bf16[4,176,128]{2,1,0:T(8,128)(2,1)S(1)}, u32[]{:S(2)}, u32[]{:S(2)}) collective-permute-start(bf16[4,176,128]{2,1,0:T(8,128)(2,1)S(1)} %get-tuple-element.106), channel_id=1, source_target_pairs={{0,4},{2,6},{4,0},{6,2},{8,12},{10,14},{12,8},{14,10},{16,20},{18,... | collective-permute-start | bytes 540680 | tf_op jit(solution)/shard_map/ppermute | solution.py:778
  66.1 6.4 %collective-permute-start.7 = (bf16[4,176,128]{2,1,0:T(8,128)(2,1)S(1)}, bf16[4,176,128]{2,1,0:T(8,128)(2,1)S(1)}, u32[]{:S(2)}, u32[]{:S(2)}) collective-permute-start(bf16[4,176,128]{2,1,0:T(8,128)(2,1)S(1)} %get-tuple-element.107), channel_id=1, source_target_pairs={{0,2},{2,0},{4,6},{6,4},{8,10},{10,8},{12,14},{14,12},{16,18},{18,... | collective-permute-start | bytes 540680 | tf_op jit(solution)/shard_map/ppermute | solution.py:778
  72.7 7.4 %collective-permute-start.10 = (bf16[2,160,128]{2,1,0:T(8,128)(2,1)S(1)}, bf16[2,160,128]{2,1,0:T(8,128)(2,1)S(1)}, u32[]{:S(2)}, u32[]{:S(2)}) collective-permute-start(bf16[2,160,128]{2,1,0:T(8,128)(2,1)S(1)} %get-tuple-element.120), channel_id=1, source_target_pairs={{0,2},{2,0},{4,6},{6,4},{8,10},{10,8},{12,14},{14,12},{16,18},{18,... | collective-permute-start | bytes 245768 | tf_op jit(solution)/shard_map/ppermute | solution.py:778
  73.4 6.6 %collective-permute-start.9 = (bf16[2,352,128]{2,1,0:T(8,128)(2,1)S(1)}, bf16[2,352,128]{2,1,0:T(8,128)(2,1)S(1)}, u32[]{:S(2)}, u32[]{:S(2)}) collective-permute-start(bf16[2,352,128]{2,1,0:T(8,128)(2,1)S(1)} %get-tuple-element.119), channel_id=1, source_target_pairs={{0,8},{2,10},{4,12},{6,14},{8,0},{10,2},{12,4},{14,6},{16,24},{18,... | collective-permute-start | bytes 540680 | tf_op jit(solution)/shard_map/ppermute | solution.py:778
  80.1 6.4 %collective-permute-start.11 = (bf16[1,352,128]{2,1,0:T(8,128)(2,1)S(1)}, bf16[1,352,128]{2,1,0:T(8,128)(2,1)S(1)}, u32[]{:S(2)}, u32[]{:S(2)}) collective-permute-start(bf16[1,352,128]{2,1,0:T(8,128)(2,1)S(1)} %get-tuple-element.129), channel_id=1, source_target_pairs={{0,16},{2,18},{4,20},{6,22},{8,24},{10,26},{12,28},{14,30},{16,0},... | collective-permute-start | bytes 270344 | tf_op jit(solution)/shard_map/ppermute | solution.py:778
  81.9 4.0 %collective-permute-start.12 = (bf16[1,160,128]{2,1,0:T(8,128)(2,1)S(1)}, bf16[1,160,128]{2,1,0:T(8,128)(2,1)S(1)}, u32[]{:S(2)}, u32[]{:S(2)}) collective-permute-start(bf16[1,160,128]{2,1,0:T(8,128)(2,1)S(1)} %get-tuple-element.130), channel_id=1, source_target_pairs={{0,4},{2,6},{4,0},{6,2},{8,12},{10,14},{12,8},{14,10},{16,20},{18,... | collective-permute-start | bytes 122888 | tf_op jit(solution)/shard_map/ppermute | solution.py:778

commit v7 on v6

--- a/solution.py
+++ b/solution.py
@@ -564,8 +564,8 @@
     base = 0
     for stream, (weight, bit) in enumerate(digits):
         kept_ref, came_ref = refs[2 * stream : 2 * stream + 2]
-        target = max(stream - 1, 0) if merge else stream
-        if not (merge and stream == 1):
+        target = 0 if merge else stream
+        if not merge:
             base = 0
         sent_ref, next_ref = outputs[2 * target : 2 * target + 2]
         rows = slice(base, base + kept_ref.shape[1])
@@ -579,7 +579,7 @@
 def fold_halves(place, digits, merge, kept, came):
     heights = [array.shape[1] for array in kept]
     if merge:
-        heights = [heights[0] + heights[1]] + heights[2:]
+        heights = [sum(heights)]
     blocks, _, depth = kept[0].shape
     shapes = []
     for height in heights:
@@ -757,9 +757,9 @@
 def bit_orders(count):
     bits = list(range(count.bit_length() - 1))
     first = len(bits) // 3
-    second = first + max(first, (len(bits) - first) // 3)
-    low, middle, high = bits[:first], bits[first:second], bits[second:]
-    return (low + middle + high, middle + low + high, high + low + middle)
+    groups = [bits[start : start + first] for start in range(0, 3 * first, first)]
+    last = bits[3 * first :]
+    return tuple(sum(groups[turn:] + groups[:turn], []) + last for turn in range(3))
 
 
 def streams_of(dom_count, width):
@@ -851,14 +851,20 @@
     grad_pre = slope_part(full, pick, given, side, pre_act, weight_out)
     left = [[bit for bit in range(bit_count) if bit != order[0]] for order, _, _ in streams]
     orders = [order for order, _, _ in streams]
-    shared = next(step for step in range(bit_count) if orders[0][step:] == orders[1][step:])
-    cuts = (0, embed_width // 2, embed_width)
+    shared = next(step for step in range(bit_count + 1) if all(order[step:] == orders[0][step:] for order in orders))
+    beside = (1, bit_count - 1)
+    half = embed_width // 2
     embed_grad = None
     for step in range(bit_count):
+        if step in beside:
+            parts, grad_pre = lax.optimization_barrier((parts, grad_pre))
+            embed_grad = embed_part(beside.index(step) * half, half, grad_pre, weight_in, embed_grad)
+        elif step > 0:
+            parts = lax.optimization_barrier(parts)
         came = [exchange(sent, order[step]) for (sent, _), order in zip(parts, orders)]
         if step == 0:
             came, grad_pre = lax.optimization_barrier((came, grad_pre))
-        elif step < len(cuts):
+        elif step in beside:
             came, embed_grad = lax.optimization_barrier((came, embed_grad))
         else:
             came = lax.optimization_barrier(came)
@@ -870,12 +876,7 @@
             bits.remove(order[step + 1])
         parts = fold_halves(place[None], digits, step + 1 == shared, kept, came)
         if step + 1 == shared:
-            left, orders = left[1:], orders[1:]
-        if step + 1 < len(cuts):
-            parts, grad_pre = lax.optimization_barrier((parts, grad_pre))
-            embed_grad = embed_part(cuts[step], cuts[step + 1] - cuts[step], grad_pre, weight_in, embed_grad)
-        else:
-            parts = lax.optimization_barrier(parts)
+            left, orders = left[:1], orders[:1]
     summed = finish(1.0 / math.sqrt(nodes * peers), kept, came)
     return (embed_grad, summed)
 

time: 87.8 us -> 86.3 us (0.983)
  transfers between devices with their start and end apart: 15 -> 15, of which waited for: 3 -> 1; matrix products, arithmetic and copies ran while one was open for 0% -> 0% of each run, Pallas kernels for 57% -> 58%
where the time goes in v7:
time: 86.3 us; the launch traced here: 86 us
  Pallas kernels  54.2 us (63%)
  starting transfers between devices  27.5 us (32%)
  waiting for transfers between devices  3.46 us (4%)
    pallas_call x1, Pallas kernels, forward(): pl.pallas_call(forward_kernel, in_specs=[SMEM] * 2 + [HBM] * 8, out_specs...  16.5 us
    ppermute x10, starting transfers between devices, exchange(): lax.ppermute(sent, 'dom', [(device, device ^ 1 << bit) for device in rang...  13.4 us
    pallas_call x2, Pallas kernels, embed_part(): pl.pallas_call(functools.partial(embed_kernel, chunk, first), in_specs=[H...  10.1 us
    pallas_call x1, Pallas kernels, received_part(): pl.pallas_call(received_kernel, in_specs=[SMEM] + [HBM] * 7, out_specs=(H...  8.4 us
    pallas_call x1, Pallas kernels, slope_part(): pl.pallas_call(functools.partial(slope_kernel, chunk), in_specs=[HBM] * 6...  7.88 us
    all_to_all x1, starting transfers between devices, body(): lax.all_to_all(outgoing.reshape(peers, slots, -1), both, split_axis=0, co...  7.42 us
    pallas_call x1, Pallas kernels, product(): pl.pallas_call(functools.partial(product_kernel, streams, chunk), in_spec...  7.26 us
    all_to_all x1, starting transfers between devices, body(): lax.all_to_all(returned.reshape(peers, slots, width), both, split_axis=0,...  5.86 us
  transfers between devices with their start and end apart: 15, of which 1 were waited for; matrix products, arithmetic and copies ran while one was open for 0% of the time, Pallas kernels for 58%

profile of v7, /device:TPU:0, one launch (start us, length us, event | category | flops | bytes accessed | tf_op | source)
XLA Modules:
  0.0 86.0 jit_solution(6513821225958403176)
XLA Ops:
  0.6 2.8 %prepare.1 = (bf16[256,1152]{1,0:T(8,128)(2,1)}, bf16[256,512]{1,0:T(8,128)(2,1)}, f32[512,128]{1,0:T(8,128)}) custom-call(s32[8,32]{1,0:T(8,128)} %bitcast.13, s32[1,32]{1,0:T(1,128)} %count_any.1, bf16[4,8,128,128]{3,2,1,0:T(8,128)(2,1)} %tiles_any.3, bf16[512,1024]{1,0:T(8,128)(2,1)} %x_any.1), custom_call_target="tpu_custom_call" | custom-call | tf_op jit(solution)/shard_map/prepare/pallas_call | solution.py:134
  3.4 7.4 %all-to-all-start = ((bf16[32,8,1152]{2,1,0:T(8,128)(2,1)}), bf16[32,8,1152]{2,1,0:T(8,128)(2,1)}, u32[]{:S(2)}, u32[]{:S(2)}) async-start(bf16[32,8,1152]{2,1,0:T(8,128)(2,1)} %bitcast.11), calls=%async_computation | async-start | bytes 1179648 | tf_op jit(solution)/shard_map/all_to_all | solution.py:810
  10.9 16.5 %forward.1 = (bf16[512,4096]{1,0:T(8,128)(2,1)}, bf16[512,2048]{1,0:T(8,128)(2,1)}, bf16[512,2048]{1,0:T(8,128)(2,1)}, f32[512,512]{1,0:T(8,128)}, bf16[2,512,256]{2,1,0:T(8,128)(2,1)}, /*index=5*/f32[256,640]{1,0:T(8,128)}) custom-call(s32[1]{0:T(128)} %bitcast.1.rep_ref, s32[4,8]{1,0:T(4,128)} %column_ref.1, bf16[512,1024]{1,0:T(8,128)(2,1)} %x_any.1, ...), custom_call_target="tpu_custom_call" | custom-call | tf_op jit(solution)/shard_map/forward/pallas_call | solution.py:344
  27.4 0.3 collective-permute-start.1
  27.7 0.0 all-to-all-done
  27.7 8.4 %received_part.1 = (bf16[256,2048]{1,0:T(8,128)(2,1)}, bf16[256,2048]{1,0:T(8,128)(2,1)}, f32[512,512]{1,0:T(8,128)}, bf16[512,768]{1,0:T(8,128)(2,1)}, bf16[256,512]{1,0:T(8,128)(2,1)}) custom-call(s32[1]{0:T(128)} %bitcast.1.rep_ref, bf16[256,1152]{1,0:T(8,128)(2,1)} %bitcast.5.x_any, bf16[1024,4096]{1,0:T(8,128)(2,1)} %win_any.7, ...), custom_call_target="tpu_custom_call" | custom-call | tf_op jit(solution)/shard_map/received_part/pallas_call | solution.py:463
  36.1 0.4 collective-permute-start.2
  36.5 0.2 collective-permute-start
  36.7 5.9 %all-to-all-start.1 = ((bf16[32,8,512]{2,1,0:T(8,128)(2,1)}), bf16[32,8,512]{2,1,0:T(8,128)(2,1)}, u32[]{:S(2)}, u32[]{:S(2)}) async-start(bf16[32,8,512]{2,1,0:T(8,128)(2,1)} %bitcast.12), calls=%async_computation.1 | async-start | bytes 524288 | tf_op jit(solution)/shard_map/all_to_all | solution.py:832
  42.5 0.0 collective-permute-done.refs_1_
  42.6 0.0 collective-permute-done.1.refs_4_
  42.6 0.0 collective-permute-done.2.refs_5_
  42.6 7.3 %product.1 = (bf16[8,176,128]{2,1,0:T(8,128)(2,1)}, f32[8,176,128]{2,1,0:T(8,128)}, bf16[8,176,128]{2,1,0:T(8,128)(2,1)}, f32[8,176,128]{2,1,0:T(8,128)}, bf16[8...) custom-call(s32[1]{0:T(128)} %bitcast.place_ref, bf16[512,768]{1,0:T(8,128)(2,1)} %get-tuple-element.71.refs_0_, ...), custom_call_target="tpu_custom_call" | custom-call | tf_op jit(solution)/shard_map/product/pallas_call | solution.py:643
  49.8 1.8 %collective-permute-start.3 = (bf16[8,176,128]{2,1,0:T(8,128)(2,1)}, bf16[8,176,128]{2,1,0:T(8,128)(2,1)S(1)}, u32[]{:S(2)}, u32[]{:S(2)}) collective-permute-start(bf16[8,176,128]{2,1,0:T(8,128)(2,1)} %get-tuple-element.84), channel_id=1, source_target_pairs={{0,2},{2,0},{4,6},{6,4},{8,10},{10,8},{12,14},{14,12},{16,18},{18,... | collective-permute-start | bytes 1081352 | tf_op jit(solution)/shard_map/ppermute | solution.py:778
  51.6 1.5 %collective-permute-start.4 = (bf16[8,176,128]{2,1,0:T(8,128)(2,1)}, bf16[8,176,128]{2,1,0:T(8,128)(2,1)S(1)}, u32[]{:S(2)}, u32[]{:S(2)}) collective-permute-start(bf16[8,176,128]{2,1,0:T(8,128)(2,1)} %get-tuple-element.85), channel_id=1, source_target_pairs={{0,4},{2,6},{4,0},{6,2},{8,12},{10,14},{12,8},{14,10},{16,20},{18,... | collective-permute-start | bytes 1081352 | tf_op jit(solution)/shard_map/ppermute | solution.py:778
  53.1 1.5 %collective-permute-start.5 = (bf16[8,160,128]{2,1,0:T(8,128)(2,1)}, bf16[8,160,128]{2,1,0:T(8,128)(2,1)S(1)}, u32[]{:S(2)}, u32[]{:S(2)}) collective-permute-start(bf16[8,160,128]{2,1,0:T(8,128)(2,1)} %get-tuple-element.86), channel_id=1, source_target_pairs={{0,8},{2,10},{4,12},{6,14},{8,0},{10,2},{12,4},{14,6},{16,24},{18,... | collective-permute-start | bytes 983048 | tf_op jit(solution)/shard_map/ppermute | solution.py:778
  54.5 0.0 all-to-all-done.1
  54.5 0.0 copy-start
  54.5 0.0 copy-start.1
  54.5 0.0 copy-start.2
  54.5 7.9 %slope_part.1.grad_any = bf16[512,4096]{1,0:T(8,128)(2,1)} custom-call(f32[512,512]{1,0:T(8,128)} %get-tuple-element.87.refs_0_, bf16[256,512]{1,0:T(8,128)(2,1)} %get-tuple-element.88.refs_1_, bf16[256,512]{1,0:T(8,128)(2,1)} %bitcast.9.refs_2_, f32[512,128]{1,0:T(8,128)} %get-tuple-element.67.side_any.refs_3_, ...), custom_call_target="tpu_custom_call" | custom-call | flops 2147483648 | bytes 16777216 | tf_op jit(solution)/shard_map/slope_part/pallas_call | solution.py:694
  62.4 0.0 collective-permute-done.5.refs_5_
  62.5 0.0 collective-permute-done.3.refs_1_
  62.5 0.0 collective-permute-done.4.refs_3_
  62.5 0.0 copy-done
  62.5 0.0 copy-done.1
  62.5 0.0 copy-done.2
  62.5 0.2 fold_halves.3
  62.7 0.6 collective-permute-start.8
  63.4 1.0 %collective-permute-start.6 = (bf16[4,176,128]{2,1,0:T(8,128)(2,1)S(1)}, bf16[4,176,128]{2,1,0:T(8,128)(2,1)S(1)}, u32[]{:S(2)}, u32[]{:S(2)}) collective-permute-start(bf16[4,176,128]{2,1,0:T(8,128)(2,1)S(1)} %get-tuple-element.104), channel_id=1, source_target_pairs={{0,4},{2,6},{4,0},{6,2},{8,12},{10,14},{12,8},{14,10},{16,20},{18,... | collective-permute-start | bytes 540680 | tf_op jit(solution)/shard_map/ppermute | solution.py:778
  64.3 1.5 %collective-permute-start.7 = (bf16[4,176,128]{2,1,0:T(8,128)(2,1)S(1)}, bf16[4,176,128]{2,1,0:T(8,128)(2,1)S(1)}, u32[]{:S(2)}, u32[]{:S(2)}) collective-permute-start(bf16[4,176,128]{2,1,0:T(8,128)(2,1)S(1)} %get-tuple-element.105), channel_id=1, source_target_pairs={{0,8},{2,10},{4,12},{6,14},{8,0},{10,2},{12,4},{14,6},{16,24},{18,... | collective-permute-start | bytes 540680 | tf_op jit(solution)/shard_map/ppermute | solution.py:778
  65.8 5.1 %embed_part.2.refs_0_ = bf16[512,1024]{1,0:T(8,128)(2,1)} custom-call(bf16[512,4096]{1,0:T(8,128)(2,1)} %slope_part.1.grad_any, bf16[1024,4096]{1,0:T(8,128)(2,1)} %win_any.7), custom_call_target="tpu_custom_call" | custom-call | flops 2147483648 | bytes 9437184 | tf_op jit(solution)/shard_map/embed_part/pallas_call | solution.py:738
  70.9 0.0 collective-permute-done.8.refs_5_
  70.9 0.0 collective-permute-done.6.refs_1_
  70.9 0.0 collective-permute-done.7.refs_3_
  70.9 0.1 fold_halves.4
  71.0 0.6 collective-permute-start.9
  71.6 1.5 %collective-permute-start.10 = (bf16[2,176,128]{2,1,0:T(8,128)(2,1)S(1)}, bf16[2,176,128]{2,1,0:T(8,128)(2,1)S(1)}, u32[]{:S(2)}, u32[]{:S(2)}) collective-permute-start(bf16[2,176,128]{2,1,0:T(8,128)(2,1)S(1)} %get-tuple-element.115), channel_id=1, source_target_pairs={{0,2},{2,0},{4,6},{6,4},{8,10},{10,8},{12,14},{14,12},{16,18},{18,... | collective-permute-start | bytes 270344 | tf_op jit(solution)/shard_map/ppermute | solution.py:778
  73.1 1.1 %collective-permute-start.11 = (bf16[2,160,128]{2,1,0:T(8,128)(2,1)S(1)}, bf16[2,160,128]{2,1,0:T(8,128)(2,1)S(1)}, u32[]{:S(2)}, u32[]{:S(2)}) collective-permute-start(bf16[2,160,128]{2,1,0:T(8,128)(2,1)S(1)} %get-tuple-element.116), channel_id=1, source_target_pairs={{0,4},{2,6},{4,0},{6,2},{8,12},{10,14},{12,8},{14,10},{16,20},{18,... | collective-permute-start | bytes 245768 | tf_op jit(solution)/shard_map/ppermute | solution.py:778
  74.2 3.4 %collective-permute-done.11.refs_5_ = bf16[2,160,128]{2,1,0:T(8,128)(2,1)S(1)} collective-permute-done((bf16[2,160,128]{2,1,0:T(8,128)(2,1)S(1)}, bf16[2,160,128]{2,1,0:T(8,128)(2,1)S(1)}, u32[]{:S(2)}, u32[]{:S(2)}) %collective-permute-start.11) | collective-permute-done | bytes 81952 | tf_op jit(solution)/shard_map/ppermute | solution.py:778
  77.5 0.0 collective-permute-done.9.refs_1_
  77.5 0.0 collective-permute-done.10.refs_3_
  77.5 0.1 fold_halves.5
  77.6 2.5 %collective-permute-start.12 = (bf16[1,512,128]{2,1,0:T(8,128)(2,1)S(1)}, bf16[1,512,128]{2,1,0:T(8,128)(2,1)S(1)}, u32[]{:S(2)}, u32[]{:S(2)}) collective-permute-start(bf16[1,512,128]{2,1,0:T(8,128)(2,1)S(1)} %get-tuple-element.124), channel_id=1, source_target_pairs={{0,16},{2,18},{4,20},{6,22},{8,24},{10,26},{12,28},{14,30},{16,0},... | collective-permute-start | bytes 393224 | tf_op jit(solution)/shard_map/ppermute | solution.py:778
  80.1 5.1 %embed_part.3 = bf16[512,1024]{1,0:T(8,128)(2,1)} custom-call(bf16[512,4096]{1,0:T(8,128)(2,1)} %slope_part.1.grad_any, bf16[1024,4096]{1,0:T(8,128)(2,1)} %win_any.7, bf16[512,1024]{1,0:T(8,128)(2,1)} %embed_part.2.refs_0_), custom_call_target="tpu_custom_call", output_to_operand_aliasing={{}: (2, {})} | custom-call | flops 2147483648 | bytes 9437184 | tf_op jit(solution)/shard_map/embed_part/pallas_call | solution.py:738
  85.1 0.0 collective-permute-done.12.refs_1_
  85.2 0.8 finish.1
Async XLA Ops:
  3.4 24.2 %all-to-all-start = ((bf16[32,8,1152]{2,1,0:T(8,128)(2,1)}), bf16[32,8,1152]{2,1,0:T(8,128)(2,1)}, u32[]{:S(2)}, u32[]{:S(2)}) async-start(bf16[32,8,1152]{2,1,0:T(8,128)(2,1)} %bitcast.11), calls=%async_computation | async-start | bytes 1179648 | tf_op jit(solution)/shard_map/all_to_all | solution.py:810
  27.4 15.1 %collective-permute-start.1 = (bf16[512,2048]{1,0:T(8,128)(2,1)}, bf16[512,2048]{1,0:T(8,128)(2,1)}, u32[]{:S(2)}, u32[]{:S(2)}) collective-permute-start(bf16[512,2048]{1,0:T(8,128)(2,1)} %get-tuple-element.74), channel_id=1, source_target_pairs={{0,1},{1,0},{2,3},{3,2},{4,5},{5,4},{6,7},{7,6},{8,9},{9,8},{10,11... | collective-permute-start | bytes 6291464 | tf_op jit(solution)/shard_map/ppermute | solution.py:826
  36.1 6.5 %collective-permute-start.2 = (bf16[256,2048]{1,0:T(8,128)(2,1)}, bf16[256,2048]{1,0:T(8,128)(2,1)}, u32[]{:S(2)}, u32[]{:S(2)}) collective-permute-start(bf16[256,2048]{1,0:T(8,128)(2,1)} %get-tuple-element.75), channel_id=1, source_target_pairs={{0,1},{1,0},{2,3},{3,2},{4,5},{5,4},{6,7},{7,6},{8,9},{9,8},{10,11... | collective-permute-start | bytes 3145736 | tf_op jit(solution)/shard_map/ppermute | solution.py:831
  36.5 6.1 %collective-permute-start = (bf16[512,768]{1,0:T(8,128)(2,1)}, bf16[512,768]{1,0:T(8,128)(2,1)}, u32[]{:S(2)}, u32[]{:S(2)}) collective-permute-start(bf16[512,768]{1,0:T(8,128)(2,1)} %get-tuple-element.71.refs_0_), channel_id=1, source_target_pairs={{0,1},{1,0},{2,3},{3,2},{4,5},{5,4},{6,7},{7,6},{8,9},{9,8},{10,11... | collective-permute-start | bytes 2359304 | tf_op jit(solution)/shard_map/ppermute | solution.py:830
  36.7 17.9 %all-to-all-start.1 = ((bf16[32,8,512]{2,1,0:T(8,128)(2,1)}), bf16[32,8,512]{2,1,0:T(8,128)(2,1)}, u32[]{:S(2)}, u32[]{:S(2)}) async-start(bf16[32,8,512]{2,1,0:T(8,128)(2,1)} %bitcast.12), calls=%async_computation.1 | async-start | bytes 524288 | tf_op jit(solution)/shard_map/all_to_all | solution.py:832
  49.8 12.6 %collective-permute-start.3 = (bf16[8,176,128]{2,1,0:T(8,128)(2,1)}, bf16[8,176,128]{2,1,0:T(8,128)(2,1)S(1)}, u32[]{:S(2)}, u32[]{:S(2)}) collective-permute-start(bf16[8,176,128]{2,1,0:T(8,128)(2,1)} %get-tuple-element.84), channel_id=1, source_target_pairs={{0,2},{2,0},{4,6},{6,4},{8,10},{10,8},{12,14},{14,12},{16,18},{18,... | collective-permute-start | bytes 1081352 | tf_op jit(solution)/shard_map/ppermute | solution.py:778
  51.6 10.9 %collective-permute-start.4 = (bf16[8,176,128]{2,1,0:T(8,128)(2,1)}, bf16[8,176,128]{2,1,0:T(8,128)(2,1)S(1)}, u32[]{:S(2)}, u32[]{:S(2)}) collective-permute-start(bf16[8,176,128]{2,1,0:T(8,128)(2,1)} %get-tuple-element.85), channel_id=1, source_target_pairs={{0,4},{2,6},{4,0},{6,2},{8,12},{10,14},{12,8},{14,10},{16,20},{18,... | collective-permute-start | bytes 1081352 | tf_op jit(solution)/shard_map/ppermute | solution.py:778
  53.1 9.4 %collective-permute-start.5 = (bf16[8,160,128]{2,1,0:T(8,128)(2,1)}, bf16[8,160,128]{2,1,0:T(8,128)(2,1)S(1)}, u32[]{:S(2)}, u32[]{:S(2)}) collective-permute-start(bf16[8,160,128]{2,1,0:T(8,128)(2,1)} %get-tuple-element.86), channel_id=1, source_target_pairs={{0,8},{2,10},{4,12},{6,14},{8,0},{10,2},{12,4},{14,6},{16,24},{18,... | collective-permute-start | bytes 983048 | tf_op jit(solution)/shard_map/ppermute | solution.py:778
  54.5 8.0 %copy-start = (f32[8,176,128]{2,1,0:T(8,128)S(1)}, f32[8,176,128]{2,1,0:T(8,128)}, u32[]{:S(2)}) copy-start(f32[8,176,128]{2,1,0:T(8,128)} %get-tuple-element.83.refs_0_) | copy-start | bytes 2162692
  54.5 8.0 %copy-start.1 = (f32[8,176,128]{2,1,0:T(8,128)S(1)}, f32[8,176,128]{2,1,0:T(8,128)}, u32[]{:S(2)}) copy-start(f32[8,176,128]{2,1,0:T(8,128)} %get-tuple-element.92.refs_2_) | copy-start | bytes 2162692
  54.5 8.0 %copy-start.2 = (f32[8,160,128]{2,1,0:T(8,128)S(1)}, f32[8,160,128]{2,1,0:T(8,128)}, u32[]{:S(2)}) copy-start(f32[8,160,128]{2,1,0:T(8,128)} %get-tuple-element.94.refs_4_) | copy-start | bytes 1966084
  62.7 8.1 %collective-permute-start.8 = (bf16[4,160,128]{2,1,0:T(8,128)(2,1)S(1)}, bf16[4,160,128]{2,1,0:T(8,128)(2,1)S(1)}, u32[]{:S(2)}, u32[]{:S(2)}) collective-permute-start(bf16[4,160,128]{2,1,0:T(8,128)(2,1)S(1)} %get-tuple-element.106), channel_id=1, source_target_pairs={{0,2},{2,0},{4,6},{6,4},{8,10},{10,8},{12,14},{14,12},{16,18},{18,... | collective-permute-start | bytes 491528 | tf_op jit(solution)/shard_map/ppermute | solution.py:778
  63.4 7.5 %collective-permute-start.6 = (bf16[4,176,128]{2,1,0:T(8,128)(2,1)S(1)}, bf16[4,176,128]{2,1,0:T(8,128)(2,1)S(1)}, u32[]{:S(2)}, u32[]{:S(2)}) collective-permute-start(bf16[4,176,128]{2,1,0:T(8,128)(2,1)S(1)} %get-tuple-element.104), channel_id=1, source_target_pairs={{0,4},{2,6},{4,0},{6,2},{8,12},{10,14},{12,8},{14,10},{16,20},{18,... | collective-permute-start | bytes 540680 | tf_op jit(solution)/shard_map/ppermute | solution.py:778
  64.3 6.6 %collective-permute-start.7 = (bf16[4,176,128]{2,1,0:T(8,128)(2,1)S(1)}, bf16[4,176,128]{2,1,0:T(8,128)(2,1)S(1)}, u32[]{:S(2)}, u32[]{:S(2)}) collective-permute-start(bf16[4,176,128]{2,1,0:T(8,128)(2,1)S(1)} %get-tuple-element.105), channel_id=1, source_target_pairs={{0,8},{2,10},{4,12},{6,14},{8,0},{10,2},{12,4},{14,6},{16,24},{18,... | collective-permute-start | bytes 540680 | tf_op jit(solution)/shard_map/ppermute | solution.py:778
  71.0 6.5 %collective-permute-start.9 = (bf16[2,176,128]{2,1,0:T(8,128)(2,1)S(1)}, bf16[2,176,128]{2,1,0:T(8,128)(2,1)S(1)}, u32[]{:S(2)}, u32[]{:S(2)}) collective-permute-start(bf16[2,176,128]{2,1,0:T(8,128)(2,1)S(1)} %get-tuple-element.114), channel_id=1, source_target_pairs={{0,8},{2,10},{4,12},{6,14},{8,0},{10,2},{12,4},{14,6},{16,24},{18,... | collective-permute-start | bytes 270344 | tf_op jit(solution)/shard_map/ppermute | solution.py:778
  71.6 5.9 %collective-permute-start.10 = (bf16[2,176,128]{2,1,0:T(8,128)(2,1)S(1)}, bf16[2,176,128]{2,1,0:T(8,128)(2,1)S(1)}, u32[]{:S(2)}, u32[]{:S(2)}) collective-permute-start(bf16[2,176,128]{2,1,0:T(8,128)(2,1)S(1)} %get-tuple-element.115), channel_id=1, source_target_pairs={{0,2},{2,0},{4,6},{6,4},{8,10},{10,8},{12,14},{14,12},{16,18},{18,... | collective-permute-start | bytes 270344 | tf_op jit(solution)/shard_map/ppermute | solution.py:778
  73.1 4.4 %collective-permute-start.11 = (bf16[2,160,128]{2,1,0:T(8,128)(2,1)S(1)}, bf16[2,160,128]{2,1,0:T(8,128)(2,1)S(1)}, u32[]{:S(2)}, u32[]{:S(2)}) collective-permute-start(bf16[2,160,128]{2,1,0:T(8,128)(2,1)S(1)} %get-tuple-element.116), channel_id=1, source_target_pairs={{0,4},{2,6},{4,0},{6,2},{8,12},{10,14},{12,8},{14,10},{16,20},{18,... | collective-permute-start | bytes 245768 | tf_op jit(solution)/shard_map/ppermute | solution.py:778
  77.6 7.5 %collective-permute-start.12 = (bf16[1,512,128]{2,1,0:T(8,128)(2,1)S(1)}, bf16[1,512,128]{2,1,0:T(8,128)(2,1)S(1)}, u32[]{:S(2)}, u32[]{:S(2)}) collective-permute-start(bf16[1,512,128]{2,1,0:T(8,128)(2,1)S(1)} %get-tuple-element.124), channel_id=1, source_target_pairs={{0,16},{2,18},{4,20},{6,22},{8,24},{10,26},{12,28},{14,30},{16,0},... | collective-permute-start | bytes 393224 | tf_op jit(solution)/shard_map/ppermute | solution.py:778

commit v8 on v7

--- a/solution.py
+++ b/solution.py
@@ -488,14 +488,16 @@
 
 
 def chip_total(chunk, copies, arrays, turned_ref, hidden_ref, total_ref, arrive):
-    steps = range(0, hidden_ref.shape[1], chunk)
+    hidden = hidden_ref.shape[1]
+    edges = [0] + list(range(chunk // 2, hidden, chunk)) + [hidden]
+    steps = list(zip(edges[:-1], edges[1:]))
     base = 0
     for index in range(2):
         length = arrays[index].shape[1]
         copies.start(index, arrays[index], turned_ref.at[:, pl.ds(base, length)])
         base += length
-    for start in steps:
-        place = pl.ds(start, chunk)
+    for start, end in steps:
+        place = pl.ds(start, end - start)
         base = 0
         for index in range(2, 6):
             length = arrays[index].shape[0]
@@ -503,12 +505,12 @@
             base += length
     copies.wait(0)
     copies.wait(1)
-    for start in steps:
+    for start, end in steps:
         for index in range(2, 6):
             copies.wait((index, start))
         arrive(start // LANES)
-        total = dot(turned_ref[...], hidden_ref[:, start : start + chunk])
-        for step in range(chunk // LANES):
+        total = dot(turned_ref[...], hidden_ref[:, start:end])
+        for step in range((end - start) // LANES):
             total_ref[start // LANES + step] = total[:, step * LANES : (step + 1) * LANES]
 
 
@@ -616,7 +618,7 @@
     )(*[array for pair in zip(kept, came) for array in pair])
 
 
-def product(place, streams, operands, chunk=512):
+def product(place, streams, operands, chunk=1024):
     width = operands[0].shape[0]
     hidden = operands[2].shape[1]
     blocks = hidden // LANES
@@ -625,7 +627,7 @@
     scratch = [
         pltpu.VMEM((width, rows), jnp.bfloat16),
         pltpu.VMEM((rows, hidden), jnp.bfloat16),
-        pltpu.SemaphoreType.DMA((2 + 10 * (hidden // chunk),)),
+        pltpu.SemaphoreType.DMA((2 + 10 * (hidden // chunk + 1),)),
     ]
     if not streams:
         return pl.pallas_call(
@@ -763,8 +765,7 @@
 
 
 def streams_of(dom_count, width):
-    cut = width * 11 // 32
-    edges = (0, cut, 2 * cut, width)
+    edges = (0, width * 12 // 32, width * 23 // 32, width)
     return tuple(zip(bit_orders(dom_count), edges[:-1], edges[1:]))
 
 

time: 86.3 us -> 86.1 us (level)
  no operation moved by 1% of the time
where the time goes in v8:
time: 86.1 us; the launch traced here: 85.8 us
  Pallas kernels  54.2 us (63%)
  starting transfers between devices  27.5 us (32%)
  waiting for transfers between devices  3.34 us (4%)
    pallas_call x1, Pallas kernels, forward(): pl.pallas_call(forward_kernel, in_specs=[SMEM] * 2 + [HBM] * 8, out_specs...  16.5 us
    ppermute x10, starting transfers between devices, exchange(): lax.ppermute(sent, 'dom', [(device, device ^ 1 << bit) for device in rang...  13.4 us
    pallas_call x2, Pallas kernels, embed_part(): pl.pallas_call(functools.partial(embed_kernel, chunk, first), in_specs=[H...  10.1 us
    pallas_call x1, Pallas kernels, received_part(): pl.pallas_call(received_kernel, in_specs=[SMEM] + [HBM] * 7, out_specs=(H...  8.4 us
    pallas_call x1, Pallas kernels, slope_part(): pl.pallas_call(functools.partial(slope_kernel, chunk), in_specs=[HBM] * 6...  7.89 us
    all_to_all x1, starting transfers between devices, body(): lax.all_to_all(outgoing.reshape(peers, slots, -1), both, split_axis=0, co...  7.42 us
    pallas_call x1, Pallas kernels, product(): pl.pallas_call(functools.partial(product_kernel, streams, chunk), in_spec...  7.22 us
    all_to_all x1, starting transfers between devices, body(): lax.all_to_all(returned.reshape(peers, slots, width), both, split_axis=0,...  5.86 us
  transfers between devices with their start and end apart: 15, of which 1 were waited for; matrix products, arithmetic and copies ran while one was open for 0% of the time, Pallas kernels for 58%

profile of v8, /device:TPU:0, one launch (start us, length us, event | category | flops | bytes accessed | tf_op | source)
XLA Modules:
  0.0 85.8 jit_solution(7138459777281016565)
XLA Ops:
  0.6 2.8 %prepare.1 = (bf16[256,1152]{1,0:T(8,128)(2,1)}, bf16[256,512]{1,0:T(8,128)(2,1)}, f32[512,128]{1,0:T(8,128)}) custom-call(s32[8,32]{1,0:T(8,128)} %bitcast.13, s32[1,32]{1,0:T(1,128)} %count_any.1, bf16[4,8,128,128]{3,2,1,0:T(8,128)(2,1)} %tiles_any.3, bf16[512,1024]{1,0:T(8,128)(2,1)} %x_any.1), custom_call_target="tpu_custom_call" | custom-call | tf_op jit(solution)/shard_map/prepare/pallas_call | solution.py:134
  3.4 7.4 %all-to-all-start = ((bf16[32,8,1152]{2,1,0:T(8,128)(2,1)}), bf16[32,8,1152]{2,1,0:T(8,128)(2,1)}, u32[]{:S(2)}, u32[]{:S(2)}) async-start(bf16[32,8,1152]{2,1,0:T(8,128)(2,1)} %bitcast.11), calls=%async_computation | async-start | bytes 1179648 | tf_op jit(solution)/shard_map/all_to_all | solution.py:811
  10.9 16.5 %forward.1 = (bf16[512,4096]{1,0:T(8,128)(2,1)}, bf16[512,2048]{1,0:T(8,128)(2,1)}, bf16[512,2048]{1,0:T(8,128)(2,1)}, f32[512,512]{1,0:T(8,128)}, bf16[2,512,256]{2,1,0:T(8,128)(2,1)}, /*index=5*/f32[256,640]{1,0:T(8,128)}) custom-call(s32[1]{0:T(128)} %bitcast.1.rep_ref, s32[4,8]{1,0:T(4,128)} %column_ref.1, bf16[512,1024]{1,0:T(8,128)(2,1)} %x_any.1, ...), custom_call_target="tpu_custom_call" | custom-call | tf_op jit(solution)/shard_map/forward/pallas_call | solution.py:344
  27.4 0.3 collective-permute-start.1
  27.7 0.0 all-to-all-done
  27.7 8.4 %received_part.1 = (bf16[256,2048]{1,0:T(8,128)(2,1)}, bf16[256,2048]{1,0:T(8,128)(2,1)}, f32[512,512]{1,0:T(8,128)}, bf16[512,768]{1,0:T(8,128)(2,1)}, bf16[256,512]{1,0:T(8,128)(2,1)}) custom-call(s32[1]{0:T(128)} %bitcast.1.rep_ref, bf16[256,1152]{1,0:T(8,128)(2,1)} %bitcast.5.x_any, bf16[1024,4096]{1,0:T(8,128)(2,1)} %win_any.7, ...), custom_call_target="tpu_custom_call" | custom-call | tf_op jit(solution)/shard_map/received_part/pallas_call | solution.py:463
  36.1 0.4 collective-permute-start.2
  36.5 0.2 collective-permute-start
  36.7 5.9 %all-to-all-start.1 = ((bf16[32,8,512]{2,1,0:T(8,128)(2,1)}), bf16[32,8,512]{2,1,0:T(8,128)(2,1)}, u32[]{:S(2)}, u32[]{:S(2)}) async-start(bf16[32,8,512]{2,1,0:T(8,128)(2,1)} %bitcast.12), calls=%async_computation.1 | async-start | bytes 524288 | tf_op jit(solution)/shard_map/all_to_all | solution.py:833
  42.5 0.0 collective-permute-done.refs_1_
  42.6 0.0 collective-permute-done.1.refs_4_
  42.6 0.0 collective-permute-done.2.refs_5_
  42.6 7.2 %product.1 = (bf16[8,192,128]{2,1,0:T(8,128)(2,1)}, f32[8,192,128]{2,1,0:T(8,128)}, bf16[8,176,128]{2,1,0:T(8,128)(2,1)}, f32[8,176,128]{2,1,0:T(8,128)}, bf16[8...) custom-call(s32[1]{0:T(128)} %bitcast.place_ref, bf16[512,768]{1,0:T(8,128)(2,1)} %get-tuple-element.71.refs_0_, ...), custom_call_target="tpu_custom_call" | custom-call | tf_op jit(solution)/shard_map/product/pallas_call | solution.py:645
  49.8 1.8 %collective-permute-start.3 = (bf16[8,192,128]{2,1,0:T(8,128)(2,1)}, bf16[8,192,128]{2,1,0:T(8,128)(2,1)S(1)}, u32[]{:S(2)}, u32[]{:S(2)}) collective-permute-start(bf16[8,192,128]{2,1,0:T(8,128)(2,1)} %get-tuple-element.84), channel_id=1, source_target_pairs={{0,2},{2,0},{4,6},{6,4},{8,10},{10,8},{12,14},{14,12},{16,18},{18,... | collective-permute-start | bytes 1179656 | tf_op jit(solution)/shard_map/ppermute | solution.py:779
  51.6 1.5 %collective-permute-start.4 = (bf16[8,176,128]{2,1,0:T(8,128)(2,1)}, bf16[8,176,128]{2,1,0:T(8,128)(2,1)S(1)}, u32[]{:S(2)}, u32[]{:S(2)}) collective-permute-start(bf16[8,176,128]{2,1,0:T(8,128)(2,1)} %get-tuple-element.85), channel_id=1, source_target_pairs={{0,4},{2,6},{4,0},{6,2},{8,12},{10,14},{12,8},{14,10},{16,20},{18,... | collective-permute-start | bytes 1081352 | tf_op jit(solution)/shard_map/ppermute | solution.py:779
  53.0 1.5 %collective-permute-start.5 = (bf16[8,144,128]{2,1,0:T(8,128)(2,1)}, bf16[8,144,128]{2,1,0:T(8,128)(2,1)S(1)}, u32[]{:S(2)}, u32[]{:S(2)}) collective-permute-start(bf16[8,144,128]{2,1,0:T(8,128)(2,1)} %get-tuple-element.86), channel_id=1, source_target_pairs={{0,8},{2,10},{4,12},{6,14},{8,0},{10,2},{12,4},{14,6},{16,24},{18,... | collective-permute-start | bytes 884744 | tf_op jit(solution)/shard_map/ppermute | solution.py:779
  54.5 0.0 all-to-all-done.1
  54.5 0.0 copy-start
  54.5 0.0 copy-start.1
  54.5 0.0 copy-start.2
  54.5 7.9 %slope_part.1.grad_any = bf16[512,4096]{1,0:T(8,128)(2,1)} custom-call(f32[512,512]{1,0:T(8,128)} %get-tuple-element.87.refs_0_, bf16[256,512]{1,0:T(8,128)(2,1)} %get-tuple-element.88.refs_1_, bf16[256,512]{1,0:T(8,128)(2,1)} %bitcast.9.refs_2_, f32[512,128]{1,0:T(8,128)} %get-tuple-element.67.side_any.refs_3_, ...), custom_call_target="tpu_custom_call" | custom-call | flops 2147483648 | bytes 16777216 | tf_op jit(solution)/shard_map/slope_part/pallas_call | solution.py:696
  62.4 0.0 collective-permute-done.5.refs_5_
  62.4 0.0 collective-permute-done.4.refs_3_
  62.4 0.0 collective-permute-done.3.refs_1_
  62.4 0.0 copy-done
  62.4 0.0 copy-done.1
  62.5 0.0 copy-done.2
  62.5 0.2 fold_halves.3
  62.7 0.6 collective-permute-start.8
  63.3 1.4 %collective-permute-start.7 = (bf16[4,176,128]{2,1,0:T(8,128)(2,1)S(1)}, bf16[4,176,128]{2,1,0:T(8,128)(2,1)S(1)}, u32[]{:S(2)}, u32[]{:S(2)}) collective-permute-start(bf16[4,176,128]{2,1,0:T(8,128)(2,1)S(1)} %get-tuple-element.105), channel_id=1, source_target_pairs={{0,8},{2,10},{4,12},{6,14},{8,0},{10,2},{12,4},{14,6},{16,24},{18,... | collective-permute-start | bytes 540680 | tf_op jit(solution)/shard_map/ppermute | solution.py:779
  64.7 1.5 %collective-permute-start.6 = (bf16[4,192,128]{2,1,0:T(8,128)(2,1)S(1)}, bf16[4,192,128]{2,1,0:T(8,128)(2,1)S(1)}, u32[]{:S(2)}, u32[]{:S(2)}) collective-permute-start(bf16[4,192,128]{2,1,0:T(8,128)(2,1)S(1)} %get-tuple-element.104), channel_id=1, source_target_pairs={{0,4},{2,6},{4,0},{6,2},{8,12},{10,14},{12,8},{14,10},{16,20},{18,... | collective-permute-start | bytes 589832 | tf_op jit(solution)/shard_map/ppermute | solution.py:779
  66.2 5.1 %embed_part.2.refs_0_ = bf16[512,1024]{1,0:T(8,128)(2,1)} custom-call(bf16[512,4096]{1,0:T(8,128)(2,1)} %slope_part.1.grad_any, bf16[1024,4096]{1,0:T(8,128)(2,1)} %win_any.7), custom_call_target="tpu_custom_call" | custom-call | flops 2147483648 | bytes 9437184 | tf_op jit(solution)/shard_map/embed_part/pallas_call | solution.py:740
  71.2 0.0 collective-permute-done.8.refs_5_
  71.2 0.0 collective-permute-done.7.refs_3_
  71.2 0.0 collective-permute-done.6.refs_1_
  71.3 0.1 fold_halves.4
  71.4 0.6 collective-permute-start.9
  72.0 1.1 %collective-permute-start.10 = (bf16[2,176,128]{2,1,0:T(8,128)(2,1)S(1)}, bf16[2,176,128]{2,1,0:T(8,128)(2,1)S(1)}, u32[]{:S(2)}, u32[]{:S(2)}) collective-permute-start(bf16[2,176,128]{2,1,0:T(8,128)(2,1)S(1)} %get-tuple-element.115), channel_id=1, source_target_pairs={{0,2},{2,0},{4,6},{6,4},{8,10},{10,8},{12,14},{14,12},{16,18},{18,... | collective-permute-start | bytes 270344 | tf_op jit(solution)/shard_map/ppermute | solution.py:779
  73.0 1.0 %collective-permute-start.11 = (bf16[2,144,128]{2,1,0:T(8,128)(2,1)S(1)}, bf16[2,144,128]{2,1,0:T(8,128)(2,1)S(1)}, u32[]{:S(2)}, u32[]{:S(2)}) collective-permute-start(bf16[2,144,128]{2,1,0:T(8,128)(2,1)S(1)} %get-tuple-element.116), channel_id=1, source_target_pairs={{0,4},{2,6},{4,0},{6,2},{8,12},{10,14},{12,8},{14,10},{16,20},{18,... | collective-permute-start | bytes 221192 | tf_op jit(solution)/shard_map/ppermute | solution.py:779
  74.1 3.3 %collective-permute-done.11.refs_5_ = bf16[2,144,128]{2,1,0:T(8,128)(2,1)S(1)} collective-permute-done((bf16[2,144,128]{2,1,0:T(8,128)(2,1)S(1)}, bf16[2,144,128]{2,1,0:T(8,128)(2,1)S(1)}, u32[]{:S(2)}, u32[]{:S(2)}) %collective-permute-start.11) | collective-permute-done | bytes 73760 | tf_op jit(solution)/shard_map/ppermute | solution.py:779
  77.4 0.0 collective-permute-done.10.refs_3_
  77.4 0.0 collective-permute-done.9.refs_1_
  77.5 2.5 %collective-permute-start.12 = (bf16[1,512,128]{2,1,0:T(8,128)(2,1)S(1)}, bf16[1,512,128]{2,1,0:T(8,128)(2,1)S(1)}, u32[]{:S(2)}, u32[]{:S(2)}) collective-permute-start(bf16[1,512,128]{2,1,0:T(8,128)(2,1)S(1)} %get-tuple-element.124), channel_id=1, source_target_pairs={{0,16},{2,18},{4,20},{6,22},{8,24},{10,26},{12,28},{14,30},{16,0},... | collective-permute-start | bytes 393224 | tf_op jit(solution)/shard_map/ppermute | solution.py:779
  79.9 5.1 %embed_part.3 = bf16[512,1024]{1,0:T(8,128)(2,1)} custom-call(bf16[512,4096]{1,0:T(8,128)(2,1)} %slope_part.1.grad_any, bf16[1024,4096]{1,0:T(8,128)(2,1)} %win_any.7, bf16[512,1024]{1,0:T(8,128)(2,1)} %embed_part.2.refs_0_), custom_call_target="tpu_custom_call", output_to_operand_aliasing={{}: (2, {})} | custom-call | flops 2147483648 | bytes 9437184 | tf_op jit(solution)/shard_map/embed_part/pallas_call | solution.py:740
  85.0 0.0 collective-permute-done.12.refs_1_
  85.0 0.8 finish.1
  (1 shorter events, 0.0 us)
Async XLA Ops:
  3.4 24.2 %all-to-all-start = ((bf16[32,8,1152]{2,1,0:T(8,128)(2,1)}), bf16[32,8,1152]{2,1,0:T(8,128)(2,1)}, u32[]{:S(2)}, u32[]{:S(2)}) async-start(bf16[32,8,1152]{2,1,0:T(8,128)(2,1)} %bitcast.11), calls=%async_computation | async-start | bytes 1179648 | tf_op jit(solution)/shard_map/all_to_all | solution.py:811
  27.4 15.1 %collective-permute-start.1 = (bf16[512,2048]{1,0:T(8,128)(2,1)}, bf16[512,2048]{1,0:T(8,128)(2,1)}, u32[]{:S(2)}, u32[]{:S(2)}) collective-permute-start(bf16[512,2048]{1,0:T(8,128)(2,1)} %get-tuple-element.74), channel_id=1, source_target_pairs={{0,1},{1,0},{2,3},{3,2},{4,5},{5,4},{6,7},{7,6},{8,9},{9,8},{10,11... | collective-permute-start | bytes 6291464 | tf_op jit(solution)/shard_map/ppermute | solution.py:827
  36.1 6.5 %collective-permute-start.2 = (bf16[256,2048]{1,0:T(8,128)(2,1)}, bf16[256,2048]{1,0:T(8,128)(2,1)}, u32[]{:S(2)}, u32[]{:S(2)}) collective-permute-start(bf16[256,2048]{1,0:T(8,128)(2,1)} %get-tuple-element.75), channel_id=1, source_target_pairs={{0,1},{1,0},{2,3},{3,2},{4,5},{5,4},{6,7},{7,6},{8,9},{9,8},{10,11... | collective-permute-start | bytes 3145736 | tf_op jit(solution)/shard_map/ppermute | solution.py:832
  36.5 6.1 %collective-permute-start = (bf16[512,768]{1,0:T(8,128)(2,1)}, bf16[512,768]{1,0:T(8,128)(2,1)}, u32[]{:S(2)}, u32[]{:S(2)}) collective-permute-start(bf16[512,768]{1,0:T(8,128)(2,1)} %get-tuple-element.71.refs_0_), channel_id=1, source_target_pairs={{0,1},{1,0},{2,3},{3,2},{4,5},{5,4},{6,7},{7,6},{8,9},{9,8},{10,11... | collective-permute-start | bytes 2359304 | tf_op jit(solution)/shard_map/ppermute | solution.py:831
  36.7 17.8 %all-to-all-start.1 = ((bf16[32,8,512]{2,1,0:T(8,128)(2,1)}), bf16[32,8,512]{2,1,0:T(8,128)(2,1)}, u32[]{:S(2)}, u32[]{:S(2)}) async-start(bf16[32,8,512]{2,1,0:T(8,128)(2,1)} %bitcast.12), calls=%async_computation.1 | async-start | bytes 524288 | tf_op jit(solution)/shard_map/all_to_all | solution.py:833
  49.8 12.6 %collective-permute-start.3 = (bf16[8,192,128]{2,1,0:T(8,128)(2,1)}, bf16[8,192,128]{2,1,0:T(8,128)(2,1)S(1)}, u32[]{:S(2)}, u32[]{:S(2)}) collective-permute-start(bf16[8,192,128]{2,1,0:T(8,128)(2,1)} %get-tuple-element.84), channel_id=1, source_target_pairs={{0,2},{2,0},{4,6},{6,4},{8,10},{10,8},{12,14},{14,12},{16,18},{18,... | collective-permute-start | bytes 1179656 | tf_op jit(solution)/shard_map/ppermute | solution.py:779
  51.6 10.9 %collective-permute-start.4 = (bf16[8,176,128]{2,1,0:T(8,128)(2,1)}, bf16[8,176,128]{2,1,0:T(8,128)(2,1)S(1)}, u32[]{:S(2)}, u32[]{:S(2)}) collective-permute-start(bf16[8,176,128]{2,1,0:T(8,128)(2,1)} %get-tuple-element.85), channel_id=1, source_target_pairs={{0,4},{2,6},{4,0},{6,2},{8,12},{10,14},{12,8},{14,10},{16,20},{18,... | collective-permute-start | bytes 1081352 | tf_op jit(solution)/shard_map/ppermute | solution.py:779
  53.0 9.4 %collective-permute-start.5 = (bf16[8,144,128]{2,1,0:T(8,128)(2,1)}, bf16[8,144,128]{2,1,0:T(8,128)(2,1)S(1)}, u32[]{:S(2)}, u32[]{:S(2)}) collective-permute-start(bf16[8,144,128]{2,1,0:T(8,128)(2,1)} %get-tuple-element.86), channel_id=1, source_target_pairs={{0,8},{2,10},{4,12},{6,14},{8,0},{10,2},{12,4},{14,6},{16,24},{18,... | collective-permute-start | bytes 884744 | tf_op jit(solution)/shard_map/ppermute | solution.py:779
  54.5 7.9 %copy-start = (f32[8,192,128]{2,1,0:T(8,128)S(1)}, f32[8,192,128]{2,1,0:T(8,128)}, u32[]{:S(2)}) copy-start(f32[8,192,128]{2,1,0:T(8,128)} %get-tuple-element.83.refs_0_) | copy-start | bytes 2359300
  54.5 7.9 %copy-start.1 = (f32[8,176,128]{2,1,0:T(8,128)S(1)}, f32[8,176,128]{2,1,0:T(8,128)}, u32[]{:S(2)}) copy-start(f32[8,176,128]{2,1,0:T(8,128)} %get-tuple-element.92.refs_2_) | copy-start | bytes 2162692
  54.5 8.0 %copy-start.2 = (f32[8,144,128]{2,1,0:T(8,128)S(1)}, f32[8,144,128]{2,1,0:T(8,128)}, u32[]{:S(2)}) copy-start(f32[8,144,128]{2,1,0:T(8,128)} %get-tuple-element.94.refs_4_) | copy-start | bytes 1769476
  62.7 8.6 %collective-permute-start.8 = (bf16[4,144,128]{2,1,0:T(8,128)(2,1)S(1)}, bf16[4,144,128]{2,1,0:T(8,128)(2,1)S(1)}, u32[]{:S(2)}, u32[]{:S(2)}) collective-permute-start(bf16[4,144,128]{2,1,0:T(8,128)(2,1)S(1)} %get-tuple-element.106), channel_id=1, source_target_pairs={{0,2},{2,0},{4,6},{6,4},{8,10},{10,8},{12,14},{14,12},{16,18},{18,... | collective-permute-start | bytes 442376 | tf_op jit(solution)/shard_map/ppermute | solution.py:779
  63.3 8.0 %collective-permute-start.7 = (bf16[4,176,128]{2,1,0:T(8,128)(2,1)S(1)}, bf16[4,176,128]{2,1,0:T(8,128)(2,1)S(1)}, u32[]{:S(2)}, u32[]{:S(2)}) collective-permute-start(bf16[4,176,128]{2,1,0:T(8,128)(2,1)S(1)} %get-tuple-element.105), channel_id=1, source_target_pairs={{0,8},{2,10},{4,12},{6,14},{8,0},{10,2},{12,4},{14,6},{16,24},{18,... | collective-permute-start | bytes 540680 | tf_op jit(solution)/shard_map/ppermute | solution.py:779
  64.7 6.6 %collective-permute-start.6 = (bf16[4,192,128]{2,1,0:T(8,128)(2,1)S(1)}, bf16[4,192,128]{2,1,0:T(8,128)(2,1)S(1)}, u32[]{:S(2)}, u32[]{:S(2)}) collective-permute-start(bf16[4,192,128]{2,1,0:T(8,128)(2,1)S(1)} %get-tuple-element.104), channel_id=1, source_target_pairs={{0,4},{2,6},{4,0},{6,2},{8,12},{10,14},{12,8},{14,10},{16,20},{18,... | collective-permute-start | bytes 589832 | tf_op jit(solution)/shard_map/ppermute | solution.py:779
  71.4 6.0 %collective-permute-start.9 = (bf16[2,192,128]{2,1,0:T(8,128)(2,1)S(1)}, bf16[2,192,128]{2,1,0:T(8,128)(2,1)S(1)}, u32[]{:S(2)}, u32[]{:S(2)}) collective-permute-start(bf16[2,192,128]{2,1,0:T(8,128)(2,1)S(1)} %get-tuple-element.114), channel_id=1, source_target_pairs={{0,8},{2,10},{4,12},{6,14},{8,0},{10,2},{12,4},{14,6},{16,24},{18,... | collective-permute-start | bytes 294920 | tf_op jit(solution)/shard_map/ppermute | solution.py:779
  72.0 5.4 %collective-permute-start.10 = (bf16[2,176,128]{2,1,0:T(8,128)(2,1)S(1)}, bf16[2,176,128]{2,1,0:T(8,128)(2,1)S(1)}, u32[]{:S(2)}, u32[]{:S(2)}) collective-permute-start(bf16[2,176,128]{2,1,0:T(8,128)(2,1)S(1)} %get-tuple-element.115), channel_id=1, source_target_pairs={{0,2},{2,0},{4,6},{6,4},{8,10},{10,8},{12,14},{14,12},{16,18},{18,... | collective-permute-start | bytes 270344 | tf_op jit(solution)/shard_map/ppermute | solution.py:779
  73.0 4.4 %collective-permute-start.11 = (bf16[2,144,128]{2,1,0:T(8,128)(2,1)S(1)}, bf16[2,144,128]{2,1,0:T(8,128)(2,1)S(1)}, u32[]{:S(2)}, u32[]{:S(2)}) collective-permute-start(bf16[2,144,128]{2,1,0:T(8,128)(2,1)S(1)} %get-tuple-element.116), channel_id=1, source_target_pairs={{0,4},{2,6},{4,0},{6,2},{8,12},{10,14},{12,8},{14,10},{16,20},{18,... | collective-permute-start | bytes 221192 | tf_op jit(solution)/shard_map/ppermute | solution.py:779
  77.5 7.5 %collective-permute-start.12 = (bf16[1,512,128]{2,1,0:T(8,128)(2,1)S(1)}, bf16[1,512,128]{2,1,0:T(8,128)(2,1)S(1)}, u32[]{:S(2)}, u32[]{:S(2)}) collective-permute-start(bf16[1,512,128]{2,1,0:T(8,128)(2,1)S(1)} %get-tuple-element.124), channel_id=1, source_target_pairs={{0,16},{2,18},{4,20},{6,22},{8,24},{10,26},{12,28},{14,30},{16,0},... | collective-permute-start | bytes 393224 | tf_op jit(solution)/shard_map/ppermute | solution.py:779

commit v9 on v8

--- a/solution.py
+++ b/solution.py
@@ -187,12 +187,14 @@
         for step in range(self.count):
             place = pl.ds(step * chunk, chunk)
             copies.start(("in", step), win_any.at[:, place], win_ref.at[:, place])
-            copies.start(("out", step), wout_any.at[place], wout_ref.at[place])
+            if step % 2 == 0:
+                place = pl.ds(step * chunk, 2 * chunk)
+                copies.start(("out", step), wout_any.at[place], wout_ref.at[place])
 
     def wait(self, step):
         if step < self.count:
             self.copies.wait(("in", step))
-        if step > 0:
+        if step % 2 == 1:
             self.copies.wait(("out", step - 1))
 
 
@@ -250,15 +252,15 @@
     copies.wait("x")
 
     def give(step):
-        whole_place = pl.ds(step * chunk, chunk)
-        half_place = pl.ds(step * chunk // 2, chunk // 2)
+        whole_place = pl.ds((step - 1) * chunk, 2 * chunk)
+        half_place = pl.ds((step - 1) * chunk // 2, chunk)
         copies.start(("pre", step), pre_ref.at[:, whole_place], pre_any.at[:, whole_place])
         copies.start(("mine", step), mine_ref.at[:, half_place], mine_any.at[:, half_place])
         copies.start(("other", step), other_ref.at[:, half_place], other_any.at[:, half_place])
 
     def arrive(step):
         weights.wait(step)
-        if step > 1:
+        if step > 1 and step % 2 == 1:
             give(step - 2)
         if step == 0:
             copies.wait("tiles")
@@ -298,7 +300,7 @@
     pull = jnp.sum(label, axis=1, keepdims=True) * projected - dot(label.astype(jnp.bfloat16), target)
     grad_ref[...] = (rowsum * unit_float - neighbour + own) * scaling + pull
     copies.start("grad", grad_ref, grad_any)
-    for step in range(weights.count):
+    for step in range(1, weights.count, 2):
         for name in ("pre", "mine", "other"):
             copies.wait((name, step))
     for name in ("high", "low", "back", "grad"):
@@ -418,14 +420,16 @@
         copies.start(name, source, target)
     copies.wait("x")
 
+    group = 4
+
     def give(step):
-        place = pl.ds(step * chunk // 2, chunk // 2)
+        place = pl.ds((step + 1 - group) * chunk // 2, group * chunk // 2)
         copies.start(("mine", step), mine_ref.at[:, place], mine_any.at[:, place])
         copies.start(("other", step), other_ref.at[:, place], other_any.at[:, place])
 
     def arrive(step):
         weights.wait(step)
-        if step > 1:
+        if step > 1 and (step - 1) % group == 0:
             give(step - 2)
 
     def take(start, hidden, values, half, square):
@@ -447,7 +451,7 @@
     turned_ref[:, :nodes] = full.T.astype(jnp.bfloat16)
     turned_ref[:, nodes:] = (back.astype(jnp.float32) * scaling).T.astype(jnp.bfloat16)
     copies.start("turned", turned_ref, turned_any)
-    for step in range(weights.count):
+    for step in range(group - 1, weights.count, group):
         copies.wait(("mine", step))
         copies.wait(("other", step))
     for name in ("full", "return", "turned"):

time: 86.1 us -> 85.4 us (level)
  transfers between devices with their start and end apart: 15 -> 15, of which waited for: 1 -> 2; matrix products, arithmetic and copies ran while one was open for 0% -> 0% of each run, Pallas kernels for 58% -> 58%
where the time goes in v9:
time: 85.4 us; the launch traced here: 85.1 us
  Pallas kernels  53.4 us (63%)
  starting transfers between devices  26.8 us (31%)
  waiting for transfers between devices  4.05 us (5%)
    pallas_call x1, Pallas kernels, forward(): pl.pallas_call(forward_kernel, in_specs=[SMEM] * 2 + [HBM] * 8, out_specs...  15.8 us
    ppermute x10, starting transfers between devices, exchange(): lax.ppermute(sent, 'dom', [(device, device ^ 1 << bit) for device in rang...  13.4 us
    pallas_call x2, Pallas kernels, embed_part(): pl.pallas_call(functools.partial(embed_kernel, chunk, first), in_specs=[H...  10.1 us
    pallas_call x1, Pallas kernels, received_part(): pl.pallas_call(received_kernel, in_specs=[SMEM] + [HBM] * 7, out_specs=(H...  8.41 us
    pallas_call x1, Pallas kernels, slope_part(): pl.pallas_call(functools.partial(slope_kernel, chunk), in_specs=[HBM] * 6...  7.89 us
    all_to_all x1, starting transfers between devices, body(): lax.all_to_all(outgoing.reshape(peers, slots, -1), both, split_axis=0, co...  7.42 us
    pallas_call x1, Pallas kernels, product(): pl.pallas_call(functools.partial(product_kernel, streams, chunk), in_spec...  7.22 us
    all_to_all x1, starting transfers between devices, body(): lax.all_to_all(returned.reshape(peers, slots, width), both, split_axis=0,...  5.17 us
  transfers between devices with their start and end apart: 15, of which 2 were waited for; matrix products, arithmetic and copies ran while one was open for 0% of the time, Pallas kernels for 58%

profile of v9, /device:TPU:0, one launch (start us, length us, event | category | flops | bytes accessed | tf_op | source)
XLA Modules:
  0.0 85.1 jit_solution(3060147882623558505)
XLA Ops:
  0.6 2.8 %prepare.1 = (bf16[256,1152]{1,0:T(8,128)(2,1)}, bf16[256,512]{1,0:T(8,128)(2,1)}, f32[512,128]{1,0:T(8,128)}) custom-call(s32[8,32]{1,0:T(8,128)} %bitcast.13, s32[1,32]{1,0:T(1,128)} %count_any.1, bf16[4,8,128,128]{3,2,1,0:T(8,128)(2,1)} %tiles_any.3, bf16[512,1024]{1,0:T(8,128)(2,1)} %x_any.1), custom_call_target="tpu_custom_call" | custom-call | tf_op jit(solution)/shard_map/prepare/pallas_call | solution.py:134
  3.4 7.4 %all-to-all-start = ((bf16[32,8,1152]{2,1,0:T(8,128)(2,1)}), bf16[32,8,1152]{2,1,0:T(8,128)(2,1)}, u32[]{:S(2)}, u32[]{:S(2)}) async-start(bf16[32,8,1152]{2,1,0:T(8,128)(2,1)} %bitcast.11), calls=%async_computation | async-start | bytes 1179648 | tf_op jit(solution)/shard_map/all_to_all | solution.py:815
  10.9 15.8 %forward.1 = (bf16[512,4096]{1,0:T(8,128)(2,1)}, bf16[512,2048]{1,0:T(8,128)(2,1)}, bf16[512,2048]{1,0:T(8,128)(2,1)}, f32[512,512]{1,0:T(8,128)}, bf16[2,512,256]{2,1,0:T(8,128)(2,1)}, /*index=5*/f32[256,640]{1,0:T(8,128)}) custom-call(s32[1]{0:T(128)} %bitcast.1.rep_ref, s32[4,8]{1,0:T(4,128)} %column_ref.1, bf16[512,1024]{1,0:T(8,128)(2,1)} %x_any.1, ...), custom_call_target="tpu_custom_call" | custom-call | tf_op jit(solution)/shard_map/forward/pallas_call | solution.py:346
  26.6 0.2 collective-permute-start.1
  26.9 0.7 all-to-all-done
  27.6 8.4 %received_part.1 = (bf16[256,2048]{1,0:T(8,128)(2,1)}, bf16[256,2048]{1,0:T(8,128)(2,1)}, f32[512,512]{1,0:T(8,128)}, bf16[512,768]{1,0:T(8,128)(2,1)}, bf16[256,512]{1,0:T(8,128)(2,1)}) custom-call(s32[1]{0:T(128)} %bitcast.1.rep_ref, bf16[256,1152]{1,0:T(8,128)(2,1)} %bitcast.5.x_any, bf16[1024,4096]{1,0:T(8,128)(2,1)} %win_any.7, ...), custom_call_target="tpu_custom_call" | custom-call | tf_op jit(solution)/shard_map/received_part/pallas_call | solution.py:467
  36.0 0.1 collective-permute-start.2
  36.1 0.5 collective-permute-start
  36.6 5.2 %all-to-all-start.1 = ((bf16[32,8,512]{2,1,0:T(8,128)(2,1)}), bf16[32,8,512]{2,1,0:T(8,128)(2,1)}, u32[]{:S(2)}, u32[]{:S(2)}) async-start(bf16[32,8,512]{2,1,0:T(8,128)(2,1)} %bitcast.12), calls=%async_computation.1 | async-start | bytes 524288 | tf_op jit(solution)/shard_map/all_to_all | solution.py:837
  41.8 0.0 collective-permute-done.refs_1_
  41.8 0.0 collective-permute-done.1.refs_4_
  41.8 0.0 collective-permute-done.2.refs_5_
  41.8 7.2 %product.1 = (bf16[8,192,128]{2,1,0:T(8,128)(2,1)}, f32[8,192,128]{2,1,0:T(8,128)}, bf16[8,176,128]{2,1,0:T(8,128)(2,1)}, f32[8,176,128]{2,1,0:T(8,128)}, bf16[8...) custom-call(s32[1]{0:T(128)} %bitcast.place_ref, bf16[512,768]{1,0:T(8,128)(2,1)} %get-tuple-element.71.refs_0_, ...), custom_call_target="tpu_custom_call" | custom-call | tf_op jit(solution)/shard_map/product/pallas_call | solution.py:649
  49.0 1.8 %collective-permute-start.3 = (bf16[8,192,128]{2,1,0:T(8,128)(2,1)}, bf16[8,192,128]{2,1,0:T(8,128)(2,1)S(1)}, u32[]{:S(2)}, u32[]{:S(2)}) collective-permute-start(bf16[8,192,128]{2,1,0:T(8,128)(2,1)} %get-tuple-element.84), channel_id=1, source_target_pairs={{0,2},{2,0},{4,6},{6,4},{8,10},{10,8},{12,14},{14,12},{16,18},{18,... | collective-permute-start | bytes 1179656 | tf_op jit(solution)/shard_map/ppermute | solution.py:783
  50.8 1.5 %collective-permute-start.4 = (bf16[8,176,128]{2,1,0:T(8,128)(2,1)}, bf16[8,176,128]{2,1,0:T(8,128)(2,1)S(1)}, u32[]{:S(2)}, u32[]{:S(2)}) collective-permute-start(bf16[8,176,128]{2,1,0:T(8,128)(2,1)} %get-tuple-element.85), channel_id=1, source_target_pairs={{0,4},{2,6},{4,0},{6,2},{8,12},{10,14},{12,8},{14,10},{16,20},{18,... | collective-permute-start | bytes 1081352 | tf_op jit(solution)/shard_map/ppermute | solution.py:783
  52.3 1.5 %collective-permute-start.5 = (bf16[8,144,128]{2,1,0:T(8,128)(2,1)}, bf16[8,144,128]{2,1,0:T(8,128)(2,1)S(1)}, u32[]{:S(2)}, u32[]{:S(2)}) collective-permute-start(bf16[8,144,128]{2,1,0:T(8,128)(2,1)} %get-tuple-element.86), channel_id=1, source_target_pairs={{0,8},{2,10},{4,12},{6,14},{8,0},{10,2},{12,4},{14,6},{16,24},{18,... | collective-permute-start | bytes 884744 | tf_op jit(solution)/shard_map/ppermute | solution.py:783
  53.7 0.0 all-to-all-done.1
  53.7 0.0 copy-start
  53.7 0.0 copy-start.1
  53.7 0.0 copy-start.2
  53.7 7.9 %slope_part.1.grad_any = bf16[512,4096]{1,0:T(8,128)(2,1)} custom-call(f32[512,512]{1,0:T(8,128)} %get-tuple-element.87.refs_0_, bf16[256,512]{1,0:T(8,128)(2,1)} %get-tuple-element.88.refs_1_, bf16[256,512]{1,0:T(8,128)(2,1)} %bitcast.9.refs_2_, f32[512,128]{1,0:T(8,128)} %get-tuple-element.67.side_any.refs_3_, ...), custom_call_target="tpu_custom_call" | custom-call | flops 2147483648 | bytes 16777216 | tf_op jit(solution)/shard_map/slope_part/pallas_call | solution.py:700
  61.6 0.0 collective-permute-done.5.refs_5_
  61.6 0.0 collective-permute-done.4.refs_3_
  61.7 0.0 collective-permute-done.3.refs_1_
  61.7 0.0 copy-done
  61.7 0.0 copy-done.1
  61.7 0.0 copy-done.2
  61.7 0.2 fold_halves.3
  61.9 0.6 collective-permute-start.8
  62.5 1.4 %collective-permute-start.7 = (bf16[4,176,128]{2,1,0:T(8,128)(2,1)S(1)}, bf16[4,176,128]{2,1,0:T(8,128)(2,1)S(1)}, u32[]{:S(2)}, u32[]{:S(2)}) collective-permute-start(bf16[4,176,128]{2,1,0:T(8,128)(2,1)S(1)} %get-tuple-element.105), channel_id=1, source_target_pairs={{0,8},{2,10},{4,12},{6,14},{8,0},{10,2},{12,4},{14,6},{16,24},{18,... | collective-permute-start | bytes 540680 | tf_op jit(solution)/shard_map/ppermute | solution.py:783
  63.9 1.5 %collective-permute-start.6 = (bf16[4,192,128]{2,1,0:T(8,128)(2,1)S(1)}, bf16[4,192,128]{2,1,0:T(8,128)(2,1)S(1)}, u32[]{:S(2)}, u32[]{:S(2)}) collective-permute-start(bf16[4,192,128]{2,1,0:T(8,128)(2,1)S(1)} %get-tuple-element.104), channel_id=1, source_target_pairs={{0,4},{2,6},{4,0},{6,2},{8,12},{10,14},{12,8},{14,10},{16,20},{18,... | collective-permute-start | bytes 589832 | tf_op jit(solution)/shard_map/ppermute | solution.py:783
  65.4 5.1 %embed_part.2.refs_0_ = bf16[512,1024]{1,0:T(8,128)(2,1)} custom-call(bf16[512,4096]{1,0:T(8,128)(2,1)} %slope_part.1.grad_any, bf16[1024,4096]{1,0:T(8,128)(2,1)} %win_any.7), custom_call_target="tpu_custom_call" | custom-call | flops 2147483648 | bytes 9437184 | tf_op jit(solution)/shard_map/embed_part/pallas_call | solution.py:744
  70.5 0.0 collective-permute-done.8.refs_5_
  70.5 0.0 collective-permute-done.7.refs_3_
  70.5 0.0 collective-permute-done.6.refs_1_
  70.5 0.1 fold_halves.4
  70.6 0.6 collective-permute-start.9
  71.2 1.1 %collective-permute-start.10 = (bf16[2,176,128]{2,1,0:T(8,128)(2,1)S(1)}, bf16[2,176,128]{2,1,0:T(8,128)(2,1)S(1)}, u32[]{:S(2)}, u32[]{:S(2)}) collective-permute-start(bf16[2,176,128]{2,1,0:T(8,128)(2,1)S(1)} %get-tuple-element.115), channel_id=1, source_target_pairs={{0,2},{2,0},{4,6},{6,4},{8,10},{10,8},{12,14},{14,12},{16,18},{18,... | collective-permute-start | bytes 270344 | tf_op jit(solution)/shard_map/ppermute | solution.py:783
  72.3 1.0 %collective-permute-start.11 = (bf16[2,144,128]{2,1,0:T(8,128)(2,1)S(1)}, bf16[2,144,128]{2,1,0:T(8,128)(2,1)S(1)}, u32[]{:S(2)}, u32[]{:S(2)}) collective-permute-start(bf16[2,144,128]{2,1,0:T(8,128)(2,1)S(1)} %get-tuple-element.116), channel_id=1, source_target_pairs={{0,4},{2,6},{4,0},{6,2},{8,12},{10,14},{12,8},{14,10},{16,20},{18,... | collective-permute-start | bytes 221192 | tf_op jit(solution)/shard_map/ppermute | solution.py:783
  73.3 3.3 %collective-permute-done.11.refs_5_ = bf16[2,144,128]{2,1,0:T(8,128)(2,1)S(1)} collective-permute-done((bf16[2,144,128]{2,1,0:T(8,128)(2,1)S(1)}, bf16[2,144,128]{2,1,0:T(8,128)(2,1)S(1)}, u32[]{:S(2)}, u32[]{:S(2)}) %collective-permute-start.11) | collective-permute-done | bytes 73760 | tf_op jit(solution)/shard_map/ppermute | solution.py:783
  76.6 0.0 collective-permute-done.10.refs_3_
  76.6 0.0 collective-permute-done.9.refs_1_
  76.7 2.5 %collective-permute-start.12 = (bf16[1,512,128]{2,1,0:T(8,128)(2,1)S(1)}, bf16[1,512,128]{2,1,0:T(8,128)(2,1)S(1)}, u32[]{:S(2)}, u32[]{:S(2)}) collective-permute-start(bf16[1,512,128]{2,1,0:T(8,128)(2,1)S(1)} %get-tuple-element.124), channel_id=1, source_target_pairs={{0,16},{2,18},{4,20},{6,22},{8,24},{10,26},{12,28},{14,30},{16,0},... | collective-permute-start | bytes 393224 | tf_op jit(solution)/shard_map/ppermute | solution.py:783
  79.1 5.1 %embed_part.3 = bf16[512,1024]{1,0:T(8,128)(2,1)} custom-call(bf16[512,4096]{1,0:T(8,128)(2,1)} %slope_part.1.grad_any, bf16[1024,4096]{1,0:T(8,128)(2,1)} %win_any.7, bf16[512,1024]{1,0:T(8,128)(2,1)} %embed_part.2.refs_0_), custom_call_target="tpu_custom_call", output_to_operand_aliasing={{}: (2, {})} | custom-call | flops 2147483648 | bytes 9437184 | tf_op jit(solution)/shard_map/embed_part/pallas_call | solution.py:744
  84.2 0.0 collective-permute-done.12.refs_1_
  84.2 0.8 finish.1
  (1 shorter events, 0.0 us)
Async XLA Ops:
  3.4 24.1 %all-to-all-start = ((bf16[32,8,1152]{2,1,0:T(8,128)(2,1)}), bf16[32,8,1152]{2,1,0:T(8,128)(2,1)}, u32[]{:S(2)}, u32[]{:S(2)}) async-start(bf16[32,8,1152]{2,1,0:T(8,128)(2,1)} %bitcast.11), calls=%async_computation | async-start | bytes 1179648 | tf_op jit(solution)/shard_map/all_to_all | solution.py:815
  26.6 15.1 %collective-permute-start.1 = (bf16[512,2048]{1,0:T(8,128)(2,1)}, bf16[512,2048]{1,0:T(8,128)(2,1)}, u32[]{:S(2)}, u32[]{:S(2)}) collective-permute-start(bf16[512,2048]{1,0:T(8,128)(2,1)} %get-tuple-element.74), channel_id=1, source_target_pairs={{0,1},{1,0},{2,3},{3,2},{4,5},{5,4},{6,7},{7,6},{8,9},{9,8},{10,11... | collective-permute-start | bytes 6291464 | tf_op jit(solution)/shard_map/ppermute | solution.py:831
  36.0 5.8 %collective-permute-start.2 = (bf16[256,2048]{1,0:T(8,128)(2,1)}, bf16[256,2048]{1,0:T(8,128)(2,1)}, u32[]{:S(2)}, u32[]{:S(2)}) collective-permute-start(bf16[256,2048]{1,0:T(8,128)(2,1)} %get-tuple-element.75), channel_id=1, source_target_pairs={{0,1},{1,0},{2,3},{3,2},{4,5},{5,4},{6,7},{7,6},{8,9},{9,8},{10,11... | collective-permute-start | bytes 3145736 | tf_op jit(solution)/shard_map/ppermute | solution.py:836
  36.1 5.7 %collective-permute-start = (bf16[512,768]{1,0:T(8,128)(2,1)}, bf16[512,768]{1,0:T(8,128)(2,1)}, u32[]{:S(2)}, u32[]{:S(2)}) collective-permute-start(bf16[512,768]{1,0:T(8,128)(2,1)} %get-tuple-element.71.refs_0_), channel_id=1, source_target_pairs={{0,1},{1,0},{2,3},{3,2},{4,5},{5,4},{6,7},{7,6},{8,9},{9,8},{10,11... | collective-permute-start | bytes 2359304 | tf_op jit(solution)/shard_map/ppermute | solution.py:835
  36.6 17.1 %all-to-all-start.1 = ((bf16[32,8,512]{2,1,0:T(8,128)(2,1)}), bf16[32,8,512]{2,1,0:T(8,128)(2,1)}, u32[]{:S(2)}, u32[]{:S(2)}) async-start(bf16[32,8,512]{2,1,0:T(8,128)(2,1)} %bitcast.12), calls=%async_computation.1 | async-start | bytes 524288 | tf_op jit(solution)/shard_map/all_to_all | solution.py:837
  49.0 12.6 %collective-permute-start.3 = (bf16[8,192,128]{2,1,0:T(8,128)(2,1)}, bf16[8,192,128]{2,1,0:T(8,128)(2,1)S(1)}, u32[]{:S(2)}, u32[]{:S(2)}) collective-permute-start(bf16[8,192,128]{2,1,0:T(8,128)(2,1)} %get-tuple-element.84), channel_id=1, source_target_pairs={{0,2},{2,0},{4,6},{6,4},{8,10},{10,8},{12,14},{14,12},{16,18},{18,... | collective-permute-start | bytes 1179656 | tf_op jit(solution)/shard_map/ppermute | solution.py:783
  50.8 10.9 %collective-permute-start.4 = (bf16[8,176,128]{2,1,0:T(8,128)(2,1)}, bf16[8,176,128]{2,1,0:T(8,128)(2,1)S(1)}, u32[]{:S(2)}, u32[]{:S(2)}) collective-permute-start(bf16[8,176,128]{2,1,0:T(8,128)(2,1)} %get-tuple-element.85), channel_id=1, source_target_pairs={{0,4},{2,6},{4,0},{6,2},{8,12},{10,14},{12,8},{14,10},{16,20},{18,... | collective-permute-start | bytes 1081352 | tf_op jit(solution)/shard_map/ppermute | solution.py:783
  52.3 9.4 %collective-permute-start.5 = (bf16[8,144,128]{2,1,0:T(8,128)(2,1)}, bf16[8,144,128]{2,1,0:T(8,128)(2,1)S(1)}, u32[]{:S(2)}, u32[]{:S(2)}) collective-permute-start(bf16[8,144,128]{2,1,0:T(8,128)(2,1)} %get-tuple-element.86), channel_id=1, source_target_pairs={{0,8},{2,10},{4,12},{6,14},{8,0},{10,2},{12,4},{14,6},{16,24},{18,... | collective-permute-start | bytes 884744 | tf_op jit(solution)/shard_map/ppermute | solution.py:783
  53.7 7.9 %copy-start = (f32[8,192,128]{2,1,0:T(8,128)S(1)}, f32[8,192,128]{2,1,0:T(8,128)}, u32[]{:S(2)}) copy-start(f32[8,192,128]{2,1,0:T(8,128)} %get-tuple-element.83.refs_0_) | copy-start | bytes 2359300
  53.7 7.9 %copy-start.1 = (f32[8,176,128]{2,1,0:T(8,128)S(1)}, f32[8,176,128]{2,1,0:T(8,128)}, u32[]{:S(2)}) copy-start(f32[8,176,128]{2,1,0:T(8,128)} %get-tuple-element.92.refs_2_) | copy-start | bytes 2162692
  53.7 8.0 %copy-start.2 = (f32[8,144,128]{2,1,0:T(8,128)S(1)}, f32[8,144,128]{2,1,0:T(8,128)}, u32[]{:S(2)}) copy-start(f32[8,144,128]{2,1,0:T(8,128)} %get-tuple-element.94.refs_4_) | copy-start | bytes 1769476
  61.9 8.6 %collective-permute-start.8 = (bf16[4,144,128]{2,1,0:T(8,128)(2,1)S(1)}, bf16[4,144,128]{2,1,0:T(8,128)(2,1)S(1)}, u32[]{:S(2)}, u32[]{:S(2)}) collective-permute-start(bf16[4,144,128]{2,1,0:T(8,128)(2,1)S(1)} %get-tuple-element.106), channel_id=1, source_target_pairs={{0,2},{2,0},{4,6},{6,4},{8,10},{10,8},{12,14},{14,12},{16,18},{18,... | collective-permute-start | bytes 442376 | tf_op jit(solution)/shard_map/ppermute | solution.py:783
  62.5 8.0 %collective-permute-start.7 = (bf16[4,176,128]{2,1,0:T(8,128)(2,1)S(1)}, bf16[4,176,128]{2,1,0:T(8,128)(2,1)S(1)}, u32[]{:S(2)}, u32[]{:S(2)}) collective-permute-start(bf16[4,176,128]{2,1,0:T(8,128)(2,1)S(1)} %get-tuple-element.105), channel_id=1, source_target_pairs={{0,8},{2,10},{4,12},{6,14},{8,0},{10,2},{12,4},{14,6},{16,24},{18,... | collective-permute-start | bytes 540680 | tf_op jit(solution)/shard_map/ppermute | solution.py:783
  63.9 6.6 %collective-permute-start.6 = (bf16[4,192,128]{2,1,0:T(8,128)(2,1)S(1)}, bf16[4,192,128]{2,1,0:T(8,128)(2,1)S(1)}, u32[]{:S(2)}, u32[]{:S(2)}) collective-permute-start(bf16[4,192,128]{2,1,0:T(8,128)(2,1)S(1)} %get-tuple-element.104), channel_id=1, source_target_pairs={{0,4},{2,6},{4,0},{6,2},{8,12},{10,14},{12,8},{14,10},{16,20},{18,... | collective-permute-start | bytes 589832 | tf_op jit(solution)/shard_map/ppermute | solution.py:783
  70.6 6.0 %collective-permute-start.9 = (bf16[2,192,128]{2,1,0:T(8,128)(2,1)S(1)}, bf16[2,192,128]{2,1,0:T(8,128)(2,1)S(1)}, u32[]{:S(2)}, u32[]{:S(2)}) collective-permute-start(bf16[2,192,128]{2,1,0:T(8,128)(2,1)S(1)} %get-tuple-element.114), channel_id=1, source_target_pairs={{0,8},{2,10},{4,12},{6,14},{8,0},{10,2},{12,4},{14,6},{16,24},{18,... | collective-permute-start | bytes 294920 | tf_op jit(solution)/shard_map/ppermute | solution.py:783
  71.2 5.4 %collective-permute-start.10 = (bf16[2,176,128]{2,1,0:T(8,128)(2,1)S(1)}, bf16[2,176,128]{2,1,0:T(8,128)(2,1)S(1)}, u32[]{:S(2)}, u32[]{:S(2)}) collective-permute-start(bf16[2,176,128]{2,1,0:T(8,128)(2,1)S(1)} %get-tuple-element.115), channel_id=1, source_target_pairs={{0,2},{2,0},{4,6},{6,4},{8,10},{10,8},{12,14},{14,12},{16,18},{18,... | collective-permute-start | bytes 270344 | tf_op jit(solution)/shard_map/ppermute | solution.py:783
  72.3 4.4 %collective-permute-start.11 = (bf16[2,144,128]{2,1,0:T(8,128)(2,1)S(1)}, bf16[2,144,128]{2,1,0:T(8,128)(2,1)S(1)}, u32[]{:S(2)}, u32[]{:S(2)}) collective-permute-start(bf16[2,144,128]{2,1,0:T(8,128)(2,1)S(1)} %get-tuple-element.116), channel_id=1, source_target_pairs={{0,4},{2,6},{4,0},{6,2},{8,12},{10,14},{12,8},{14,10},{16,20},{18,... | collective-permute-start | bytes 221192 | tf_op jit(solution)/shard_map/ppermute | solution.py:783
  76.7 7.5 %collective-permute-start.12 = (bf16[1,512,128]{2,1,0:T(8,128)(2,1)S(1)}, bf16[1,512,128]{2,1,0:T(8,128)(2,1)S(1)}, u32[]{:S(2)}, u32[]{:S(2)}) collective-permute-start(bf16[1,512,128]{2,1,0:T(8,128)(2,1)S(1)} %get-tuple-element.124), channel_id=1, source_target_pairs={{0,16},{2,18},{4,20},{6,22},{8,24},{10,26},{12,28},{14,30},{16,0},... | collective-permute-start | bytes 393224 | tf_op jit(solution)/shard_map/ppermute | solution.py:783

commit v10 on v9

--- a/solution.py
+++ b/solution.py
@@ -11,7 +11,7 @@
 gelu_inner = 0.7978845608028654
 gelu_cubic = 0.044715
 LANES = 128
-SLOPED = 2048
+SLOPED = 2560
 MIB = 1024 * 1024
 both = ("dom", "rep")
 

time: 85.4 us -> 85.6 us (level)
  no operation moved by 1% of the time
where the time goes in v10:
time: 85.6 us; the launch traced here: 85.3 us
  Pallas kernels  53.3 us (62%)
  starting transfers between devices  27 us (32%)
  waiting for transfers between devices  4.14 us (5%)
    pallas_call x1, Pallas kernels, forward(): pl.pallas_call(forward_kernel, in_specs=[SMEM] * 2 + [HBM] * 8, out_specs...  16 us
    ppermute x10, starting transfers between devices, exchange(): lax.ppermute(sent, 'dom', [(device, device ^ 1 << bit) for device in rang...  13.4 us
    pallas_call x2, Pallas kernels, embed_part(): pl.pallas_call(functools.partial(embed_kernel, chunk, first), in_specs=[H...  10.1 us
    pallas_call x1, Pallas kernels, received_part(): pl.pallas_call(received_kernel, in_specs=[SMEM] + [HBM] * 7, out_specs=(H...  8.37 us
    pallas_call x1, Pallas kernels, slope_part(): pl.pallas_call(functools.partial(slope_kernel, chunk), in_specs=[HBM] * 6...  7.53 us
    all_to_all x1, starting transfers between devices, body(): lax.all_to_all(outgoing.reshape(peers, slots, -1), both, split_axis=0, co...  7.42 us
    pallas_call x1, Pallas kernels, product(): pl.pallas_call(functools.partial(product_kernel, streams, chunk), in_spec...  7.22 us
    all_to_all x1, starting transfers between devices, body(): lax.all_to_all(returned.reshape(peers, slots, width), both, split_axis=0,...  5.41 us
  transfers between devices with their start and end apart: 15, of which 2 were waited for; matrix products, arithmetic and copies ran while one was open for 0% of the time, Pallas kernels for 58%

profile of v10, /device:TPU:0, one launch (start us, length us, event | category | flops | bytes accessed | tf_op | source)
XLA Modules:
  0.0 85.3 jit_solution(6078637275474149428)
XLA Ops:
  0.6 2.8 %prepare.1 = (bf16[256,1152]{1,0:T(8,128)(2,1)}, bf16[256,512]{1,0:T(8,128)(2,1)}, f32[512,128]{1,0:T(8,128)}) custom-call(s32[8,32]{1,0:T(8,128)} %bitcast.13, s32[1,32]{1,0:T(1,128)} %count_any.1, bf16[4,8,128,128]{3,2,1,0:T(8,128)(2,1)} %tiles_any.3, bf16[512,1024]{1,0:T(8,128)(2,1)} %x_any.1), custom_call_target="tpu_custom_call" | custom-call | tf_op jit(solution)/shard_map/prepare/pallas_call | solution.py:134
  3.4 7.4 %all-to-all-start = ((bf16[32,8,1152]{2,1,0:T(8,128)(2,1)}), bf16[32,8,1152]{2,1,0:T(8,128)(2,1)}, u32[]{:S(2)}, u32[]{:S(2)}) async-start(bf16[32,8,1152]{2,1,0:T(8,128)(2,1)} %bitcast.11), calls=%async_computation | async-start | bytes 1179648 | tf_op jit(solution)/shard_map/all_to_all | solution.py:815
  10.9 16.0 %forward.1 = (bf16[512,4096]{1,0:T(8,128)(2,1)}, bf16[512,2048]{1,0:T(8,128)(2,1)}, bf16[512,2048]{1,0:T(8,128)(2,1)}, f32[512,512]{1,0:T(8,128)}, bf16[2,512,256]{2,1,0:T(8,128)(2,1)}, /*index=5*/f32[256,640]{1,0:T(8,128)}) custom-call(s32[1]{0:T(128)} %bitcast.1.rep_ref, s32[4,8]{1,0:T(4,128)} %column_ref.1, bf16[512,1024]{1,0:T(8,128)(2,1)} %x_any.1, ...), custom_call_target="tpu_custom_call" | custom-call | tf_op jit(solution)/shard_map/forward/pallas_call | solution.py:346
  26.9 0.3 collective-permute-start.1
  27.1 0.4 all-to-all-done
  27.6 8.4 %received_part.1 = (bf16[256,2048]{1,0:T(8,128)(2,1)}, bf16[256,2048]{1,0:T(8,128)(2,1)}, f32[512,512]{1,0:T(8,128)}, bf16[512,768]{1,0:T(8,128)(2,1)}, bf16[256,512]{1,0:T(8,128)(2,1)}) custom-call(s32[1]{0:T(128)} %bitcast.1.rep_ref, bf16[256,1152]{1,0:T(8,128)(2,1)} %bitcast.5.x_any, bf16[1024,4096]{1,0:T(8,128)(2,1)} %win_any.7, ...), custom_call_target="tpu_custom_call" | custom-call | tf_op jit(solution)/shard_map/received_part/pallas_call | solution.py:467
  36.0 0.1 collective-permute-start.2
  36.1 0.5 collective-permute-start
  36.6 5.4 %all-to-all-start.1 = ((bf16[32,8,512]{2,1,0:T(8,128)(2,1)}), bf16[32,8,512]{2,1,0:T(8,128)(2,1)}, u32[]{:S(2)}, u32[]{:S(2)}) async-start(bf16[32,8,512]{2,1,0:T(8,128)(2,1)} %bitcast.12), calls=%async_computation.1 | async-start | bytes 524288 | tf_op jit(solution)/shard_map/all_to_all | solution.py:837
  42.0 0.0 collective-permute-done.refs_1_
  42.0 0.0 collective-permute-done.1.refs_4_
  42.0 0.0 collective-permute-done.2.refs_5_
  42.0 7.2 %product.1 = (bf16[8,192,128]{2,1,0:T(8,128)(2,1)}, f32[8,192,128]{2,1,0:T(8,128)}, bf16[8,176,128]{2,1,0:T(8,128)(2,1)}, f32[8,176,128]{2,1,0:T(8,128)}, bf16[8...) custom-call(s32[1]{0:T(128)} %bitcast.place_ref, bf16[512,768]{1,0:T(8,128)(2,1)} %get-tuple-element.71.refs_0_, ...), custom_call_target="tpu_custom_call" | custom-call | tf_op jit(solution)/shard_map/product/pallas_call | solution.py:649
  49.2 1.8 %collective-permute-start.3 = (bf16[8,192,128]{2,1,0:T(8,128)(2,1)}, bf16[8,192,128]{2,1,0:T(8,128)(2,1)S(1)}, u32[]{:S(2)}, u32[]{:S(2)}) collective-permute-start(bf16[8,192,128]{2,1,0:T(8,128)(2,1)} %get-tuple-element.84), channel_id=1, source_target_pairs={{0,2},{2,0},{4,6},{6,4},{8,10},{10,8},{12,14},{14,12},{16,18},{18,... | collective-permute-start | bytes 1179656 | tf_op jit(solution)/shard_map/ppermute | solution.py:783
  51.0 1.5 %collective-permute-start.4 = (bf16[8,176,128]{2,1,0:T(8,128)(2,1)}, bf16[8,176,128]{2,1,0:T(8,128)(2,1)S(1)}, u32[]{:S(2)}, u32[]{:S(2)}) collective-permute-start(bf16[8,176,128]{2,1,0:T(8,128)(2,1)} %get-tuple-element.85), channel_id=1, source_target_pairs={{0,4},{2,6},{4,0},{6,2},{8,12},{10,14},{12,8},{14,10},{16,20},{18,... | collective-permute-start | bytes 1081352 | tf_op jit(solution)/shard_map/ppermute | solution.py:783
  52.5 1.5 %collective-permute-start.5 = (bf16[8,144,128]{2,1,0:T(8,128)(2,1)}, bf16[8,144,128]{2,1,0:T(8,128)(2,1)S(1)}, u32[]{:S(2)}, u32[]{:S(2)}) collective-permute-start(bf16[8,144,128]{2,1,0:T(8,128)(2,1)} %get-tuple-element.86), channel_id=1, source_target_pairs={{0,8},{2,10},{4,12},{6,14},{8,0},{10,2},{12,4},{14,6},{16,24},{18,... | collective-permute-start | bytes 884744 | tf_op jit(solution)/shard_map/ppermute | solution.py:783
  53.9 0.0 all-to-all-done.1
  53.9 0.0 copy-start
  53.9 0.0 copy-start.1
  53.9 0.0 copy-start.2
  53.9 7.5 %slope_part.1.grad_any = bf16[512,4096]{1,0:T(8,128)(2,1)} custom-call(f32[512,512]{1,0:T(8,128)} %get-tuple-element.87.refs_0_, bf16[256,512]{1,0:T(8,128)(2,1)} %get-tuple-element.88.refs_1_, bf16[256,512]{1,0:T(8,128)(2,1)} %bitcast.9.refs_2_, f32[512,128]{1,0:T(8,128)} %get-tuple-element.67.side_any.refs_3_, ...), custom_call_target="tpu_custom_call" | custom-call | flops 2147483648 | bytes 16777216 | tf_op jit(solution)/shard_map/slope_part/pallas_call | solution.py:700
  61.5 0.0 collective-permute-done.5.refs_5_
  61.5 0.0 collective-permute-done.4.refs_3_
  61.5 0.0 collective-permute-done.3.refs_1_
  61.5 0.0 copy-done
  61.5 0.0 copy-done.1
  61.5 0.0 copy-done.2
  61.5 0.2 fold_halves.3
  61.7 0.9 %collective-permute-start.8 = (bf16[4,144,128]{2,1,0:T(8,128)(2,1)S(1)}, bf16[4,144,128]{2,1,0:T(8,128)(2,1)S(1)}, u32[]{:S(2)}, u32[]{:S(2)}) collective-permute-start(bf16[4,144,128]{2,1,0:T(8,128)(2,1)S(1)} %get-tuple-element.106), channel_id=1, source_target_pairs={{0,2},{2,0},{4,6},{6,4},{8,10},{10,8},{12,14},{14,12},{16,18},{18,... | collective-permute-start | bytes 442376 | tf_op jit(solution)/shard_map/ppermute | solution.py:783
  62.7 1.5 %collective-permute-start.7 = (bf16[4,176,128]{2,1,0:T(8,128)(2,1)S(1)}, bf16[4,176,128]{2,1,0:T(8,128)(2,1)S(1)}, u32[]{:S(2)}, u32[]{:S(2)}) collective-permute-start(bf16[4,176,128]{2,1,0:T(8,128)(2,1)S(1)} %get-tuple-element.105), channel_id=1, source_target_pairs={{0,8},{2,10},{4,12},{6,14},{8,0},{10,2},{12,4},{14,6},{16,24},{18,... | collective-permute-start | bytes 540680 | tf_op jit(solution)/shard_map/ppermute | solution.py:783
  64.1 1.5 %collective-permute-start.6 = (bf16[4,192,128]{2,1,0:T(8,128)(2,1)S(1)}, bf16[4,192,128]{2,1,0:T(8,128)(2,1)S(1)}, u32[]{:S(2)}, u32[]{:S(2)}) collective-permute-start(bf16[4,192,128]{2,1,0:T(8,128)(2,1)S(1)} %get-tuple-element.104), channel_id=1, source_target_pairs={{0,4},{2,6},{4,0},{6,2},{8,12},{10,14},{12,8},{14,10},{16,20},{18,... | collective-permute-start | bytes 589832 | tf_op jit(solution)/shard_map/ppermute | solution.py:783
  65.6 5.1 %embed_part.2.refs_0_ = bf16[512,1024]{1,0:T(8,128)(2,1)} custom-call(bf16[512,4096]{1,0:T(8,128)(2,1)} %slope_part.1.grad_any, bf16[1024,4096]{1,0:T(8,128)(2,1)} %win_any.7), custom_call_target="tpu_custom_call" | custom-call | flops 2147483648 | bytes 9437184 | tf_op jit(solution)/shard_map/embed_part/pallas_call | solution.py:744
  70.7 0.0 collective-permute-done.8.refs_5_
  70.7 0.0 collective-permute-done.7.refs_3_
  70.7 0.0 collective-permute-done.6.refs_1_
  70.7 0.1 fold_halves.4
  70.8 0.6 collective-permute-start.9
  71.4 1.1 %collective-permute-start.10 = (bf16[2,176,128]{2,1,0:T(8,128)(2,1)S(1)}, bf16[2,176,128]{2,1,0:T(8,128)(2,1)S(1)}, u32[]{:S(2)}, u32[]{:S(2)}) collective-permute-start(bf16[2,176,128]{2,1,0:T(8,128)(2,1)S(1)} %get-tuple-element.115), channel_id=1, source_target_pairs={{0,2},{2,0},{4,6},{6,4},{8,10},{10,8},{12,14},{14,12},{16,18},{18,... | collective-permute-start | bytes 270344 | tf_op jit(solution)/shard_map/ppermute | solution.py:783
  72.5 0.7 collective-permute-start.11
  73.2 3.7 %collective-permute-done.11.refs_5_ = bf16[2,144,128]{2,1,0:T(8,128)(2,1)S(1)} collective-permute-done((bf16[2,144,128]{2,1,0:T(8,128)(2,1)S(1)}, bf16[2,144,128]{2,1,0:T(8,128)(2,1)S(1)}, u32[]{:S(2)}, u32[]{:S(2)}) %collective-permute-start.11) | collective-permute-done | bytes 73760 | tf_op jit(solution)/shard_map/ppermute | solution.py:783
  76.8 0.0 collective-permute-done.10.refs_3_
  76.8 0.0 collective-permute-done.9.refs_1_
  76.9 2.5 %collective-permute-start.12 = (bf16[1,512,128]{2,1,0:T(8,128)(2,1)S(1)}, bf16[1,512,128]{2,1,0:T(8,128)(2,1)S(1)}, u32[]{:S(2)}, u32[]{:S(2)}) collective-permute-start(bf16[1,512,128]{2,1,0:T(8,128)(2,1)S(1)} %get-tuple-element.124), channel_id=1, source_target_pairs={{0,16},{2,18},{4,20},{6,22},{8,24},{10,26},{12,28},{14,30},{16,0},... | collective-permute-start | bytes 393224 | tf_op jit(solution)/shard_map/ppermute | solution.py:783
  79.4 5.1 %embed_part.3 = bf16[512,1024]{1,0:T(8,128)(2,1)} custom-call(bf16[512,4096]{1,0:T(8,128)(2,1)} %slope_part.1.grad_any, bf16[1024,4096]{1,0:T(8,128)(2,1)} %win_any.7, bf16[512,1024]{1,0:T(8,128)(2,1)} %embed_part.2.refs_0_), custom_call_target="tpu_custom_call", output_to_operand_aliasing={{}: (2, {})} | custom-call | flops 2147483648 | bytes 9437184 | tf_op jit(solution)/shard_map/embed_part/pallas_call | solution.py:744
  84.4 0.0 collective-permute-done.12.refs_1_
  84.4 0.8 finish.1
  (1 shorter events, 0.0 us)
Async XLA Ops:
  3.4 24.1 %all-to-all-start = ((bf16[32,8,1152]{2,1,0:T(8,128)(2,1)}), bf16[32,8,1152]{2,1,0:T(8,128)(2,1)}, u32[]{:S(2)}, u32[]{:S(2)}) async-start(bf16[32,8,1152]{2,1,0:T(8,128)(2,1)} %bitcast.11), calls=%async_computation | async-start | bytes 1179648 | tf_op jit(solution)/shard_map/all_to_all | solution.py:815
  26.9 15.1 %collective-permute-start.1 = (bf16[512,2048]{1,0:T(8,128)(2,1)}, bf16[512,2048]{1,0:T(8,128)(2,1)}, u32[]{:S(2)}, u32[]{:S(2)}) collective-permute-start(bf16[512,2048]{1,0:T(8,128)(2,1)} %get-tuple-element.74), channel_id=1, source_target_pairs={{0,1},{1,0},{2,3},{3,2},{4,5},{5,4},{6,7},{7,6},{8,9},{9,8},{10,11... | collective-permute-start | bytes 6291464 | tf_op jit(solution)/shard_map/ppermute | solution.py:831
  36.0 6.0 %collective-permute-start.2 = (bf16[256,2048]{1,0:T(8,128)(2,1)}, bf16[256,2048]{1,0:T(8,128)(2,1)}, u32[]{:S(2)}, u32[]{:S(2)}) collective-permute-start(bf16[256,2048]{1,0:T(8,128)(2,1)} %get-tuple-element.75), channel_id=1, source_target_pairs={{0,1},{1,0},{2,3},{3,2},{4,5},{5,4},{6,7},{7,6},{8,9},{9,8},{10,11... | collective-permute-start | bytes 3145736 | tf_op jit(solution)/shard_map/ppermute | solution.py:836
  36.1 5.9 %collective-permute-start = (bf16[512,768]{1,0:T(8,128)(2,1)}, bf16[512,768]{1,0:T(8,128)(2,1)}, u32[]{:S(2)}, u32[]{:S(2)}) collective-permute-start(bf16[512,768]{1,0:T(8,128)(2,1)} %get-tuple-element.71.refs_0_), channel_id=1, source_target_pairs={{0,1},{1,0},{2,3},{3,2},{4,5},{5,4},{6,7},{7,6},{8,9},{9,8},{10,11... | collective-permute-start | bytes 2359304 | tf_op jit(solution)/shard_map/ppermute | solution.py:835
  36.6 17.4 %all-to-all-start.1 = ((bf16[32,8,512]{2,1,0:T(8,128)(2,1)}), bf16[32,8,512]{2,1,0:T(8,128)(2,1)}, u32[]{:S(2)}, u32[]{:S(2)}) async-start(bf16[32,8,512]{2,1,0:T(8,128)(2,1)} %bitcast.12), calls=%async_computation.1 | async-start | bytes 524288 | tf_op jit(solution)/shard_map/all_to_all | solution.py:837
  49.2 12.3 %collective-permute-start.3 = (bf16[8,192,128]{2,1,0:T(8,128)(2,1)}, bf16[8,192,128]{2,1,0:T(8,128)(2,1)S(1)}, u32[]{:S(2)}, u32[]{:S(2)}) collective-permute-start(bf16[8,192,128]{2,1,0:T(8,128)(2,1)} %get-tuple-element.84), channel_id=1, source_target_pairs={{0,2},{2,0},{4,6},{6,4},{8,10},{10,8},{12,14},{14,12},{16,18},{18,... | collective-permute-start | bytes 1179656 | tf_op jit(solution)/shard_map/ppermute | solution.py:783
  51.0 10.5 %collective-permute-start.4 = (bf16[8,176,128]{2,1,0:T(8,128)(2,1)}, bf16[8,176,128]{2,1,0:T(8,128)(2,1)S(1)}, u32[]{:S(2)}, u32[]{:S(2)}) collective-permute-start(bf16[8,176,128]{2,1,0:T(8,128)(2,1)} %get-tuple-element.85), channel_id=1, source_target_pairs={{0,4},{2,6},{4,0},{6,2},{8,12},{10,14},{12,8},{14,10},{16,20},{18,... | collective-permute-start | bytes 1081352 | tf_op jit(solution)/shard_map/ppermute | solution.py:783
  52.5 9.0 %collective-permute-start.5 = (bf16[8,144,128]{2,1,0:T(8,128)(2,1)}, bf16[8,144,128]{2,1,0:T(8,128)(2,1)S(1)}, u32[]{:S(2)}, u32[]{:S(2)}) collective-permute-start(bf16[8,144,128]{2,1,0:T(8,128)(2,1)} %get-tuple-element.86), channel_id=1, source_target_pairs={{0,8},{2,10},{4,12},{6,14},{8,0},{10,2},{12,4},{14,6},{16,24},{18,... | collective-permute-start | bytes 884744 | tf_op jit(solution)/shard_map/ppermute | solution.py:783
  53.9 7.6 %copy-start = (f32[8,192,128]{2,1,0:T(8,128)S(1)}, f32[8,192,128]{2,1,0:T(8,128)}, u32[]{:S(2)}) copy-start(f32[8,192,128]{2,1,0:T(8,128)} %get-tuple-element.83.refs_0_) | copy-start | bytes 2359300
  53.9 7.6 %copy-start.1 = (f32[8,176,128]{2,1,0:T(8,128)S(1)}, f32[8,176,128]{2,1,0:T(8,128)}, u32[]{:S(2)}) copy-start(f32[8,176,128]{2,1,0:T(8,128)} %get-tuple-element.92.refs_2_) | copy-start | bytes 2162692
  53.9 7.6 %copy-start.2 = (f32[8,144,128]{2,1,0:T(8,128)S(1)}, f32[8,144,128]{2,1,0:T(8,128)}, u32[]{:S(2)}) copy-start(f32[8,144,128]{2,1,0:T(8,128)} %get-tuple-element.94.refs_4_) | copy-start | bytes 1769476
  61.7 8.9 %collective-permute-start.8 = (bf16[4,144,128]{2,1,0:T(8,128)(2,1)S(1)}, bf16[4,144,128]{2,1,0:T(8,128)(2,1)S(1)}, u32[]{:S(2)}, u32[]{:S(2)}) collective-permute-start(bf16[4,144,128]{2,1,0:T(8,128)(2,1)S(1)} %get-tuple-element.106), channel_id=1, source_target_pairs={{0,2},{2,0},{4,6},{6,4},{8,10},{10,8},{12,14},{14,12},{16,18},{18,... | collective-permute-start | bytes 442376 | tf_op jit(solution)/shard_map/ppermute | solution.py:783
  62.7 8.0 %collective-permute-start.7 = (bf16[4,176,128]{2,1,0:T(8,128)(2,1)S(1)}, bf16[4,176,128]{2,1,0:T(8,128)(2,1)S(1)}, u32[]{:S(2)}, u32[]{:S(2)}) collective-permute-start(bf16[4,176,128]{2,1,0:T(8,128)(2,1)S(1)} %get-tuple-element.105), channel_id=1, source_target_pairs={{0,8},{2,10},{4,12},{6,14},{8,0},{10,2},{12,4},{14,6},{16,24},{18,... | collective-permute-start | bytes 540680 | tf_op jit(solution)/shard_map/ppermute | solution.py:783
  64.1 6.6 %collective-permute-start.6 = (bf16[4,192,128]{2,1,0:T(8,128)(2,1)S(1)}, bf16[4,192,128]{2,1,0:T(8,128)(2,1)S(1)}, u32[]{:S(2)}, u32[]{:S(2)}) collective-permute-start(bf16[4,192,128]{2,1,0:T(8,128)(2,1)S(1)} %get-tuple-element.104), channel_id=1, source_target_pairs={{0,4},{2,6},{4,0},{6,2},{8,12},{10,14},{12,8},{14,10},{16,20},{18,... | collective-permute-start | bytes 589832 | tf_op jit(solution)/shard_map/ppermute | solution.py:783
  70.8 6.0 %collective-permute-start.9 = (bf16[2,192,128]{2,1,0:T(8,128)(2,1)S(1)}, bf16[2,192,128]{2,1,0:T(8,128)(2,1)S(1)}, u32[]{:S(2)}, u32[]{:S(2)}) collective-permute-start(bf16[2,192,128]{2,1,0:T(8,128)(2,1)S(1)} %get-tuple-element.114), channel_id=1, source_target_pairs={{0,8},{2,10},{4,12},{6,14},{8,0},{10,2},{12,4},{14,6},{16,24},{18,... | collective-permute-start | bytes 294920 | tf_op jit(solution)/shard_map/ppermute | solution.py:783
  71.4 5.4 %collective-permute-start.10 = (bf16[2,176,128]{2,1,0:T(8,128)(2,1)S(1)}, bf16[2,176,128]{2,1,0:T(8,128)(2,1)S(1)}, u32[]{:S(2)}, u32[]{:S(2)}) collective-permute-start(bf16[2,176,128]{2,1,0:T(8,128)(2,1)S(1)} %get-tuple-element.115), channel_id=1, source_target_pairs={{0,2},{2,0},{4,6},{6,4},{8,10},{10,8},{12,14},{14,12},{16,18},{18,... | collective-permute-start | bytes 270344 | tf_op jit(solution)/shard_map/ppermute | solution.py:783
  72.5 4.4 %collective-permute-start.11 = (bf16[2,144,128]{2,1,0:T(8,128)(2,1)S(1)}, bf16[2,144,128]{2,1,0:T(8,128)(2,1)S(1)}, u32[]{:S(2)}, u32[]{:S(2)}) collective-permute-start(bf16[2,144,128]{2,1,0:T(8,128)(2,1)S(1)} %get-tuple-element.116), channel_id=1, source_target_pairs={{0,4},{2,6},{4,0},{6,2},{8,12},{10,14},{12,8},{14,10},{16,20},{18,... | collective-permute-start | bytes 221192 | tf_op jit(solution)/shard_map/ppermute | solution.py:783
  76.9 7.5 %collective-permute-start.12 = (bf16[1,512,128]{2,1,0:T(8,128)(2,1)S(1)}, bf16[1,512,128]{2,1,0:T(8,128)(2,1)S(1)}, u32[]{:S(2)}, u32[]{:S(2)}) collective-permute-start(bf16[1,512,128]{2,1,0:T(8,128)(2,1)S(1)} %get-tuple-element.124), channel_id=1, source_target_pairs={{0,16},{2,18},{4,20},{6,22},{8,24},{10,26},{12,28},{14,30},{16,0},... | collective-permute-start | bytes 393224 | tf_op jit(solution)/shard_map/ppermute | solution.py:783
